TPU v7x, 32 devices: a whole 2x2x4 slice. The times are simulated.
32 devices in a mesh: bucket: 8 (over y, x, core), fsdp: 4 (over z).
Axes of the slice: x: 2, y: 2, z: 4, core: 2. Of those that a mesh axis runs over, the one named last changes fastest.
Arguments:
- inputs: bfloat16 [16384, 1152], P(('bucket', 'fsdp')), may hold values from -6 to 6
- condition: bfloat16 [256, 1152], P(('bucket', 'fsdp')), may hold values from -6 to 6
- segment_ids: int32 [16384], P(('bucket', 'fsdp')), may hold values from 0 to 7, as said below
- grid_widths: int32 [256], P(('bucket', 'fsdp')), may hold values from 0 to 32, as said below
- bucket_counts: int32 [8], replicated, may hold values from 512 to 2048
- modulate_weight: bfloat16 [1152, 6912], P('fsdp'), may hold values from -0.1875 to 0.1875
- joint_weight: bfloat16 [1152, 3456], P('fsdp'), may hold values from -0.1875 to 0.1875
- project_weight: bfloat16 [1152, 1152], P('fsdp'), may hold values from -2 to 2
- gate_weight: bfloat16 [1152, 3072], P('fsdp'), may hold values from -0.1875 to 0.1875
- up_weight: bfloat16 [1152, 3072], P('fsdp'), may hold values from -0.1875 to 0.1875
- down_weight: bfloat16 [3072, 1152], P('fsdp'), may hold values from -0.109375 to 0.109375
- cotangent: bfloat16 [16384, 1152], P(('bucket', 'fsdp')), may hold values from -6 to 6
Outputs:
- output: bfloat16 [16384, 1152], P(('bucket', 'fsdp'))
- grad_inputs: float32 [16384, 1152], P(('bucket', 'fsdp'))
- grad_condition: float32 [256, 1152], P(('bucket', 'fsdp'))
- modulate_gradient: float32 [1152, 6912], P('fsdp')
- joint_gradient: float32 [1152, 3456], P('fsdp')
- project_gradient: float32 [1152, 1152], P('fsdp')
- gate_gradient: float32 [1152, 3072], P('fsdp')
- up_gradient: float32 [1152, 3072], P('fsdp')
- down_gradient: float32 [3072, 1152], P('fsdp')
Inputs may be any that keep to these rules, and one draw needn't show every extreme that they name: `segment_ids`: each device's 512 tokens are whole images numbered 0, 1, 2, ... in order on that device; an image has 64, 128 or 256 tokens and never crosses a multiple of 256 tokens. `grid_widths`: an image's grid height is its token count divided by its width, from a quarter to four times the width; slots past a device's last image hold 0.
All inputs are finite; a program needn't handle non-finite values.
Results may differ from a plain program's by a relative error of at most 0.02.
The roundings to bfloat16 on the way count: a program that leaves them out, or rounds other values in their place, can miss the bound.
Values may be sent and summed in bfloat16 or wider, within the bound.
No kernel may reach another device: no remote copies, remote signals or barrier semaphores. Data moves between devices by JAX's collectives and lax.ppermute only.
A program may use at most 384 MiB of HBM per device.

v0:
```python
import jax
import jax.numpy as jnp
from jax import lax
from jax.sharding import PartitionSpec as P

HEADS = 16
HEAD_DIM = 72


epsilon = 1e-06
masked_score = -1e30


def rope_tables(segments, widths, quarter):
    slots = widths.shape[0]
    one_hot = (segments[:, None] == jnp.arange(slots, dtype=jnp.int32)[None, :]).astype(jnp.int32)
    counts = jnp.sum(one_hot, axis=0)
    starts = jnp.cumsum(counts) - counts
    start_token = jnp.sum(one_hot * starts[None, :], axis=1)
    width_token = jnp.maximum(jnp.sum(one_hot * widths[None, :], axis=1), 1)
    place = jnp.arange(segments.shape[0], dtype=jnp.int32) - start_token
    row_place = (place // width_token).astype(jnp.float32)
    col_place = (place % width_token).astype(jnp.float32)
    freqs = 10000.0 ** (-jnp.arange(quarter, dtype=jnp.float32) / quarter)
    angle_row = row_place[:, None] * freqs[None, :]
    angle_col = col_place[:, None] * freqs[None, :]
    return (jnp.cos(angle_row), jnp.sin(angle_row), jnp.cos(angle_col), jnp.sin(angle_col))


def rotate(values, tables, direction):
    cos_row, sin_row, cos_col, sin_col = tables
    quarter = cos_row.shape[-1]
    first_part = values[..., :quarter]
    second_part = values[..., quarter : 2 * quarter]
    third_part = values[..., 2 * quarter : 3 * quarter]
    fourth_part = values[..., 3 * quarter :]
    return jnp.concatenate(
        [
            first_part * cos_row - direction * second_part * sin_row,
            second_part * cos_row + direction * first_part * sin_row,
            third_part * cos_col - direction * fourth_part * sin_col,
            fourth_part * cos_col + direction * third_part * sin_col,
        ],
        axis=-1,
    )


def normalize(values):
    average = jnp.mean(values, axis=-1, keepdims=True)
    centered = values - average
    inverse = lax.rsqrt(jnp.mean(centered * centered, axis=-1, keepdims=True) + epsilon)
    return (centered * inverse, inverse)


def normalize_back(normed, inverse, upstream):
    return inverse * (
        upstream
        - jnp.mean(upstream, axis=-1, keepdims=True)
        - normed * jnp.mean(upstream * normed, axis=-1, keepdims=True)
    )


def matmul(left, right):
    return jnp.dot(left, right, preferred_element_type=jnp.float32)


def contract_rows(left, right):
    return lax.dot_general(
        left, right, (((0,), (0,)), ((), ())), preferred_element_type=jnp.float32
    )


def times_transposed(left, right):
    return lax.dot_general(
        left, right, (((1,), (1,)), ((), ())), preferred_element_type=jnp.float32
    )


def silu_slope(values):
    sigmoid = jax.nn.sigmoid(values)
    return sigmoid * (1.0 + values * (1.0 - sigmoid))


def on_device(
    inputs,
    condition,
    segment_ids,
    grid_widths,
    bucket_counts,
    modulate_weight,
    joint_weight,
    project_weight,
    gate_weight,
    up_weight,
    down_weight,
    cotangent,
):
    joint_full, project_full, gate_full, up_full, down_full = (
        lax.all_gather(joint_weight, "fsdp", axis=0, tiled=True),
        lax.all_gather(project_weight, "fsdp", axis=0, tiled=True),
        lax.all_gather(gate_weight, "fsdp", axis=0, tiled=True),
        lax.all_gather(up_weight, "fsdp", axis=0, tiled=True),
        lax.all_gather(down_weight, "fsdp", axis=0, tiled=True),
    )
    tokens, width = inputs.shape
    slots = condition.shape[0]
    heads = HEADS
    head_size = HEAD_DIM
    scaling = head_size ** (-0.5)
    tables = tuple(
        (table[:, None, :] for table in rope_tables(segment_ids, grid_widths, head_size // 4))
    )
    one_hot = (segment_ids[:, None] == jnp.arange(slots, dtype=jnp.int32)[None, :]).astype(
        jnp.float32
    )
    cond_float = condition.astype(jnp.float32)
    lifted = jax.nn.silu(cond_float).astype(jnp.bfloat16)
    modulate_full = lax.all_gather(modulate_weight, "fsdp", axis=0, tiled=True)
    modulation = matmul(lifted, modulate_full)
    per_token = jnp.dot(
        one_hot, modulation, precision=lax.Precision.HIGHEST, preferred_element_type=jnp.float32
    )
    shift_one, scale_one, gate_one, shift_two, scale_two, gate_two = jnp.split(per_token, 6, axis=1)
    residual = inputs.astype(jnp.float32)
    normed_one, inverse_one = normalize(residual)
    first = (normed_one * (1.0 + scale_one) + shift_one).astype(jnp.bfloat16)
    joint = matmul(first, joint_full).reshape(tokens, 3, heads, head_size)
    query = rotate(joint[:, 0], tables, 1.0).astype(jnp.bfloat16)
    keys = rotate(joint[:, 1], tables, 1.0).astype(jnp.bfloat16)
    values = joint[:, 2].astype(jnp.bfloat16)
    rows = min(tokens, 512)
    starts = jnp.arange(tokens // rows, dtype=jnp.int32) * rows

    def block_scores():
        scores = (
            jnp.einsum("qhd,khd->hqk", query, keys, preferred_element_type=jnp.float32) * scaling
        )
        allowed = segment_ids[:, None] == segment_ids[None, :]
        return (query, keys, jnp.where(allowed[None], scores, masked_score))

    def attend(start):
        query_block, keys_block, scores = block_scores()
        highest = jnp.max(scores, axis=-1, keepdims=True)
        exponent = jnp.exp(scores - highest)
        totals = jnp.sum(exponent, axis=-1, keepdims=True)
        probs = (exponent / totals).astype(jnp.bfloat16)
        mixed = jnp.einsum("hqk,khd->qhd", probs, values, preferred_element_type=jnp.float32)
        return (mixed, highest + jnp.log(totals))

    mixed, log_totals = lax.map(attend, starts)
    attended = mixed.reshape(tokens, width).astype(jnp.bfloat16)
    branch = matmul(attended, project_full)
    middle = residual + gate_one * branch
    normed_two, inverse_two = normalize(middle)
    second = (normed_two * (1.0 + scale_two) + shift_two).astype(jnp.bfloat16)
    gate = matmul(second, gate_full)
    upval = matmul(second, up_full)
    hidden = (jax.nn.silu(gate) * upval).astype(jnp.bfloat16)
    feed = matmul(hidden, down_full)
    output = (middle + gate_two * feed).astype(jnp.bfloat16)
    joint_full, project_full, gate_full, up_full, down_full = (
        lax.all_gather(joint_weight, "fsdp", axis=0, tiled=True),
        lax.all_gather(project_weight, "fsdp", axis=0, tiled=True),
        lax.all_gather(gate_weight, "fsdp", axis=0, tiled=True),
        lax.all_gather(up_weight, "fsdp", axis=0, tiled=True),
        lax.all_gather(down_weight, "fsdp", axis=0, tiled=True),
    )
    counts = bucket_counts.astype(jnp.float32)
    bucket = lax.axis_index("bucket")
    mine = jnp.sum(jnp.where(jnp.arange(counts.shape[0], dtype=jnp.int32) == bucket, counts, 0.0))
    upstream = cotangent.astype(jnp.float32) * (mine * counts.shape[0] / jnp.sum(counts))
    feed_back = (upstream * gate_two).astype(jnp.bfloat16)
    down_gradient = contract_rows(hidden, feed_back)
    hidden_back = times_transposed(feed_back, down_full)
    up_back = (hidden_back * jax.nn.silu(gate)).astype(jnp.bfloat16)
    gate_back = (hidden_back * upval * silu_slope(gate)).astype(jnp.bfloat16)
    gate_gradient = contract_rows(second, gate_back)
    up_gradient = contract_rows(second, up_back)
    second_back = times_transposed(gate_back, gate_full) + times_transposed(up_back, up_full)
    middle_back = upstream + normalize_back(
        normed_two, inverse_two, second_back * (1.0 + scale_two)
    )
    branch_back = (middle_back * gate_one).astype(jnp.bfloat16)
    project_gradient = contract_rows(attended, branch_back)
    attended_back = (
        times_transposed(branch_back, project_full)
        .astype(jnp.bfloat16)
        .reshape(tokens, heads, head_size)
    )

    def attend_back(item):
        start, log_total = item
        query_block, keys_block, scores = block_scores()
        probs = jnp.exp(scores - log_total)
        probs_back = jnp.einsum(
            "qhd,khd->hqk", attended_back, values, preferred_element_type=jnp.float32
        )
        scores_back = (
            probs * (probs_back - jnp.sum(probs * probs_back, axis=-1, keepdims=True))
        ).astype(jnp.bfloat16)
        query_back = (
            jnp.einsum("hqk,khd->qhd", scores_back, keys_block, preferred_element_type=jnp.float32)
            * scaling
        )
        keys_back = (
            jnp.einsum("hqk,qhd->khd", scores_back, query_block, preferred_element_type=jnp.float32)
            * scaling
        )
        values_back = jnp.einsum(
            "hqk,qhd->khd",
            probs.astype(jnp.bfloat16),
            attended_back,
            preferred_element_type=jnp.float32,
        )
        return (query_back, keys_back, values_back)

    query_back, keys_back, values_back = lax.map(attend_back, (starts, log_totals))
    query_back = query_back.reshape(tokens, heads, head_size)
    keys_back = keys_back.reshape(tokens, heads, head_size)
    values_back = values_back.reshape(tokens, heads, head_size)
    joint_back = (
        jnp.stack(
            [rotate(query_back, tables, -1.0), rotate(keys_back, tables, -1.0), values_back], axis=1
        )
        .reshape(tokens, 3 * width)
        .astype(jnp.bfloat16)
    )
    joint_gradient = contract_rows(first, joint_back)
    first_back = times_transposed(joint_back, joint_full)
    grad_inputs = middle_back + normalize_back(
        normed_one, inverse_one, first_back * (1.0 + scale_one)
    )
    per_token_back = jnp.concatenate(
        [
            first_back,
            first_back * normed_one,
            middle_back * branch,
            second_back,
            second_back * normed_two,
            upstream * feed,
        ],
        axis=1,
    )
    modulation_back = lax.dot_general(
        one_hot,
        per_token_back,
        (((0,), (0,)), ((), ())),
        precision=lax.Precision.HIGHEST,
        preferred_element_type=jnp.float32,
    ).astype(jnp.bfloat16)
    modulate_rows = lax.psum_scatter(
        contract_rows(lifted, modulation_back).astype(jnp.bfloat16),
        "fsdp",
        scatter_dimension=0,
        tiled=True,
    )
    condition_slope = times_transposed(modulation_back, modulate_full)
    grad_condition = condition_slope * silu_slope(cond_float)
    modulate_gradient = lax.psum(modulate_rows, "bucket").astype(jnp.float32)
    fsdp_count = lax.axis_size("fsdp")
    bucket_count = lax.axis_size("bucket")

    def reorder(matrix):
        height, breadth = matrix.shape
        return (
            matrix.reshape(fsdp_count, bucket_count, height // (fsdp_count * bucket_count), breadth)
            .swapaxes(0, 1)
            .reshape(height, breadth)
        )

    pieces = (
        lax.psum_scatter(
            reorder(joint_gradient), ("bucket", "fsdp"), scatter_dimension=0, tiled=True
        ),
        lax.psum_scatter(
            reorder(project_gradient), ("bucket", "fsdp"), scatter_dimension=0, tiled=True
        ),
        lax.psum_scatter(
            reorder(gate_gradient), ("bucket", "fsdp"), scatter_dimension=0, tiled=True
        ),
        lax.psum_scatter(reorder(up_gradient), ("bucket", "fsdp"), scatter_dimension=0, tiled=True),
        lax.psum_scatter(
            reorder(down_gradient), ("bucket", "fsdp"), scatter_dimension=0, tiled=True
        ),
    )
    shares = (
        lax.all_gather(pieces[0].astype(jnp.bfloat16), "bucket", axis=0, tiled=True).astype(
            jnp.float32
        ),
        lax.all_gather(pieces[1].astype(jnp.bfloat16), "bucket", axis=0, tiled=True).astype(
            jnp.float32
        ),
        lax.all_gather(pieces[2].astype(jnp.bfloat16), "bucket", axis=0, tiled=True).astype(
            jnp.float32
        ),
        lax.all_gather(pieces[3].astype(jnp.bfloat16), "bucket", axis=0, tiled=True).astype(
            jnp.float32
        ),
        lax.all_gather(pieces[4].astype(jnp.bfloat16), "bucket", axis=0, tiled=True).astype(
            jnp.float32
        ),
    )
    return (
        output,
        grad_inputs,
        grad_condition,
        modulate_gradient,
        shares[0],
        shares[1],
        shares[2],
        shares[3],
        shares[4],
    )


def solution(mesh):
    in_specs = (
        P(("bucket", "fsdp"), None),
        P(("bucket", "fsdp"), None),
        P(("bucket", "fsdp")),
        P(("bucket", "fsdp")),
        P(),
        P("fsdp", None),
        P("fsdp", None),
        P("fsdp", None),
        P("fsdp", None),
        P("fsdp", None),
        P("fsdp", None),
        P(("bucket", "fsdp"), None),
    )
    out_specs = (
        P(("bucket", "fsdp"), None),
        P(("bucket", "fsdp"), None),
        P(("bucket", "fsdp"), None),
        P("fsdp", None),
        P("fsdp", None),
        P("fsdp", None),
        P("fsdp", None),
        P("fsdp", None),
        P("fsdp", None),
    )
    return jax.shard_map(
        on_device, mesh=mesh, in_specs=in_specs, out_specs=out_specs, check_vma=False
    )
```

profile of v0, /device:TPU:25, one launch (start us, length us, event | category | flops | bytes accessed | tf_op | source)
XLA Modules:
  0.0 2944.8 jit_solution(11033708485431027990)
XLA Ops:
  15.8 264.8 %all-gather.15.cloned.1.call-done = bf16[1152,6912]{1,0:T(8,128)(2,1)} async-done(((bf16[288,6912]{1,0:T(8,128)(2,1)}), bf16[1152,6912]{1,0:T(8,128)(2,1)}) %all-gather.15.cloned.1.call-update) | async-done | bytes 15925264 | tf_op jit(solution)/shard_map/all_gather | solution.py:118
  299.9 123.1 %all-gather.17.cloned.1.call-done = bf16[1152,3456]{1,0:T(8,128)(2,1)} async-done(((bf16[288,3456]{1,0:T(8,128)(2,1)}), bf16[1152,3456]{1,0:T(8,128)(2,1)}) %all-gather.17.cloned.1.call-update) | async-done | bytes 7962640 | tf_op jit(solution)/shard_map/all_gather | solution.py:99
  462.0 16.8 all-gather.19.cloned.1.call-done
  491.7 115.0 %all-gather.21.cloned.1.call-done = bf16[1152,3072]{1,0:T(8,128)(2,1)} async-done(((bf16[288,3072]{1,0:T(8,128)(2,1)}), bf16[1152,3072]{1,0:T(8,128)(2,1)}) %all-gather.21.cloned.1.call-update) | async-done | bytes 7077904 | tf_op jit(solution)/shard_map/all_gather | solution.py:101
  617.0 117.6 %all-gather.23.cloned.1.call-done = bf16[1152,3072]{1,0:T(8,128)(2,1)} async-done(((bf16[288,3072]{1,0:T(8,128)(2,1)}), bf16[1152,3072]{1,0:T(8,128)(2,1)}) %all-gather.23.cloned.1.call-update) | async-done | bytes 7077904 | tf_op jit(solution)/shard_map/all_gather | solution.py:102
  745.2 117.3 %all-gather.25.cloned.1.call-done = bf16[3072,1152]{1,0:T(8,128)(2,1)} async-done(((bf16[768,1152]{1,0:T(8,128)(2,1)}), bf16[3072,1152]{1,0:T(8,128)(2,1)}) %all-gather.25.cloned.1.call-update) | async-done | bytes 7077904 | tf_op jit(solution)/shard_map/all_gather | solution.py:103
  862.5 13.2 multiply_convert_fusion.1
  912.6 12.3 multiply_convert_fusion.4
  932.1 14.2 multiply_reduce_fusion
  946.3 13.3 multiply_convert_fusion
  978.9 11.9 fusion.61
  1029.6 17.7 reshape.317
  1069.6 12.7 reshape.319
  1082.3 13.5 copy.69
  1095.9 12.9 reshape.320
  1108.7 1139.3 %fusion.62 = (f32[48,3456]{1,0:T(8,128)S(1)}, f32[48,1152]{1,0:T(8,128)S(1)}, f32[40,3072]{1,0:T(8,128)S(1)}) fusion(f32[1152,3456]{1,0:T(8,128)} %reshape.317, f32[1152,1152]{1,0:T(8,128)} %reshape.318, f32[1152,3072]{1,0:T(8,128)} %reshape.320), kind=kCustom, calls=%all-reduce-scatter.4 | all-reduce-scatter fusion | flops 11010050 | bytes 36765696
  2273.0 12.7 reshape.321
  2285.6 13.4 copy.70
  2299.1 12.8 reshape.322
  2317.4 334.6 %fusion.3 = f32[40,3072]{1,0:T(8,128)S(1)} fusion(f32[1152,3072]{1,0:T(8,128)} %reshape.322), kind=kCustom, calls=%all-reduce-scatter.3 | all-reduce-scatter fusion | flops 3932161 | bytes 14647296
  2712.1 16.6 collective-permute-start.1
  2732.5 14.3 collective-permute-done.1
  2746.8 32.2 %concatenate.22 = bf16[420,3456]{1,0:T(8,128)(2,1)} concatenate(bf16[36,3456]{1,0:T(8,128)(2,1)} %copy-done.41, bf16[48,3456]{1,0:T(8,128)(2,1)S(1)} %collective-permute-done.6, bf16[48,3456]{1,0:T(8,128)(2,1)S(1)} %collective-permute-done.5, bf16[48,3456]{1,0:T(8,128)(2,1)S(1)} %collective-permute-done.4, bf16[48,3456]{1,0:T(8,128)(2,1)S(1)} %collective-permute-done.3, ...), dimensions={0} | concatenate | bytes 6137856
  2853.4 78.8 %all-reduce.11.cloned.1.call-done = bf16[288,6912]{1,0:T(8,128)(2,1)} async-done(((bf16[288,6912]{1,0:T(8,128)(2,1)}), bf16[288,6912]{1,0:T(8,128)(2,1)}) %all-reduce.11.cloned.1.call-update) | async-done | bytes 3981328 | tf_op jit(solution)/shard_map/psum | solution.py:259
  (286 shorter events, 397.0 us)
Async XLA Ops:
  7.2 273.4 %all-gather.15.cloned.1.call-start = ((), (), s32[]{:S(2)}) async-start(), calls=%async_computation.2 | async-start | bytes 19906560 | tf_op jit(solution)/shard_map/all_gather | solution.py:118
  7.9 415.2 %all-gather.17.cloned.1.call-start = ((), (), s32[]{:S(2)}) async-start(), calls=%async_computation.3 | async-start | bytes 9953280 | tf_op jit(solution)/shard_map/all_gather | solution.py:99
  8.7 470.2 %all-gather.19.cloned.1.call-start = ((), (), s32[]{:S(2)}) async-start(), calls=%async_computation.4 | async-start | bytes 3317760 | tf_op jit(solution)/shard_map/all_gather | solution.py:100
  9.4 597.3 %all-gather.21.cloned.1.call-start = ((), (), s32[]{:S(2)}) async-start(), calls=%async_computation.5 | async-start | bytes 8847360 | tf_op jit(solution)/shard_map/all_gather | solution.py:101
  10.0 724.6 %all-gather.23.cloned.1.call-start = ((), (), s32[]{:S(2)}) async-start(), calls=%async_computation.6 | async-start | bytes 8847360 | tf_op jit(solution)/shard_map/all_gather | solution.py:102
  10.6 851.9 %all-gather.25.cloned.1.call-start = ((), (), s32[]{:S(2)}) async-start(), calls=%async_computation.7 | async-start | bytes 8847360 | tf_op jit(solution)/shard_map/all_gather | solution.py:103
  11.2 2769.7 %reduce-scatter.13.cloned.1.call-start = ((), (), s32[]{:S(2)}) async-start(), calls=%async_computation.10 | async-start | bytes 14598144 | tf_op jit(solution)/shard_map/reduce_scatter | solution.py:282
  894.4 1888.3 %reduce-scatter.11.cloned.1.call-start = ((), (), s32[]{:S(2)}) async-start(), calls=%async_computation.8 | async-start | bytes 19906560 | tf_op jit(solution)/shard_map/reduce_scatter | solution.py:251
  1013.8 1824.7 %all-gather.31.cloned.1.call-start = ((), (), s32[]{:S(2)}) async-start(), calls=%async_computation.13 | async-start | bytes 2211840 | tf_op jit(solution)/shard_map/all_gather | solution.py:293
  2248.1 63.8 %collective-permute-start.18 = (bf16[40,3072]{1,0:T(8,128)(2,1)S(1)}, bf16[40,3072]{1,0:T(8,128)(2,1)S(1)}, u32[]{:S(2)}, u32[]{:S(2)}) collective-permute-start(bf16[40,3072]{1,0:T(8,128)(2,1)S(1)} %convert.91), channel_id=1, source_target_pairs={{0,3},{1,4},{2,5},{3,6},{4,7},{5,8},{6,9},{7,10},{8,11},{9,12},{10... | collective-permute-start | bytes 737288
  2250.0 61.9 %collective-permute-start.17 = (bf16[40,3072]{1,0:T(8,128)(2,1)S(1)}, bf16[40,3072]{1,0:T(8,128)(2,1)}, u32[]{:S(2)}, u32[]{:S(2)}) collective-permute-start(bf16[40,3072]{1,0:T(8,128)(2,1)S(1)} %convert.91), channel_id=1, source_target_pairs={{0,2},{1,3},{2,4},{3,5},{4,6},{5,7},{6,8},{7,9},{8,10},{9,11},{10,... | collective-permute-start | bytes 737288
  2257.1 54.8 %collective-permute-start.16 = (bf16[40,3072]{1,0:T(8,128)(2,1)S(1)}, bf16[40,3072]{1,0:T(8,128)(2,1)}, u32[]{:S(2)}, u32[]{:S(2)}) collective-permute-start(bf16[40,3072]{1,0:T(8,128)(2,1)S(1)} %convert.91), channel_id=1, source_target_pairs={{0,1},{1,2},{2,3},{3,4},{4,5},{5,6},{6,7},{7,8},{8,9},{9,10},{10,1... | collective-permute-start | bytes 737288
  2259.1 52.8 %collective-permute-start.19 = (bf16[4,3072]{1,0:T(4,128)(2,1)S(1)}, bf16[4,3072]{1,0:T(4,128)(2,1)S(1)}, u32[]{:S(2)}, u32[]{:S(2)}) collective-permute-start(bf16[4,3072]{1,0:T(4,128)(2,1)S(1)} %slice.98), channel_id=1, source_target_pairs={{0,4},{1,5},{2,6},{3,7},{4,8},{5,9},{6,10},{7,11},{8,12},{9,13},{1... | collective-permute-start | bytes 73736
  2317.4 524.3 %all-gather.33.cloned.1.call-start = ((), (), s32[]{:S(2)}) async-start(), calls=%async_computation.14 | async-start | bytes 2211840 | tf_op jit(solution)/shard_map/all_gather | solution.py:296
  2680.1 164.7 %all-gather.29.cloned.1.call-start = ((), (), s32[]{:S(2)}) async-start(), calls=%async_computation.12 | async-start | bytes 2488320 | tf_op jit(solution)/shard_map/all_gather | solution.py:287
  2680.2 31.9 %collective-permute-start.6 = (bf16[48,3456]{1,0:T(8,128)(2,1)S(1)}, bf16[48,3456]{1,0:T(8,128)(2,1)S(1)}, u32[]{:S(2)}, u32[]{:S(2)}) collective-permute-start(bf16[48,3456]{1,0:T(8,128)(2,1)S(1)} %convert.89), channel_id=1, source_target_pairs={{0,7},{1,8},{2,9},{3,10},{4,11},{5,12},{6,13},{7,14},{8,15},{9,16}... | collective-permute-start | bytes 995336
  2687.0 41.8 %collective-permute-start.5 = (bf16[48,3456]{1,0:T(8,128)(2,1)S(1)}, bf16[48,3456]{1,0:T(8,128)(2,1)S(1)}, u32[]{:S(2)}, u32[]{:S(2)}) collective-permute-start(bf16[48,3456]{1,0:T(8,128)(2,1)S(1)} %convert.89), channel_id=1, source_target_pairs={{0,6},{1,7},{2,8},{3,9},{4,10},{5,11},{6,12},{7,13},{8,14},{9,15},... | collective-permute-start | bytes 995336
  2690.3 40.4 %collective-permute-start.4 = (bf16[48,3456]{1,0:T(8,128)(2,1)S(1)}, bf16[48,3456]{1,0:T(8,128)(2,1)S(1)}, u32[]{:S(2)}, u32[]{:S(2)}) collective-permute-start(bf16[48,3456]{1,0:T(8,128)(2,1)S(1)} %convert.89), channel_id=1, source_target_pairs={{0,5},{1,6},{2,7},{3,8},{4,9},{5,10},{6,11},{7,12},{8,13},{9,14},{... | collective-permute-start | bytes 995336
  2694.3 36.4 %collective-permute-start.3 = (bf16[48,3456]{1,0:T(8,128)(2,1)S(1)}, bf16[48,3456]{1,0:T(8,128)(2,1)S(1)}, u32[]{:S(2)}, u32[]{:S(2)}) collective-permute-start(bf16[48,3456]{1,0:T(8,128)(2,1)S(1)} %convert.89), channel_id=1, source_target_pairs={{0,4},{1,5},{2,6},{3,7},{4,8},{5,9},{6,10},{7,11},{8,12},{9,13},{1... | collective-permute-start | bytes 995336
  2712.1 34.6 %collective-permute-start.1 = (bf16[48,3456]{1,0:T(8,128)(2,1)S(1)}, bf16[48,3456]{1,0:T(8,128)(2,1)}, u32[]{:S(2)}, u32[]{:S(2)}) collective-permute-start(bf16[48,3456]{1,0:T(8,128)(2,1)S(1)} %convert.89), channel_id=1, source_target_pairs={{0,2},{1,3},{2,4},{3,5},{4,6},{5,7},{6,8},{7,9},{8,10},{9,11},{10,... | collective-permute-start | bytes 995336
  2780.8 69.1 %all-gather.27.cloned.1.call-start = ((), (), s32[]{:S(2)}) async-start(), calls=%async_computation.11 | async-start | bytes 1990656 | tf_op jit(solution)/shard_map/all_gather | solution.py:299
  2782.6 149.5 %all-reduce.11.cloned.1.call-start = ((), (), s32[]{:S(2)}) async-start(), calls=%async_computation.9 | async-start | bytes 7962624 | tf_op jit(solution)/shard_map/psum | solution.py:259
  2792.2 32.2 %collective-permute-start.12 = (bf16[48,1152]{1,0:T(8,128)(2,1)S(1)}, bf16[48,1152]{1,0:T(8,128)(2,1)S(1)}, u32[]{:S(2)}, u32[]{:S(2)}) collective-permute-start(bf16[48,1152]{1,0:T(8,128)(2,1)S(1)} %convert.92), channel_id=1, source_target_pairs={{0,5},{1,6},{2,7},{3,8},{4,9},{5,10},{6,11},{7,12},{8,13},{9,14},{... | collective-permute-start | bytes 331784
  2794.8 29.7 %collective-permute-start.11 = (bf16[48,1152]{1,0:T(8,128)(2,1)S(1)}, bf16[48,1152]{1,0:T(8,128)(2,1)S(1)}, u32[]{:S(2)}, u32[]{:S(2)}) collective-permute-start(bf16[48,1152]{1,0:T(8,128)(2,1)S(1)} %convert.92), channel_id=1, source_target_pairs={{0,4},{1,5},{2,6},{3,7},{4,8},{5,9},{6,10},{7,11},{8,12},{9,13},{1... | collective-permute-start | bytes 331784
  (72 other events, 2338.4 us)
Sparse Core Ops, SparseCore 0:
  9.6 270.9 all-gather.14
  282.2 140.8 all-gather.16
  424.7 54.1 all-gather.18
  480.2 126.4 all-gather.20
  608.1 126.4 all-gather.22
  736.0 126.4 all-gather.24
  894.5 160.5 reduce-scatter.12
  1057.5 473.6 reduce-scatter.10
  2317.5 29.6 all-gather.30
  2680.2 44.7 all-gather.32
  2780.9 38.1 all-gather.28
  2821.6 28.2 all-gather.26
  2853.7 78.4 all-reduce.10
where the time goes:
time: 2960 us; the launch traced here: 2940 us
  blocking collectives  1480 us (50%)
  waiting for transfers between devices  872 us (29%)
  matrix products  211 us (7%)
  local copies, waits for them, and re-layouts  204 us (7%)
  starting transfers between devices  102 us (3%)
  other arithmetic  55.4 us (2%)
    unnamed x2, blocking collectives  1470 us
    all_gather x1, waiting for transfers between devices, on_device(): modulate_full = lax.all_gather(modulate_weight, 'fsdp', axis=0, tiled=True)  265 us
    all_gather x1, waiting for transfers between devices, on_device(): lax.all_gather(joint_weight, 'fsdp', axis=0, tiled=True)  123 us
    all_gather x1, waiting for transfers between devices, on_device(): lax.all_gather(up_weight, 'fsdp', axis=0, tiled=True)  118 us
    all_gather x1, waiting for transfers between devices, on_device(): lax.all_gather(down_weight, 'fsdp', axis=0, tiled=True)  117 us
    all_gather x1, waiting for transfers between devices, on_device(): lax.all_gather(gate_weight, 'fsdp', axis=0, tiled=True)  115 us
    unnamed x24, starting transfers between devices  101 us
    psum x1, waiting for transfers between devices, on_device(): modulate_gradient = lax.psum(modulate_rows, 'bucket').astype(jnp.float32)  78.8 us
  transfers between devices with their start and end apart: 37, of which 14 were waited for; matrix products, arithmetic and copies ran while one was open for 64% of the time, Pallas kernels for 0%

commit v1 on v0

--- a/solution.py
+++ b/solution.py
@@ -81,6 +81,52 @@
     return sigmoid * (1.0 + values * (1.0 - sigmoid))
 
 
+BLOCK = 256
+
+
+def shifts(count, by):
+    return [(i, (i + by) % count) for i in range(count)]
+
+
+def pick(array, index):
+    return lax.dynamic_index_in_dim(array, index, 0, keepdims=False)
+
+
+def gather_pieces(piece, own):
+    count = lax.axis_size("fsdp")
+    place = lax.axis_index("fsdp")
+    foreign = jnp.stack(
+        [lax.ppermute(piece, "fsdp", shifts(count, by)) for by in range(1, count)]
+    )
+    everyone = lax.all_gather(foreign, "bucket", axis=0, tiled=False)
+    relative = [own] + [everyone[:, by - 1] for by in range(1, count)]
+    relative = jnp.stack(relative)
+    return jnp.stack([pick(relative, (place - j) % count) for j in range(count)])
+
+
+def reduce_pieces(parts):
+    count = lax.axis_size("fsdp")
+    place = lax.axis_index("fsdp")
+    mine = lax.psum_scatter(parts, "bucket", scatter_dimension=0, tiled=False)
+    total = pick(mine, place).astype(jnp.float32)
+    for by in range(1, count):
+        total = total + lax.ppermute(
+            pick(mine, (place + by) % count), "fsdp", shifts(count, by)
+        ).astype(jnp.float32)
+    return lax.all_gather(total.astype(jnp.bfloat16), "bucket", axis=0, tiled=False)
+
+
+def to_group(rows, count, place):
+    relative = jnp.stack(
+        [pick(rows, place)]
+        + [
+            lax.ppermute(pick(rows, (place + by) % count), "fsdp", shifts(count, by))
+            for by in range(1, count)
+        ]
+    )
+    return jnp.stack([pick(relative, (place - j) % count) for j in range(count)])
+
+
 def on_device(
     inputs,
     condition,
@@ -95,13 +141,44 @@
     down_weight,
     cotangent,
 ):
-    joint_full, project_full, gate_full, up_full, down_full = (
-        lax.all_gather(joint_weight, "fsdp", axis=0, tiled=True),
-        lax.all_gather(project_weight, "fsdp", axis=0, tiled=True),
-        lax.all_gather(gate_weight, "fsdp", axis=0, tiled=True),
-        lax.all_gather(up_weight, "fsdp", axis=0, tiled=True),
-        lax.all_gather(down_weight, "fsdp", axis=0, tiled=True),
-    )
+    fsdp_count = lax.axis_size("fsdp")
+    bucket_count = lax.axis_size("bucket")
+    place = lax.axis_index("fsdp")
+    bucket = lax.axis_index("bucket")
+    columns = bucket_count // 2
+    height = joint_weight.shape[0]
+    width = inputs.shape[1]
+    ff = gate_weight.shape[1]
+    down_rows = down_weight.shape[0] // bucket_count
+    attn_shard = (
+        jnp.concatenate([joint_weight, project_weight], axis=1)
+        .reshape(2, height // 2, columns, 4 * width // columns)
+        .transpose(2, 0, 1, 3)
+        .reshape(bucket_count, height // 2, 4 * width // columns)
+    )
+    ffn_shard = jnp.stack(
+        [
+            gate_weight.reshape(height, columns, ff // columns).transpose(1, 0, 2),
+            up_weight.reshape(height, columns, ff // columns).transpose(1, 0, 2),
+        ],
+        axis=1,
+    ).reshape(bucket_count, height, ff // columns)
+    down_shard = down_weight.reshape(bucket_count, down_rows, width)
+    attn_full = gather_pieces(pick(attn_shard, bucket), attn_shard)
+    attn_full = (
+        attn_full.reshape(fsdp_count, columns, 2, height // 2, 4 * width // columns)
+        .transpose(0, 2, 3, 1, 4)
+        .reshape(width, 4 * width)
+    )
+    joint_full, project_full = attn_full[:, : 3 * width], attn_full[:, 3 * width :]
+    ffn_full = gather_pieces(pick(ffn_shard, bucket), ffn_shard)
+    ffn_full = (
+        ffn_full.reshape(fsdp_count, columns, 2, height, ff // columns)
+        .transpose(2, 0, 3, 1, 4)
+        .reshape(2, width, ff)
+    )
+    gate_full, up_full = ffn_full[0], ffn_full[1]
+    down_full = gather_pieces(pick(down_shard, bucket), down_shard).reshape(ff, width)
     tokens, width = inputs.shape
     slots = condition.shape[0]
     heads = HEADS
@@ -115,8 +192,17 @@
     )
     cond_float = condition.astype(jnp.float32)
     lifted = jax.nn.silu(cond_float).astype(jnp.bfloat16)
-    modulate_full = lax.all_gather(modulate_weight, "fsdp", axis=0, tiled=True)
-    modulation = matmul(lifted, modulate_full)
+    lifted_rows = to_group(
+        lifted.reshape(slots, fsdp_count, height).transpose(1, 0, 2), fsdp_count, place
+    ).reshape(fsdp_count * slots, height)
+    modulation = jnp.sum(
+        to_group(
+            matmul(lifted_rows, modulate_weight).reshape(fsdp_count, slots, 6 * width),
+            fsdp_count,
+            place,
+        ),
+        axis=0,
+    )
     per_token = jnp.dot(
         one_hot, modulation, precision=lax.Precision.HIGHEST, preferred_element_type=jnp.float32
     )
@@ -128,26 +214,20 @@
     query = rotate(joint[:, 0], tables, 1.0).astype(jnp.bfloat16)
     keys = rotate(joint[:, 1], tables, 1.0).astype(jnp.bfloat16)
     values = joint[:, 2].astype(jnp.bfloat16)
-    rows = min(tokens, 512)
-    starts = jnp.arange(tokens // rows, dtype=jnp.int32) * rows
-
-    def block_scores():
-        scores = (
-            jnp.einsum("qhd,khd->hqk", query, keys, preferred_element_type=jnp.float32) * scaling
-        )
-        allowed = segment_ids[:, None] == segment_ids[None, :]
-        return (query, keys, jnp.where(allowed[None], scores, masked_score))
-
-    def attend(start):
-        query_block, keys_block, scores = block_scores()
-        highest = jnp.max(scores, axis=-1, keepdims=True)
-        exponent = jnp.exp(scores - highest)
-        totals = jnp.sum(exponent, axis=-1, keepdims=True)
-        probs = (exponent / totals).astype(jnp.bfloat16)
-        mixed = jnp.einsum("hqk,khd->qhd", probs, values, preferred_element_type=jnp.float32)
-        return (mixed, highest + jnp.log(totals))
-
-    mixed, log_totals = lax.map(attend, starts)
+    blocks = tokens // BLOCK
+    query, keys, values = (
+        part.reshape(blocks, BLOCK, heads, head_size) for part in (query, keys, values)
+    )
+    block_ids = segment_ids.reshape(blocks, BLOCK)
+    allowed = block_ids[:, :, None] == block_ids[:, None, :]
+    scores = (
+        jnp.einsum("bqhd,bkhd->bhqk", query, keys, preferred_element_type=jnp.float32) * scaling
+    )
+    scores = jnp.where(allowed[:, None], scores, masked_score)
+    exponent = jnp.exp(scores - jnp.max(scores, axis=-1, keepdims=True))
+    soft = exponent / jnp.sum(exponent, axis=-1, keepdims=True)
+    probs = soft.astype(jnp.bfloat16)
+    mixed = jnp.einsum("bhqk,bkhd->bqhd", probs, values, preferred_element_type=jnp.float32)
     attended = mixed.reshape(tokens, width).astype(jnp.bfloat16)
     branch = matmul(attended, project_full)
     middle = residual + gate_one * branch
@@ -158,15 +238,7 @@
     hidden = (jax.nn.silu(gate) * upval).astype(jnp.bfloat16)
     feed = matmul(hidden, down_full)
     output = (middle + gate_two * feed).astype(jnp.bfloat16)
-    joint_full, project_full, gate_full, up_full, down_full = (
-        lax.all_gather(joint_weight, "fsdp", axis=0, tiled=True),
-        lax.all_gather(project_weight, "fsdp", axis=0, tiled=True),
-        lax.all_gather(gate_weight, "fsdp", axis=0, tiled=True),
-        lax.all_gather(up_weight, "fsdp", axis=0, tiled=True),
-        lax.all_gather(down_weight, "fsdp", axis=0, tiled=True),
-    )
     counts = bucket_counts.astype(jnp.float32)
-    bucket = lax.axis_index("bucket")
     mine = jnp.sum(jnp.where(jnp.arange(counts.shape[0], dtype=jnp.int32) == bucket, counts, 0.0))
     upstream = cotangent.astype(jnp.float32) * (mine * counts.shape[0] / jnp.sum(counts))
     feed_back = (upstream * gate_two).astype(jnp.bfloat16)
@@ -185,36 +257,25 @@
     attended_back = (
         times_transposed(branch_back, project_full)
         .astype(jnp.bfloat16)
-        .reshape(tokens, heads, head_size)
-    )
-
-    def attend_back(item):
-        start, log_total = item
-        query_block, keys_block, scores = block_scores()
-        probs = jnp.exp(scores - log_total)
-        probs_back = jnp.einsum(
-            "qhd,khd->hqk", attended_back, values, preferred_element_type=jnp.float32
-        )
-        scores_back = (
-            probs * (probs_back - jnp.sum(probs * probs_back, axis=-1, keepdims=True))
-        ).astype(jnp.bfloat16)
-        query_back = (
-            jnp.einsum("hqk,khd->qhd", scores_back, keys_block, preferred_element_type=jnp.float32)
-            * scaling
-        )
-        keys_back = (
-            jnp.einsum("hqk,qhd->khd", scores_back, query_block, preferred_element_type=jnp.float32)
-            * scaling
-        )
-        values_back = jnp.einsum(
-            "hqk,qhd->khd",
-            probs.astype(jnp.bfloat16),
-            attended_back,
-            preferred_element_type=jnp.float32,
-        )
-        return (query_back, keys_back, values_back)
-
-    query_back, keys_back, values_back = lax.map(attend_back, (starts, log_totals))
+        .reshape(blocks, BLOCK, heads, head_size)
+    )
+
+    probs_back = jnp.einsum(
+        "bqhd,bkhd->bhqk", attended_back, values, preferred_element_type=jnp.float32
+    )
+    scores_back = (
+        soft * (probs_back - jnp.sum(soft * probs_back, axis=-1, keepdims=True))
+    ).astype(jnp.bfloat16)
+    query_back = (
+        jnp.einsum("bhqk,bkhd->bqhd", scores_back, keys, preferred_element_type=jnp.float32) * scaling
+    )
+    keys_back = (
+        jnp.einsum("bhqk,bqhd->bkhd", scores_back, query, preferred_element_type=jnp.float32)
+        * scaling
+    )
+    values_back = jnp.einsum(
+        "bhqk,bqhd->bkhd", probs, attended_back, preferred_element_type=jnp.float32
+    )
     query_back = query_back.reshape(tokens, heads, head_size)
     keys_back = keys_back.reshape(tokens, heads, head_size)
     values_back = values_back.reshape(tokens, heads, head_size)
@@ -248,57 +309,63 @@
         precision=lax.Precision.HIGHEST,
         preferred_element_type=jnp.float32,
     ).astype(jnp.bfloat16)
-    modulate_rows = lax.psum_scatter(
-        contract_rows(lifted, modulation_back).astype(jnp.bfloat16),
-        "fsdp",
-        scatter_dimension=0,
-        tiled=True,
-    )
-    condition_slope = times_transposed(modulation_back, modulate_full)
+    everyone = lax.all_gather(
+        jnp.concatenate([modulation_back, lifted], axis=1), ("bucket", "fsdp"), axis=0, tiled=True
+    )
+    all_back = everyone[:, : 6 * width]
+    all_lifted = lax.dynamic_slice_in_dim(everyone, 6 * width + place * height, height, 1)
+    modulate_gradient = contract_rows(all_lifted, all_back)
+    group_back = lax.dynamic_slice_in_dim(
+        all_back, bucket * fsdp_count * slots, fsdp_count * slots, 0
+    )
+    slope_rows = times_transposed(group_back, modulate_weight)
+    condition_slope = (
+        to_group(slope_rows.reshape(fsdp_count, slots, height), fsdp_count, place)
+        .transpose(1, 0, 2)
+        .reshape(slots, width)
+    )
     grad_condition = condition_slope * silu_slope(cond_float)
-    modulate_gradient = lax.psum(modulate_rows, "bucket").astype(jnp.float32)
-    fsdp_count = lax.axis_size("fsdp")
-    bucket_count = lax.axis_size("bucket")
-
-    def reorder(matrix):
-        height, breadth = matrix.shape
-        return (
-            matrix.reshape(fsdp_count, bucket_count, height // (fsdp_count * bucket_count), breadth)
-            .swapaxes(0, 1)
-            .reshape(height, breadth)
+    down_parts = (
+        down_gradient.astype(jnp.bfloat16)
+        .reshape(fsdp_count, bucket_count, down_rows, width)
+        .swapaxes(0, 1)
+    )
+    down_sum = reduce_pieces(down_parts).reshape(bucket_count * down_rows, width)
+    ffn_parts = (
+        jnp.stack([gate_gradient.astype(jnp.bfloat16), up_gradient.astype(jnp.bfloat16)])
+        .reshape(2, fsdp_count, height, columns, ff // columns)
+        .transpose(3, 0, 1, 2, 4)
+        .reshape(bucket_count, fsdp_count, height, ff // columns)
+    )
+    ffn_sum = (
+        reduce_pieces(ffn_parts)
+        .reshape(columns, 2, height, ff // columns)
+        .transpose(1, 2, 0, 3)
+        .reshape(2, height, ff)
+    )
+    attn_parts = (
+        jnp.concatenate(
+            [joint_gradient.astype(jnp.bfloat16), project_gradient.astype(jnp.bfloat16)], axis=1
         )
-
-    pieces = (
-        lax.psum_scatter(
-            reorder(joint_gradient), ("bucket", "fsdp"), scatter_dimension=0, tiled=True
-        ),
-        lax.psum_scatter(
-            reorder(project_gradient), ("bucket", "fsdp"), scatter_dimension=0, tiled=True
-        ),
-        lax.psum_scatter(
-            reorder(gate_gradient), ("bucket", "fsdp"), scatter_dimension=0, tiled=True
-        ),
-        lax.psum_scatter(reorder(up_gradient), ("bucket", "fsdp"), scatter_dimension=0, tiled=True),
-        lax.psum_scatter(
-            reorder(down_gradient), ("bucket", "fsdp"), scatter_dimension=0, tiled=True
-        ),
-    )
-    shares = (
-        lax.all_gather(pieces[0].astype(jnp.bfloat16), "bucket", axis=0, tiled=True).astype(
-            jnp.float32
-        ),
-        lax.all_gather(pieces[1].astype(jnp.bfloat16), "bucket", axis=0, tiled=True).astype(
-            jnp.float32
-        ),
-        lax.all_gather(pieces[2].astype(jnp.bfloat16), "bucket", axis=0, tiled=True).astype(
-            jnp.float32
-        ),
-        lax.all_gather(pieces[3].astype(jnp.bfloat16), "bucket", axis=0, tiled=True).astype(
-            jnp.float32
-        ),
-        lax.all_gather(pieces[4].astype(jnp.bfloat16), "bucket", axis=0, tiled=True).astype(
-            jnp.float32
-        ),
+        .reshape(fsdp_count, 2, height // 2, columns, 4 * width // columns)
+        .transpose(3, 1, 0, 2, 4)
+        .reshape(bucket_count, fsdp_count, height // 2, 4 * width // columns)
+    )
+    attn_sum = (
+        reduce_pieces(attn_parts)
+        .reshape(columns, 2, height // 2, 4 * width // columns)
+        .transpose(1, 2, 0, 3)
+        .reshape(height, 4 * width)
+    )
+    shares = tuple(
+        part.astype(jnp.float32)
+        for part in (
+            attn_sum[:, : 3 * width],
+            attn_sum[:, 3 * width :],
+            ffn_sum[0],
+            ffn_sum[1],
+            down_sum,
+        )
     )
     return (
         output,

time: 2960 us -> 890 us (0.30)
  blocking collectives: 1480 us -> 0 us
  waiting for transfers between devices: 872 us -> 305 us
  local copies, waits for them, and re-layouts: 204 us -> 261 us
  matrix products: 211 us -> 157 us
  starting transfers between devices: 102 us -> 48.9 us
  other arithmetic: 55.4 us -> 88.8 us
    unnamed x2 -> x0, blocking collectives: 1470 us -> none
    all_gather x10 -> x7, waiting for transfers between devices: 756 us -> 108 us  [the longest x3 73.9 us: reduce_pieces(): lax.all_gather(total.astype(jnp.bfloat16), 'bucket', axis=0, tiled=False)]
    ppermute x0 -> x27, waiting for transfers between devices: none -> 158 us  [the longest x9 85.1 us: reduce_pieces(): lax.ppermute(pick(mine, (place + by) % count), 'fsdp', shifts(count, by))]
    unnamed x24 -> x0, starting transfers between devices: 101 us -> none
    psum x1 -> x0, waiting for transfers between devices: 78.8 us -> none  [on_device(): modulate_gradient = lax.psum(modulate_rows, 'bucket').astype(jnp.float32)]
    another operation x0 -> x13, local copies, waits for them, and re-layouts: none -> 57.4 us  [the longest x4 40.1 us: on_device(): jnp.stack([gate_gradient.astype(jnp.bfloat16), up_gradient.astype(jnp.bfl...]
    ppermute x0 -> x27, starting transfers between devices: none -> 48.5 us  [the longest x9 20.3 us: gather_pieces(): lax.ppermute(piece, 'fsdp', shifts(count, by))]
    another operation x3 -> x19, other arithmetic: 1.51 us -> 46.2 us  [the longest x3 15 us: gather_pieces(): jnp.stack([pick(relative, (place - j) % count) for j in range(count)])]
  transfers between devices with their start and end apart: 37 -> 37, of which waited for: 14 -> 23; matrix products, arithmetic and copies ran while one was open for 64% -> 39% of each run, Pallas kernels for 0% -> 0%
where the time goes in v1:
time: 890 us; the launch traced here: 878 us
  waiting for transfers between devices  305 us (34%)
  local copies, waits for them, and re-layouts  261 us (29%)
  matrix products  157 us (18%)
  other arithmetic  88.8 us (10%)
  starting transfers between devices  48.9 us (5%)
  between operations  17.3 us (2%)
    ppermute x9, waiting for transfers between devices, reduce_pieces(): lax.ppermute(pick(mine, (place + by) % count), 'fsdp', shifts(count, by))  85.1 us
    all_gather x3, waiting for transfers between devices, reduce_pieces(): lax.all_gather(total.astype(jnp.bfloat16), 'bucket', axis=0, tiled=False)  73.9 us
    ppermute x9, waiting for transfers between devices, gather_pieces(): lax.ppermute(piece, 'fsdp', shifts(count, by))  53.9 us
    dot_general x6, matrix products, times_transposed(): lax.dot_general(left, right, (((1,), (1,)), ((), ())), preferred_element_...  48.1 us
    unnamed x173, local copies, waits for them, and re-layouts  45.6 us
    dot_general x6, matrix products, matmul(): return jnp.dot(left, right, preferred_element_type=jnp.float32)  42.6 us
    another operation x4, local copies, waits for them, and re-layouts, on_device(): jnp.stack([gate_gradient.astype(jnp.bfloat16), up_gradient.astype(jnp.bfl...  40.1 us
    reduce_scatter x3, waiting for transfers between devices, reduce_pieces(): mine = lax.psum_scatter(parts, 'bucket', scatter_dimension=0, tiled=False)  39.1 us
  transfers between devices with their start and end apart: 37, of which 23 were waited for; matrix products, arithmetic and copies ran while one was open for 39% of the time, Pallas kernels for 0%

profile of v1, /device:TPU:25, one launch (start us, length us, event | category | flops | bytes accessed | tf_op | source)
XLA Modules:
  0.0 877.7 jit_solution(12124138448334574043)
XLA Ops:
  46.7 15.9 %collective-permute-done.7 = bf16[144,1152]{1,0:T(8,128)(2,1)S(1)} collective-permute-done((bf16[144,1152]{1,0:T(8,128)(2,1)S(1)}, bf16[144,1152]{1,0:T(8,128)(2,1)S(1)}, u32[]{:S(2)}, u32[]{:S(2)}) %collective-permute-start.7) | collective-permute-done | bytes 331808 | tf_op jit(solution)/shard_map/ppermute | solution.py:99
  92.5 19.3 %collective-permute-done.10 = bf16[288,768]{1,0:T(8,128)(2,1)S(1)} collective-permute-done((bf16[288,768]{1,0:T(8,128)(2,1)S(1)}, bf16[288,768]{1,0:T(8,128)(2,1)S(1)}, u32[]{:S(2)}, u32[]{:S(2)}) %collective-permute-start.10) | collective-permute-done | bytes 442400 | tf_op jit(solution)/shard_map/ppermute | solution.py:99
  133.4 10.9 %collective-permute-done.4 = f32[8,6912]{1,0:T(8,128)S(1)} collective-permute-done((f32[8,6912]{1,0:T(8,128)S(1)}, f32[8,6912]{1,0:T(8,128)S(1)}, u32[]{:S(2)}, u32[]{:S(2)}) %collective-permute-start.4) | collective-permute-done | bytes 221216 | tf_op jit(solution)/shard_map/ppermute | solution.py:123
  187.2 10.7 %copy.208 = bf16[4,4,2,144,1152]{4,1,3,2,0:T(4,128)(2,1)S(1)} copy(bf16[4,4,2,144,1152]{4,3,2,1,0:T(8,128)(2,1)S(1)} %bitcast.263) | data formatting | bytes 21233664 | tf_op jit(solution)/shard_map/reshape | solution.py:169
  284.4 31.0 %copy.314 = bf16[4,4,2,288,768]{4,1,3,0,2:T(4,128)(2,1)} copy(bf16[4,4,2,288,768]{4,3,2,1,0:T(8,128)(2,1)S(1)} %bitcast.260) | data formatting | bytes 28311552 | tf_op jit(solution)/shard_map/reshape | solution.py:176
  315.4 12.1 %fusion.107 = (bf16[1,4,288,4,768]{4,3,2,1,0:T(4,128)(2,1)}, bf16[1,4,288,4,768]{4,3,2,1,0:T(4,128)(2,1)S(1)}) fusion(bf16[2,4,288,4,768]{4,3,2,1,0:T(4,128)(2,1)} %bitcast.261), kind=kLoop, calls=%fused_computation.277 | loop fusion | bytes 28311552 | tf_op jit(solution)/shard_map/slice | solution.py:180
  355.1 11.7 %multiply_convert_fusion.1 = (bf16[512,3072]{1,0:T(8,128)(2,1)}, bf16[512,3072]{1,0:T(8,128)(2,1)}, bf16[512,3072]{1,0:T(8,128)(2,1)}) fusion(f32[512,3072]{1,0:T(8,128)} %fusion.109, f32[512,3072]{1,0:T(8,128)} %fusion.110, bf16[512,1152]{1,0:T(8,128)(2,1)S(1)} %copy-done.48, bf16[3072,1152]{1,0:T(8,128)(2,1)S(1)} %bitcast.293), kind=kOutput, calls=%fused_computation.26 | convolution fusion | flops 3647471616 | bytes 30277632 | tf_op jit(solution)/shard_map/dot_general | solution.py:74
  366.8 9.8 %fusion.111 = f32[512,1152]{1,0:T(8,128)} fusion(bf16[512,3072]{1,0:T(8,128)(2,1)} %get-tuple-element.31, bf16[1152,3072]{1,0:T(8,128)(2,1)} %bitcast.296), kind=kOutput, calls=%fused_computation.281 | convolution fusion | flops 3623878656 | bytes 12582912 | tf_op jit(solution)/shard_map/dot_general | solution.py:74
  384.9 10.1 %fusion.104 = (f32[512]{0:T(512)S(1)}, f32[512]{0:T(512)S(1)}, f32[512,1152]{1,0:T(8,128)S(1)}) fusion(f32[512,6912]{1,0:T(8,128)} %copy-done, f32[512]{0:T(512)S(1)} %add_rsqrt_fusion, f32[512,1152]{1,0:T(8,128)S(1)} %get-tuple-element.20, f32[512]{0:T(512)S(1)} %broadcast_multiply_fusion.6, f32[512,1152]{1,0:T(8,128)} %fusion.111, ...), kind=kOutput, calls=%fused_computation.274 | convolution fusion | flops 3628596224 | bytes 19668992 | tf_op jit(solution)/shard_map/dot_general | solution.py:74
  395.1 14.1 %multiply_convert_fusion.4 = (bf16[512,1152]{1,0:T(8,128)(2,1)S(1)}, f32[512,1152]{1,0:T(8,128)}, bf16[512,1152]{1,0:T(8,128)(2,1)}, f32[512,1152]{1,0:T(8,128)}) fusion(f32[512,6912]{1,0:T(8,128)} %copy-done, f32[512]{0:T(512)S(1)} %get-tuple-element.129, f32[512,1152]{1,0:T(8,128)S(1)} %get-tuple-element.20, f32[512]{0:T(512)S(1)} %broadcast_multiply_fusion.6, ...), kind=kOutput, calls=%fused_computation.77 | convolution fusion | flops 3633315840 | bytes 30285828 | tf_op jit(solution)/shard_map/dot_general | solution.py:64
  462.7 14.6 %reshape.415 = bf16[4,2,144,4,1152]{4,3,2,1,0:T(4,128)(2,1)} reshape(bf16[1152,4608]{1,0:T(8,128)(2,1)} %pad_maximum_fusion.5) | data formatting | bytes 21233664 | tf_op jit(solution)/shard_map/reshape | solution.py:350
  477.4 10.6 %copy.249 = bf16[4,2,144,4,1152]{4,2,0,1,3:T(8,128)(2,1)} copy(bf16[4,2,144,4,1152]{4,3,2,1,0:T(4,128)(2,1)} %reshape.415) | data formatting | bytes 21233664 | tf_op jit(solution)/shard_map/reshape | solution.py:350
  496.9 14.5 %stack.193 = bf16[1,4,288,4,768]{4,3,2,1,0:T(4,128)(2,1)} reshape(bf16[1152,3072]{1,0:T(8,128)(2,1)} %convolution_convert_fusion.2) | data formatting | bytes 14155776 | tf_op jit(solution)/shard_map/stack | solution.py:335
  524.9 14.0 %stack.192 = bf16[1,4,288,4,768]{4,3,2,1,0:T(4,128)(2,1)} reshape(bf16[1152,3072]{1,0:T(8,128)(2,1)} %convolution_convert_fusion.3) | data formatting | bytes 14155776 | tf_op jit(solution)/shard_map/stack | solution.py:335
  552.7 11.7 %fusion.105 = (f32[512]{0:T(512)S(1)}, f32[512]{0:T(512)S(1)}, f32[512,6912]{1,0:T(8,128)S(1)}, f32[512,1152]{1,0:T(8,128)}) fusion(f32[512,6912]{1,0:T(8,128)} %copy-done, f32[512]{0:T(512)S(1)} %copy-done.66, f32[512]{0:T(512)S(1)} %copy-done.64, bf16[512,1152]{1,0:T(8,128)(2,1)S(1)} %copy-done.2, bf16[512,3456]{0,1:T(8,128)(2,1)} %bitcast.304, ...), kind=kOutput, calls=%fused_computation.275 | convolution fusion | flops 4081581056 | bytes 19767296 | tf_op jit(solution)/shard_map/dot_general | solution.py:74
  627.3 11.8 %collective-permute-done.19 = bf16[144,1152]{1,0:T(8,128)(2,1)S(1)} collective-permute-done((bf16[144,1152]{1,0:T(8,128)(2,1)S(1)}, bf16[144,1152]{1,0:T(8,128)(2,1)S(1)}, u32[]{:S(2)}, u32[]{:S(2)}) %collective-permute-start.19) | collective-permute-done | bytes 331808 | tf_op jit(solution)/shard_map/ppermute | solution.py:113
  641.1 39.1 %reduce-scatter.6.cloned.1.call-done = bf16[1,4,288,768]{3,2,1,0:T(8,128)(2,1)} async-done(((bf16[8,4,288,768]{3,2,1,0:T(8,128)(2,1)}), bf16[1,4,288,768]{3,2,1,0:T(8,128)(2,1)}) %reduce-scatter.6.cloned.1.call-update) | async-done | bytes 1769488 | tf_op jit(solution)/shard_map/reduce_scatter | solution.py:110
  683.3 9.3 %collective-permute-done.21 = bf16[288,768]{1,0:T(8,128)(2,1)S(1)} collective-permute-done((bf16[288,768]{1,0:T(8,128)(2,1)S(1)}, bf16[288,768]{1,0:T(8,128)(2,1)S(1)}, u32[]{:S(2)}, u32[]{:S(2)}) %collective-permute-start.21) | collective-permute-done | bytes 442400 | tf_op jit(solution)/shard_map/ppermute | solution.py:113
  692.6 12.2 %collective-permute-done.23 = bf16[288,768]{1,0:T(8,128)(2,1)S(1)} collective-permute-done((bf16[288,768]{1,0:T(8,128)(2,1)S(1)}, bf16[288,768]{1,0:T(8,128)(2,1)S(1)}, u32[]{:S(2)}, u32[]{:S(2)}) %collective-permute-start.23) | collective-permute-done | bytes 442400 | tf_op jit(solution)/shard_map/ppermute | solution.py:113
  704.9 19.0 %collective-permute-done.22 = bf16[288,768]{1,0:T(8,128)(2,1)S(1)} collective-permute-done((bf16[288,768]{1,0:T(8,128)(2,1)S(1)}, bf16[288,768]{1,0:T(8,128)(2,1)S(1)}, u32[]{:S(2)}, u32[]{:S(2)}) %collective-permute-start.22) | collective-permute-done | bytes 442400 | tf_op jit(solution)/shard_map/ppermute | solution.py:113
  725.8 33.9 %all-gather.14.cloned.1.call-done = bf16[256,8064]{1,0:T(8,128)(2,1)} async-done(((bf16[8,8064]{1,0:T(8,128)(2,1)}), bf16[256,8064]{1,0:T(8,128)(2,1)}) %all-gather.14.cloned.1.call-update) | async-done | bytes 4128784 | tf_op jit(solution)/shard_map/all_gather | solution.py:312
  774.0 14.9 %all-gather.26.cloned.1.call-done = bf16[768,1152]{1,0:T(8,128)(2,1)} async-done(((bf16[96,1152]{1,0:T(8,128)(2,1)}), bf16[768,1152]{1,0:T(8,128)(2,1)}) %all-gather.26.cloned.1.call-update) | async-done | bytes 1769488 | tf_op jit(solution)/shard_map/all_gather | solution.py:116
  792.4 29.4 %all-gather.22.cloned.1.call-done = bf16[1152,1152]{1,0:T(8,128)(2,1)} async-done(((bf16[144,1152]{1,0:T(8,128)(2,1)}), bf16[1152,1152]{1,0:T(8,128)(2,1)}) %all-gather.22.cloned.1.call-update) | async-done | bytes 2654224 | tf_op jit(solution)/shard_map/all_gather | solution.py:116
  828.6 29.6 %all-gather.24.cloned.1.call-done = bf16[2304,768]{1,0:T(8,128)(2,1)} async-done(((bf16[288,768]{1,0:T(8,128)(2,1)}), bf16[2304,768]{1,0:T(8,128)(2,1)}) %all-gather.24.cloned.1.call-update) | async-done | bytes 3538960 | tf_op jit(solution)/shard_map/all_gather | solution.py:116
  (389 shorter events, 450.3 us)
Async XLA Ops:
  7.2 148.5 %all-gather.20.cloned.1.call-start = ((), (), s32[]{:S(2)}) async-start(), calls=%async_computation.9 | async-start | bytes 5971968 | tf_op jit(solution)/shard_map/all_gather | solution.py:101
  8.6 17.0 %collective-permute-start.13 = (bf16[96,1152]{1,0:T(8,128)(2,1)S(1)}, bf16[96,1152]{1,0:T(8,128)(2,1)S(1)}, u32[]{:S(2)}, u32[]{:S(2)}) collective-permute-start(bf16[96,1152]{1,0:T(8,128)(2,1)S(1)} %dynamic-slice_bitcast_fusion.11), channel_id=1, source_target_pairs={{0,2},{1,3},{2,0},{3,1},{4,6},{5,7},{6,4},{7,5},{8,10},{9,11},{10,... | collective-permute-start | bytes 663560 | tf_op jit(solution)/shard_map/ppermute | solution.py:99
  8.6 17.0 %collective-permute-start.12 = (bf16[96,1152]{1,0:T(8,128)(2,1)S(1)}, bf16[96,1152]{1,0:T(8,128)(2,1)S(1)}, u32[]{:S(2)}, u32[]{:S(2)}) collective-permute-start(bf16[96,1152]{1,0:T(8,128)(2,1)S(1)} %dynamic-slice_bitcast_fusion.11), channel_id=1, source_target_pairs={{0,1},{1,2},{2,3},{3,0},{4,5},{5,6},{6,7},{7,4},{8,9},{9,10},{10,1... | collective-permute-start | bytes 663560 | tf_op jit(solution)/shard_map/ppermute | solution.py:99
  26.5 139.3 %all-gather.16.cloned.1.call-start = ((), (), s32[]{:S(2)}) async-start(), calls=%async_computation.7 | async-start | bytes 8957952 | tf_op jit(solution)/shard_map/all_gather | solution.py:101
  40.8 21.8 %collective-permute-start.7 = (bf16[144,1152]{1,0:T(8,128)(2,1)S(1)}, bf16[144,1152]{1,0:T(8,128)(2,1)S(1)}, u32[]{:S(2)}, u32[]{:S(2)}) collective-permute-start(bf16[144,1152]{1,0:T(8,128)(2,1)S(1)} %dynamic-slice_bitcast_fusion.7), channel_id=1, source_target_pairs={{0,2},{1,3},{2,0},{3,1},{4,6},{5,7},{6,4},{7,5},{8,10},{9,11},{10,... | collective-permute-start | bytes 995336 | tf_op jit(solution)/shard_map/ppermute | solution.py:99
  40.8 21.8 %collective-permute-start.6 = (bf16[144,1152]{1,0:T(8,128)(2,1)S(1)}, bf16[144,1152]{1,0:T(8,128)(2,1)S(1)}, u32[]{:S(2)}, u32[]{:S(2)}) collective-permute-start(bf16[144,1152]{1,0:T(8,128)(2,1)S(1)} %dynamic-slice_bitcast_fusion.7), channel_id=1, source_target_pairs={{0,1},{1,2},{2,3},{3,0},{4,5},{5,6},{6,7},{7,4},{8,9},{9,10},{10,1... | collective-permute-start | bytes 995336 | tf_op jit(solution)/shard_map/ppermute | solution.py:99
  63.7 198.8 %all-gather.18.cloned.1.call-start = ((), (), s32[]{:S(2)}) async-start(), calls=%async_computation.8 | async-start | bytes 11943936 | tf_op jit(solution)/shard_map/all_gather | solution.py:101
  73.6 17.1 %collective-permute-start.11 = (bf16[288,768]{1,0:T(8,128)(2,1)S(1)}, bf16[288,768]{1,0:T(8,128)(2,1)S(1)}, u32[]{:S(2)}, u32[]{:S(2)}) collective-permute-start(bf16[288,768]{1,0:T(8,128)(2,1)S(1)} %dynamic-slice_bitcast_fusion.3), channel_id=1, source_target_pairs={{0,3},{1,0},{2,1},{3,2},{4,7},{5,4},{6,5},{7,6},{8,11},{9,8},{10,9... | collective-permute-start | bytes 1327112 | tf_op jit(solution)/shard_map/ppermute | solution.py:99
  81.1 30.7 %collective-permute-start.10 = (bf16[288,768]{1,0:T(8,128)(2,1)S(1)}, bf16[288,768]{1,0:T(8,128)(2,1)S(1)}, u32[]{:S(2)}, u32[]{:S(2)}) collective-permute-start(bf16[288,768]{1,0:T(8,128)(2,1)S(1)} %dynamic-slice_bitcast_fusion.3), channel_id=1, source_target_pairs={{0,2},{1,3},{2,0},{3,1},{4,6},{5,7},{6,4},{7,5},{8,10},{9,11},{10,... | collective-permute-start | bytes 1327112 | tf_op jit(solution)/shard_map/ppermute | solution.py:99
  82.3 29.5 %collective-permute-start.9 = (bf16[288,768]{1,0:T(8,128)(2,1)S(1)}, bf16[288,768]{1,0:T(8,128)(2,1)S(1)}, u32[]{:S(2)}, u32[]{:S(2)}) collective-permute-start(bf16[288,768]{1,0:T(8,128)(2,1)S(1)} %dynamic-slice_bitcast_fusion.3), channel_id=1, source_target_pairs={{0,1},{1,2},{2,3},{3,0},{4,5},{5,6},{6,7},{7,4},{8,9},{9,10},{10,1... | collective-permute-start | bytes 1327112 | tf_op jit(solution)/shard_map/ppermute | solution.py:99
  83.5 32.0 %collective-permute-start.2 = (bf16[8,288]{1,0:T(8,128)(2,1)S(1)}, bf16[8,288]{1,0:T(8,128)(2,1)S(1)}, u32[]{:S(2)}, u32[]{:S(2)}) collective-permute-start(bf16[8,288]{1,0:T(8,128)(2,1)S(1)} %bitcast.327), channel_id=1, source_target_pairs={{0,3},{1,0},{2,1},{3,2},{4,7},{5,4},{6,5},{7,6},{8,11},{9,8},{10,9... | collective-permute-start | bytes 13832 | tf_op jit(solution)/shard_map/ppermute | solution.py:123
  84.1 31.4 %collective-permute-start = (bf16[8,288]{1,0:T(8,128)(2,1)S(1)}, bf16[8,288]{1,0:T(8,128)(2,1)S(1)}, u32[]{:S(2)}, u32[]{:S(2)}) collective-permute-start(bf16[8,288]{1,0:T(8,128)(2,1)S(1)} %bitcast.328), channel_id=1, source_target_pairs={{0,1},{1,2},{2,3},{3,0},{4,5},{5,6},{6,7},{7,4},{8,9},{9,10},{10,1... | collective-permute-start | bytes 13832 | tf_op jit(solution)/shard_map/ppermute | solution.py:123
  90.6 30.8 %collective-permute-start.1 = (bf16[8,288]{1,0:T(8,128)(2,1)S(1)}, bf16[8,288]{1,0:T(8,128)(2,1)S(1)}, u32[]{:S(2)}, u32[]{:S(2)}) collective-permute-start(bf16[8,288]{1,0:T(8,128)(2,1)S(1)} %bitcast.329), channel_id=1, source_target_pairs={{0,2},{1,3},{2,0},{3,1},{4,6},{5,7},{6,4},{7,5},{8,10},{9,11},{10,... | collective-permute-start | bytes 13832 | tf_op jit(solution)/shard_map/ppermute | solution.py:123
  113.1 466.5 %reduce-scatter.8.cloned.1.call-start = ((), (), s32[]{:S(2)}) async-start(), calls=%async_computation.6 | async-start | bytes 7962624 | tf_op jit(solution)/shard_map/reduce_scatter | solution.py:110
  384.9 224.4 %reduce-scatter.4.cloned.1.call-start = ((), (), s32[]{:S(2)}) async-start(), calls=%async_computation.4 | async-start | bytes 11943936 | tf_op jit(solution)/shard_map/reduce_scatter | solution.py:110
  487.9 192.2 %reduce-scatter.6.cloned.1.call-start = ((), (), s32[]{:S(2)}) async-start(), calls=%async_computation.5 | async-start | bytes 15925248 | tf_op jit(solution)/shard_map/reduce_scatter | solution.py:110
  551.4 208.3 %all-gather.14.cloned.1.call-start = ((), (), s32[]{:S(2)}) async-start(), calls=%async_computation.3 | async-start | bytes 4257792 | tf_op jit(solution)/shard_map/all_gather | solution.py:312
  579.5 209.4 %all-gather.26.cloned.1.call-start = ((), (), s32[]{:S(2)}) async-start(), calls=%async_computation.12 | async-start | bytes 1990656 | tf_op jit(solution)/shard_map/all_gather | solution.py:116
  588.0 19.4 %collective-permute-start.25 = (bf16[96,1152]{1,0:T(8,128)(2,1)S(1)}, bf16[96,1152]{1,0:T(8,128)(2,1)S(1)}, u32[]{:S(2)}, u32[]{:S(2)}) collective-permute-start(bf16[96,1152]{1,0:T(8,128)(2,1)S(1)} %get-tuple-element.89), channel_id=1, source_target_pairs={{0,2},{1,3},{2,0},{3,1},{4,6},{5,7},{6,4},{7,5},{8,10},{9,11},{10,... | collective-permute-start | bytes 663560 | tf_op jit(solution)/shard_map/ppermute | solution.py:113
  609.2 212.6 %all-gather.22.cloned.1.call-start = ((), (), s32[]{:S(2)}) async-start(), calls=%async_computation.10 | async-start | bytes 2985984 | tf_op jit(solution)/shard_map/all_gather | solution.py:116
  613.2 25.9 %collective-permute-start.19 = (bf16[144,1152]{1,0:T(8,128)(2,1)S(1)}, bf16[144,1152]{1,0:T(8,128)(2,1)S(1)}, u32[]{:S(2)}, u32[]{:S(2)}) collective-permute-start(bf16[144,1152]{1,0:T(8,128)(2,1)S(1)} %get-tuple-element.86), channel_id=1, source_target_pairs={{0,2},{1,3},{2,0},{3,1},{4,6},{5,7},{6,4},{7,5},{8,10},{9,11},{10,... | collective-permute-start | bytes 995336 | tf_op jit(solution)/shard_map/ppermute | solution.py:113
  641.0 217.3 %all-gather.24.cloned.1.call-start = ((), (), s32[]{:S(2)}) async-start(), calls=%async_computation.11 | async-start | bytes 3981312 | tf_op jit(solution)/shard_map/all_gather | solution.py:116
  681.8 23.0 %collective-permute-start.23 = (bf16[288,768]{1,0:T(8,128)(2,1)S(1)}, bf16[288,768]{1,0:T(8,128)(2,1)S(1)}, u32[]{:S(2)}, u32[]{:S(2)}) collective-permute-start(bf16[288,768]{1,0:T(8,128)(2,1)S(1)} %get-tuple-element.82), channel_id=1, source_target_pairs={{0,3},{1,0},{2,1},{3,2},{4,7},{5,4},{6,5},{7,6},{8,11},{9,8},{10,9... | collective-permute-start | bytes 1327112 | tf_op jit(solution)/shard_map/ppermute | solution.py:113
  683.1 40.8 %collective-permute-start.22 = (bf16[288,768]{1,0:T(8,128)(2,1)S(1)}, bf16[288,768]{1,0:T(8,128)(2,1)S(1)}, u32[]{:S(2)}, u32[]{:S(2)}) collective-permute-start(bf16[288,768]{1,0:T(8,128)(2,1)S(1)} %get-tuple-element.83), channel_id=1, source_target_pairs={{0,2},{1,3},{2,0},{3,1},{4,6},{5,7},{6,4},{7,5},{8,10},{9,11},{10,... | collective-permute-start | bytes 1327112 | tf_op jit(solution)/shard_map/ppermute | solution.py:113
  (93 other events, 766.0 us)
Sparse Core Ops, SparseCore 0:
  26.6 47.2 all-gather.19
  76.4 52.5 all-gather.15
  131.4 63.8 all-gather.17
  385.0 70.8 reduce-scatter.7
  488.1 87.4 reduce-scatter.3
  579.4 100.7 reduce-scatter.5
  684.0 75.7 all-gather.13
  762.4 26.5 all-gather.25
  791.5 30.2 all-gather.21
  824.3 33.9 all-gather.23

commit v2 on v1

v2 whole, which is shorter than its diff:
```python
import functools

import jax
import jax.numpy as jnp
from jax import lax
from jax.experimental import pallas as pl
from jax.experimental.pallas import tpu as pltpu
from jax.sharding import PartitionSpec as P

HEADS = 16
HEAD_DIM = 72
WIDTH = HEADS * HEAD_DIM
QUARTER = HEAD_DIM // 4
BLOCK = 256
CHUNK = 64
COLUMNS = 4
HALVES = 2
PIECES = COLUMNS * HALVES
LANES = 128

epsilon = 1e-06
masked_score = -1e30
f32 = jnp.float32
bf16 = jnp.bfloat16
MEGA = 2**20


def normalize(values):
    average = jnp.mean(values, axis=-1, keepdims=True)
    centered = values - average
    inverse = lax.rsqrt(jnp.mean(centered * centered, axis=-1, keepdims=True) + epsilon)
    return (centered * inverse, inverse)


def normalize_back(normed, inverse, upstream):
    return inverse * (
        upstream
        - jnp.mean(upstream, axis=-1, keepdims=True)
        - normed * jnp.mean(upstream * normed, axis=-1, keepdims=True)
    )


def matmul(left, right):
    return jnp.dot(left, right, preferred_element_type=f32)


def contract_rows(left, right):
    return lax.dot_general(left, right, (((0,), (0,)), ((), ())), preferred_element_type=f32)


def times_transposed(left, right):
    return lax.dot_general(left, right, (((1,), (1,)), ((), ())), preferred_element_type=f32)


def silu_slope(values):
    sigmoid = jax.nn.sigmoid(values)
    return sigmoid * (1.0 + values * (1.0 - sigmoid))


def rope_tables(segments, widths):
    slots = widths.shape[0]
    one_hot = (segments[:, None] == jnp.arange(slots, dtype=jnp.int32)[None, :]).astype(jnp.int32)
    counts = jnp.sum(one_hot, axis=0)
    starts = jnp.cumsum(counts) - counts
    start_token = jnp.sum(one_hot * starts[None, :], axis=1)
    width_token = jnp.maximum(jnp.sum(one_hot * widths[None, :], axis=1), 1)
    place = jnp.arange(segments.shape[0], dtype=jnp.int32) - start_token
    row_place = (place // width_token).astype(f32)
    col_place = (place % width_token).astype(f32)
    freqs = 10000.0 ** (-jnp.arange(QUARTER, dtype=f32) / QUARTER)
    angle_row = row_place[:, None] * freqs[None, :]
    angle_col = col_place[:, None] * freqs[None, :]
    cos_row, sin_row, cos_col, sin_col = (
        jnp.cos(angle_row),
        jnp.sin(angle_row),
        jnp.cos(angle_col),
        jnp.sin(angle_col),
    )
    cos = jnp.concatenate([cos_row, cos_row, cos_col, cos_col], axis=1)
    sin = jnp.concatenate([-sin_row, sin_row, -sin_col, sin_col], axis=1)
    return jnp.tile(cos, (1, HEADS)), jnp.tile(sin, (1, HEADS))


def part(index):
    return slice(index * WIDTH, (index + 1) * WIDTH)


def rotate(values, cos, sin):
    lane = lax.broadcasted_iota(jnp.int32, values.shape, 1)
    leading = lane % (2 * QUARTER) < QUARTER
    partner = jnp.where(
        leading,
        pltpu.roll(values, WIDTH - QUARTER, 1),
        pltpu.roll(values, QUARTER, 1),
    )
    return values * cos + partner * sin


def attn_copies(place, column, shard, everyone, target, sems, count):
    rows = shard.shape[0]
    half = rows // HALVES
    copies = [
        pltpu.make_async_copy(
            shard, target.at[pl.ds(pl.multiple_of(place * rows, 16), rows)], sems.at[0]
        )
    ]
    for by in range(1, count):
        start = ((place + (count - by)) % count) * rows
        for h in range(HALVES):
            copies.append(
                pltpu.make_async_copy(
                    everyone.at[column * HALVES + h, by - 1],
                    target.at[pl.ds(pl.multiple_of(start + h * half, 16), half)],
                    sems.at[1 + (by - 1) * HALVES + h],
                )
            )
    return copies


def first_kernel(
    count, place_ref, x_ref, mod_ref, cos_ref, sin_ref, joint_ref, every_ref,
    first_ref, query_ref, keys_ref, values_ref, weight, total, sems,
):
    place = place_ref[0]
    copies = [
        attn_copies(
            place, c, joint_ref.at[:, pl.ds(c * WIDTH, WIDTH)], every_ref, weight.at[c], sems.at[c], count
        )
        for c in range(3)
    ]
    for group in copies:
        for copy in group:
            copy.start()
    tokens = x_ref.shape[0]
    for i in range(tokens // CHUNK):
        rows = slice(i * CHUNK, (i + 1) * CHUNK)
        normed, _ = normalize(x_ref[rows, :].astype(f32))
        first_ref[rows, :] = (
            normed * (1.0 + mod_ref[i : i + 1, part(1)]) + mod_ref[i : i + 1, part(0)]
        ).astype(bf16)
    for c, out in enumerate((query_ref, keys_ref, values_ref)):
        for copy in copies[c]:
            copy.wait()
        if c == 2:
            out[...] = matmul(first_ref[...], weight[c]).astype(bf16)
        else:
            total[...] = matmul(first_ref[...], weight[c])

            @pl.loop(0, tokens // CHUNK)
            def _(i):
                rows = pl.ds(pl.multiple_of(i * CHUNK, CHUNK), CHUNK)
                out[rows, :] = rotate(total[rows, :], cos_ref[rows, :], sin_ref[rows, :]).astype(bf16)


def window(head):
    start = head * HEAD_DIM // LANES * LANES
    stop = -(-(head + 1) * HEAD_DIM // LANES) * LANES
    lane = lax.broadcasted_iota(jnp.int32, (1, stop - start), 1) + start
    inside = (lane >= head * HEAD_DIM) & (lane < (head + 1) * HEAD_DIM)
    return slice(start, stop), inside


def soft_scores(query, keys, allowed):
    scores = times_transposed(query, keys) * HEAD_DIM ** (-0.5)
    scores = jnp.where(allowed, scores, masked_score)
    exponent = jnp.exp(scores - jnp.max(scores, axis=-1, keepdims=True))
    return exponent * (1.0 / jnp.sum(exponent, axis=-1, keepdims=True))


def attend_kernel(
    count, place_ref, query_ref, keys_ref, values_ref, column_ids, row_ids, x_ref, mod_ref,
    project_ref, every_ref, attended_ref, branch_ref, middle_ref, second_ref, weight, mixed, sems,
):
    copies = attn_copies(place_ref[0], 3, project_ref, every_ref, weight, sems, count)

    @pl.when(pl.program_id(0) == 0)
    def _():
        for copy in copies:
            copy.start()

    allowed = column_ids[...] == row_ids[...]
    for head in range(HEADS):
        lanes, inside = window(head)
        query = jnp.where(inside, query_ref[:, lanes], jnp.zeros((), bf16))
        probs = soft_scores(query, keys_ref[:, lanes], allowed).astype(bf16)
        mixed[:, lanes] = jnp.where(inside, matmul(probs, values_ref[:, lanes]), mixed[:, lanes])
    attended_ref[...] = mixed[...].astype(bf16)

    @pl.when(pl.program_id(0) == 0)
    def _():
        for copy in copies:
            copy.wait()

    branch_ref[...] = matmul(attended_ref[...], weight[...])
    for i in range(BLOCK // CHUNK):
        rows = slice(i * CHUNK, (i + 1) * CHUNK)
        mod = mod_ref.at[0]
        middle = x_ref[rows, :].astype(f32) + mod[i : i + 1, part(2)] * branch_ref[rows, :]
        middle_ref[rows, :] = middle
        normed, _ = normalize(middle)
        second_ref[rows, :] = (
            normed * (1.0 + mod[i : i + 1, part(4)]) + mod[i : i + 1, part(3)]
        ).astype(bf16)


def ffn_kernel(
    count, place_ref, factor_ref, second_ref, middle_ref, branch_ref, cot_ref, mod_ref,
    gate_ref, up_ref, down_ref, every_ref, every_down,
    output_ref, hidden_ref, gate_back_ref, up_back_ref, feed_back_ref, middle_back_ref,
    branch_back_ref, sums_ref, gate_w, up_w, down_w, feed, second_back, sems,
):
    step = pl.program_id(0)
    steps = pl.num_programs(0)
    place = place_ref[0]
    rows_in = gate_ref.shape[0]
    tile = hidden_ref.shape[1]
    tokens = second_ref.shape[0]

    def copies(c, slot):
        found = []
        for which, (shard, target) in enumerate(((gate_ref, gate_w), (up_ref, up_w))):
            found.append(
                pltpu.make_async_copy(
                    shard.at[:, pl.ds(pl.multiple_of(c * tile, LANES), tile)],
                    target.at[slot, pl.ds(pl.multiple_of(place * rows_in, 16), rows_in)],
                    sems.at[slot, which * count],
                )
            )
            for by in range(1, count):
                start = ((place + (count - by)) % count) * rows_in
                found.append(
                    pltpu.make_async_copy(
                        every_ref.at[c * HALVES + which, by - 1],
                        target.at[slot, pl.ds(pl.multiple_of(start, 16), rows_in)],
                        sems.at[slot, which * count + by],
                    )
                )
        return found

    def down_copies(c, slot):
        sem = sems.at[slot, 2 * count]
        own = pltpu.make_async_copy(down_ref, down_w.at[slot], sem)
        by = (place + count - c) % count
        other = pltpu.make_async_copy(
            every_down.at[:, jnp.maximum(by, 1) - 1], down_w.at[slot], sem
        )
        return own, other

    def start(c, slot):
        for copy in copies(c, slot):
            copy.start()
        own, other = down_copies(c, slot)

        @pl.when(c == place)
        def _():
            own.start()

        @pl.when(c != place)
        def _():
            other.start()

    slot = step % 2

    @pl.when(step == 0)
    def _():
        start(step, slot)
        for i in range(tokens // CHUNK):
            rows = slice(i * CHUNK, (i + 1) * CHUNK)
            upstream = cot_ref[rows, :].astype(f32) * factor_ref[0]
            feed_back_ref[rows, :] = (upstream * mod_ref[i : i + 1, part(5)]).astype(bf16)

    @pl.when(step + 1 < steps)
    def _():
        start(step + 1, 1 - slot)

    for copy in copies(step, slot):
        copy.wait()
    down_copies(step, slot)[0].wait()

    sub = 256
    for n in range(tile // sub):
        lanes = slice(n * sub, (n + 1) * sub)
        gate = matmul(second_ref[...], gate_w[slot, :, lanes])
        upval = matmul(second_ref[...], up_w[slot, :, lanes])
        down = down_w[slot].reshape(tile, WIDTH)[lanes, :]
        hidden_back = times_transposed(feed_back_ref[...], down)
        sigmoid = jax.nn.sigmoid(gate)
        silu = gate * sigmoid
        hidden_ref[:, lanes] = (silu * upval).astype(bf16)
        up_back_ref[:, lanes] = (hidden_back * silu).astype(bf16)
        gate_back_ref[:, lanes] = (
            hidden_back * upval * (sigmoid * (1.0 + gate * (1.0 - sigmoid)))
        ).astype(bf16)

    feed_part = matmul(hidden_ref[...], down_w[slot].reshape(tile, WIDTH))
    back_part = times_transposed(gate_back_ref[...], gate_w[slot]) + times_transposed(
        up_back_ref[...], up_w[slot]
    )

    @pl.when(step == 0)
    def _():
        feed[...] = feed_part
        second_back[...] = back_part

    @pl.when(step > 0)
    def _():
        feed[...] += feed_part
        second_back[...] += back_part

    @pl.when(step == steps - 1)
    def _():
        for i in range(tokens // CHUNK):
            rows = slice(i * CHUNK, (i + 1) * CHUNK)
            gate_one = mod_ref[i : i + 1, part(2)]
            scale_two = mod_ref[i : i + 1, part(4)]
            gate_two = mod_ref[i : i + 1, part(5)]
            middle = middle_ref[rows, :]
            output_ref[rows, :] = (middle + gate_two * feed[rows, :]).astype(bf16)
            upstream = cot_ref[rows, :].astype(f32) * factor_ref[0]
            normed, inverse = normalize(middle)
            back = second_back[rows, :]
            middle_back = upstream + normalize_back(normed, inverse, back * (1.0 + scale_two))
            middle_back_ref[rows, :] = middle_back
            branch_back_ref[rows, :] = (middle_back * gate_one).astype(bf16)
            for where, values in enumerate(
                (middle_back * branch_ref[rows, :], back, back * normed, upstream * feed[rows, :])
            ):
                sums_ref[i : i + 1, part(where)] = jnp.sum(values, axis=0, keepdims=True)


def ffn_grad_kernel(second_ref, gate_back_ref, up_back_ref, out_ref, turned):
    @pl.when((pl.program_id(0) == 0) & (pl.program_id(1) == 0))
    def _():
        turned[...] = second_ref[...].T

    @pl.when(pl.program_id(1) == 0)
    def _():
        out_ref[0, 0] = matmul(turned[...], gate_back_ref[...]).astype(bf16)

    @pl.when(pl.program_id(1) == 1)
    def _():
        out_ref[0, 0] = matmul(turned[...], up_back_ref[...]).astype(bf16)


def down_grad_kernel(hidden_ref, feed_back_ref, out_ref):
    grad = contract_rows(hidden_ref[...], feed_back_ref[...]).astype(bf16)
    out_ref[...] = grad.reshape(out_ref.shape)


def attn_grad_kernel(first_ref, attended_ref, joint_back_ref, branch_back_ref, out_ref, turned):
    column = pl.program_id(0)
    count, half = out_ref.shape[2], out_ref.shape[3]

    @pl.when(column == 0)
    def _():
        turned[...] = first_ref[...].T

    @pl.when(column == 3)
    def _():
        turned[...] = attended_ref[...].T

    def put(right):
        for z in range(count):
            for h in range(HALVES):
                start = (z * HALVES + h) * half
                out_ref[0, h, z] = matmul(turned[start : start + half, :], right).astype(bf16)

    @pl.when(column < 3)
    def _():
        put(joint_back_ref[...])

    @pl.when(column == 3)
    def _():
        put(branch_back_ref[...])


def attend_back_kernel(
    count, place_ref, query_ref, keys_ref, values_ref, branch_back_ref, column_ids, row_ids, cos_ref,
    sin_ref, project_ref, every_ref, joint_back_ref, weight, mixed_back, query_back, keys_back,
    values_back, sems,
):
    copies = attn_copies(place_ref[0], 3, project_ref, every_ref, weight, sems, count)

    @pl.when(pl.program_id(0) == 0)
    def _():
        for copy in copies:
            copy.start()
        for copy in copies:
            copy.wait()

    mixed_back[...] = times_transposed(branch_back_ref[...], weight[...]).astype(bf16)
    allowed = column_ids[...] == row_ids[...]
    scaling = HEAD_DIM ** (-0.5)
    for head in range(HEADS):
        lanes, inside = window(head)
        zero = jnp.zeros((), bf16)
        query = jnp.where(inside, query_ref[:, lanes], zero)
        back = jnp.where(inside, mixed_back[:, lanes], zero)
        soft = soft_scores(query, keys_ref[:, lanes], allowed)
        probs_back = times_transposed(back, values_ref[:, lanes])
        scores_back = (
            soft * (probs_back - jnp.sum(soft * probs_back, axis=-1, keepdims=True))
        ).astype(bf16)
        query_back[:, lanes] = jnp.where(
            inside, matmul(scores_back, keys_ref[:, lanes]) * scaling, query_back[:, lanes]
        )
        keys_back[:, lanes] = jnp.where(
            inside, contract_rows(scores_back, query) * scaling, keys_back[:, lanes]
        )
        values_back[:, lanes] = jnp.where(
            inside, contract_rows(soft.astype(bf16), back), values_back[:, lanes]
        )

    @pl.loop(0, BLOCK // CHUNK)
    def _(i):
        rows = pl.ds(pl.multiple_of(i * CHUNK, CHUNK), CHUNK)
        cos, sin = cos_ref[rows, :], sin_ref[rows, :]
        joint_back_ref[rows, part(0)] = rotate(query_back[rows, :], cos, -sin).astype(bf16)
        joint_back_ref[rows, part(1)] = rotate(keys_back[rows, :], cos, -sin).astype(bf16)
        joint_back_ref[rows, part(2)] = values_back[rows, :].astype(bf16)


def first_back_kernel(
    count, place_ref, joint_back_ref, x_ref, middle_back_ref, mod_ref, joint_ref, every_ref,
    grad_ref, sums_ref, weight, first_back, sems,
):
    place = place_ref[0]
    copies = [
        attn_copies(
            place, c, joint_ref.at[:, pl.ds(c * WIDTH, WIDTH)], every_ref, weight.at[c], sems.at[c], count
        )
        for c in range(3)
    ]
    for group in copies:
        for copy in group:
            copy.start()
    for c in range(3):
        for copy in copies[c]:
            copy.wait()
        product = times_transposed(joint_back_ref[:, part(c)], weight[c])
        if c == 0:
            first_back[...] = product
        else:
            first_back[...] += product
    for i in range(x_ref.shape[0] // CHUNK):
        rows = slice(i * CHUNK, (i + 1) * CHUNK)
        normed, inverse = normalize(x_ref[rows, :].astype(f32))
        back = first_back[rows, :]
        grad_ref[rows, :] = middle_back_ref[rows, :] + normalize_back(
            normed, inverse, back * (1.0 + mod_ref[i : i + 1, part(1)])
        )
        sums_ref[i : i + 1, part(0)] = jnp.sum(back, axis=0, keepdims=True)
        sums_ref[i : i + 1, part(1)] = jnp.sum(back * normed, axis=0, keepdims=True)


SMEM = pl.BlockSpec(memory_space=pltpu.SMEM)
VMEM = pl.BlockSpec(memory_space=pltpu.VMEM)
ANY = pl.BlockSpec(memory_space=pl.ANY)


def struct(shape, dtype):
    return jax.ShapeDtypeStruct(shape, dtype)


def params(mega=56):
    return pltpu.CompilerParams(vmem_limit_bytes=mega * MEGA)


def cost(flops, *arrays):
    size = sum(a.size * a.dtype.itemsize for a in arrays)
    return pl.CostEstimate(flops=flops, bytes_accessed=size, transcendentals=0)


def by_block(*shape):
    return pl.BlockSpec(shape, lambda b: (b,) + (0,) * (len(shape) - 1))


def whole(*shape):
    return pl.BlockSpec(shape, lambda *_: (0,) * len(shape))


def first_call(place, x, mod, cos, sin, joint, every):
    tokens = x.shape[0]
    count = every.shape[1] + 1
    shape = struct((tokens, WIDTH), bf16)
    return pl.pallas_call(
        functools.partial(first_kernel, count),
        out_shape=(shape,) * 4,
        in_specs=[SMEM, VMEM, VMEM, VMEM, VMEM, ANY, ANY],
        out_specs=(VMEM,) * 4,
        scratch_shapes=[
            pltpu.VMEM((3, WIDTH, WIDTH), bf16),
            pltpu.VMEM((tokens, WIDTH), f32),
            pltpu.SemaphoreType.DMA((3, 1 + HALVES * (count - 1))),
        ],
        compiler_params=params(),
        cost_estimate=cost(6 * tokens * WIDTH * WIDTH, x, every, cos, sin),
    )(place, x, mod, cos, sin, joint, every)


def attend_call(place, query, keys, values, ids, x, mod, project, every):
    tokens = x.shape[0]
    count = every.shape[1] + 1
    return pl.pallas_call(
        functools.partial(attend_kernel, count),
        grid=(tokens // BLOCK,),
        out_shape=(
            struct((tokens, WIDTH), bf16),
            struct((tokens, WIDTH), f32),
            struct((tokens, WIDTH), f32),
            struct((tokens, WIDTH), bf16),
        ),
        in_specs=[SMEM]
        + [by_block(BLOCK, WIDTH)] * 3
        + [by_block(BLOCK, 1), pl.BlockSpec((1, BLOCK), lambda b: (0, b)), by_block(BLOCK, WIDTH)]
        + [by_block(1, BLOCK // CHUNK, 6 * WIDTH), ANY, ANY],
        out_specs=(by_block(BLOCK, WIDTH),) * 4,
        scratch_shapes=[
            pltpu.VMEM((WIDTH, WIDTH), bf16),
            pltpu.VMEM((BLOCK, WIDTH), f32),
            pltpu.SemaphoreType.DMA((1 + HALVES * (count - 1),)),
        ],
        compiler_params=params(),
        cost_estimate=cost(4 * tokens * WIDTH * WIDTH, query, keys, values, x, x, x, x, x),
    )(
        place, query, keys, values, ids[:, None], ids[None, :], x,
        mod.reshape(tokens // BLOCK, BLOCK // CHUNK, 6 * WIDTH), project, every,
    )


def ffn_call(place, factor, second, middle, branch, cot, mod, gate, up, down, every, every_down):
    tokens = second.shape[0]
    count = every.shape[1] + 1
    ff = gate.shape[1]
    tile = ff // COLUMNS
    down = down.reshape(PIECES, -1, WIDTH)
    tiled = pl.BlockSpec((tokens, tile), lambda c: (0, c))
    full = whole(tokens, WIDTH)
    chunks = tokens // CHUNK
    return pl.pallas_call(
        functools.partial(ffn_kernel, count),
        grid=(COLUMNS,),
        out_shape=(struct((tokens, WIDTH), bf16),)
        + (struct((tokens, ff), bf16),) * 3
        + (
            struct((tokens, WIDTH), bf16),
            struct((tokens, WIDTH), f32),
            struct((tokens, WIDTH), bf16),
            struct((chunks, 4 * WIDTH), f32),
        ),
        in_specs=[SMEM, SMEM, full, full, full, full, whole(chunks, 6 * WIDTH)] + [ANY] * 5,
        out_specs=(full, tiled, tiled, tiled, full, full, full, whole(chunks, 4 * WIDTH)),
        scratch_shapes=[
            pltpu.VMEM((2, WIDTH, tile), bf16),
            pltpu.VMEM((2, WIDTH, tile), bf16),
            pltpu.VMEM((2, PIECES, tile // PIECES, WIDTH), bf16),
            pltpu.VMEM((tokens, WIDTH), f32),
            pltpu.VMEM((tokens, WIDTH), f32),
            pltpu.SemaphoreType.DMA((2, 2 * count + 1)),
        ],
        compiler_params=params(),
        cost_estimate=cost(12 * tokens * WIDTH * ff, every, every_down, gate, gate, gate),
    )(place, factor, second, middle, branch, cot, mod, gate, up, down, every, every_down)


def ffn_grad_call(second, gate_back, up_back):
    tokens, ff = gate_back.shape
    tile = ff // COLUMNS
    tiled = pl.BlockSpec((tokens, tile), lambda c, h: (0, c))
    out = struct((COLUMNS, HALVES, WIDTH, tile), bf16)
    return pl.pallas_call(
        ffn_grad_kernel,
        grid=(COLUMNS, HALVES),
        out_shape=out,
        in_specs=[whole(tokens, WIDTH), tiled, tiled],
        out_specs=pl.BlockSpec((1, 1, WIDTH, tile), lambda c, h: (c, h, 0, 0)),
        scratch_shapes=[pltpu.VMEM((WIDTH, tokens), bf16)],
        compiler_params=params(),
        cost_estimate=cost(4 * tokens * WIDTH * ff, second, gate_back, up_back, out),
    )(second, gate_back, up_back)


def down_grad_call(count, hidden, feed_back):
    tokens, ff = hidden.shape
    rows = ff // count
    out = struct((PIECES, count, rows // PIECES, WIDTH), bf16)
    return pl.pallas_call(
        down_grad_kernel,
        grid=(count,),
        out_shape=out,
        in_specs=[pl.BlockSpec((tokens, rows), lambda z: (0, z)), whole(tokens, WIDTH)],
        out_specs=pl.BlockSpec((PIECES, 1, rows // PIECES, WIDTH), lambda z: (0, z, 0, 0)),
        compiler_params=params(),
        cost_estimate=cost(2 * tokens * WIDTH * ff, hidden, feed_back, out),
    )(hidden, feed_back)


def attn_grad_call(count, first, attended, joint_back, branch_back):
    tokens = first.shape[0]
    half = WIDTH // count // HALVES
    full = whole(tokens, WIDTH)
    out = struct((COLUMNS, HALVES, count, half, WIDTH), bf16)
    return pl.pallas_call(
        attn_grad_kernel,
        grid=(COLUMNS,),
        out_shape=out,
        in_specs=[
            full,
            full,
            pl.BlockSpec((tokens, WIDTH), lambda c: (0, jnp.minimum(c, 2))),
            full,
        ],
        out_specs=pl.BlockSpec((1, HALVES, count, half, WIDTH), lambda c: (c, 0, 0, 0, 0)),
        scratch_shapes=[pltpu.VMEM((WIDTH, tokens), bf16)],
        compiler_params=params(),
        cost_estimate=cost(8 * tokens * WIDTH * WIDTH, first, attended, joint_back, branch_back, out),
    )(first, attended, joint_back, branch_back)


def attend_back_call(place, query, keys, values, branch_back, ids, cos, sin, project, every):
    tokens = query.shape[0]
    count = every.shape[1] + 1
    block = by_block(BLOCK, WIDTH)
    return pl.pallas_call(
        functools.partial(attend_back_kernel, count),
        grid=(tokens // BLOCK,),
        out_shape=struct((tokens, 3 * WIDTH), bf16),
        in_specs=[SMEM, block, block, block, block]
        + [by_block(BLOCK, 1), pl.BlockSpec((1, BLOCK), lambda b: (0, b)), block, block, ANY, ANY],
        out_specs=by_block(BLOCK, 3 * WIDTH),
        scratch_shapes=[
            pltpu.VMEM((WIDTH, WIDTH), bf16),
            pltpu.VMEM((BLOCK, WIDTH), bf16),
            pltpu.VMEM((BLOCK, WIDTH), f32),
            pltpu.VMEM((BLOCK, WIDTH), f32),
            pltpu.VMEM((BLOCK, WIDTH), f32),
            pltpu.SemaphoreType.DMA((1 + HALVES * (count - 1),)),
        ],
        compiler_params=params(),
        cost_estimate=cost(8 * tokens * WIDTH * WIDTH, query, keys, values, branch_back, cos, sin),
    )(place, query, keys, values, branch_back, ids[:, None], ids[None, :], cos, sin, project, every)


def first_back_call(place, joint_back, x, middle_back, mod, joint, every):
    tokens = x.shape[0]
    count = every.shape[1] + 1
    return pl.pallas_call(
        functools.partial(first_back_kernel, count),
        out_shape=(struct((tokens, WIDTH), f32), struct((tokens // CHUNK, 2 * WIDTH), f32)),
        in_specs=[SMEM, VMEM, VMEM, VMEM, VMEM, ANY, ANY],
        out_specs=(VMEM, VMEM),
        scratch_shapes=[
            pltpu.VMEM((3, WIDTH, WIDTH), bf16),
            pltpu.VMEM((tokens, WIDTH), f32),
            pltpu.SemaphoreType.DMA((3, 1 + HALVES * (count - 1))),
        ],
        compiler_params=params(),
        cost_estimate=cost(6 * tokens * WIDTH * WIDTH, joint_back, x, middle_back, middle_back, every),
    )(place, joint_back, x, middle_back, mod, joint, every)


def shifts(count, by):
    return [(i, (i + by) % count) for i in range(count)]


def pick(array, index):
    return lax.dynamic_index_in_dim(array, index, 0, keepdims=False)


def gather_pieces(piece):
    count = lax.axis_size("fsdp")
    foreign = jnp.stack(
        [lax.ppermute(piece, "fsdp", shifts(count, by)) for by in range(1, count)]
    )
    return lax.all_gather(foreign, "bucket", axis=0, tiled=False)


def gather_whole(pieces):
    count = lax.axis_size("fsdp")
    place = lax.axis_index("fsdp")
    full = lax.all_gather(pieces, "fsdp", axis=0, tiled=False)
    return jnp.stack([pick(full, (place - by) % count) for by in range(1, count)], axis=1)


def reduce_pieces(parts):
    count = lax.axis_size("fsdp")
    place = lax.axis_index("fsdp")
    split = lax.axis_size("bucket") == PIECES
    if split:
        mine = lax.psum_scatter(parts, "bucket", scatter_dimension=0, tiled=False)
    else:
        mine = lax.psum(parts, "bucket").swapaxes(0, 1)
    total = pick(mine, place).astype(f32)
    for by in range(1, count):
        total = total + lax.ppermute(
            pick(mine, (place + by) % count), "fsdp", shifts(count, by)
        ).astype(f32)
    total = total.astype(bf16)
    return lax.all_gather(total, "bucket", axis=0, tiled=False) if split else total


def to_group(rows, count, place):
    relative = jnp.stack(
        [pick(rows, place)]
        + [
            lax.ppermute(pick(rows, (place + by) % count), "fsdp", shifts(count, by))
            for by in range(1, count)
        ]
    )
    return jnp.stack([pick(relative, (place - j) % count) for j in range(count)])


def on_device(
    inputs,
    condition,
    segment_ids,
    grid_widths,
    bucket_counts,
    modulate_weight,
    joint_weight,
    project_weight,
    gate_weight,
    up_weight,
    down_weight,
    cotangent,
):
    fsdp_count = lax.axis_size("fsdp")
    place = lax.axis_index("fsdp")
    bucket = lax.axis_index("bucket")
    height = joint_weight.shape[0]
    half = height // HALVES
    ff = gate_weight.shape[1]
    tile = ff // COLUMNS
    down_rows = down_weight.shape[0] // PIECES
    slots = condition.shape[0]
    place_array = place.astype(jnp.int32).reshape(1)

    if lax.axis_size("bucket") == PIECES:
        column, side = bucket // HALVES, bucket % HALVES
        attn_piece = jnp.where(
            column == 3,
            lax.dynamic_slice(project_weight, (side * half, 0), (half, WIDTH)),
            lax.dynamic_slice(joint_weight, (side * half, column * WIDTH), (half, WIDTH)),
        )
        ffn_piece = jnp.where(
            side == 0,
            lax.dynamic_slice(gate_weight, (0, column * tile), (height, tile)),
            lax.dynamic_slice(up_weight, (0, column * tile), (height, tile)),
        )
        down_piece = lax.dynamic_slice_in_dim(down_weight, bucket * down_rows, down_rows, 0)
        every_attn = gather_pieces(attn_piece)
        every_ffn = gather_pieces(ffn_piece)
        every_down = gather_pieces(down_piece)
    else:
        every_attn = gather_whole(
            jnp.concatenate([joint_weight, project_weight], axis=1)
            .reshape(HALVES, half, COLUMNS, WIDTH)
            .transpose(2, 0, 1, 3)
            .reshape(PIECES, half, WIDTH)
        )
        every_ffn = gather_whole(
            jnp.stack([gate_weight, up_weight])
            .reshape(HALVES, height, COLUMNS, tile)
            .transpose(2, 0, 1, 3)
            .reshape(PIECES, height, tile)
        )
        every_down = gather_whole(down_weight.reshape(PIECES, down_rows, WIDTH))

    cond_float = condition.astype(f32)
    lifted = jax.nn.silu(cond_float).astype(bf16)
    lifted_rows = to_group(
        lifted.reshape(slots, fsdp_count, height).transpose(1, 0, 2), fsdp_count, place
    ).reshape(fsdp_count * slots, height)
    modulation = jnp.sum(
        to_group(
            matmul(lifted_rows, modulate_weight).reshape(fsdp_count, slots, 6 * WIDTH),
            fsdp_count,
            place,
        ),
        axis=0,
    )
    one_hot = (
        segment_ids[::CHUNK, None] == jnp.arange(slots, dtype=jnp.int32)[None, :]
    ).astype(f32)
    mod = jnp.dot(one_hot, modulation, precision=lax.Precision.HIGHEST, preferred_element_type=f32)
    counts = bucket_counts.astype(f32)
    mine = jnp.sum(jnp.where(jnp.arange(counts.shape[0], dtype=jnp.int32) == bucket, counts, 0.0))
    factor = (mine * counts.shape[0] / jnp.sum(counts)).reshape(1)
    cos, sin = rope_tables(segment_ids, grid_widths)

    first, query, keys, values = first_call(
        place_array, inputs, mod, cos, sin, joint_weight, every_attn
    )
    attended, branch, middle, second = attend_call(
        place_array, query, keys, values, segment_ids, inputs, mod, project_weight, every_attn
    )
    output, hidden, gate_back, up_back, feed_back, middle_back, branch_back, late_sums = ffn_call(
        place_array, factor, second, middle, branch, cotangent, mod,
        gate_weight, up_weight, down_weight, every_ffn, every_down,
    )
    down_sum = reduce_pieces(down_grad_call(fsdp_count, hidden, feed_back)).reshape(-1, WIDTH)
    ffn_parts = ffn_grad_call(second, gate_back, up_back).reshape(
        PIECES, fsdp_count, height, tile
    )
    ffn_sum = (
        reduce_pieces(ffn_parts)
        .reshape(COLUMNS, HALVES, height, tile)
        .transpose(1, 2, 0, 3)
        .reshape(HALVES, height, ff)
    )
    joint_back = attend_back_call(
        place_array, query, keys, values, branch_back, segment_ids, cos, sin, project_weight, every_attn
    )
    attn_parts = attn_grad_call(fsdp_count, first, attended, joint_back, branch_back).reshape(
        PIECES, fsdp_count, half, WIDTH
    )
    attn_sum = (
        reduce_pieces(attn_parts)
        .reshape(COLUMNS, HALVES, half, WIDTH)
        .transpose(1, 2, 0, 3)
        .reshape(height, COLUMNS * WIDTH)
    )
    grad_inputs, early_sums = first_back_call(
        place_array, joint_back, inputs, middle_back, mod, joint_weight, every_attn
    )
    modulation_back = lax.dot_general(
        one_hot,
        jnp.concatenate([early_sums, late_sums], axis=1),
        (((0,), (0,)), ((), ())),
        precision=lax.Precision.HIGHEST,
        preferred_element_type=f32,
    ).astype(bf16)

    everyone = lax.all_gather(
        jnp.concatenate([modulation_back, lifted], axis=1), ("bucket", "fsdp"), axis=0, tiled=True
    )
    all_back = everyone[:, : 6 * WIDTH]
    all_lifted = lax.dynamic_slice_in_dim(everyone, 6 * WIDTH + place * height, height, 1)
    modulate_gradient = contract_rows(all_lifted, all_back)
    group_back = lax.dynamic_slice_in_dim(
        all_back, bucket * fsdp_count * slots, fsdp_count * slots, 0
    )
    slope_rows = times_transposed(group_back, modulate_weight)
    condition_slope = (
        to_group(slope_rows.reshape(fsdp_count, slots, height), fsdp_count, place)
        .transpose(1, 0, 2)
        .reshape(slots, WIDTH)
    )
    grad_condition = condition_slope * silu_slope(cond_float)
    return (
        output,
        grad_inputs,
        grad_condition,
        modulate_gradient,
        attn_sum[:, : 3 * WIDTH].astype(f32),
        attn_sum[:, 3 * WIDTH :].astype(f32),
        ffn_sum[0].astype(f32),
        ffn_sum[1].astype(f32),
        down_sum.astype(f32),
    )


def solution(mesh):
    spread = P(("bucket", "fsdp"), None)
    rows = P("fsdp", None)
    in_specs = (
        spread, spread, P(("bucket", "fsdp")), P(("bucket", "fsdp")), P(),
        rows, rows, rows, rows, rows, rows, spread,
    )
    out_specs = (spread, spread, spread, rows, rows, rows, rows, rows, rows)
    return jax.shard_map(
        on_device, mesh=mesh, in_specs=in_specs, out_specs=out_specs, check_vma=False
    )
```

time: 890 us -> 711 us (0.80)
  local copies, waits for them, and re-layouts: 261 us -> 28.6 us
  waiting for transfers between devices: 305 us -> 457 us
  Pallas kernels: 0 us -> 149 us
  matrix products: 157 us -> 10.3 us
  other arithmetic: 88.8 us -> 22.3 us
  starting transfers between devices: 48.9 us -> 21.5 us
    pallas_call x0 -> x8, Pallas kernels: none -> 149 us  [the longest x1 40.9 us: ffn_call(): pl.pallas_call(functools.partial(ffn_kernel, count), grid=(COLUMNS,), out...]
    reduce_scatter x3, waiting for transfers between devices: 39.1 us -> 124 us  [reduce_pieces(): mine = lax.psum_scatter(parts, 'bucket', scatter_dimension=0, tiled=False)]
    reshape x12 -> x3, local copies, waits for them, and re-layouts: 88.3 us -> 8.6 us  [the longest x1 4.73 us: on_device(): ffn_sum = reduce_pieces(ffn_parts).reshape(COLUMNS, HALVES, height, tile)...]
    dot_general x12 -> x2, matrix products: 65.1 us -> 4.18 us  [the longest x1 2.93 us: matmul(): return jnp.dot(left, right, preferred_element_type=f32)]
    another operation x10 -> x5, local copies, waits for them, and re-layouts: 57.4 us -> 4.53 us  [the longest x4 4.47 us: rope_tables(): return (jnp.tile(cos, (1, HEADS)), jnp.tile(sin, (1, HEADS)))]
    dot_general x6 -> x1, matrix products: 48.1 us -> 1.28 us  [times_transposed(): lax.dot_general(left, right, (((1,), (1,)), ((), ())), preferred_element_...]
    another operation x16 -> x1, other arithmetic: 44.3 us -> 0.18 us  [the longest x3 15 us: gather_pieces(): jnp.stack([pick(relative, (place - j) % count) for j in range(count)])]
    all_gather x6, waiting for transfers between devices: 73.9 us -> 115 us  [the longest x3 75.1 us: reduce_pieces(): lax.all_gather(total, 'bucket', axis=0, tiled=False)]
  transfers between devices with their start and end apart: 37 -> 37, of which waited for: 23 -> 21; matrix products, arithmetic and copies ran while one was open for 39% -> 7% of each run, Pallas kernels for 0% -> 14%
where the time goes in v2:
time: 711 us; the launch traced here: 705 us
  waiting for transfers between devices  457 us (64%)
  Pallas kernels  149 us (21%)
  local copies, waits for them, and re-layouts  28.6 us (4%)
  other arithmetic  22.3 us (3%)
  starting transfers between devices  21.5 us (3%)
  between operations  16.4 us (2%)
  matrix products  10.3 us (1%)
    reduce_scatter x3, waiting for transfers between devices, reduce_pieces(): mine = lax.psum_scatter(parts, 'bucket', scatter_dimension=0, tiled=False)  124 us
    ppermute x9, waiting for transfers between devices, reduce_pieces(): lax.ppermute(pick(mine, (place + by) % count), 'fsdp', shifts(count, by))  88 us
    ppermute x9, waiting for transfers between devices, gather_pieces(): lax.ppermute(piece, 'fsdp', shifts(count, by))  83.7 us
    all_gather x3, waiting for transfers between devices, reduce_pieces(): lax.all_gather(total, 'bucket', axis=0, tiled=False)  75.1 us
    pallas_call x1, Pallas kernels, ffn_call(): pl.pallas_call(functools.partial(ffn_kernel, count), grid=(COLUMNS,), out...  40.9 us
    all_gather x3, waiting for transfers between devices, gather_pieces(): return lax.all_gather(foreign, 'bucket', axis=0, tiled=False)  39.7 us
    all_gather x1, waiting for transfers between devices, on_device(): lax.all_gather(jnp.concatenate([modulation_back, lifted], axis=1), ('buck...  33.9 us
    pallas_call x1, Pallas kernels, attend_back_call(): pl.pallas_call(functools.partial(attend_back_kernel, count), grid=(tokens...  30.1 us
  transfers between devices with their start and end apart: 37, of which 21 were waited for; matrix products, arithmetic and copies ran while one was open for 7% of the time, Pallas kernels for 14%

profile of v2, /device:TPU:25, one launch (start us, length us, event | category | flops | bytes accessed | tf_op | source)
XLA Modules:
  0.0 705.4 jit_solution(2477493334086906471)
XLA Ops:
  17.1 21.2 %collective-permute-done.7 = bf16[144,1152]{1,0:T(8,128)(2,1)S(1)} collective-permute-done((bf16[144,1152]{1,0:T(8,128)(2,1)S(1)}, bf16[144,1152]{1,0:T(8,128)(2,1)S(1)}, u32[]{:S(2)}, u32[]{:S(2)}) %collective-permute-start.7) | collective-permute-done | bytes 331808 | tf_op jit(solution)/shard_map/ppermute | solution.py:673
  45.9 16.3 %collective-permute-done.13 = bf16[96,1152]{1,0:T(8,128)(2,1)S(1)} collective-permute-done((bf16[96,1152]{1,0:T(8,128)(2,1)S(1)}, bf16[96,1152]{1,0:T(8,128)(2,1)S(1)}, u32[]{:S(2)}, u32[]{:S(2)}) %collective-permute-start.13) | collective-permute-done | bytes 221216 | tf_op jit(solution)/shard_map/ppermute | solution.py:673
  67.0 8.4 %collective-permute-done.9 = bf16[288,768]{1,0:T(8,128)(2,1)S(1)} collective-permute-done((bf16[288,768]{1,0:T(8,128)(2,1)S(1)}, bf16[288,768]{1,0:T(8,128)(2,1)S(1)}, u32[]{:S(2)}, u32[]{:S(2)}) %collective-permute-start.9) | collective-permute-done | bytes 442400 | tf_op jit(solution)/shard_map/ppermute | solution.py:673
  75.3 28.8 %collective-permute-done.10 = bf16[288,768]{1,0:T(8,128)(2,1)S(1)} collective-permute-done((bf16[288,768]{1,0:T(8,128)(2,1)S(1)}, bf16[288,768]{1,0:T(8,128)(2,1)S(1)}, u32[]{:S(2)}, u32[]{:S(2)}) %collective-permute-start.10) | collective-permute-done | bytes 442400 | tf_op jit(solution)/shard_map/ppermute | solution.py:673
  124.9 10.3 %collective-permute-done.4 = f32[8,6912]{1,0:T(8,128)S(1)} collective-permute-done((f32[8,6912]{1,0:T(8,128)}, f32[8,6912]{1,0:T(8,128)S(1)}, u32[]{:S(2)}, u32[]{:S(2)}) %collective-permute-start.4) | collective-permute-done | bytes 221216 | tf_op jit(solution)/shard_map/ppermute | solution.py:706
  136.3 15.7 %shard_map.187 = (bf16[512,1152]{1,0:T(8,128)(2,1)}, bf16[512,1152]{1,0:T(8,128)(2,1)}, bf16[512,1152]{1,0:T(8,128)(2,1)}, bf16[512,1152]{1,0:T(8,128)(2,1)}) custom-call(s32[1]{0:T(128)} %bitcast.place_ref, bf16[512,1152]{1,0:T(8,128)(2,1)} %x_ref.5, f32[8,6912]{1,0:T(8,128)} %copy-done.2, f32[512,1152]{1,0:T(8,128)} %copy.58.cos_ref, ...), custom_call_target="tpu_custom_call" | custom-call | flops 4076863488 | bytes 13860864 | tf_op jit(solution)/shard_map/pallas_call | solution.py:486
  152.0 12.9 %shard_map.188 = (bf16[512,1152]{1,0:T(8,128)(2,1)}, f32[512,1152]{1,0:T(8,128)}, f32[512,1152]{1,0:T(8,128)}, bf16[512,1152]{1,0:T(8,128)(2,1)}) custom-call(s32[1]{0:T(128)} %bitcast.place_ref, bf16[512,1152]{1,0:T(8,128)(2,1)} %get-tuple-element.27.query_ref, bf16[512,1152]{1,0:T(8,128)(2,1)} %get-tuple-element.28.keys_ref, ...), custom_call_target="tpu_custom_call" | custom-call | flops 2717908992 | bytes 9437184 | tf_op jit(solution)/shard_map/pallas_call | solution.py:504
  165.0 39.7 %all-gather.18.cloned.1.call-done = bf16[24,288,768]{2,1,0:T(8,128)(2,1)} async-done(((bf16[3,288,768]{2,1,0:T(8,128)(2,1)}), bf16[24,288,768]{2,1,0:T(8,128)(2,1)}) %all-gather.18.cloned.1.call-update) | async-done | bytes 10616848 | tf_op jit(solution)/shard_map/all_gather | solution.py:675
  204.7 40.9 %shard_map.189 = (bf16[512,1152]{1,0:T(8,128)(2,1)}, bf16[512,3072]{1,0:T(8,128)(2,1)}, bf16[512,3072]{1,0:T(8,128)(2,1)}, bf16[512,3072]{1,0:T(8,128)(2,1)}, bf...) custom-call(s32[1]{0:T(128)} %bitcast.place_ref, ...), custom_call_target="tpu_custom_call" | custom-call | flops 21743271936 | bytes 21233664 | tf_op jit(solution)/shard_map/pallas_call | solution.py:540
  245.6 8.2 %shard_map.194 = bf16[8,4,96,1152]{3,2,1,0:T(8,128)(2,1)} custom-call(bf16[512,3072]{1,0:T(8,128)(2,1)} %get-tuple-element.43.hidden_ref, bf16[512,1152]{1,0:T(8,128)(2,1)} %get-tuple-element.44.feed_back_ref), custom_call_target="tpu_custom_call" | custom-call | flops 3623878656 | bytes 11403264 | tf_op jit(solution)/shard_map/pallas_call | solution.py:587
  253.9 30.1 %shard_map.190.joint_back_ref = bf16[512,3456]{1,0:T(8,128)(2,1)} custom-call(s32[1]{0:T(128)} %bitcast.place_ref, bf16[512,1152]{1,0:T(8,128)(2,1)} %get-tuple-element.27.query_ref, bf16[512,1152]{1,0:T(8,128)(2,1)} %get-tuple-element.28.keys_ref, bf16[512,1152]{1,0:T(8,128)(2,1)} %get-tuple-element.29.values_ref, ...), custom_call_target="tpu_custom_call" | custom-call | flops 5435817984 | bytes 9437184 | tf_op jit(solution)/shard_map/pallas_call | solution.py:624
  284.0 12.2 %shard_map.192 = bf16[4,2,4,144,1152]{4,3,2,1,0:T(8,128)(2,1)} custom-call(bf16[512,1152]{1,0:T(8,128)(2,1)} %get-tuple-element.39.first_ref, bf16[512,1152]{1,0:T(8,128)(2,1)} %get-tuple-element.40.attended_ref, bf16[512,3456]{1,0:T(8,128)(2,1)} %shard_map.190.joint_back_ref, bf16[512,1152]{1,0:T(8,128)(2,1)} %get-tuple-element.34.branch_back_ref), custom_call_target="tpu_custom_call" | custom-call | flops 5435817984 | bytes 17694720 | tf_op jit(solution)/shard_map/pallas_call | solution.py:603
  296.3 15.5 %shard_map.193 = bf16[4,2,1152,768]{3,2,1,0:T(8,128)(2,1)} custom-call(bf16[512,1152]{1,0:T(8,128)(2,1)} %get-tuple-element.30.second_ref, bf16[512,3072]{1,0:T(8,128)(2,1)} %get-tuple-element.41.gate_back_ref, bf16[512,3072]{1,0:T(8,128)(2,1)} %get-tuple-element.42.up_back_ref), custom_call_target="tpu_custom_call" | custom-call | flops 7247757312 | bytes 21626880 | tf_op jit(solution)/shard_map/pallas_call | solution.py:571
  311.9 13.7 %shard_map.191 = (f32[512,1152]{1,0:T(8,128)}, f32[8,2304]{1,0:T(8,128)}) custom-call(s32[1]{0:T(128)} %bitcast.place_ref, bf16[512,3456]{1,0:T(8,128)(2,1)} %shard_map.190.joint_back_ref, bf16[512,1152]{1,0:T(8,128)(2,1)} %x_ref.5, f32[512,1152]{1,0:T(8,128)} %get-tuple-element.35.middle_back_ref, f32[8,6912]{1,0:T(8,128)} %copy-done.2, ...), custom_call_target="tpu_custom_call" | custom-call | flops 4076863488 | bytes 17399808 | tf_op jit(solution)/shard_map/pallas_call | solution.py:647
  335.7 14.2 %collective-permute-done.25 = bf16[96,1152]{1,0:T(8,128)(2,1)S(1)} collective-permute-done((bf16[96,1152]{1,0:T(8,128)(2,1)S(1)}, bf16[96,1152]{1,0:T(8,128)(2,1)S(1)}, u32[]{:S(2)}, u32[]{:S(2)}) %collective-permute-start.25) | collective-permute-done | bytes 221216 | tf_op jit(solution)/shard_map/ppermute | solution.py:695
  352.0 53.1 %reduce-scatter.4.cloned.1.call-done = bf16[1,4,144,1152]{3,2,1,0:T(8,128)(2,1)} async-done(((bf16[8,4,144,1152]{3,2,1,0:T(8,128)(2,1)}), bf16[1,4,144,1152]{3,2,1,0:T(8,128)(2,1)}) %reduce-scatter.4.cloned.1.call-update) | async-done | bytes 1327120 | tf_op jit(solution)/shard_map/reduce_scatter | solution.py:690
  415.0 21.3 %collective-permute-done.19 = bf16[144,1152]{1,0:T(8,128)(2,1)S(1)} collective-permute-done((bf16[144,1152]{1,0:T(8,128)(2,1)S(1)}, bf16[144,1152]{1,0:T(8,128)(2,1)S(1)}, u32[]{:S(2)}, u32[]{:S(2)}) %collective-permute-start.19) | collective-permute-done | bytes 331808 | tf_op jit(solution)/shard_map/ppermute | solution.py:695
  438.3 71.4 %reduce-scatter.6.cloned.1.call-done = bf16[1,4,288,768]{3,2,1,0:T(8,128)(2,1)} async-done(((bf16[8,4,288,768]{3,2,1,0:T(8,128)(2,1)}), bf16[1,4,288,768]{3,2,1,0:T(8,128)(2,1)}) %reduce-scatter.6.cloned.1.call-update) | async-done | bytes 1769488 | tf_op jit(solution)/shard_map/reduce_scatter | solution.py:690
  512.8 9.3 %collective-permute-done.21 = bf16[288,768]{1,0:T(8,128)(2,1)S(1)} collective-permute-done((bf16[288,768]{1,0:T(8,128)(2,1)S(1)}, bf16[288,768]{1,0:T(8,128)(2,1)S(1)}, u32[]{:S(2)}, u32[]{:S(2)}) %collective-permute-start.21) | collective-permute-done | bytes 442400 | tf_op jit(solution)/shard_map/ppermute | solution.py:695
  522.1 31.2 %collective-permute-done.22 = bf16[288,768]{1,0:T(8,128)(2,1)S(1)} collective-permute-done((bf16[288,768]{1,0:T(8,128)(2,1)S(1)}, bf16[288,768]{1,0:T(8,128)(2,1)S(1)}, u32[]{:S(2)}, u32[]{:S(2)}) %collective-permute-start.22) | collective-permute-done | bytes 442400 | tf_op jit(solution)/shard_map/ppermute | solution.py:695
  555.4 33.9 %all-gather.14.cloned.1.call-done = bf16[256,8064]{1,0:T(8,128)(2,1)} async-done(((bf16[8,8064]{1,0:T(8,128)(2,1)}), bf16[256,8064]{1,0:T(8,128)(2,1)}) %all-gather.14.cloned.1.call-update) | async-done | bytes 4128784 | tf_op jit(solution)/shard_map/all_gather | solution.py:834
  602.4 16.0 %all-gather.26.cloned.1.call-done = bf16[768,1152]{1,0:T(8,128)(2,1)} async-done(((bf16[96,1152]{1,0:T(8,128)(2,1)}), bf16[768,1152]{1,0:T(8,128)(2,1)}) %all-gather.26.cloned.1.call-update) | async-done | bytes 1769488 | tf_op jit(solution)/shard_map/all_gather | solution.py:699
  621.9 29.4 %all-gather.22.cloned.1.call-done = bf16[1152,1152]{1,0:T(8,128)(2,1)} async-done(((bf16[144,1152]{1,0:T(8,128)(2,1)}), bf16[1152,1152]{1,0:T(8,128)(2,1)}) %all-gather.22.cloned.1.call-update) | async-done | bytes 2654224 | tf_op jit(solution)/shard_map/all_gather | solution.py:699
  658.2 29.6 %all-gather.24.cloned.1.call-done = bf16[2304,768]{1,0:T(8,128)(2,1)} async-done(((bf16[288,768]{1,0:T(8,128)(2,1)}), bf16[2304,768]{1,0:T(8,128)(2,1)}) %all-gather.24.cloned.1.call-update) | async-done | bytes 3538960 | tf_op jit(solution)/shard_map/all_gather | solution.py:699
  (149 shorter events, 105.6 us)
Async XLA Ops:
  7.2 129.1 %all-gather.16.cloned.1.call-start = ((), (), s32[]{:S(2)}) async-start(), calls=%async_computation.7 | async-start | bytes 8957952 | tf_op jit(solution)/shard_map/all_gather | solution.py:675
  8.5 29.9 %collective-permute-start.7 = (bf16[144,1152]{1,0:T(8,128)(2,1)S(1)}, bf16[144,1152]{1,0:T(8,128)(2,1)S(1)}, u32[]{:S(2)}, u32[]{:S(2)}) collective-permute-start(bf16[144,1152]{1,0:T(8,128)(2,1)S(1)} %dynamic-slice_select_fusion.1), channel_id=1, source_target_pairs={{0,2},{1,3},{2,0},{3,1},{4,6},{5,7},{6,4},{7,5},{8,10},{9,11},{10,... | collective-permute-start | bytes 995336 | tf_op jit(solution)/shard_map/ppermute | solution.py:673
  9.8 28.5 %collective-permute-start.8 = (bf16[144,1152]{1,0:T(8,128)(2,1)S(1)}, bf16[144,1152]{1,0:T(8,128)(2,1)S(1)}, u32[]{:S(2)}, u32[]{:S(2)}) collective-permute-start(bf16[144,1152]{1,0:T(8,128)(2,1)S(1)} %dynamic-slice_select_fusion.1), channel_id=1, source_target_pairs={{0,3},{1,0},{2,1},{3,2},{4,7},{5,4},{6,5},{7,6},{8,11},{9,8},{10,9... | collective-permute-start | bytes 995336 | tf_op jit(solution)/shard_map/ppermute | solution.py:673
  39.5 125.5 %all-gather.20.cloned.1.call-start = ((), (), s32[]{:S(2)}) async-start(), calls=%async_computation.9 | async-start | bytes 5971968 | tf_op jit(solution)/shard_map/all_gather | solution.py:675
  40.5 21.7 %collective-permute-start.13 = (bf16[96,1152]{1,0:T(8,128)(2,1)S(1)}, bf16[96,1152]{1,0:T(8,128)(2,1)S(1)}, u32[]{:S(2)}, u32[]{:S(2)}) collective-permute-start(bf16[96,1152]{1,0:T(8,128)(2,1)S(1)} %constant_dynamic-slice_fusion.5), channel_id=1, source_target_pairs={{0,2},{1,3},{2,0},{3,1},{4,6},{5,7},{6,4},{7,5},{8,10},{9,11},{10,... | collective-permute-start | bytes 663560 | tf_op jit(solution)/shard_map/ppermute | solution.py:673
  42.7 19.5 %collective-permute-start.14 = (bf16[96,1152]{1,0:T(8,128)(2,1)S(1)}, bf16[96,1152]{1,0:T(8,128)(2,1)S(1)}, u32[]{:S(2)}, u32[]{:S(2)}) collective-permute-start(bf16[96,1152]{1,0:T(8,128)(2,1)S(1)} %constant_dynamic-slice_fusion.5), channel_id=1, source_target_pairs={{0,3},{1,0},{2,1},{3,2},{4,7},{5,4},{6,5},{7,6},{8,11},{9,8},{10,9... | collective-permute-start | bytes 663560 | tf_op jit(solution)/shard_map/ppermute | solution.py:673
  63.2 141.5 %all-gather.18.cloned.1.call-start = ((), (), s32[]{:S(2)}) async-start(), calls=%async_computation.8 | async-start | bytes 11943936 | tf_op jit(solution)/shard_map/all_gather | solution.py:675
  64.6 39.5 %collective-permute-start.10 = (bf16[288,768]{1,0:T(8,128)(2,1)S(1)}, bf16[288,768]{1,0:T(8,128)(2,1)S(1)}, u32[]{:S(2)}, u32[]{:S(2)}) collective-permute-start(bf16[288,768]{1,0:T(8,128)(2,1)S(1)} %dynamic-slice_select_fusion), channel_id=1, source_target_pairs={{0,2},{1,3},{2,0},{3,1},{4,6},{5,7},{6,4},{7,5},{8,10},{9,11},{10,... | collective-permute-start | bytes 1327112 | tf_op jit(solution)/shard_map/ppermute | solution.py:673
  65.6 38.6 %collective-permute-start.11 = (bf16[288,768]{1,0:T(8,128)(2,1)S(1)}, bf16[288,768]{1,0:T(8,128)(2,1)S(1)}, u32[]{:S(2)}, u32[]{:S(2)}) collective-permute-start(bf16[288,768]{1,0:T(8,128)(2,1)S(1)} %dynamic-slice_select_fusion), channel_id=1, source_target_pairs={{0,3},{1,0},{2,1},{3,2},{4,7},{5,4},{6,5},{7,6},{8,11},{9,8},{10,9... | collective-permute-start | bytes 1327112 | tf_op jit(solution)/shard_map/ppermute | solution.py:673
  105.4 222.2 %reduce-scatter.8.cloned.1.call-start = ((), (), s32[]{:S(2)}) async-start(), calls=%async_computation.6 | async-start | bytes 7962624 | tf_op jit(solution)/shard_map/reduce_scatter | solution.py:690
  116.1 19.0 %collective-permute-start.4 = (f32[8,6912]{1,0:T(8,128)}, f32[8,6912]{1,0:T(8,128)S(1)}, u32[]{:S(2)}, u32[]{:S(2)}) collective-permute-start(f32[8,6912]{1,0:T(8,128)} %get-tuple-element.62), channel_id=1, source_target_pairs={{0,2},{1,3},{2,0},{3,1},{4,6},{5,7},{6,4},{7,5},{8,10},{9,11},{10,... | collective-permute-start | bytes 663560 | tf_op jit(solution)/shard_map/ppermute | solution.py:706
  117.1 18.1 %collective-permute-start.5 = (f32[8,6912]{1,0:T(8,128)}, f32[8,6912]{1,0:T(8,128)S(1)}, u32[]{:S(2)}, u32[]{:S(2)}) collective-permute-start(f32[8,6912]{1,0:T(8,128)} %get-tuple-element.61), channel_id=1, source_target_pairs={{0,3},{1,0},{2,1},{3,2},{4,7},{5,4},{6,5},{7,6},{8,11},{9,8},{10,9... | collective-permute-start | bytes 663560 | tf_op jit(solution)/shard_map/ppermute | solution.py:706
  253.8 151.2 %reduce-scatter.4.cloned.1.call-start = ((), (), s32[]{:S(2)}) async-start(), calls=%async_computation.4 | async-start | bytes 11943936 | tf_op jit(solution)/shard_map/reduce_scatter | solution.py:690
  296.3 213.4 %reduce-scatter.6.cloned.1.call-start = ((), (), s32[]{:S(2)}) async-start(), calls=%async_computation.5 | async-start | bytes 15925248 | tf_op jit(solution)/shard_map/reduce_scatter | solution.py:690
  311.9 277.4 %all-gather.14.cloned.1.call-start = ((), (), s32[]{:S(2)}) async-start(), calls=%async_computation.3 | async-start | bytes 4257792 | tf_op jit(solution)/shard_map/all_gather | solution.py:834
  327.6 290.9 %all-gather.26.cloned.1.call-start = ((), (), s32[]{:S(2)}) async-start(), calls=%async_computation.12 | async-start | bytes 1990656 | tf_op jit(solution)/shard_map/all_gather | solution.py:699
  328.9 20.9 %collective-permute-start.25 = (bf16[96,1152]{1,0:T(8,128)(2,1)S(1)}, bf16[96,1152]{1,0:T(8,128)(2,1)S(1)}, u32[]{:S(2)}, u32[]{:S(2)}) collective-permute-start(bf16[96,1152]{1,0:T(8,128)(2,1)S(1)} %get-tuple-element.59), channel_id=1, source_target_pairs={{0,2},{1,3},{2,0},{3,1},{4,6},{5,7},{6,4},{7,5},{8,10},{9,11},{10,... | collective-permute-start | bytes 663560 | tf_op jit(solution)/shard_map/ppermute | solution.py:695
  330.4 19.5 %collective-permute-start.26 = (bf16[96,1152]{1,0:T(8,128)(2,1)S(1)}, bf16[96,1152]{1,0:T(8,128)(2,1)S(1)}, u32[]{:S(2)}, u32[]{:S(2)}) collective-permute-start(bf16[96,1152]{1,0:T(8,128)(2,1)S(1)} %get-tuple-element.58), channel_id=1, source_target_pairs={{0,3},{1,0},{2,1},{3,2},{4,7},{5,4},{6,5},{7,6},{8,11},{9,8},{10,9... | collective-permute-start | bytes 663560 | tf_op jit(solution)/shard_map/ppermute | solution.py:695
  351.7 299.6 %all-gather.22.cloned.1.call-start = ((), (), s32[]{:S(2)}) async-start(), calls=%async_computation.10 | async-start | bytes 2985984 | tf_op jit(solution)/shard_map/all_gather | solution.py:699
  406.6 29.8 %collective-permute-start.19 = (bf16[144,1152]{1,0:T(8,128)(2,1)S(1)}, bf16[144,1152]{1,0:T(8,128)(2,1)S(1)}, u32[]{:S(2)}, u32[]{:S(2)}) collective-permute-start(bf16[144,1152]{1,0:T(8,128)(2,1)S(1)} %get-tuple-element.56), channel_id=1, source_target_pairs={{0,2},{1,3},{2,0},{3,1},{4,6},{5,7},{6,4},{7,5},{8,10},{9,11},{10,... | collective-permute-start | bytes 995336 | tf_op jit(solution)/shard_map/ppermute | solution.py:695
  407.8 28.5 %collective-permute-start.20 = (bf16[144,1152]{1,0:T(8,128)(2,1)S(1)}, bf16[144,1152]{1,0:T(8,128)(2,1)S(1)}, u32[]{:S(2)}, u32[]{:S(2)}) collective-permute-start(bf16[144,1152]{1,0:T(8,128)(2,1)S(1)} %get-tuple-element.55), channel_id=1, source_target_pairs={{0,3},{1,0},{2,1},{3,2},{4,7},{5,4},{6,5},{7,6},{8,11},{9,8},{10,9... | collective-permute-start | bytes 995336 | tf_op jit(solution)/shard_map/ppermute | solution.py:695
  438.3 249.6 %all-gather.24.cloned.1.call-start = ((), (), s32[]{:S(2)}) async-start(), calls=%async_computation.11 | async-start | bytes 3981312 | tf_op jit(solution)/shard_map/all_gather | solution.py:699
  511.3 42.0 %collective-permute-start.22 = (bf16[288,768]{1,0:T(8,128)(2,1)S(1)}, bf16[288,768]{1,0:T(8,128)(2,1)S(1)}, u32[]{:S(2)}, u32[]{:S(2)}) collective-permute-start(bf16[288,768]{1,0:T(8,128)(2,1)S(1)} %get-tuple-element.53), channel_id=1, source_target_pairs={{0,2},{1,3},{2,0},{3,1},{4,6},{5,7},{6,4},{7,5},{8,10},{9,11},{10,... | collective-permute-start | bytes 1327112 | tf_op jit(solution)/shard_map/ppermute | solution.py:695
  512.6 40.8 %collective-permute-start.23 = (bf16[288,768]{1,0:T(8,128)(2,1)S(1)}, bf16[288,768]{1,0:T(8,128)(2,1)S(1)}, u32[]{:S(2)}, u32[]{:S(2)}) collective-permute-start(bf16[288,768]{1,0:T(8,128)(2,1)S(1)} %get-tuple-element.52), channel_id=1, source_target_pairs={{0,3},{1,0},{2,1},{3,2},{4,7},{5,4},{6,5},{7,6},{8,11},{9,8},{10,9... | collective-permute-start | bytes 1327112 | tf_op jit(solution)/shard_map/ppermute | solution.py:695
  (21 other events, 252.6 us)
Sparse Core Ops, SparseCore 0:
  39.6 54.8 all-gather.15
  96.9 41.3 all-gather.19
  140.8 63.8 all-gather.17
  254.0 65.0 reduce-scatter.7
  322.9 82.1 reduce-scatter.3
  408.9 100.7 reduce-scatter.5
  513.5 75.7 all-gather.13
  591.9 26.5 all-gather.25
  621.1 30.2 all-gather.21
  653.8 33.9 all-gather.23

commit v3 on v2

--- a/solution.py
+++ b/solution.py
@@ -96,41 +96,52 @@
     return values * cos + partner * sin
 
 
-def attn_copies(place, column, shard, everyone, target, sems, count):
-    rows = shard.shape[0]
-    half = rows // HALVES
-    copies = [
-        pltpu.make_async_copy(
-            shard, target.at[pl.ds(pl.multiple_of(place * rows, 16), rows)], sems.at[0]
-        )
-    ]
-    for by in range(1, count):
-        start = ((place + (count - by)) % count) * rows
-        for h in range(HALVES):
-            copies.append(
-                pltpu.make_async_copy(
-                    everyone.at[column * HALVES + h, by - 1],
-                    target.at[pl.ds(pl.multiple_of(start + h * half, 16), half)],
-                    sems.at[1 + (by - 1) * HALVES + h],
-                )
-            )
+def take(start, size):
+    return pl.ds(pl.multiple_of(start, 16), size)
+
+
+def first_part(rows):
+    return -(-rows // 32) * 16
+
+
+def piece_copies(where, count, sources, target, rows, sem):
+    place, column, side = where
+    first = first_part(rows)
+    copies = []
+    for other in range(HALVES):
+        here = sources[5 * other : 5 * other + 5]
+        for by in range(1, count):
+            owner = (place + (count - by)) % count
+            for j in range(COLUMNS):
+                spans = [(here[j], 0, rows)] if j < 3 else [(here[3], 0, first), (here[4], first, rows - first)]
+                for ref, start, size in spans:
+                    to = target(column ^ j, side ^ other, owner, start, size)
+                    copies.append(pltpu.make_async_copy(ref.at[by - 1], to, sem(column ^ j, side ^ other, owner)))
     return copies
 
 
+def wait_for(ref, sem):
+    pltpu.make_async_copy(ref, ref, sem).wait()
+
+
 def first_kernel(
-    count, place_ref, x_ref, mod_ref, cos_ref, sin_ref, joint_ref, every_ref,
-    first_ref, query_ref, keys_ref, values_ref, weight, total, sems,
+    count, where_ref, x_ref, mod_ref, cos_ref, sin_ref, joint_ref, project_ref, *refs
 ):
-    place = place_ref[0]
-    copies = [
-        attn_copies(
-            place, c, joint_ref.at[:, pl.ds(c * WIDTH, WIDTH)], every_ref, weight.at[c], sems.at[c], count
-        )
-        for c in range(3)
-    ]
-    for group in copies:
-        for copy in group:
-            copy.start()
+    sources = refs[:10]
+    first_ref, query_ref, keys_ref, values_ref, weight_ref, weight, total, sems = refs[10:]
+    where = where_ref[0], where_ref[1], where_ref[2]
+    rows_in = joint_ref.shape[0]
+    half = rows_in // HALVES
+
+    def target(column, side, place, start, size):
+        return weight.at[column, take(place * rows_in + side * half + start, size)]
+
+    copies = piece_copies(where, count, sources, target, half, lambda c, s, z: sems.at[c])
+    for c in range(COLUMNS):
+        shard = project_ref if c == 3 else joint_ref.at[:, pl.ds(c * WIDTH, WIDTH)]
+        copies.append(pltpu.make_async_copy(shard, weight.at[c, take(where[0] * rows_in, rows_in)], sems.at[c]))
+    for copy in copies:
+        copy.start()
     tokens = x_ref.shape[0]
     for i in range(tokens // CHUNK):
         rows = slice(i * CHUNK, (i + 1) * CHUNK)
@@ -139,8 +150,7 @@
             normed * (1.0 + mod_ref[i : i + 1, part(1)]) + mod_ref[i : i + 1, part(0)]
         ).astype(bf16)
     for c, out in enumerate((query_ref, keys_ref, values_ref)):
-        for copy in copies[c]:
-            copy.wait()
+        wait_for(weight.at[c], sems.at[c])
         if c == 2:
             out[...] = matmul(first_ref[...], weight[c]).astype(bf16)
         else:
@@ -150,6 +160,11 @@
             def _(i):
                 rows = pl.ds(pl.multiple_of(i * CHUNK, CHUNK), CHUNK)
                 out[rows, :] = rotate(total[rows, :], cos_ref[rows, :], sin_ref[rows, :]).astype(bf16)
+
+    wait_for(weight.at[3], sems.at[3])
+    write = pltpu.make_async_copy(weight, weight_ref, sems.at[0])
+    write.start()
+    write.wait()
 
 
 def window(head):
@@ -168,16 +183,9 @@
 
 
 def attend_kernel(
-    count, place_ref, query_ref, keys_ref, values_ref, column_ids, row_ids, x_ref, mod_ref,
-    project_ref, every_ref, attended_ref, branch_ref, middle_ref, second_ref, weight, mixed, sems,
+    query_ref, keys_ref, values_ref, column_ids, row_ids, x_ref, mod_ref,
+    weight, attended_ref, branch_ref, middle_ref, second_ref, mixed,
 ):
-    copies = attn_copies(place_ref[0], 3, project_ref, every_ref, weight, sems, count)
-
-    @pl.when(pl.program_id(0) == 0)
-    def _():
-        for copy in copies:
-            copy.start()
-
     allowed = column_ids[...] == row_ids[...]
     for head in range(HEADS):
         lanes, inside = window(head)
@@ -185,13 +193,7 @@
         probs = soft_scores(query, keys_ref[:, lanes], allowed).astype(bf16)
         mixed[:, lanes] = jnp.where(inside, matmul(probs, values_ref[:, lanes]), mixed[:, lanes])
     attended_ref[...] = mixed[...].astype(bf16)
-
-    @pl.when(pl.program_id(0) == 0)
-    def _():
-        for copy in copies:
-            copy.wait()
-
-    branch_ref[...] = matmul(attended_ref[...], weight[...])
+    branch_ref[...] = matmul(attended_ref[...], weight[0])
     for i in range(BLOCK // CHUNK):
         rows = slice(i * CHUNK, (i + 1) * CHUNK)
         mod = mod_ref.at[0]
@@ -204,85 +206,62 @@
 
 
 def ffn_kernel(
-    count, place_ref, factor_ref, second_ref, middle_ref, branch_ref, cot_ref, mod_ref,
-    gate_ref, up_ref, down_ref, every_ref, every_down,
-    output_ref, hidden_ref, gate_back_ref, up_back_ref, feed_back_ref, middle_back_ref,
-    branch_back_ref, sums_ref, gate_w, up_w, down_w, feed, second_back, sems,
+    count, where_ref, factor_ref, second_ref, middle_ref, branch_ref, cot_ref, mod_ref,
+    gate_ref, up_ref, down_ref, *refs
 ):
+    pairs, downs = refs[:10], refs[10:20]
+    (
+        output_ref, hidden_ref, gate_back_ref, up_back_ref, feed_back_ref, middle_back_ref,
+        branch_back_ref, sums_ref, pair_w, down_w, feed, second_back, pair_sems, down_sems,
+    ) = refs[20:]
     step = pl.program_id(0)
     steps = pl.num_programs(0)
-    place = place_ref[0]
     rows_in = gate_ref.shape[0]
     tile = hidden_ref.shape[1]
     tokens = second_ref.shape[0]
-
-    def copies(c, slot):
-        found = []
-        for which, (shard, target) in enumerate(((gate_ref, gate_w), (up_ref, up_w))):
-            found.append(
-                pltpu.make_async_copy(
-                    shard.at[:, pl.ds(pl.multiple_of(c * tile, LANES), tile)],
-                    target.at[slot, pl.ds(pl.multiple_of(place * rows_in, 16), rows_in)],
-                    sems.at[slot, which * count],
-                )
-            )
-            for by in range(1, count):
-                start = ((place + (count - by)) % count) * rows_in
-                found.append(
+    down_rows = tile // PIECES
+
+    @pl.when(step == 0)
+    def _():
+        where = where_ref[0], where_ref[1], where_ref[2]
+        own = take(where[0] * rows_in, rows_in)
+
+        def pair_target(column, side, place, start, size):
+            return pair_w.at[side, column, take(place * rows_in + start, size)]
+
+        def down_target(column, side, place, start, size):
+            return down_w.at[place, take((column * HALVES + side) * down_rows + start, size)]
+
+        copies = piece_copies(
+            where, count, pairs, pair_target, rows_in, lambda c, s, z: pair_sems.at[s, c]
+        ) + piece_copies(where, count, downs, down_target, down_rows, lambda c, s, z: down_sems.at[z])
+        for which, shard in enumerate((gate_ref, up_ref)):
+            for c in range(COLUMNS):
+                copies.append(
                     pltpu.make_async_copy(
-                        every_ref.at[c * HALVES + which, by - 1],
-                        target.at[slot, pl.ds(pl.multiple_of(start, 16), rows_in)],
-                        sems.at[slot, which * count + by],
+                        shard.at[:, pl.ds(c * tile, tile)], pair_w.at[which, c, own], pair_sems.at[which, c]
                     )
                 )
-        return found
-
-    def down_copies(c, slot):
-        sem = sems.at[slot, 2 * count]
-        own = pltpu.make_async_copy(down_ref, down_w.at[slot], sem)
-        by = (place + count - c) % count
-        other = pltpu.make_async_copy(
-            every_down.at[:, jnp.maximum(by, 1) - 1], down_w.at[slot], sem
-        )
-        return own, other
-
-    def start(c, slot):
-        for copy in copies(c, slot):
+        copies.append(pltpu.make_async_copy(down_ref, down_w.at[where[0]], down_sems.at[where[0]]))
+        for copy in copies:
             copy.start()
-        own, other = down_copies(c, slot)
-
-        @pl.when(c == place)
-        def _():
-            own.start()
-
-        @pl.when(c != place)
-        def _():
-            other.start()
-
-    slot = step % 2
-
-    @pl.when(step == 0)
-    def _():
-        start(step, slot)
         for i in range(tokens // CHUNK):
             rows = slice(i * CHUNK, (i + 1) * CHUNK)
             upstream = cot_ref[rows, :].astype(f32) * factor_ref[0]
             feed_back_ref[rows, :] = (upstream * mod_ref[i : i + 1, part(5)]).astype(bf16)
 
-    @pl.when(step + 1 < steps)
-    def _():
-        start(step + 1, 1 - slot)
-
-    for copy in copies(step, slot):
-        copy.wait()
-    down_copies(step, slot)[0].wait()
+    for which in range(2):
+        wait_for(pair_w.at[which, step], pair_sems.at[which, step])
+    wait_for(down_w.at[step], down_sems.at[step])
+    gate_w, up_w = pair_w.at[0], pair_w.at[1]
+    slot = step
 
     sub = 256
     for n in range(tile // sub):
         lanes = slice(n * sub, (n + 1) * sub)
         gate = matmul(second_ref[...], gate_w[slot, :, lanes])
         upval = matmul(second_ref[...], up_w[slot, :, lanes])
-        down = down_w[slot].reshape(tile, WIDTH)[lanes, :]
+        down = down_w[slot, lanes, :]
         hidden_back = times_transposed(feed_back_ref[...], down)
         sigmoid = jax.nn.sigmoid(gate)
         silu = gate * sigmoid
@@ -292,7 +271,7 @@
             hidden_back * upval * (sigmoid * (1.0 + gate * (1.0 - sigmoid)))
         ).astype(bf16)
 
-    feed_part = matmul(hidden_ref[...], down_w[slot].reshape(tile, WIDTH))
+    feed_part = matmul(hidden_ref[...], down_w[slot])
     back_part = times_transposed(gate_back_ref[...], gate_w[slot]) + times_transposed(
         up_back_ref[...], up_w[slot]
     )
@@ -375,20 +354,10 @@
 
 
 def attend_back_kernel(
-    count, place_ref, query_ref, keys_ref, values_ref, branch_back_ref, column_ids, row_ids, cos_ref,
-    sin_ref, project_ref, every_ref, joint_back_ref, weight, mixed_back, query_back, keys_back,
-    values_back, sems,
+    query_ref, keys_ref, values_ref, branch_back_ref, column_ids, row_ids, cos_ref,
+    sin_ref, weight, joint_back_ref, mixed_back, query_back, keys_back, values_back,
 ):
-    copies = attn_copies(place_ref[0], 3, project_ref, every_ref, weight, sems, count)
-
-    @pl.when(pl.program_id(0) == 0)
-    def _():
-        for copy in copies:
-            copy.start()
-        for copy in copies:
-            copy.wait()
-
-    mixed_back[...] = times_transposed(branch_back_ref[...], weight[...]).astype(bf16)
+    mixed_back[...] = times_transposed(branch_back_ref[...], weight[0]).astype(bf16)
     allowed = column_ids[...] == row_ids[...]
     scaling = HEAD_DIM ** (-0.5)
     for head in range(HEADS):
@@ -421,27 +390,25 @@
 
 
 def first_back_kernel(
-    count, place_ref, joint_back_ref, x_ref, middle_back_ref, mod_ref, joint_ref, every_ref,
-    grad_ref, sums_ref, weight, first_back, sems,
+    joint_back_ref, x_ref, middle_back_ref, mod_ref, weight, grad_ref, sums_ref, first_back
 ):
-    place = place_ref[0]
-    copies = [
-        attn_copies(
-            place, c, joint_ref.at[:, pl.ds(c * WIDTH, WIDTH)], every_ref, weight.at[c], sems.at[c], count
-        )
-        for c in range(3)
-    ]
-    for group in copies:
-        for copy in group:
-            copy.start()
-    for c in range(3):
-        for copy in copies[c]:
-            copy.wait()
-        product = times_transposed(joint_back_ref[:, part(c)], weight[c])
-        if c == 0:
-            first_back[...] = product
-        else:
-            first_back[...] += product
+    step = pl.program_id(0)
+    product = times_transposed(joint_back_ref[...], weight[0])
+
+    @pl.when(step == 0)
+    def _():
+        first_back[...] = product
+
+    @pl.when(step > 0)
+    def _():
+        first_back[...] += product
+
+    @pl.when(step == pl.num_programs(0) - 1)
+    def _():
+        finish_first_back(x_ref, middle_back_ref, mod_ref, grad_ref, sums_ref, first_back)
+
+
+def finish_first_back(x_ref, middle_back_ref, mod_ref, grad_ref, sums_ref, first_back):
     for i in range(x_ref.shape[0] // CHUNK):
         rows = slice(i * CHUNK, (i + 1) * CHUNK)
         normed, inverse = normalize(x_ref[rows, :].astype(f32))
@@ -479,30 +446,29 @@
     return pl.BlockSpec(shape, lambda *_: (0,) * len(shape))
 
 
-def first_call(place, x, mod, cos, sin, joint, every):
+def first_call(where, x, mod, cos, sin, joint, project, arrived):
     tokens = x.shape[0]
-    count = every.shape[1] + 1
+    count = arrived[0].shape[0] + 1
     shape = struct((tokens, WIDTH), bf16)
     return pl.pallas_call(
         functools.partial(first_kernel, count),
-        out_shape=(shape,) * 4,
-        in_specs=[SMEM, VMEM, VMEM, VMEM, VMEM, ANY, ANY],
-        out_specs=(VMEM,) * 4,
+        out_shape=(shape,) * 4 + (struct((COLUMNS, WIDTH, WIDTH), bf16),),
+        in_specs=[SMEM, VMEM, VMEM, VMEM, VMEM] + [ANY] * (2 + len(arrived)),
+        out_specs=(VMEM,) * 4 + (ANY,),
         scratch_shapes=[
-            pltpu.VMEM((3, WIDTH, WIDTH), bf16),
+            pltpu.VMEM((COLUMNS, WIDTH, WIDTH), bf16),
             pltpu.VMEM((tokens, WIDTH), f32),
-            pltpu.SemaphoreType.DMA((3, 1 + HALVES * (count - 1))),
+            pltpu.SemaphoreType.DMA((COLUMNS,)),
         ],
         compiler_params=params(),
-        cost_estimate=cost(6 * tokens * WIDTH * WIDTH, x, every, cos, sin),
-    )(place, x, mod, cos, sin, joint, every)
-
-
-def attend_call(place, query, keys, values, ids, x, mod, project, every):
+        cost_estimate=cost(18 * tokens * WIDTH * WIDTH, x, x, x, x, cos, sin, joint, *arrived),
+    )(where, x, mod, cos, sin, joint, project, *arrived)
+
+
+def attend_call(query, keys, values, ids, x, mod, weight):
     tokens = x.shape[0]
-    count = every.shape[1] + 1
     return pl.pallas_call(
-        functools.partial(attend_kernel, count),
+        attend_kernel,
         grid=(tokens // BLOCK,),
         out_shape=(
             struct((tokens, WIDTH), bf16),
@@ -510,30 +476,24 @@
             struct((tokens, WIDTH), f32),
             struct((tokens, WIDTH), bf16),
         ),
-        in_specs=[SMEM]
-        + [by_block(BLOCK, WIDTH)] * 3
+        in_specs=[by_block(BLOCK, WIDTH)] * 3
         + [by_block(BLOCK, 1), pl.BlockSpec((1, BLOCK), lambda b: (0, b)), by_block(BLOCK, WIDTH)]
-        + [by_block(1, BLOCK // CHUNK, 6 * WIDTH), ANY, ANY],
+        + [by_block(1, BLOCK // CHUNK, 6 * WIDTH), pl.BlockSpec((1, WIDTH, WIDTH), lambda b: (3, 0, 0))],
         out_specs=(by_block(BLOCK, WIDTH),) * 4,
-        scratch_shapes=[
-            pltpu.VMEM((WIDTH, WIDTH), bf16),
-            pltpu.VMEM((BLOCK, WIDTH), f32),
-            pltpu.SemaphoreType.DMA((1 + HALVES * (count - 1),)),
-        ],
+        scratch_shapes=[pltpu.VMEM((BLOCK, WIDTH), f32)],
         compiler_params=params(),
-        cost_estimate=cost(4 * tokens * WIDTH * WIDTH, query, keys, values, x, x, x, x, x),
+        cost_estimate=cost(14 * tokens * WIDTH * WIDTH, query, keys, values, x, x, x, x, x),
     )(
-        place, query, keys, values, ids[:, None], ids[None, :], x,
-        mod.reshape(tokens // BLOCK, BLOCK // CHUNK, 6 * WIDTH), project, every,
-    )
-
-
-def ffn_call(place, factor, second, middle, branch, cot, mod, gate, up, down, every, every_down):
+        query, keys, values, ids[:, None], ids[None, :], x,
+        mod.reshape(tokens // BLOCK, BLOCK // CHUNK, 6 * WIDTH), weight,
+    )
+
+
+def ffn_call(where, factor, second, middle, branch, cot, mod, gate, up, down, pairs, downs):
     tokens = second.shape[0]
-    count = every.shape[1] + 1
+    count = pairs[0].shape[0] + 1
     ff = gate.shape[1]
     tile = ff // COLUMNS
-    down = down.reshape(PIECES, -1, WIDTH)
     tiled = pl.BlockSpec((tokens, tile), lambda c: (0, c))
     full = whole(tokens, WIDTH)
     chunks = tokens // CHUNK
@@ -548,19 +508,19 @@
             struct((tokens, WIDTH), bf16),
             struct((chunks, 4 * WIDTH), f32),
         ),
-        in_specs=[SMEM, SMEM, full, full, full, full, whole(chunks, 6 * WIDTH)] + [ANY] * 5,
+        in_specs=[SMEM, SMEM, full, full, full, full, whole(chunks, 6 * WIDTH)] + [ANY] * 23,
         out_specs=(full, tiled, tiled, tiled, full, full, full, whole(chunks, 4 * WIDTH)),
         scratch_shapes=[
-            pltpu.VMEM((2, WIDTH, tile), bf16),
-            pltpu.VMEM((2, WIDTH, tile), bf16),
-            pltpu.VMEM((2, PIECES, tile // PIECES, WIDTH), bf16),
+            pltpu.VMEM((HALVES, COLUMNS, WIDTH, tile), bf16),
+            pltpu.VMEM((count, ff // count, WIDTH), bf16),
             pltpu.VMEM((tokens, WIDTH), f32),
             pltpu.VMEM((tokens, WIDTH), f32),
-            pltpu.SemaphoreType.DMA((2, 2 * count + 1)),
+            pltpu.SemaphoreType.DMA((HALVES, COLUMNS)),
+            pltpu.SemaphoreType.DMA((count,)),
         ],
-        compiler_params=params(),
-        cost_estimate=cost(12 * tokens * WIDTH * ff, every, every_down, gate, gate, gate),
-    )(place, factor, second, middle, branch, cot, mod, gate, up, down, every, every_down)
+        compiler_params=params(62),
+        cost_estimate=cost(24 * tokens * WIDTH * ff, gate, gate, gate),
+    )(where, factor, second, middle, branch, cot, mod, gate, up, down, *pairs, *downs)
 
 
 def ffn_grad_call(second, gate_back, up_back):
@@ -617,46 +577,48 @@
     )(first, attended, joint_back, branch_back)
 
 
-def attend_back_call(place, query, keys, values, branch_back, ids, cos, sin, project, every):
+def attend_back_call(query, keys, values, branch_back, ids, cos, sin, weight):
     tokens = query.shape[0]
-    count = every.shape[1] + 1
     block = by_block(BLOCK, WIDTH)
     return pl.pallas_call(
-        functools.partial(attend_back_kernel, count),
+        attend_back_kernel,
         grid=(tokens // BLOCK,),
         out_shape=struct((tokens, 3 * WIDTH), bf16),
-        in_specs=[SMEM, block, block, block, block]
-        + [by_block(BLOCK, 1), pl.BlockSpec((1, BLOCK), lambda b: (0, b)), block, block, ANY, ANY],
+        in_specs=[block, block, block, block]
+        + [by_block(BLOCK, 1), pl.BlockSpec((1, BLOCK), lambda b: (0, b)), block, block]
+        + [pl.BlockSpec((1, WIDTH, WIDTH), lambda b: (3, 0, 0))],
         out_specs=by_block(BLOCK, 3 * WIDTH),
         scratch_shapes=[
-            pltpu.VMEM((WIDTH, WIDTH), bf16),
             pltpu.VMEM((BLOCK, WIDTH), bf16),
             pltpu.VMEM((BLOCK, WIDTH), f32),
             pltpu.VMEM((BLOCK, WIDTH), f32),
             pltpu.VMEM((BLOCK, WIDTH), f32),
-            pltpu.SemaphoreType.DMA((1 + HALVES * (count - 1),)),
         ],
         compiler_params=params(),
-        cost_estimate=cost(8 * tokens * WIDTH * WIDTH, query, keys, values, branch_back, cos, sin),
-    )(place, query, keys, values, branch_back, ids[:, None], ids[None, :], cos, sin, project, every)
-
-
-def first_back_call(place, joint_back, x, middle_back, mod, joint, every):
+        cost_estimate=cost(32 * tokens * WIDTH * WIDTH, query, keys, values, branch_back, cos, sin),
+    )(query, keys, values, branch_back, ids[:, None], ids[None, :], cos, sin, weight)
+
+
+def first_back_call(joint_back, x, middle_back, mod, weight):
     tokens = x.shape[0]
-    count = every.shape[1] + 1
+    chunks = tokens // CHUNK
+    full = whole(tokens, WIDTH)
     return pl.pallas_call(
-        functools.partial(first_back_kernel, count),
-        out_shape=(struct((tokens, WIDTH), f32), struct((tokens // CHUNK, 2 * WIDTH), f32)),
-        in_specs=[SMEM, VMEM, VMEM, VMEM, VMEM, ANY, ANY],
-        out_specs=(VMEM, VMEM),
-        scratch_shapes=[
-            pltpu.VMEM((3, WIDTH, WIDTH), bf16),
-            pltpu.VMEM((tokens, WIDTH), f32),
-            pltpu.SemaphoreType.DMA((3, 1 + HALVES * (count - 1))),
+        first_back_kernel,
+        grid=(3,),
+        out_shape=(struct((tokens, WIDTH), f32), struct((chunks, 2 * WIDTH), f32)),
+        in_specs=[
+            pl.BlockSpec((tokens, WIDTH), lambda c: (0, c)),
+            full,
+            full,
+            whole(chunks, 6 * WIDTH),
+            pl.BlockSpec((1, WIDTH, WIDTH), lambda c: (c, 0, 0)),
         ],
+        out_specs=(full, whole(chunks, 2 * WIDTH)),
+        scratch_shapes=[pltpu.VMEM((tokens, WIDTH), f32)],
         compiler_params=params(),
-        cost_estimate=cost(6 * tokens * WIDTH * WIDTH, joint_back, x, middle_back, middle_back, every),
-    )(place, joint_back, x, middle_back, mod, joint, every)
+        cost_estimate=cost(14 * tokens * WIDTH * WIDTH, joint_back, x, middle_back, middle_back, weight),
+    )(joint_back, x, middle_back, mod, weight)
 
 
 def shifts(count, by):
@@ -667,19 +629,37 @@
     return lax.dynamic_index_in_dim(array, index, 0, keepdims=False)
 
 
-def gather_pieces(piece):
+def across(bit):
+    return [(i, i ^ bit) for i in range(PIECES)]
+
+
+def swap(array, bit):
+    return lax.ppermute(array, "bucket", across(bit))
+
+
+def arrived(piece):
     count = lax.axis_size("fsdp")
-    foreign = jnp.stack(
+    first = first_part(piece.shape[0])
+    own = jnp.stack(
         [lax.ppermute(piece, "fsdp", shifts(count, by)) for by in range(1, count)]
     )
-    return lax.all_gather(foreign, "bucket", axis=0, tiled=False)
-
-
-def gather_whole(pieces):
+    by_x, by_y = swap(own, 2), swap(own, 4)
+    here = (own, by_x, by_y, swap(by_x[:, :first], 4), swap(by_y[:, first:], 2))
+    return here + tuple(swap(array, 1) for array in here)
+
+
+def arrived_whole(pieces):
     count = lax.axis_size("fsdp")
     place = lax.axis_index("fsdp")
+    first = first_part(pieces.shape[1])
     full = lax.all_gather(pieces, "fsdp", axis=0, tiled=False)
-    return jnp.stack([pick(full, (place - by) % count) for by in range(1, count)], axis=1)
+    full = jnp.stack([pick(full, (place - by) % count) for by in range(1, count)])
+
+    def of(side):
+        own, by_x, by_y, cross = (full[:, c * HALVES + side] for c in range(COLUMNS))
+        return own, by_x, by_y, cross[:, :first], cross[:, first:]
+
+    return of(0) + of(1)
 
 
 def reduce_pieces(parts):
@@ -733,10 +713,10 @@
     tile = ff // COLUMNS
     down_rows = down_weight.shape[0] // PIECES
     slots = condition.shape[0]
-    place_array = place.astype(jnp.int32).reshape(1)
 
     if lax.axis_size("bucket") == PIECES:
         column, side = bucket // HALVES, bucket % HALVES
+        where = jnp.stack([place, column, side])
         attn_piece = jnp.where(
             column == 3,
             lax.dynamic_slice(project_weight, (side * half, 0), (half, WIDTH)),
@@ -748,23 +728,22 @@
             lax.dynamic_slice(up_weight, (0, column * tile), (height, tile)),
         )
         down_piece = lax.dynamic_slice_in_dim(down_weight, bucket * down_rows, down_rows, 0)
-        every_attn = gather_pieces(attn_piece)
-        every_ffn = gather_pieces(ffn_piece)
-        every_down = gather_pieces(down_piece)
+        attn_arrived, downs, pairs = arrived(attn_piece), arrived(down_piece), arrived(ffn_piece)
     else:
-        every_attn = gather_whole(
+        where = jnp.stack([place, 0 * place, 0 * place])
+        attn_arrived = arrived_whole(
             jnp.concatenate([joint_weight, project_weight], axis=1)
             .reshape(HALVES, half, COLUMNS, WIDTH)
             .transpose(2, 0, 1, 3)
             .reshape(PIECES, half, WIDTH)
         )
-        every_ffn = gather_whole(
+        pairs = arrived_whole(
             jnp.stack([gate_weight, up_weight])
             .reshape(HALVES, height, COLUMNS, tile)
             .transpose(2, 0, 1, 3)
             .reshape(PIECES, height, tile)
         )
-        every_down = gather_whole(down_weight.reshape(PIECES, down_rows, WIDTH))
+        downs = arrived_whole(down_weight.reshape(PIECES, down_rows, WIDTH))
 
     cond_float = condition.astype(f32)
     lifted = jax.nn.silu(cond_float).astype(bf16)
@@ -788,15 +767,15 @@
     factor = (mine * counts.shape[0] / jnp.sum(counts)).reshape(1)
     cos, sin = rope_tables(segment_ids, grid_widths)
 
-    first, query, keys, values = first_call(
-        place_array, inputs, mod, cos, sin, joint_weight, every_attn
+    first, query, keys, values, weight = first_call(
+        where, inputs, mod, cos, sin, joint_weight, project_weight, attn_arrived
     )
     attended, branch, middle, second = attend_call(
-        place_array, query, keys, values, segment_ids, inputs, mod, project_weight, every_attn
+        query, keys, values, segment_ids, inputs, mod, weight
     )
     output, hidden, gate_back, up_back, feed_back, middle_back, branch_back, late_sums = ffn_call(
-        place_array, factor, second, middle, branch, cotangent, mod,
-        gate_weight, up_weight, down_weight, every_ffn, every_down,
+        where, factor, second, middle, branch, cotangent, mod,
+        gate_weight, up_weight, down_weight, pairs, downs,
     )
     down_sum = reduce_pieces(down_grad_call(fsdp_count, hidden, feed_back)).reshape(-1, WIDTH)
     ffn_parts = ffn_grad_call(second, gate_back, up_back).reshape(
@@ -809,7 +788,7 @@
         .reshape(HALVES, height, ff)
     )
     joint_back = attend_back_call(
-        place_array, query, keys, values, branch_back, segment_ids, cos, sin, project_weight, every_attn
+        query, keys, values, branch_back, segment_ids, cos, sin, weight
     )
     attn_parts = attn_grad_call(fsdp_count, first, attended, joint_back, branch_back).reshape(
         PIECES, fsdp_count, half, WIDTH
@@ -820,9 +799,7 @@
         .transpose(1, 2, 0, 3)
         .reshape(height, COLUMNS * WIDTH)
     )
-    grad_inputs, early_sums = first_back_call(
-        place_array, joint_back, inputs, middle_back, mod, joint_weight, every_attn
-    )
+    grad_inputs, early_sums = first_back_call(joint_back, inputs, middle_back, mod, weight)
     modulation_back = lax.dot_general(
         one_hot,
         jnp.concatenate([early_sums, late_sums], axis=1),

time: 711 us -> 641 us (0.902)
  waiting for transfers between devices: 457 us -> 317 us
  starting transfers between devices: 21.5 us -> 73.7 us
  Pallas kernels: 149 us -> 157 us
  local copies, waits for them, and re-layouts: 28.6 us -> 36.5 us
    all_gather x3, waiting for transfers between devices: 75.1 us -> 11.3 us  [reduce_pieces(): lax.all_gather(total, 'bucket', axis=0, tiled=False)]
    ppermute x9 -> x36, starting transfers between devices: 7.58 us -> 54.5 us  [the longest x27 31.3 us: swap(): return lax.ppermute(array, 'bucket', across(bit))]
    all_gather x3 -> x0, waiting for transfers between devices: 39.7 us -> none  [gather_pieces(): return lax.all_gather(foreign, 'bucket', axis=0, tiled=False)]
    all_gather x1, waiting for transfers between devices: 33.9 us -> 0.03 us  [on_device(): lax.all_gather(jnp.concatenate([modulation_back, lifted], axis=1), ('buck...]
    ppermute x9 -> x36, waiting for transfers between devices: 83.7 us -> 54.8 us  [the longest x27 37.6 us: swap(): return lax.ppermute(array, 'bucket', across(bit))]
    ppermute x9, waiting for transfers between devices: 12 us -> 30.1 us  [to_group(): lax.ppermute(pick(rows, (place + by) % count), 'fsdp', shifts(count, by))]
    reduce_scatter x3, waiting for transfers between devices: 124 us -> 134 us  [reduce_pieces(): mine = lax.psum_scatter(parts, 'bucket', scatter_dimension=0, tiled=False)]
  transfers between devices with their start and end apart: 37 -> 61, of which waited for: 21 -> 21; matrix products, arithmetic and copies ran while one was open for 7% -> 9% of each run, Pallas kernels for 14% -> 16%
where the time goes in v3:
time: 641 us; the launch traced here: 634 us
  waiting for transfers between devices  317 us (49%)
  Pallas kernels  157 us (24%)
  starting transfers between devices  73.7 us (11%)
  local copies, waits for them, and re-layouts  36.5 us (6%)
  other arithmetic  21.7 us (3%)
  between operations  17.9 us (3%)
  matrix products  10.3 us (2%)
    reduce_scatter x3, waiting for transfers between devices, reduce_pieces(): mine = lax.psum_scatter(parts, 'bucket', scatter_dimension=0, tiled=False)  134 us
    ppermute x9, waiting for transfers between devices, reduce_pieces(): lax.ppermute(pick(mine, (place + by) % count), 'fsdp', shifts(count, by))  86.7 us
    pallas_call x1, Pallas kernels, ffn_call(): pl.pallas_call(functools.partial(ffn_kernel, count), grid=(COLUMNS,), out...  44.7 us
    ppermute x27, waiting for transfers between devices, swap(): return lax.ppermute(array, 'bucket', across(bit))  37.6 us
    ppermute x27, starting transfers between devices, swap(): return lax.ppermute(array, 'bucket', across(bit))  31.3 us
    ppermute x9, waiting for transfers between devices, to_group(): lax.ppermute(pick(rows, (place + by) % count), 'fsdp', shifts(count, by))  30.1 us
    pallas_call x1, Pallas kernels, attend_back_call(): pl.pallas_call(attend_back_kernel, grid=(tokens // BLOCK,), out_shape=str...  28.7 us
    ppermute x9, starting transfers between devices, arrived(): lax.ppermute(piece, 'fsdp', shifts(count, by))  23.2 us
  transfers between devices with their start and end apart: 61, of which 21 were waited for; matrix products, arithmetic and copies ran while one was open for 9% of the time, Pallas kernels for 16%

profile of v3, /device:TPU:25, one launch (start us, length us, event | category | flops | bytes accessed | tf_op | source)
XLA Modules:
  0.0 633.6 jit_solution(10291981428611855631)
XLA Ops:
  34.1 11.4 %collective-permute-done.5 = f32[8,6912]{1,0:T(8,128)S(1)} collective-permute-done((f32[8,6912]{1,0:T(8,128)S(1)}, f32[8,6912]{1,0:T(8,128)S(1)}, u32[]{:S(2)}, u32[]{:S(2)}) %collective-permute-start.5) | collective-permute-done | bytes 221216 | tf_op jit(solution)/shard_map/ppermute | solution.py:686
  46.8 14.1 %collective-permute-done.4 = f32[8,6912]{1,0:T(8,128)S(1)} collective-permute-done((f32[8,6912]{1,0:T(8,128)S(1)}, f32[8,6912]{1,0:T(8,128)S(1)}, u32[]{:S(2)}, u32[]{:S(2)}) %collective-permute-start.4) | collective-permute-done | bytes 221216 | tf_op jit(solution)/shard_map/ppermute | solution.py:686
  64.4 11.9 %collective-permute-done.7 = bf16[144,1152]{1,0:T(8,128)(2,1)S(1)} collective-permute-done((bf16[144,1152]{1,0:T(8,128)(2,1)S(1)}, bf16[144,1152]{1,0:T(8,128)(2,1)S(1)}, u32[]{:S(2)}, u32[]{:S(2)}) %collective-permute-start.7) | collective-permute-done | bytes 331808 | tf_op jit(solution)/shard_map/ppermute | solution.py:644
  80.2 16.0 %collective-permute-start.18 = (bf16[288,768]{1,0:T(8,128)(2,1)S(1)}, bf16[288,768]{1,0:T(8,128)(2,1)S(1)}, u32[]{:S(2)}, u32[]{:S(2)}) collective-permute-start(bf16[288,768]{1,0:T(8,128)(2,1)S(1)} %dynamic-slice_select_fusion), channel_id=1, source_target_pairs={{0,1},{1,2},{2,3},{3,0},{4,5},{5,6},{6,7},{7,4},{8,9},{9,10},{10,1... | collective-permute-start | bytes 1327112 | tf_op jit(solution)/shard_map/ppermute | solution.py:644
  105.1 7.3 %collective-permute-start.13 = (bf16[3,144,1152]{2,1,0:T(8,128)(2,1)S(1)}, bf16[3,144,1152]{2,1,0:T(8,128)(2,1)}, u32[]{:S(2)}, u32[]{:S(2)}) collective-permute-start(bf16[3,144,1152]{2,1,0:T(8,128)(2,1)S(1)} %pad_maximum_fusion.1.refs_0_), channel_id=1, source_target_pairs={{0,4},{4,0},{8,12},{12,8},{16,20},{20,16},{24,28},{28,24},{1,5},{5... | collective-permute-start | bytes 2985992 | tf_op jit(solution)/shard_map/ppermute | solution.py:637
  113.7 17.6 %collective-permute-done.36.refs_14_ = bf16[3,48,1152]{2,1,0:T(8,128)(2,1)S(1)} collective-permute-done((bf16[3,48,1152]{2,1,0:T(8,128)(2,1)S(1)}, bf16[3,48,1152]{2,1,0:T(8,128)(2,1)S(1)}, u32[]{:S(2)}, u32[]{:S(2)}) %collective-permute-start.36) | collective-permute-done | bytes 331808 | tf_op jit(solution)/shard_map/ppermute | solution.py:637
  150.8 19.9 %collective-permute-done.12.refs_4_ = bf16[3,64,1152]{2,1,0:T(8,128)(2,1)} collective-permute-done((bf16[3,64,1152]{2,1,0:T(8,128)(2,1)}, bf16[3,64,1152]{2,1,0:T(8,128)(2,1)}, u32[]{:S(2)}, u32[]{:S(2)}) %collective-permute-start.12) | collective-permute-done | bytes 442400 | tf_op jit(solution)/shard_map/ppermute | solution.py:637
  181.3 22.4 %shard_map.187 = (bf16[512,1152]{1,0:T(8,128)(2,1)}, bf16[512,1152]{1,0:T(8,128)(2,1)}, bf16[512,1152]{1,0:T(8,128)(2,1)}, bf16[512,1152]{1,0:T(8,128)(2,1)}, bf16[4,1152,1152]{2,1,0:T(8,128)(2,1)}) custom-call(s32[3]{0:T(128)} %pad_add_fusion.where_ref, bf16[512,1152]{1,0:T(8,128)(2,1)} %x_ref.5, f32[8,6912]{1,0:T(8,128)} %copy-done.4, ...), custom_call_target="tpu_custom_call" | custom-call | flops 12230590464 | bytes 19390464 | tf_op jit(solution)/shard_map/pallas_call | solution.py:453
  204.3 12.5 %shard_map.188 = (bf16[512,1152]{1,0:T(8,128)(2,1)}, f32[512,1152]{1,0:T(8,128)}, f32[512,1152]{1,0:T(8,128)}, bf16[512,1152]{1,0:T(8,128)(2,1)}) custom-call(bf16[512,1152]{1,0:T(8,128)(2,1)} %get-tuple-element.28.query_ref, bf16[512,1152]{1,0:T(8,128)(2,1)} %get-tuple-element.29.keys_ref, bf16[512,1152]{1,0:T(8,128)(2,1)} %get-tuple-element.30.values_ref, ...), custom_call_target="tpu_custom_call" | custom-call | flops 9512681472 | bytes 9437184 | tf_op jit(solution)/shard_map/pallas_call | solution.py:470
  218.6 44.7 %shard_map.189 = (bf16[512,1152]{1,0:T(8,128)(2,1)}, bf16[512,3072]{1,0:T(8,128)(2,1)}, bf16[512,3072]{1,0:T(8,128)(2,1)}, bf16[512,3072]{1,0:T(8,128)(2,1)}, bf...) custom-call(s32[3]{0:T(128)} %pad_add_fusion.where_ref, ...), custom_call_target="tpu_custom_call" | custom-call | flops 43486543872 | bytes 5308416 | tf_op jit(solution)/shard_map/pallas_call | solution.py:500
  263.3 8.2 %shard_map.194 = bf16[8,4,96,1152]{3,2,1,0:T(8,128)(2,1)} custom-call(bf16[512,3072]{1,0:T(8,128)(2,1)} %get-tuple-element.45.hidden_ref, bf16[512,1152]{1,0:T(8,128)(2,1)} %get-tuple-element.46.feed_back_ref), custom_call_target="tpu_custom_call" | custom-call | flops 3623878656 | bytes 11403264 | tf_op jit(solution)/shard_map/pallas_call | solution.py:547
  271.6 28.7 %shard_map.190.joint_back_ref = bf16[512,3456]{1,0:T(8,128)(2,1)} custom-call(bf16[512,1152]{1,0:T(8,128)(2,1)} %get-tuple-element.28.query_ref, bf16[512,1152]{1,0:T(8,128)(2,1)} %get-tuple-element.29.keys_ref, bf16[512,1152]{1,0:T(8,128)(2,1)} %get-tuple-element.30.values_ref, bf16[512,1152]{1,0:T(8,128)(2,1)} %get-tuple-element.36.branch_back_ref, ...), custom_call_target="tpu_custom_call" | custom-call | flops 21743271936 | bytes 9437184 | tf_op jit(solution)/shard_map/pallas_call | solution.py:583
  300.3 12.1 %shard_map.192 = bf16[4,2,4,144,1152]{4,3,2,1,0:T(8,128)(2,1)} custom-call(bf16[512,1152]{1,0:T(8,128)(2,1)} %get-tuple-element.41.first_ref, bf16[512,1152]{1,0:T(8,128)(2,1)} %get-tuple-element.42.attended_ref, bf16[512,3456]{1,0:T(8,128)(2,1)} %shard_map.190.joint_back_ref, bf16[512,1152]{1,0:T(8,128)(2,1)} %get-tuple-element.36.branch_back_ref), custom_call_target="tpu_custom_call" | custom-call | flops 5435817984 | bytes 17694720 | tf_op jit(solution)/shard_map/pallas_call | solution.py:563
  312.5 15.1 %shard_map.193 = bf16[4,2,1152,768]{3,2,1,0:T(8,128)(2,1)} custom-call(bf16[512,1152]{1,0:T(8,128)(2,1)} %get-tuple-element.32.second_ref, bf16[512,3072]{1,0:T(8,128)(2,1)} %get-tuple-element.43.gate_back_ref, bf16[512,3072]{1,0:T(8,128)(2,1)} %get-tuple-element.44.up_back_ref), custom_call_target="tpu_custom_call" | custom-call | flops 7247757312 | bytes 21626880 | tf_op jit(solution)/shard_map/pallas_call | solution.py:531
  327.7 12.9 %shard_map.191 = (f32[512,1152]{1,0:T(8,128)}, f32[8,2304]{1,0:T(8,128)}) custom-call(bf16[512,3456]{1,0:T(8,128)(2,1)} %shard_map.190.joint_back_ref, bf16[512,1152]{1,0:T(8,128)(2,1)} %x_ref.5, f32[512,1152]{1,0:T(8,128)} %get-tuple-element.37.middle_back_ref, f32[8,6912]{1,0:T(8,128)} %copy-done.4, bf16[4,1152,1152]{2,1,0:T(8,128)(2,1)} %get-tuple-element.31.weight), custom_call_target="tpu_custom_call" | custom-call | flops 9512681472 | bytes 20054016 | tf_op jit(solution)/shard_map/pallas_call | solution.py:606
  350.7 8.1 %collective-permute-done.53 = bf16[96,1152]{1,0:T(8,128)(2,1)S(1)} collective-permute-done((bf16[96,1152]{1,0:T(8,128)(2,1)S(1)}, bf16[96,1152]{1,0:T(8,128)(2,1)S(1)}, u32[]{:S(2)}, u32[]{:S(2)}) %collective-permute-start.53) | collective-permute-done | bytes 221216 | tf_op jit(solution)/shard_map/ppermute | solution.py:675
  358.8 9.5 %collective-permute-done.52 = bf16[96,1152]{1,0:T(8,128)(2,1)S(1)} collective-permute-done((bf16[96,1152]{1,0:T(8,128)(2,1)S(1)}, bf16[96,1152]{1,0:T(8,128)(2,1)S(1)}, u32[]{:S(2)}, u32[]{:S(2)}) %collective-permute-start.52) | collective-permute-done | bytes 221216 | tf_op jit(solution)/shard_map/ppermute | solution.py:675
  370.2 58.3 %reduce-scatter.4.cloned.1.call-done = bf16[1,4,144,1152]{3,2,1,0:T(8,128)(2,1)} async-done(((bf16[8,4,144,1152]{3,2,1,0:T(8,128)(2,1)}), bf16[1,4,144,1152]{3,2,1,0:T(8,128)(2,1)}) %reduce-scatter.4.cloned.1.call-update) | async-done | bytes 1327120 | tf_op jit(solution)/shard_map/reduce_scatter | solution.py:670
  445.4 14.2 %collective-permute-done.46 = bf16[144,1152]{1,0:T(8,128)(2,1)S(1)} collective-permute-done((bf16[144,1152]{1,0:T(8,128)(2,1)S(1)}, bf16[144,1152]{1,0:T(8,128)(2,1)S(1)}, u32[]{:S(2)}, u32[]{:S(2)}) %collective-permute-start.46) | collective-permute-done | bytes 331808 | tf_op jit(solution)/shard_map/ppermute | solution.py:675
  461.6 75.6 %reduce-scatter.6.cloned.1.call-done = bf16[1,4,288,768]{3,2,1,0:T(8,128)(2,1)} async-done(((bf16[8,4,288,768]{3,2,1,0:T(8,128)(2,1)}), bf16[1,4,288,768]{3,2,1,0:T(8,128)(2,1)}) %reduce-scatter.6.cloned.1.call-update) | async-done | bytes 1769488 | tf_op jit(solution)/shard_map/reduce_scatter | solution.py:670
  540.5 9.1 %collective-permute-done.48 = bf16[288,768]{1,0:T(8,128)(2,1)S(1)} collective-permute-done((bf16[288,768]{1,0:T(8,128)(2,1)S(1)}, bf16[288,768]{1,0:T(8,128)(2,1)S(1)}, u32[]{:S(2)}, u32[]{:S(2)}) %collective-permute-start.48) | collective-permute-done | bytes 442400 | tf_op jit(solution)/shard_map/ppermute | solution.py:675
  549.6 9.5 %collective-permute-done.50 = bf16[288,768]{1,0:T(8,128)(2,1)S(1)} collective-permute-done((bf16[288,768]{1,0:T(8,128)(2,1)S(1)}, bf16[288,768]{1,0:T(8,128)(2,1)S(1)}, u32[]{:S(2)}, u32[]{:S(2)}) %collective-permute-start.50) | collective-permute-done | bytes 442400 | tf_op jit(solution)/shard_map/ppermute | solution.py:675
  559.1 18.9 %collective-permute-done.49 = bf16[288,768]{1,0:T(8,128)(2,1)S(1)} collective-permute-done((bf16[288,768]{1,0:T(8,128)(2,1)S(1)}, bf16[288,768]{1,0:T(8,128)(2,1)S(1)}, u32[]{:S(2)}, u32[]{:S(2)}) %collective-permute-start.49) | collective-permute-done | bytes 442400 | tf_op jit(solution)/shard_map/ppermute | solution.py:675
  603.9 11.3 %all-gather.12.cloned.1.call-done = bf16[2304,768]{1,0:T(8,128)(2,1)} async-done(((bf16[288,768]{1,0:T(8,128)(2,1)}), bf16[2304,768]{1,0:T(8,128)(2,1)}) %all-gather.12.cloned.1.call-update) | async-done | bytes 3538960 | tf_op jit(solution)/shard_map/all_gather | solution.py:679
  (245 shorter events, 146.4 us)
Async XLA Ops:
  8.0 334.5 %reduce-scatter.8.cloned.1.call-start = ((), (), s32[]{:S(2)}) async-start(), calls=%async_computation.6 | async-start | bytes 7962624 | tf_op jit(solution)/shard_map/reduce_scatter | solution.py:670
  21.9 41.3 %collective-permute-start.8 = (bf16[144,1152]{1,0:T(8,128)(2,1)S(1)}, bf16[144,1152]{1,0:T(8,128)(2,1)S(1)}, u32[]{:S(2)}, u32[]{:S(2)}) collective-permute-start(bf16[144,1152]{1,0:T(8,128)(2,1)S(1)} %dynamic-slice_select_fusion.1), channel_id=1, source_target_pairs={{0,3},{1,0},{2,1},{3,2},{4,7},{5,4},{6,5},{7,6},{8,11},{9,8},{10,9... | collective-permute-start | bytes 995336 | tf_op jit(solution)/shard_map/ppermute | solution.py:644
  26.8 69.4 %collective-permute-start.20 = (bf16[288,768]{1,0:T(8,128)(2,1)S(1)}, bf16[288,768]{1,0:T(8,128)(2,1)S(1)}, u32[]{:S(2)}, u32[]{:S(2)}) collective-permute-start(bf16[288,768]{1,0:T(8,128)(2,1)S(1)} %dynamic-slice_select_fusion), channel_id=1, source_target_pairs={{0,3},{1,0},{2,1},{3,2},{4,7},{5,4},{6,5},{7,6},{8,11},{9,8},{10,9... | collective-permute-start | bytes 1327112 | tf_op jit(solution)/shard_map/ppermute | solution.py:644
  30.5 30.3 %collective-permute-start.4 = (f32[8,6912]{1,0:T(8,128)S(1)}, f32[8,6912]{1,0:T(8,128)S(1)}, u32[]{:S(2)}, u32[]{:S(2)}) collective-permute-start(f32[8,6912]{1,0:T(8,128)S(1)} %get-tuple-element.64), channel_id=1, source_target_pairs={{0,2},{1,3},{2,0},{3,1},{4,6},{5,7},{6,4},{7,5},{8,10},{9,11},{10,... | collective-permute-start | bytes 663560 | tf_op jit(solution)/shard_map/ppermute | solution.py:686
  45.5 53.9 %collective-permute-start.34 = (bf16[3,96,1152]{2,1,0:T(8,128)(2,1)S(1)}, bf16[3,96,1152]{2,1,0:T(8,128)(2,1)S(1)}, u32[]{:S(2)}, u32[]{:S(2)}) collective-permute-start(bf16[3,96,1152]{2,1,0:T(8,128)(2,1)S(1)} %pad_maximum_fusion.3.refs_10_), channel_id=1, source_target_pairs={{0,16},{4,20},{8,24},{12,28},{16,0},{20,4},{24,8},{28,12},{1,17},{... | collective-permute-start | bytes 1990664 | tf_op jit(solution)/shard_map/ppermute | solution.py:637
  63.2 37.6 %collective-permute-start.33 = (bf16[3,96,1152]{2,1,0:T(8,128)(2,1)S(1)}, bf16[3,96,1152]{2,1,0:T(8,128)(2,1)S(1)}, u32[]{:S(2)}, u32[]{:S(2)}) collective-permute-start(bf16[3,96,1152]{2,1,0:T(8,128)(2,1)S(1)} %pad_maximum_fusion.3.refs_10_), channel_id=1, source_target_pairs={{0,8},{4,12},{8,0},{12,4},{16,24},{20,28},{24,16},{28,20},{1,9},{5... | collective-permute-start | bytes 1990664 | tf_op jit(solution)/shard_map/ppermute | solution.py:637
  99.5 33.6 %collective-permute-start.10 = (bf16[3,144,1152]{2,1,0:T(8,128)(2,1)S(1)}, bf16[3,144,1152]{2,1,0:T(8,128)(2,1)}, u32[]{:S(2)}, u32[]{:S(2)}) collective-permute-start(bf16[3,144,1152]{2,1,0:T(8,128)(2,1)S(1)} %pad_maximum_fusion.1.refs_0_), channel_id=1, source_target_pairs={{0,16},{4,20},{8,24},{12,28},{16,0},{20,4},{24,8},{28,12},{1,17},{... | collective-permute-start | bytes 2985992 | tf_op jit(solution)/shard_map/ppermute | solution.py:637
  100.8 34.0 %collective-permute-start.9 = (bf16[3,144,1152]{2,1,0:T(8,128)(2,1)S(1)}, bf16[3,144,1152]{2,1,0:T(8,128)(2,1)}, u32[]{:S(2)}, u32[]{:S(2)}) collective-permute-start(bf16[3,144,1152]{2,1,0:T(8,128)(2,1)S(1)} %pad_maximum_fusion.1.refs_0_), channel_id=1, source_target_pairs={{0,8},{4,12},{8,0},{12,4},{16,24},{20,28},{24,16},{28,20},{1,9},{5... | collective-permute-start | bytes 2985992 | tf_op jit(solution)/shard_map/ppermute | solution.py:637
  102.1 29.1 %collective-permute-start.36 = (bf16[3,48,1152]{2,1,0:T(8,128)(2,1)S(1)}, bf16[3,48,1152]{2,1,0:T(8,128)(2,1)S(1)}, u32[]{:S(2)}, u32[]{:S(2)}) collective-permute-start(bf16[3,48,1152]{2,1,0:T(8,128)(2,1)S(1)} %slice.55), channel_id=1, source_target_pairs={{0,8},{4,12},{8,0},{12,4},{16,24},{20,28},{24,16},{28,20},{1,9},{5... | collective-permute-start | bytes 995336 | tf_op jit(solution)/shard_map/ppermute | solution.py:637
  105.1 33.7 %collective-permute-start.13 = (bf16[3,144,1152]{2,1,0:T(8,128)(2,1)S(1)}, bf16[3,144,1152]{2,1,0:T(8,128)(2,1)}, u32[]{:S(2)}, u32[]{:S(2)}) collective-permute-start(bf16[3,144,1152]{2,1,0:T(8,128)(2,1)S(1)} %pad_maximum_fusion.1.refs_0_), channel_id=1, source_target_pairs={{0,4},{4,0},{8,12},{12,8},{16,20},{20,16},{24,28},{28,24},{1,5},{5... | collective-permute-start | bytes 2985992 | tf_op jit(solution)/shard_map/ppermute | solution.py:637
  131.3 41.7 %collective-permute-start.22 = (bf16[3,288,768]{2,1,0:T(8,128)(2,1)}, bf16[3,288,768]{2,1,0:T(8,128)(2,1)}, u32[]{:S(2)}, u32[]{:S(2)}) collective-permute-start(bf16[3,288,768]{2,1,0:T(8,128)(2,1)} %pad_maximum_fusion.refs_0_), channel_id=1, source_target_pairs={{0,16},{4,20},{8,24},{12,28},{16,0},{20,4},{24,8},{28,12},{1,17},{... | collective-permute-start | bytes 3981320 | tf_op jit(solution)/shard_map/ppermute | solution.py:637
  131.6 41.4 %collective-permute-start.21 = (bf16[3,288,768]{2,1,0:T(8,128)(2,1)}, bf16[3,288,768]{2,1,0:T(8,128)(2,1)}, u32[]{:S(2)}, u32[]{:S(2)}) collective-permute-start(bf16[3,288,768]{2,1,0:T(8,128)(2,1)} %pad_maximum_fusion.refs_0_), channel_id=1, source_target_pairs={{0,8},{4,12},{8,0},{12,4},{16,24},{20,28},{24,16},{28,20},{1,9},{5... | collective-permute-start | bytes 3981320 | tf_op jit(solution)/shard_map/ppermute | solution.py:637
  138.8 31.9 %collective-permute-start.12 = (bf16[3,64,1152]{2,1,0:T(8,128)(2,1)}, bf16[3,64,1152]{2,1,0:T(8,128)(2,1)}, u32[]{:S(2)}, u32[]{:S(2)}) collective-permute-start(bf16[3,64,1152]{2,1,0:T(8,128)(2,1)} %slice.51), channel_id=1, source_target_pairs={{0,8},{4,12},{8,0},{12,4},{16,24},{20,28},{24,16},{28,20},{1,9},{5... | collective-permute-start | bytes 1327112 | tf_op jit(solution)/shard_map/ppermute | solution.py:637
  139.1 34.4 %collective-permute-start.11 = (bf16[3,80,1152]{2,1,0:T(8,128)(2,1)}, bf16[3,80,1152]{2,1,0:T(8,128)(2,1)}, u32[]{:S(2)}, u32[]{:S(2)}) collective-permute-start(bf16[3,80,1152]{2,1,0:T(8,128)(2,1)} %slice.50), channel_id=1, source_target_pairs={{0,16},{4,20},{8,24},{12,28},{16,0},{20,4},{24,8},{28,12},{1,17},{... | collective-permute-start | bytes 1658888 | tf_op jit(solution)/shard_map/ppermute | solution.py:637
  178.4 38.4 %collective-permute-start.25 = (bf16[3,288,768]{2,1,0:T(8,128)(2,1)}, bf16[3,288,768]{2,1,0:T(8,128)(2,1)S(1)}, u32[]{:S(2)}, u32[]{:S(2)}) collective-permute-start(bf16[3,288,768]{2,1,0:T(8,128)(2,1)} %pad_maximum_fusion.refs_0_), channel_id=1, source_target_pairs={{0,4},{4,0},{8,12},{12,8},{16,20},{20,16},{24,28},{28,24},{1,5},{5... | collective-permute-start | bytes 3981320 | tf_op jit(solution)/shard_map/ppermute | solution.py:637
  180.3 36.6 %collective-permute-start.27 = (bf16[3,288,768]{2,1,0:T(8,128)(2,1)}, bf16[3,288,768]{2,1,0:T(8,128)(2,1)}, u32[]{:S(2)}, u32[]{:S(2)}) collective-permute-start(bf16[3,288,768]{2,1,0:T(8,128)(2,1)} %collective-permute-done.22.refs_2_), channel_id=1, source_target_pairs={{0,4},{4,0},{8,12},{12,8},{16,20},{20,16},{24,28},{28,24},{1,5},{5... | collective-permute-start | bytes 3981320 | tf_op jit(solution)/shard_map/ppermute | solution.py:637
  181.3 36.5 %collective-permute-start.26 = (bf16[3,288,768]{2,1,0:T(8,128)(2,1)}, bf16[3,288,768]{2,1,0:T(8,128)(2,1)}, u32[]{:S(2)}, u32[]{:S(2)}) collective-permute-start(bf16[3,288,768]{2,1,0:T(8,128)(2,1)} %collective-permute-done.21.refs_1_), channel_id=1, source_target_pairs={{0,4},{4,0},{8,12},{12,8},{16,20},{20,16},{24,28},{28,24},{1,5},{5... | collective-permute-start | bytes 3981320 | tf_op jit(solution)/shard_map/ppermute | solution.py:637
  271.5 156.9 %reduce-scatter.4.cloned.1.call-start = ((), (), s32[]{:S(2)}) async-start(), calls=%async_computation.4 | async-start | bytes 11943936 | tf_op jit(solution)/shard_map/reduce_scatter | solution.py:670
  312.4 224.8 %reduce-scatter.6.cloned.1.call-start = ((), (), s32[]{:S(2)}) async-start(), calls=%async_computation.5 | async-start | bytes 15925248 | tf_op jit(solution)/shard_map/reduce_scatter | solution.py:670
  327.6 252.5 %all-gather.8.cloned.1.call-start = ((), (), s32[]{:S(2)}) async-start(), calls=%async_computation.3 | async-start | bytes 4257792 | tf_op jit(solution)/shard_map/all_gather | solution.py:811
  342.5 251.1 %all-gather.14.cloned.1.call-start = ((), (), s32[]{:S(2)}) async-start(), calls=%async_computation.9 | async-start | bytes 1990656 | tf_op jit(solution)/shard_map/all_gather | solution.py:679
  370.1 227.0 %all-gather.10.cloned.1.call-start = ((), (), s32[]{:S(2)}) async-start(), calls=%async_computation.7 | async-start | bytes 2985984 | tf_op jit(solution)/shard_map/all_gather | solution.py:679
  461.5 153.7 %all-gather.12.cloned.1.call-start = ((), (), s32[]{:S(2)}) async-start(), calls=%async_computation.8 | async-start | bytes 3981312 | tf_op jit(solution)/shard_map/all_gather | solution.py:679
  540.3 37.8 %collective-permute-start.49 = (bf16[288,768]{1,0:T(8,128)(2,1)S(1)}, bf16[288,768]{1,0:T(8,128)(2,1)S(1)}, u32[]{:S(2)}, u32[]{:S(2)}) collective-permute-start(bf16[288,768]{1,0:T(8,128)(2,1)S(1)} %get-tuple-element.55), channel_id=1, source_target_pairs={{0,2},{1,3},{2,0},{3,1},{4,6},{5,7},{6,4},{7,5},{8,10},{9,11},{10,... | collective-permute-start | bytes 1327112 | tf_op jit(solution)/shard_map/ppermute | solution.py:675
  (67 other events, 1026.3 us)
Sparse Core Ops, SparseCore 0:
  271.7 64.9 reduce-scatter.7
  340.6 87.8 reduce-scatter.3
  432.5 104.6 reduce-scatter.5
Sparse Core Ops, SparseCore 1:
  342.5 78.2 all-gather.7
  423.3 26.3 all-gather.13
  461.6 54.1 all-gather.9
  580.1 35.1 all-gather.11

commit v4 on v3

v4 whole, which is shorter than its diff:
```python
import functools

import jax
import jax.numpy as jnp
from jax import lax
from jax.experimental import pallas as pl
from jax.experimental.pallas import tpu as pltpu
from jax.sharding import PartitionSpec as P

HEADS = 16
HEAD_DIM = 72
WIDTH = HEADS * HEAD_DIM
QUARTER = HEAD_DIM // 4
BLOCK = 256
CHUNK = 64
COLUMNS = 4
HALVES = 2
PIECES = COLUMNS * HALVES
LANES = 128

epsilon = 1e-06
masked_score = -1e30
f32 = jnp.float32
bf16 = jnp.bfloat16
MEGA = 2**20


def normalize(values):
    average = jnp.mean(values, axis=-1, keepdims=True)
    centered = values - average
    inverse = lax.rsqrt(jnp.mean(centered * centered, axis=-1, keepdims=True) + epsilon)
    return (centered * inverse, inverse)


def normalize_back(normed, inverse, upstream):
    return inverse * (
        upstream
        - jnp.mean(upstream, axis=-1, keepdims=True)
        - normed * jnp.mean(upstream * normed, axis=-1, keepdims=True)
    )


def matmul(left, right):
    return jnp.dot(left, right, preferred_element_type=f32)


def contract_rows(left, right):
    return lax.dot_general(left, right, (((0,), (0,)), ((), ())), preferred_element_type=f32)


def times_transposed(left, right):
    return lax.dot_general(left, right, (((1,), (1,)), ((), ())), preferred_element_type=f32)


def silu_slope(values):
    sigmoid = jax.nn.sigmoid(values)
    return sigmoid * (1.0 + values * (1.0 - sigmoid))


def rope_tables(segments, widths):
    slots = widths.shape[0]
    one_hot = (segments[:, None] == jnp.arange(slots, dtype=jnp.int32)[None, :]).astype(jnp.int32)
    counts = jnp.sum(one_hot, axis=0)
    starts = jnp.cumsum(counts) - counts
    start_token = jnp.sum(one_hot * starts[None, :], axis=1)
    width_token = jnp.maximum(jnp.sum(one_hot * widths[None, :], axis=1), 1)
    place = jnp.arange(segments.shape[0], dtype=jnp.int32) - start_token
    row_place = (place // width_token).astype(f32)
    col_place = (place % width_token).astype(f32)
    freqs = 10000.0 ** (-jnp.arange(QUARTER, dtype=f32) / QUARTER)
    angle_row = row_place[:, None] * freqs[None, :]
    angle_col = col_place[:, None] * freqs[None, :]
    cos_row, sin_row, cos_col, sin_col = (
        jnp.cos(angle_row),
        jnp.sin(angle_row),
        jnp.cos(angle_col),
        jnp.sin(angle_col),
    )
    cos = jnp.concatenate([cos_row, cos_row, cos_col, cos_col], axis=1)
    sin = jnp.concatenate([-sin_row, sin_row, -sin_col, sin_col], axis=1)
    return jnp.tile(cos, (1, HEADS)), jnp.tile(sin, (1, HEADS))


def part(index):
    return slice(index * WIDTH, (index + 1) * WIDTH)


def rotate(values, cos, sin):
    lane = lax.broadcasted_iota(jnp.int32, values.shape, 1)
    leading = lane % (2 * QUARTER) < QUARTER
    partner = jnp.where(
        leading,
        pltpu.roll(values, WIDTH - QUARTER, 1),
        pltpu.roll(values, QUARTER, 1),
    )
    return values * cos + partner * sin


def take(start, size):
    return pl.ds(pl.multiple_of(start, 128 if size % 128 == 0 else 16), size)


def first_part(rows):
    return -(-rows // 32) * 16


def piece_copies(where, count, sources, target, rows, sem):
    place, column, side = where
    first = first_part(rows)
    copies = []
    for other in range(HALVES):
        here = sources[5 * other : 5 * other + 5]
        for by in range(1, count):
            owner = (place + (count - by)) % count
            for j in range(COLUMNS):
                spans = [(here[j], 0, rows)] if j < 3 else [(here[3], 0, first), (here[4], first, rows - first)]
                for ref, start, size in spans:
                    to = target(column ^ j, side ^ other, owner, start, size)
                    copies.append(pltpu.make_async_copy(ref.at[by - 1], to, sem(column ^ j, side ^ other, owner)))
    return copies


def wait_for(ref, sem):
    pltpu.make_async_copy(ref, ref, sem).wait()


def first_kernel(
    count, where_ref, x_ref, mod_ref, cos_ref, sin_ref, joint_ref, project_ref, *refs
):
    sources = refs[:10]
    turned_ref, query_ref, keys_ref, values_ref, weight_ref, weight, first_ref, total, sems = refs[10:]
    where = where_ref[0], where_ref[1], where_ref[2]
    rows_in = joint_ref.shape[0]
    half = rows_in // HALVES

    def target(column, side, place, start, size):
        return weight.at[column, take(place * rows_in + side * half + start, size)]

    copies = piece_copies(where, count, sources, target, half, lambda c, s, z: sems.at[c])
    for c in range(COLUMNS):
        shard = project_ref if c == 3 else joint_ref.at[:, pl.ds(c * WIDTH, WIDTH)]
        copies.append(pltpu.make_async_copy(shard, weight.at[c, take(where[0] * rows_in, rows_in)], sems.at[c]))
    for copy in copies:
        copy.start()
    tokens = x_ref.shape[0]
    for i in range(tokens // CHUNK):
        rows = slice(i * CHUNK, (i + 1) * CHUNK)
        normed, _ = normalize(x_ref[rows, :].astype(f32))
        first_ref[rows, :] = (
            normed * (1.0 + mod_ref[i : i + 1, part(1)]) + mod_ref[i : i + 1, part(0)]
        ).astype(bf16)
    turned_ref[...] = first_ref[...].T
    for c, out in enumerate((query_ref, keys_ref, values_ref)):
        wait_for(weight.at[c], sems.at[c])
        if c == 2:
            out[...] = matmul(first_ref[...], weight[c]).astype(bf16)
        else:
            total[...] = matmul(first_ref[...], weight[c])

            @pl.loop(0, tokens // CHUNK)
            def _(i):
                rows = pl.ds(pl.multiple_of(i * CHUNK, CHUNK), CHUNK)
                out[rows, :] = rotate(total[rows, :], cos_ref[rows, :], sin_ref[rows, :]).astype(bf16)

    wait_for(weight.at[3], sems.at[3])
    write = pltpu.make_async_copy(weight, weight_ref, sems.at[0])
    write.start()
    write.wait()


def window(head):
    start = head * HEAD_DIM // LANES * LANES
    stop = -(-(head + 1) * HEAD_DIM // LANES) * LANES
    lane = lax.broadcasted_iota(jnp.int32, (1, stop - start), 1) + start
    inside = (lane >= head * HEAD_DIM) & (lane < (head + 1) * HEAD_DIM)
    return slice(start, stop), inside


def soft_scores(query, keys, allowed):
    scores = times_transposed(query, keys) * HEAD_DIM ** (-0.5)
    scores = jnp.where(allowed, scores, masked_score)
    exponent = jnp.exp(scores - jnp.max(scores, axis=-1, keepdims=True))
    return exponent * (1.0 / jnp.sum(exponent, axis=-1, keepdims=True))


def attend_kernel(
    query_ref, keys_ref, values_ref, column_ids, row_ids, x_ref, mod_ref,
    weight, turned_ref, branch_ref, middle_ref, second_ref, mixed,
):
    allowed = column_ids[...] == row_ids[...]
    for head in range(HEADS):
        lanes, inside = window(head)
        query = jnp.where(inside, query_ref[:, lanes], jnp.zeros((), bf16))
        probs = soft_scores(query, keys_ref[:, lanes], allowed).astype(bf16)
        mixed[:, lanes] = jnp.where(inside, matmul(probs, values_ref[:, lanes]), mixed[:, lanes])
    attended = mixed[...].astype(bf16)
    turned_ref[...] = attended.T
    branch_ref[...] = matmul(attended, weight[0])
    for i in range(BLOCK // CHUNK):
        rows = slice(i * CHUNK, (i + 1) * CHUNK)
        mod = mod_ref.at[0]
        middle = x_ref[rows, :].astype(f32) + mod[i : i + 1, part(0)] * branch_ref[rows, :]
        middle_ref[rows, :] = middle
        normed, _ = normalize(middle)
        second_ref[rows, :] = (
            normed * (1.0 + mod[i : i + 1, part(2)]) + mod[i : i + 1, part(1)]
        ).astype(bf16)


def placed(refs, rows):
    first = first_part(rows)
    for other in range(HALVES):
        here = refs[5 * other : 5 * other + 5]
        for j in range(3):
            yield j, other, 0, rows, here[j]
        yield 3, other, 0, first, here[3]
        yield 3, other, first, rows - first, here[4]


def tile_copies(r, where, count, tile, pair, downs):
    place, mine, side = where
    t, j = tile
    column = mine ^ j
    rows, width = r["gate"].shape[0], r["hidden_w"].shape[1]
    sem = r["pair_sems"].at[t]
    copies = [
        pltpu.make_async_copy(
            r[name].at[:, take(column * width, width)], r["pair_w"].at[t, which, take(place * rows, rows)], sem
        )
        for which, name in enumerate(("gate", "up"))
    ]
    first = first_part(rows)
    for other in range(HALVES):
        for by in range(1, count):
            owner = (place + (count - by)) % count
            if j < 3:
                spans = [(pair[other][0].at[by - 1], 0, rows)]
            else:
                spans = [(pair[other][0].at[by - 1], 0, first), (pair[other][1].at[by - 1], first, rows - first)]
            for ref, start, size in spans:
                to = r["pair_w"].at[t, side ^ other, take(owner * rows + start, size)]
                copies.append(pltpu.make_async_copy(ref, to, sem))
    for copy in copies:
        copy.start()

    sem = r["down_sems"].at[t]
    target = r["down_w"].at[t]
    piece = width // PIECES

    @pl.when(column == place)
    def _():
        pltpu.make_async_copy(r["down"], target, sem).start()

    @pl.when(column != place)
    def _():
        by = jnp.maximum((place + count - column) % count, 1)
        for i, other, start, size, ref in placed(downs, piece):
            to = target.at[take(((mine ^ i) * HALVES + (side ^ other)) * piece + start, size)]
            pltpu.make_async_copy(ref.at[by - 1], to, sem).start()


def ffn_kernel(count, js, names, *refs):
    r = dict(zip(names, refs, strict=True))
    r["hidden_w"] = r["hidden"]
    first, last = js[0] == 0, js[-1] == COLUMNS - 1
    step = pl.program_id(0)
    tile = r["hidden"].shape[1]
    tokens = r["second"].shape[0]
    second, feed_back = r["second"], r["feed_back"]
    feed, second_back = r["feed"], r["second_back"]

    @pl.when(step == 0)
    def _():
        where = r["where"][0], r["where"][1], r["where"][2]
        for t, j in enumerate(js):
            pair = [
                [r[f"pair{j}_{other}_{i}"] for i in range(1 if j < 3 else 2)]
                for other in range(HALVES)
            ]
            tile_copies(r, where, count, (t, j), pair, [r[f"down_{i}"] for i in range(10)])
        if first:
            r["turned"][...] = second[...].T
            for i in range(tokens // CHUNK):
                rows = slice(i * CHUNK, (i + 1) * CHUNK)
                upstream = r["cot"][rows, :].astype(f32) * r["factor"][0]
                feed_back[rows, :] = (upstream * r["mod"][i : i + 1, part(3)]).astype(bf16)

    pair_w, down_w = r["pair_w"].at[step], r["down_w"].at[step]
    wait_for(pair_w, r["pair_sems"].at[step])
    wait_for(down_w, r["down_sems"].at[step])
    sub = 256
    for n in range(tile // sub):
        lanes = slice(n * sub, (n + 1) * sub)
        gate = matmul(second[...], pair_w[0, :, lanes])
        upval = matmul(second[...], pair_w[1, :, lanes])
        hidden_back = times_transposed(feed_back[...], down_w[lanes, :])
        sigmoid = jax.nn.sigmoid(gate)
        silu = gate * sigmoid
        r["hidden"][:, lanes] = (silu * upval).astype(bf16)
        r["pair_back"][0, 1, :, lanes] = (hidden_back * silu).astype(bf16)
        r["pair_back"][0, 0, :, lanes] = (
            hidden_back * upval * (sigmoid * (1.0 + gate * (1.0 - sigmoid)))
        ).astype(bf16)

    r["hidden_turned"][0] = r["hidden"][...].T
    feed_part = matmul(r["hidden"][...], down_w[...])
    back_part = times_transposed(r["pair_back"][0, 0], pair_w[0]) + times_transposed(
        r["pair_back"][0, 1], pair_w[1]
    )

    @pl.when(step == 0)
    def _():
        feed[...] = feed_part if first else r["feed_in"][...] + feed_part
        second_back[...] = back_part if first else r["back_in"][...] + back_part

    @pl.when(step > 0)
    def _():
        feed[...] += feed_part
        second_back[...] += back_part

    if not last:
        return

    @pl.when(step == len(js) - 1)
    def _():
        for i in range(tokens // CHUNK):
            rows = slice(i * CHUNK, (i + 1) * CHUNK)
            gate_one = r["mod"][i : i + 1, part(0)]
            scale_two = r["mod"][i : i + 1, part(2)]
            gate_two = r["mod"][i : i + 1, part(3)]
            middle = r["middle"][rows, :]
            r["output"][rows, :] = (middle + gate_two * feed[rows, :]).astype(bf16)
            upstream = r["cot"][rows, :].astype(f32) * r["factor"][0]
            normed, inverse = normalize(middle)
            back = second_back[rows, :]
            middle_back = upstream + normalize_back(normed, inverse, back * (1.0 + scale_two))
            r["middle_back"][rows, :] = middle_back
            r["branch_back"][rows, :] = (middle_back * gate_one).astype(bf16)
            for where, values in enumerate(
                (middle_back * r["branch"][rows, :], back, back * normed, upstream * feed[rows, :])
            ):
                r["sums"][i : i + 1, part(where)] = jnp.sum(values, axis=0, keepdims=True)


ORDER = (1, 3, 2, 0)
SEND_X, KEEP_X, SEND_Y, KEEP_Y = (1, 3), (2, 0), (3, 2), (1, 0)
CUT = (SEND_X, KEEP_X, SEND_Y, KEEP_Y)


def put_grad(grad, other_ref, out_refs):
    step = pl.program_id(0)
    if other_ref is None:
        out_refs[0][0] = grad.astype(bf16)
        return
    total = (grad + other_ref[0].astype(f32)).astype(bf16)
    first = first_part(total.shape[1])
    for at, j in enumerate(ORDER):

        @pl.when(step == at)
        def _():
            for columns, ref in zip(CUT, out_refs, strict=True):
                if j in columns:
                    ref[0] = total[:, :first] if columns in (SEND_X, KEEP_X) else total[:, first:]


def cut_specs(count, rows, breadth):
    first = first_part(rows)
    shapes, specs = [], []
    for columns in CUT:
        size = first if columns in (SEND_X, KEEP_X) else rows - first
        shapes.append(struct((2, count, size, breadth), bf16))
        second = ORDER.index(columns[1])
        specs.append(
            pl.BlockSpec(
                (1, count, size, breadth),
                lambda s, where, second=second: (jnp.where(s >= second, 1, 0), 0, 0, 0),
            )
        )
    return tuple(shapes), tuple(specs)


def split_refs(mine, refs):
    return (refs[0], refs[1:]) if mine else (None, refs)


def pair_grad_kernel(mine, count, where_ref, turned_ref, own_ref, near_ref, far_ref, *refs):
    other_ref, out_refs = split_refs(mine, refs)
    for at, j in enumerate(ORDER):

        @pl.when(pl.program_id(0) == at)
        def _():
            back = {0: own_ref, 3: far_ref}.get(j, near_ref)
            grad = matmul(turned_ref[...], back[0, 0])
            put_grad(grad.reshape(count, grad.shape[0] // count, grad.shape[1]), other_ref, out_refs)


def down_grad_kernel(mine, where_ref, *refs):
    hiddens, feed_back_ref, out_ref = refs[:3], refs[3], refs[-1]
    other_ref = refs[4] if mine else None
    side = where_ref[2] if mine else where_ref[2] ^ 1
    count, _, rows, _ = out_ref.shape
    tiles = [(hidden, t) for hidden in hiddens for t in range(hidden.shape[0])]
    for j, (hidden, t) in enumerate(tiles):
        pieces = [hidden[t, take(((where_ref[1] ^ c) * HALVES + side) * rows, rows), :] for c in ORDER]
        grad = matmul(jnp.concatenate(pieces, axis=0), feed_back_ref[...]).reshape(COLUMNS, rows, WIDTH)
        owner = where_ref[1] ^ j
        if mine:
            grad = grad + other_ref[owner].astype(f32)
        out_ref[owner] = grad.astype(bf16)


def attn_grad_kernel(
    mine, where_ref, first_ref, attended_ref, joint_back_ref, branch_back_ref, *refs
):
    other_ref, out_refs = split_refs(mine, refs)
    column = where_ref[1] ^ where_ref[3 + pl.program_id(0)]
    side = where_ref[2] if mine else where_ref[2] ^ 1
    _, count, _, _ = out_refs[0].shape
    rows = WIDTH // count // HALVES

    def put(turned, right):
        taken = [turned[take((z * HALVES + side) * rows, rows), :] for z in range(count)]
        grad = matmul(jnp.concatenate(taken, axis=0), right[...])
        put_grad(grad.reshape(count, rows, WIDTH), other_ref, out_refs)

    @pl.when(column < 3)
    def _():
        put(first_ref, joint_back_ref)

    @pl.when(column == 3)
    def _():
        put(attended_ref, branch_back_ref)


def place_pair_kernel(where_ref, *refs):
    sources, outs = refs[:10], refs[10:]
    rows, tile = sources[0].shape
    for way in range(HALVES):

        @pl.when(where_ref[2] == way)
        def _():
            for j, other, start, size, ref in placed(sources, rows):
                lanes = take((where_ref[1] ^ j) * tile, tile)
                outs[way ^ other][start : start + size, lanes] = ref[...].astype(f32)


def place_down_kernel(where_ref, *refs):
    sources, out = refs[:10], refs[10]
    rows = sources[0].shape[0]
    for j, other, start, size, ref in placed(sources, rows):
        piece = (where_ref[1] ^ j) * HALVES + (where_ref[2] ^ other)
        out[take(piece * rows + start, size), :] = ref[...].astype(f32)


def place_attn_kernel(where_ref, *refs):
    sources, joint_ref, project_ref = refs[:10], refs[10], refs[11]
    rows = sources[0].shape[0]
    for column in range(COLUMNS):

        @pl.when(where_ref[1] == column)
        def _():
            for j, other, start, size, ref in placed(sources, rows):
                to = take((where_ref[2] ^ other) * rows + start, size)
                if column ^ j == 3:
                    project_ref[to, :] = ref[...].astype(f32)
                else:
                    joint_ref[to, part(column ^ j)] = ref[...].astype(f32)


def attend_back_kernel(
    query_ref, keys_ref, values_ref, branch_back_ref, column_ids, row_ids, cos_ref,
    sin_ref, weight, joint_back_ref, mixed_back, query_back, keys_back, values_back,
):
    mixed_back[...] = times_transposed(branch_back_ref[...], weight[0]).astype(bf16)
    allowed = column_ids[...] == row_ids[...]
    scaling = HEAD_DIM ** (-0.5)
    for head in range(HEADS):
        lanes, inside = window(head)
        zero = jnp.zeros((), bf16)
        query = jnp.where(inside, query_ref[:, lanes], zero)
        back = jnp.where(inside, mixed_back[:, lanes], zero)
        soft = soft_scores(query, keys_ref[:, lanes], allowed)
        probs_back = times_transposed(back, values_ref[:, lanes])
        scores_back = (
            soft * (probs_back - jnp.sum(soft * probs_back, axis=-1, keepdims=True))
        ).astype(bf16)
        query_back[:, lanes] = jnp.where(
            inside, matmul(scores_back, keys_ref[:, lanes]) * scaling, query_back[:, lanes]
        )
        keys_back[:, lanes] = jnp.where(
            inside, contract_rows(scores_back, query) * scaling, keys_back[:, lanes]
        )
        values_back[:, lanes] = jnp.where(
            inside, contract_rows(soft.astype(bf16), back), values_back[:, lanes]
        )

    @pl.loop(0, BLOCK // CHUNK)
    def _(i):
        rows = pl.ds(pl.multiple_of(i * CHUNK, CHUNK), CHUNK)
        cos, sin = cos_ref[rows, :], sin_ref[rows, :]
        joint_back_ref[rows, part(0)] = rotate(query_back[rows, :], cos, -sin).astype(bf16)
        joint_back_ref[rows, part(1)] = rotate(keys_back[rows, :], cos, -sin).astype(bf16)
        joint_back_ref[rows, part(2)] = values_back[rows, :].astype(bf16)


def first_back_kernel(
    joint_back_ref, x_ref, middle_back_ref, mod_ref, weight, grad_ref, sums_ref, first_back
):
    step = pl.program_id(0)
    product = times_transposed(joint_back_ref[...], weight[0])

    @pl.when(step == 0)
    def _():
        first_back[...] = product

    @pl.when(step > 0)
    def _():
        first_back[...] += product

    @pl.when(step == pl.num_programs(0) - 1)
    def _():
        finish_first_back(x_ref, middle_back_ref, mod_ref, grad_ref, sums_ref, first_back)


def finish_first_back(x_ref, middle_back_ref, mod_ref, grad_ref, sums_ref, first_back):
    for i in range(x_ref.shape[0] // CHUNK):
        rows = slice(i * CHUNK, (i + 1) * CHUNK)
        normed, inverse = normalize(x_ref[rows, :].astype(f32))
        back = first_back[rows, :]
        grad_ref[rows, :] = middle_back_ref[rows, :] + normalize_back(
            normed, inverse, back * (1.0 + mod_ref[i : i + 1, part(1)])
        )
        sums_ref[i : i + 1, part(0)] = jnp.sum(back, axis=0, keepdims=True)
        sums_ref[i : i + 1, part(1)] = jnp.sum(back * normed, axis=0, keepdims=True)


SMEM = pl.BlockSpec(memory_space=pltpu.SMEM)
VMEM = pl.BlockSpec(memory_space=pltpu.VMEM)
ANY = pl.BlockSpec(memory_space=pl.ANY)


def struct(shape, dtype):
    return jax.ShapeDtypeStruct(shape, dtype)


def params(mega=56):
    return pltpu.CompilerParams(vmem_limit_bytes=mega * MEGA)


def cost(microseconds):
    return pl.CostEstimate(flops=int(microseconds * 1e9), bytes_accessed=1000, transcendentals=0)


def by_block(*shape):
    return pl.BlockSpec(shape, lambda b: (b,) + (0,) * (len(shape) - 1))


def whole(*shape):
    return pl.BlockSpec(shape, lambda *_: (0,) * len(shape))


def first_call(where, x, mod, cos, sin, joint, project, arrived):
    tokens = x.shape[0]
    count = arrived[0].shape[0] + 1
    shape = struct((tokens, WIDTH), bf16)
    return pl.pallas_call(
        functools.partial(first_kernel, count),
        out_shape=(struct((WIDTH, tokens), bf16),)
        + (shape,) * 3
        + (struct((COLUMNS, WIDTH, WIDTH), bf16),),
        in_specs=[SMEM, VMEM, VMEM, VMEM, VMEM] + [ANY] * (2 + len(arrived)),
        out_specs=(VMEM,) * 4 + (ANY,),
        scratch_shapes=[
            pltpu.VMEM((COLUMNS, WIDTH, WIDTH), bf16),
            pltpu.VMEM((tokens, WIDTH), bf16),
            pltpu.VMEM((tokens, WIDTH), f32),
            pltpu.SemaphoreType.DMA((COLUMNS,)),
        ],
        compiler_params=params(),
        cost_estimate=cost(20),
    )(where, x, mod, cos, sin, joint, project, *arrived)


def attend_call(query, keys, values, ids, x, mod, weight):
    tokens = x.shape[0]
    return pl.pallas_call(
        attend_kernel,
        grid=(tokens // BLOCK,),
        out_shape=(
            struct((WIDTH, tokens), bf16),
            struct((tokens, WIDTH), f32),
            struct((tokens, WIDTH), f32),
            struct((tokens, WIDTH), bf16),
        ),
        in_specs=[by_block(BLOCK, WIDTH)] * 3
        + [by_block(BLOCK, 1), pl.BlockSpec((1, BLOCK), lambda b: (0, b)), by_block(BLOCK, WIDTH)]
        + [by_block(1, BLOCK // CHUNK, 4 * WIDTH), pl.BlockSpec((1, WIDTH, WIDTH), lambda b: (3, 0, 0))],
        out_specs=(pl.BlockSpec((WIDTH, BLOCK), lambda b: (0, b)),) + (by_block(BLOCK, WIDTH),) * 3,
        scratch_shapes=[pltpu.VMEM((BLOCK, WIDTH), f32)],
        compiler_params=params(),
        cost_estimate=cost(12),
    )(
        query, keys, values, ids[:, None], ids[None, :], x,
        mod.reshape(tokens // BLOCK, BLOCK // CHUNK, 4 * WIDTH), weight,
    )


def ffn_call(js, where, given, shards, pairs, downs):
    second = given["second"]
    tokens = second.shape[0]
    ff = shards["gate"].shape[1]
    tile = ff // COLUMNS
    count = ff // shards["down"].shape[0]
    chunks = tokens // CHUNK
    first, last = js[0] == 0, js[-1] == COLUMNS - 1
    full = whole(tokens, WIDTH)
    wide = struct((tokens, WIDTH), f32)
    narrow = struct((tokens, WIDTH), bf16)
    inputs = [("where", where, SMEM), ("second", second, full)]
    if first or last:
        inputs += [
            ("factor", given["factor"], SMEM),
            ("cot", given["cot"], full),
            ("mod", given["mod"], whole(chunks, 4 * WIDTH)),
        ]
    if not first:
        inputs += [
            ("feed_back", given["feed_back"], full),
            ("feed_in", given["feed"], full),
            ("back_in", given["second_back"], full),
        ]
    if last:
        inputs += [("middle", given["middle"], full), ("branch", given["branch"], full)]
    inputs += [(name, shards[name], ANY) for name in ("gate", "up", "down")]
    for j in js:
        for other in range(HALVES):
            inputs += [(f"pair{j}_{other}_{i}", a, ANY) for i, a in enumerate(pairs[other][j])]
    inputs += [(f"down_{i}", a, ANY) for i, a in enumerate(downs)]
    outputs = [
        (
            "hidden_turned",
            struct((len(js), tile, tokens), bf16),
            pl.BlockSpec((1, tile, tokens), lambda t: (t, 0, 0)),
        ),
        (
            "pair_back",
            struct((len(js), HALVES, tokens, tile), bf16),
            pl.BlockSpec((1, HALVES, tokens, tile), lambda t: (t, 0, 0, 0)),
        ),
    ]
    if first:
        outputs += [
            ("turned", struct((WIDTH, tokens), bf16), whole(WIDTH, tokens)),
            ("feed_back", narrow, full),
        ]
    sums = ("feed", "second_back")
    scratch = [
        ("pair_w", pltpu.VMEM((len(js), HALVES, WIDTH, tile), bf16)),
        ("down_w", pltpu.VMEM((len(js), ff // count, WIDTH), bf16)),
        ("hidden", pltpu.VMEM((tokens, tile), bf16)),
        ("pair_sems", pltpu.SemaphoreType.DMA((len(js),))),
        ("down_sems", pltpu.SemaphoreType.DMA((len(js),))),
    ]
    if last:
        outputs += [
            ("output", narrow, full),
            ("middle_back", wide, full),
            ("branch_back", narrow, full),
            ("sums", struct((chunks, 4 * WIDTH), f32), whole(chunks, 4 * WIDTH)),
        ]
        scratch += [(name, pltpu.VMEM((tokens, WIDTH), f32)) for name in sums]
    else:
        outputs += [(name, wide, full) for name in sums]
    names = [each[0] for each in inputs + outputs + scratch]
    found = pl.pallas_call(
        functools.partial(ffn_kernel, count, js, names),
        grid=(len(js),),
        out_shape=tuple(shape for _, shape, _ in outputs),
        in_specs=[spec for _, _, spec in inputs],
        out_specs=tuple(spec for _, _, spec in outputs),
        scratch_shapes=[shape for _, shape in scratch],
        compiler_params=params(),
        cost_estimate=cost(12 * len(js)),
    )(*[array for _, array, _ in inputs])
    return {name: array for (name, _, _), array in zip(outputs, found, strict=True)}


def by_column(call, count, rows, breadth, in_specs, where, arrays, other):
    shapes, specs = cut_specs(count, rows, breadth)
    block = pl.BlockSpec((1, count, rows, breadth), lambda s, where: (s, 0, 0, 0))
    if other is None:
        shapes, specs = (struct((COLUMNS, count, rows, breadth), bf16),), (block,)
    else:
        in_specs, arrays = in_specs + [block], arrays + (other,)
    found = pl.pallas_call(
        call,
        out_shape=shapes,
        grid_spec=pltpu.PrefetchScalarGridSpec(
            num_scalar_prefetch=1, grid=(COLUMNS,), in_specs=in_specs, out_specs=specs
        ),
        compiler_params=params(),
        cost_estimate=cost(10),
    )(where, *arrays)
    return found[0] if other is None else found


def pair_grad_call(count, where, turned, backs, other=None):
    tokens, tile = backs[0].shape[2:]
    mine = other is not None

    def spec(tile_of):
        return pl.BlockSpec(
            (1, 1, tokens, tile),
            lambda s, where: (tile_of(where[3 + s]), where[2] if mine else where[2] ^ 1, 0, 0),
        )

    return by_column(
        functools.partial(pair_grad_kernel, mine, count),
        count, WIDTH // count, tile,
        [whole(WIDTH, tokens), spec(lambda j: 0), spec(lambda j: jnp.clip(j - 1, 0, 1)), spec(lambda j: 0)],
        where, (turned,) + tuple(backs), other,
    )


def attn_grad_call(count, where, first, attended, joint_back, branch_back, other=None):
    tokens = first.shape[1]
    return by_column(
        functools.partial(attn_grad_kernel, other is not None),
        count, WIDTH // count // HALVES, WIDTH,
        [
            whole(WIDTH, tokens),
            whole(WIDTH, tokens),
            pl.BlockSpec((tokens, WIDTH), lambda s, where: (0, jnp.minimum(where[1] ^ where[3 + s], 2))),
            whole(tokens, WIDTH),
        ],
        where, (first, attended, joint_back, branch_back), other,
    )


def down_grad_call(count, where, hiddens, feed_back, other=None):
    ff = sum(h.shape[0] * h.shape[1] for h in hiddens)
    out = struct((count, COLUMNS, ff // count // PIECES, WIDTH), bf16)
    arrays = tuple(hiddens) + (feed_back,) + (() if other is None else (other,))
    return pl.pallas_call(
        functools.partial(down_grad_kernel, other is not None),
        out_shape=out,
        in_specs=[SMEM] + [VMEM] * len(arrays),
        out_specs=VMEM,
        compiler_params=params(),
        cost_estimate=cost(7),
    )(where, *arrays)


def place_call(kernel, where, arrays, outs):
    return pl.pallas_call(
        kernel,
        out_shape=outs,
        in_specs=[SMEM] + [VMEM] * len(arrays),
        out_specs=jax.tree.map(lambda _: VMEM, outs),
        compiler_params=params(),
        cost_estimate=cost(4),
    )(where, *arrays)


def attend_back_call(query, keys, values, branch_back, ids, cos, sin, weight):
    tokens = query.shape[0]
    block = by_block(BLOCK, WIDTH)
    return pl.pallas_call(
        attend_back_kernel,
        grid=(tokens // BLOCK,),
        out_shape=struct((tokens, 3 * WIDTH), bf16),
        in_specs=[block, block, block, block]
        + [by_block(BLOCK, 1), pl.BlockSpec((1, BLOCK), lambda b: (0, b)), block, block]
        + [pl.BlockSpec((1, WIDTH, WIDTH), lambda b: (3, 0, 0))],
        out_specs=by_block(BLOCK, 3 * WIDTH),
        scratch_shapes=[
            pltpu.VMEM((BLOCK, WIDTH), bf16),
            pltpu.VMEM((BLOCK, WIDTH), f32),
            pltpu.VMEM((BLOCK, WIDTH), f32),
            pltpu.VMEM((BLOCK, WIDTH), f32),
        ],
        compiler_params=params(),
        cost_estimate=cost(29),
    )(query, keys, values, branch_back, ids[:, None], ids[None, :], cos, sin, weight)


def first_back_call(joint_back, x, middle_back, mod, weight):
    tokens = x.shape[0]
    chunks = tokens // CHUNK
    full = whole(tokens, WIDTH)
    return pl.pallas_call(
        first_back_kernel,
        grid=(3,),
        out_shape=(struct((tokens, WIDTH), f32), struct((chunks, 2 * WIDTH), f32)),
        in_specs=[
            pl.BlockSpec((tokens, WIDTH), lambda c: (0, c)),
            full,
            full,
            whole(chunks, 2 * WIDTH),
            pl.BlockSpec((1, WIDTH, WIDTH), lambda c: (c, 0, 0)),
        ],
        out_specs=(full, whole(chunks, 2 * WIDTH)),
        scratch_shapes=[pltpu.VMEM((tokens, WIDTH), f32)],
        compiler_params=params(),
        cost_estimate=cost(13),
    )(joint_back, x, middle_back, mod, weight)


def shifts(count, by):
    return [(i, (i + by) % count) for i in range(count)]


def pick(array, index):
    return lax.dynamic_index_in_dim(array, index, 0, keepdims=False)


def across(bit):
    return [(i, i ^ bit) for i in range(PIECES)]


def swap(array, bit):
    return lax.ppermute(array, "bucket", across(bit))


def after(arrays, *others):
    return lax.optimization_barrier((arrays, others))[0]


def add(left, right):
    return (left.astype(f32) + right.astype(f32)).astype(bf16)


def over_z(piece):
    count = lax.axis_size("fsdp")
    return [lax.ppermute(piece, "fsdp", shifts(count, by)) for by in range(1, count)]


def gather_z(piece):
    count = lax.axis_size("fsdp")
    place = lax.axis_index("fsdp")
    full = lax.all_gather(piece, "fsdp", axis=0, tiled=False)
    return jnp.stack([pick(full, (place + count - by) % count) for by in range(1, count)])


def cross(by_x, by_y, first):
    if first is not None:
        by_x, by_y = by_x[..., :first, :], by_y[..., first:, :]
    return swap(by_x, 4), swap(by_y, 2)


def both(here):
    return here + tuple(None if array is None else swap(array, 1) for array in here)


def spread(total):
    by_x, by_y = swap(total, 2), swap(total, 4)
    return both((total, by_x, by_y) + cross(by_x, by_y, first_part(total.shape[0])))


def spread_whole(pieces):
    first = first_part(pieces.shape[1])

    def of(side):
        own, by_x, by_y, far = (pieces[c * HALVES + side] for c in range(COLUMNS))
        return own, by_x, by_y, far[:first], far[first:]

    return of(0) + of(1)


def halve_once(cut):
    send_x, (a2, a0), send_y, (b1, b0) = cut
    from_x, from_y = swap(send_x, 2), swap(send_y, 4)
    return add(a0, from_x[0]), add(a2, from_x[1]), add(b0, from_y[1]), add(b1, from_y[0])


def halve_twice(once):
    a0, a2, b0, b1 = once
    return jnp.concatenate([add(a0, swap(a2, 4)), add(b0, swap(b1, 2))], axis=-2)


def sum_z(parts):
    count = lax.axis_size("fsdp")
    place = lax.axis_index("fsdp")
    total = pick(parts, place).astype(f32)
    for by in range(1, count):
        total = total + lax.ppermute(
            pick(parts, (place + by) % count), "fsdp", shifts(count, by)
        ).astype(f32)
    return total.astype(bf16)


def cut_down(part, first):
    cut = []
    for columns in CUT:
        both_columns = jnp.stack([part[ORDER.index(j)] for j in columns])
        cut.append(both_columns[:, :first] if columns in (SEND_X, KEEP_X) else both_columns[:, first:])
    return cut


def uncut(cut):
    def of(j, pair):
        columns = next(c for c in pair if j in c)
        return cut[CUT.index(columns)][columns.index(j)]

    return jnp.stack(
        [jnp.concatenate([of(j, (SEND_X, KEEP_X)), of(j, (SEND_Y, KEEP_Y))], axis=1) for j in ORDER]
    )


def sum_whole(mine, theirs):
    parts = jnp.stack([mine, theirs], axis=1)
    parts = jnp.stack([parts[ORDER.index(c)] for c in range(COLUMNS)])
    rows, breadth = mine.shape[2:]
    parts = lax.psum(parts, "bucket").transpose(2, 0, 1, 3, 4)
    return spread_whole(sum_z(parts).reshape(PIECES, rows, breadth))


def arrived_whole(pieces):
    count = lax.axis_size("fsdp")
    place = lax.axis_index("fsdp")
    first = first_part(pieces.shape[1])
    full = lax.all_gather(pieces, "fsdp", axis=0, tiled=False)
    full = jnp.stack([pick(full, (place + count - by) % count) for by in range(1, count)])

    def of(side):
        own, by_x, by_y, far = (full[:, c * HALVES + side] for c in range(COLUMNS))
        return own, by_x, by_y, far[:, :first], far[:, first:]

    return of(0) + of(1)


def to_group(rows, count, place):
    relative = jnp.stack(
        [pick(rows, place)]
        + [
            lax.ppermute(pick(rows, (place + by) % count), "fsdp", shifts(count, by))
            for by in range(1, count)
        ]
    )
    return jnp.stack([pick(relative, (place - j) % count) for j in range(count)])


def on_device(
    inputs,
    condition,
    segment_ids,
    grid_widths,
    bucket_counts,
    modulate_weight,
    joint_weight,
    project_weight,
    gate_weight,
    up_weight,
    down_weight,
    cotangent,
):
    fsdp_count = lax.axis_size("fsdp")
    place = lax.axis_index("fsdp")
    bucket = lax.axis_index("bucket")
    height = joint_weight.shape[0]
    half = height // HALVES
    ff = gate_weight.shape[1]
    tile = ff // COLUMNS
    down_rows = down_weight.shape[0] // PIECES
    slots = condition.shape[0]

    fast = lax.axis_size("bucket") == PIECES
    if fast:
        column, side = bucket // HALVES, bucket % HALVES
        where = jnp.stack([place, column, side] + [jnp.int32(j) for j in ORDER])
        attn_piece = jnp.where(
            column == 3,
            lax.dynamic_slice(project_weight, (side * half, 0), (half, WIDTH)),
            lax.dynamic_slice(joint_weight, (side * half, column * WIDTH), (half, WIDTH)),
        )
        ffn_piece = jnp.where(
            side == 0,
            lax.dynamic_slice(gate_weight, (0, column * tile), (height, tile)),
            lax.dynamic_slice(up_weight, (0, column * tile), (height, tile)),
        )
        down_piece = lax.dynamic_slice_in_dim(down_weight, bucket * down_rows, down_rows, 0)
        attn_z = gather_z(attn_piece)
        pair_z = gather_z(after(ffn_piece, attn_z))
        down_k = over_z(after(down_piece, attn_z))
        attn_x, attn_y = swap(attn_z, 2), swap(attn_z, 4)
        attn_arrived = both((attn_z, attn_x, attn_y) + cross(attn_x, attn_y, first_part(half)))
    else:
        where = jnp.stack([place, 0 * place, 0 * place] + [jnp.int32(j) for j in ORDER])
        attn_arrived = arrived_whole(
            jnp.concatenate([joint_weight, project_weight], axis=1)
            .reshape(HALVES, half, COLUMNS, WIDTH)
            .transpose(2, 0, 1, 3)
            .reshape(PIECES, half, WIDTH)
        )
        pairs = arrived_whole(
            jnp.stack([gate_weight, up_weight])
            .reshape(HALVES, height, COLUMNS, tile)
            .transpose(2, 0, 1, 3)
            .reshape(PIECES, height, tile)
        )
        downs = arrived_whole(down_weight.reshape(PIECES, down_rows, WIDTH))

    cond_float = condition.astype(f32)
    lifted = jax.nn.silu(cond_float).astype(bf16)
    lifted_rows = to_group(
        lifted.reshape(slots, fsdp_count, height).transpose(1, 0, 2), fsdp_count, place
    ).reshape(fsdp_count * slots, height)
    one_hot = (
        segment_ids[::CHUNK, None] == jnp.arange(slots, dtype=jnp.int32)[None, :]
    ).astype(f32)

    def modulation_parts(weight, rows):
        parts = matmul(rows, weight).reshape(fsdp_count, slots, weight.shape[1])
        return to_group(parts, fsdp_count, place)

    def modulation(parts):
        return jnp.dot(
            one_hot,
            jnp.sum(parts, axis=0),
            precision=lax.Precision.HIGHEST,
            preferred_element_type=f32,
        )

    mod_one = modulation(modulation_parts(modulate_weight[:, : 2 * WIDTH], lifted_rows))
    if fast:
        lifted_rows = after(lifted_rows, attn_z)
    mod_parts = modulation_parts(modulate_weight[:, 2 * WIDTH :], lifted_rows)
    counts = bucket_counts.astype(f32)
    mine = jnp.sum(jnp.where(jnp.arange(counts.shape[0], dtype=jnp.int32) == bucket, counts, 0.0))
    factor = (mine * counts.shape[0] / jnp.sum(counts)).reshape(1)
    cos, sin = rope_tables(segment_ids, grid_widths)

    first, query, keys, values, weight = first_call(
        where, inputs, mod_one, cos, sin, joint_weight, project_weight, attn_arrived
    )
    if fast:
        mod_parts, down_k = after((mod_parts, down_k), query)
        down_z = jnp.stack(down_k)
        down_x, down_y = swap(down_z, 2), swap(down_z, 4)
    mod = modulation(mod_parts)
    attended, branch, middle, second = attend_call(
        query, keys, values, segment_ids, inputs, mod, weight
    )
    shards = dict(gate=gate_weight, up=up_weight, down=down_weight)
    given = dict(
        second=second, factor=factor, cot=cotangent, mod=mod, middle=middle, branch=branch
    )
    if fast:
        down_x, down_y, pair_z = after((down_x, down_y, pair_z), second)
        down_far = cross(down_x, down_y, first_part(down_rows))
        downs = both((down_z, down_x, down_y) + down_far)
        pair_z = after(pair_z, down_far)
        pair_x, pair_y = swap(pair_z, 2), swap(pair_z, 4)
        pairs = (pair_z, pair_x, pair_y, None, None, swap(pair_z, 1), None, None, None, None)
    pairs = [
        [[group] for group in pairs[5 * k : 5 * k + 3]] + [list(pairs[5 * k + 3 : 5 * k + 5])]
        for k in range(HALVES)
    ]
    found = ffn_call((0,), where, given, shards, pairs, downs)
    turned, feed_back = found["turned"], found["feed_back"]
    steps = [found]
    if fast:
        pair_x, pair_y = after((pair_x, pair_y), feed_back)
        far = cross(pair_x, pair_y, first_part(height))
        pairs[1][1:3] = [swap(pair_x, 1)], [swap(pair_y, 1)]
    for js in ((1, 2), (3,)):
        given.update(feed_back=feed_back, feed=found["feed"], second_back=found["second_back"])
        if fast and js == (3,):
            far = after(far, found["feed"])
            pairs[0][3], pairs[1][3] = list(far), [swap(array, 1) for array in far]
        found = ffn_call(js, where, given, shards, pairs, downs)
        steps.append(found)
    output, middle_back, branch_back = found["output"], found["middle_back"], found["branch_back"]
    late_sums = found["sums"]

    count = fsdp_count
    hiddens = [step["hidden_turned"] for step in steps]
    backs = [step["pair_back"] for step in steps]
    down_theirs = down_grad_call(count, where, hiddens, feed_back)
    if fast:
        turned = after(turned, down_theirs)
    pair_theirs = pair_grad_call(count, where, turned, backs)
    if fast:
        down_other = swap(down_theirs, 1)
        down_other, pair_theirs = after((down_other, pair_theirs))
        pair_other = swap(pair_theirs, 1)
    else:
        down_other, pair_other = jnp.zeros_like(down_theirs), jnp.zeros_like(pair_theirs)
    down_mine = down_grad_call(count, where, hiddens, feed_back, down_other)
    if fast:
        turned = after(turned, down_mine)
    pair_cut = pair_grad_call(count, where, turned, backs, pair_other)
    if fast:
        down_part = lax.psum_scatter(down_mine, "fsdp", scatter_dimension=0, tiled=False)
        branch_back = after(branch_back, pair_cut)
    joint_back = attend_back_call(
        query, keys, values, branch_back, segment_ids, cos, sin, weight
    )
    if fast:
        send_x, keep_x, send_y, keep_y = pair_cut
        keep_x, keep_y = after((keep_x, keep_y), joint_back)
        pair_once = halve_once((send_x, keep_x, send_y, keep_y))
        branch_back = after(branch_back, pair_once)
        branch_back = after(branch_back, pair_once)
    attn_theirs = attn_grad_call(count, where, first, attended, joint_back, branch_back)
    if fast:
        pair_parts, down_part = after((halve_twice(pair_once), down_part), attn_theirs)
        pair_sum = lax.psum_scatter(pair_parts, "fsdp", scatter_dimension=0, tiled=False)
        down_cut = cut_down(down_part, first_part(down_rows))
        middle_back = after(middle_back, attn_theirs, down_cut)
    grad_inputs, early_sums = first_back_call(joint_back, inputs, middle_back, mod_one, weight)
    if fast:
        down_cut = [down_cut[0], after(down_cut[1], grad_inputs), down_cut[2], after(down_cut[3], grad_inputs)]
        down_once = halve_once(down_cut)
        attn_other, down_once = after((swap(attn_theirs, 1), down_once), grad_inputs)
        attn_cut = attn_grad_call(
            count, where, first, attended, joint_back, branch_back, attn_other
        )
        down_total = after(halve_twice(down_once), attn_cut)
        attn_once = halve_once(attn_cut)
        pair_sum, down_total = after((pair_sum, down_total), attn_once)
        attn_parts = halve_twice(attn_once)
        pair_x, pair_y = swap(pair_sum, 2), swap(pair_sum, 4)
        down_x, down_y = swap(down_total, 2), swap(down_total, 4)
        attn_z = [
            lax.ppermute(pick(attn_parts, (place + by) % count), "fsdp", shifts(count, by))
            for by in range(1, count)
        ]
        pair_x, pair_y, down_x, down_y = after((pair_x, pair_y, down_x, down_y), attn_parts)
        down_far = cross(down_x, down_y, first_part(down_rows))
        pair_far = cross(pair_x, pair_y, first_part(height))
        attn_sum = pick(attn_parts, place).astype(f32)
        for array in after(attn_z, pair_far, down_far):
            attn_sum = attn_sum + array.astype(f32)
        attn_sum = attn_sum.astype(bf16)
        down_sums = both((down_total, down_x, down_y) + down_far)
        pair_sums = both((pair_sum, pair_x, pair_y) + pair_far)
        attn_sums = spread(attn_sum)
    else:
        down_sums = sum_whole(down_mine.swapaxes(0, 1), down_theirs.swapaxes(0, 1))
        pair_sums = sum_whole(uncut(pair_cut), pair_theirs)
        attn_cut = attn_grad_call(
            count, where, first, attended, joint_back, branch_back, jnp.zeros_like(attn_theirs)
        )
        attn_sums = sum_whole(uncut(attn_cut), attn_theirs)
    down_grad = place_call(place_down_kernel, where, down_sums, struct(down_weight.shape, f32))
    pair_grad = place_call(
        place_pair_kernel, where, pair_sums, (struct(gate_weight.shape, f32),) * 2
    )
    attn_grad = place_call(
        place_attn_kernel,
        where,
        attn_sums,
        (struct(joint_weight.shape, f32), struct(project_weight.shape, f32)),
    )

    def by_slot(chunk_sums):
        return lax.dot_general(
            one_hot,
            chunk_sums,
            (((0,), (0,)), ((), ())),
            precision=lax.Precision.HIGHEST,
            preferred_element_type=f32,
        ).astype(bf16)

    everyone = lax.all_gather(
        jnp.concatenate([by_slot(early_sums), by_slot(late_sums), lifted], axis=1),
        ("bucket", "fsdp"),
        axis=0,
        tiled=True,
    )
    if fast:
        everyone = after(everyone, attn_sum)
    all_back = everyone[:, : 6 * WIDTH]
    all_lifted = lax.dynamic_slice_in_dim(everyone, 6 * WIDTH + place * height, height, 1)
    modulate_gradient = contract_rows(all_lifted, all_back)
    group_back = lax.dynamic_slice_in_dim(
        all_back, bucket * fsdp_count * slots, fsdp_count * slots, 0
    )
    slope_rows = times_transposed(group_back, modulate_weight)
    condition_slope = (
        to_group(slope_rows.reshape(fsdp_count, slots, height), fsdp_count, place)
        .transpose(1, 0, 2)
        .reshape(slots, WIDTH)
    )
    grad_condition = condition_slope * silu_slope(cond_float)
    return (
        output,
        grad_inputs,
        grad_condition,
        modulate_gradient,
        *attn_grad,
        *pair_grad,
        down_grad,
    )


def solution(mesh):
    spread = P(("bucket", "fsdp"), None)
    rows = P("fsdp", None)
    in_specs = (
        spread, spread, P(("bucket", "fsdp")), P(("bucket", "fsdp")), P(),
        rows, rows, rows, rows, rows, rows, spread,
    )
    out_specs = (spread, spread, spread, rows, rows, rows, rows, rows, rows)
    return jax.shard_map(
        on_device, mesh=mesh, in_specs=in_specs, out_specs=out_specs, check_vma=False
    )
```

time: 641 us -> 554 us (0.86)
  waiting for transfers between devices: 317 us -> 175 us
  Pallas kernels: 157 us -> 196 us
  starting transfers between devices: 73.7 us -> 104 us
  local copies, waits for them, and re-layouts: 36.5 us -> 27.6 us
  other arithmetic: 21.7 us -> 14.4 us
    reduce_scatter x3 -> x2, waiting for transfers between devices: 134 us -> 0.02 us  [the longest x1 0.02 us: on_device(): lax.psum_scatter(pair_parts, 'fsdp', scatter_dimension=0, tiled=False)]
    ppermute x27 -> x69, waiting for transfers between devices: 37.6 us -> 147 us  [swap(): return lax.ppermute(array, 'bucket', across(bit))]
    ppermute x18 -> x6, waiting for transfers between devices: 104 us -> 1.92 us  [the longest x3 1.37 us: on_device(): lax.ppermute(pick(attn_parts, (place + by) % count), 'fsdp', shifts(count...]
    ppermute x27 -> x69, starting transfers between devices: 31.3 us -> 77.7 us  [swap(): return lax.ppermute(array, 'bucket', across(bit))]
    pallas_call x5 -> x13, Pallas kernels: 103 us -> 142 us  [the longest x3 53 us: ffn_call(): pl.pallas_call(functools.partial(ffn_kernel, count, js, names), grid=(len...]
    ppermute x18 -> x6, starting transfers between devices: 30.5 us -> 17.2 us  [the longest x3 13.9 us: on_device(): lax.ppermute(pick(attn_parts, (place + by) % count), 'fsdp', shifts(count...]
    convert_element_type x7 -> x13, other arithmetic: 13.4 us -> 3.29 us  [the longest x12 3.1 us: add(): return (left.astype(f32) + right.astype(f32)).astype(bf16)]
    ppermute x9 -> x12, waiting for transfers between devices: 30.1 us -> 20.5 us  [to_group(): lax.ppermute(pick(rows, (place + by) % count), 'fsdp', shifts(count, by))]
  transfers between devices with their start and end apart: 61 -> 92, of which waited for: 21 -> 33; matrix products, arithmetic and copies ran while one was open for 9% -> 7% of each run, Pallas kernels for 16% -> 31%
where the time goes in v4:
time: 554 us; the launch traced here: 545 us
  Pallas kernels  196 us (35%)
  waiting for transfers between devices  175 us (32%)
  starting transfers between devices  104 us (19%)
  local copies, waits for them, and re-layouts  27.6 us (5%)
  between operations  16.6 us (3%)
  other arithmetic  14.4 us (3%)
  matrix products  11.2 us (2%)
    ppermute x69, waiting for transfers between devices, swap(): return lax.ppermute(array, 'bucket', across(bit))  147 us
    ppermute x69, starting transfers between devices, swap(): return lax.ppermute(array, 'bucket', across(bit))  77.7 us
    pallas_call x3, Pallas kernels, ffn_call(): pl.pallas_call(functools.partial(ffn_kernel, count, js, names), grid=(len...  53 us
    pallas_call x4, Pallas kernels, by_column(): pl.pallas_call(call, out_shape=shapes, grid_spec=pltpu.PrefetchScalarGrid...  39.6 us
    pallas_call x1, Pallas kernels, attend_back_call(): pl.pallas_call(attend_back_kernel, grid=(tokens // BLOCK,), out_shape=str...  28.9 us
    pallas_call x1, Pallas kernels, first_call(): pl.pallas_call(functools.partial(first_kernel, count), out_shape=(struct(...  22.2 us
    ppermute x12, waiting for transfers between devices, to_group(): lax.ppermute(pick(rows, (place + by) % count), 'fsdp', shifts(count, by))  20.5 us
    ppermute x3, starting transfers between devices, on_device(): lax.ppermute(pick(attn_parts, (place + by) % count), 'fsdp', shifts(count...  13.9 us
  transfers between devices with their start and end apart: 92, of which 33 were waited for; matrix products, arithmetic and copies ran while one was open for 7% of the time, Pallas kernels for 31%

profile of v4, /device:TPU:25, one launch (start us, length us, event | category | flops | bytes accessed | tf_op | source)
XLA Modules:
  0.0 545.0 jit_solution(625060084013777849)
XLA Ops:
  32.3 10.3 %collective-permute-done.4 = f32[8,2304]{1,0:T(8,128)S(1)} collective-permute-done((f32[8,2304]{1,0:T(8,128)S(1)}, f32[8,2304]{1,0:T(8,128)S(1)}, u32[]{:S(2)}, u32[]{:S(2)}) %collective-permute-start.4) | collective-permute-done | bytes 73760 | tf_op jit(solution)/shard_map/ppermute | solution.py:936
  79.0 7.3 %collective-permute-done.9.refs_4_ = bf16[3,64,1152]{2,1,0:T(8,128)(2,1)S(1)} collective-permute-done((bf16[3,64,1152]{2,1,0:T(8,128)(2,1)S(1)}, bf16[3,64,1152]{2,1,0:T(8,128)(2,1)S(1)}, u32[]{:S(2)}, u32[]{:S(2)}) %collective-permute-start.9) | collective-permute-done | bytes 442400 | tf_op jit(solution)/shard_map/ppermute | solution.py:822
  93.8 22.2 %shard_map.187 = (bf16[1152,512]{1,0:T(8,128)(2,1)}, bf16[512,1152]{1,0:T(8,128)(2,1)}, bf16[512,1152]{1,0:T(8,128)(2,1)}, bf16[512,1152]{1,0:T(8,128)(2,1)}, bf16[4,1152,1152]{2,1,0:T(8,128)(2,1)}) custom-call(s32[7]{0:T(128)} %stack.123.where_ref.refs_0_, bf16[512,1152]{1,0:T(8,128)(2,1)} %x_ref.5, f32[8,2304]{1,0:T(8,128)} %fusion.30.mod_ref, ...), custom_call_target="tpu_custom_call" | custom-call | flops 20000000000 | bytes 1000 | tf_op jit(solution)/shard_map/pallas_call | solution.py:566
  119.7 12.5 %shard_map.188 = (bf16[1152,512]{1,0:T(8,128)(2,1)}, f32[512,1152]{1,0:T(8,128)}, f32[512,1152]{1,0:T(8,128)}, bf16[512,1152]{1,0:T(8,128)(2,1)}) custom-call(bf16[512,1152]{1,0:T(8,128)(2,1)} %get-tuple-element.93.query_ref, bf16[512,1152]{1,0:T(8,128)(2,1)} %get-tuple-element.94.keys_ref, bf16[512,1152]{1,0:T(8,128)(2,1)} %get-tuple-element.95.values_ref, ...), custom_call_target="tpu_custom_call" | custom-call | flops 12000000000 | bytes 1000 | tf_op jit(solution)/shard_map/pallas_call | solution.py:586
  156.5 12.5 %shard_map.189 = (bf16[1,768,512]{2,1,0:T(8,128)(2,1)}, bf16[1,2,512,768]{3,2,1,0:T(8,128)(2,1)}, bf16[1152,512]{1,0:T(8,128)(2,1)}, bf16[512,1152]{1,0:T(8,128)...) custom-call(s32[7]{0:T(128)} %stack.123.where_ref.refs_0_, bf16[512,1152]{1,0:T(8,128)(2,1)} %get-tuple-element.100.refs_1_, ...), custom_call_target="tpu_custom_call" | custom-call | flops 12000000000 | bytes 1000 | tf_op jit(solution)/shard_map/pallas_call | solution.py:675
  168.9 13.9 %collective-permute-done.31.refs_8_ = bf16[3,288,768]{2,1,0:T(8,128)(2,1)S(1)} collective-permute-done((bf16[3,288,768]{2,1,0:T(8,128)(2,1)S(1)}, bf16[3,288,768]{2,1,0:T(8,128)(2,1)S(1)}, u32[]{:S(2)}, u32[]{:S(2)}) %collective-permute-start.31) | collective-permute-done | bytes 1327136 | tf_op jit(solution)/shard_map/ppermute | solution.py:822
  191.4 23.6 %shard_map.190 = (bf16[2,768,512]{2,1,0:T(8,128)(2,1)}, bf16[2,2,512,768]{3,2,1,0:T(8,128)(2,1)}, f32[512,1152]{1,0:T(8,128)}, f32[512,1152]{1,0:T(8,128)}) custom-call(s32[7]{0:T(128)} %stack.123.where_ref.refs_0_, bf16[512,1152]{1,0:T(8,128)(2,1)} %get-tuple-element.100.refs_1_, bf16[512,1152]{1,0:T(8,128)(2,1)} %get-tuple-element.109.refs_2_.refs_5_.refs_3_, ...), custom_call_target="tpu_custom_call" | custom-call | flops 24000000000 | bytes 1000 | tf_op jit(solution)/shard_map/pallas_call | solution.py:675
  219.1 16.9 %shard_map.191 = (bf16[1,768,512]{2,1,0:T(8,128)(2,1)}, bf16[1,2,512,768]{3,2,1,0:T(8,128)(2,1)}, bf16[512,1152]{1,0:T(8,128)(2,1)}, f32[512,1152]{1,0:T(8,128)}...) custom-call(s32[7]{0:T(128)} %stack.123.where_ref.refs_0_, bf16[512,1152]{1,0:T(8,128)(2,1)} %get-tuple-element.100.refs_1_, ...), custom_call_target="tpu_custom_call" | custom-call | flops 12000000000 | bytes 1000 | tf_op jit(solution)/shard_map/pallas_call | solution.py:675
  242.6 9.1 %shard_map.193 = bf16[4,4,288,768]{3,2,1,0:T(8,128)(2,1)} custom-call(s32[7]{0:T(128)} %stack.123.where_ref.refs_0_, bf16[1152,512]{1,0:T(8,128)(2,1)} %get-tuple-element.131.turned_ref, bf16[1,2,512,768]{3,2,1,0:T(8,128)(2,1)} %get-tuple-element.127.own_ref, bf16[2,2,512,768]{3,2,1,0:T(8,128)(2,1)} %get-tuple-element.128.near_ref, ...), custom_call_target="tpu_custom_call" | custom-call | flops 10000000000 | bytes 1000 | tf_op jit(solution)/shard_map/pallas_call | solution.py:695
  253.6 7.3 %shard_map.194 = bf16[4,4,96,1152]{3,2,1,0:T(8,128)(2,1)} custom-call(s32[7]{0:T(128)} %stack.123.where_ref.refs_0_, bf16[1,768,512]{2,1,0:T(8,128)(2,1)} %get-tuple-element.123.refs_0_, bf16[2,768,512]{2,1,0:T(8,128)(2,1)} %get-tuple-element.124.refs_1_, bf16[1,768,512]{2,1,0:T(8,128)(2,1)} %get-tuple-element.125.refs_2_, ...), custom_call_target="tpu_custom_call" | custom-call | flops 7000000000 | bytes 1000 | tf_op jit(solution)/shard_map/pallas_call | solution.py:744
  263.5 11.0 %shard_map.195 = (bf16[2,4,144,768]{3,2,1,0:T(8,128)(2,1)}, bf16[2,4,144,768]{3,2,1,0:T(8,128)(2,1)}, bf16[2,4,144,768]{3,2,1,0:T(8,128)(2,1)}, bf16[2,4,144,768]{3,2,1,0:T(8,128)(2,1)}) custom-call(s32[7]{0:T(128)} %stack.123.where_ref.refs_0_, bf16[1152,512]{1,0:T(8,128)(2,1)} %get-tuple-element.131.turned_ref, ...), custom_call_target="tpu_custom_call" | custom-call | flops 10000000000 | bytes 1000 | tf_op jit(solution)/shard_map/pallas_call | solution.py:695
  276.0 28.9 %shard_map.196.joint_back_ref = bf16[512,3456]{1,0:T(8,128)(2,1)} custom-call(bf16[512,1152]{1,0:T(8,128)(2,1)} %get-tuple-element.93.query_ref, bf16[512,1152]{1,0:T(8,128)(2,1)} %get-tuple-element.94.keys_ref, bf16[512,1152]{1,0:T(8,128)(2,1)} %get-tuple-element.95.values_ref, bf16[512,1152]{1,0:T(8,128)(2,1)} %get-tuple-element.144.branch_back_ref, ...), custom_call_target="tpu_custom_call" | custom-call | flops 28999999488 | bytes 1000 | tf_op jit(solution)/shard_map/pallas_call | solution.py:768
  304.9 10.0 %collective-permute-done.42 = bf16[2,4,144,768]{3,2,1,0:T(8,128)(2,1)S(1)} collective-permute-done((bf16[2,4,144,768]{3,2,1,0:T(8,128)(2,1)}, bf16[2,4,144,768]{3,2,1,0:T(8,128)(2,1)S(1)}, u32[]{:S(2)}, u32[]{:S(2)}) %collective-permute-start.42) | collective-permute-done | bytes 1769504 | tf_op jit(solution)/shard_map/ppermute | solution.py:822
  317.3 18.2 %collective-permute-done.44 = bf16[4,144,768]{2,1,0:T(8,128)(2,1)S(1)} collective-permute-done((bf16[4,144,768]{2,1,0:T(8,128)(2,1)S(1)}, bf16[4,144,768]{2,1,0:T(8,128)(2,1)S(1)}, u32[]{:S(2)}, u32[]{:S(2)}) %collective-permute-start.44) | collective-permute-done | bytes 884768 | tf_op jit(solution)/shard_map/ppermute | solution.py:822
  337.0 9.1 %shard_map.197 = bf16[4,4,144,1152]{3,2,1,0:T(8,128)(2,1)} custom-call(s32[7]{0:T(128)} %stack.123.where_ref.refs_0_, bf16[1152,512]{1,0:T(8,128)(2,1)} %get-tuple-element.139.first_ref, bf16[1152,512]{1,0:T(8,128)(2,1)} %get-tuple-element.140.attended_ref, bf16[512,3456]{1,0:T(8,128)(2,1)} %shard_map.196.joint_back_ref, ...), custom_call_target="tpu_custom_call" | custom-call | flops 10000000000 | bytes 1000 | tf_op jit(solution)/shard_map/pallas_call | solution.py:695
  350.8 12.7 %shard_map.198 = (f32[512,1152]{1,0:T(8,128)}, f32[8,2304]{1,0:T(8,128)}) custom-call(bf16[512,3456]{1,0:T(8,128)(2,1)} %shard_map.196.joint_back_ref, bf16[512,1152]{1,0:T(8,128)(2,1)} %x_ref.5, f32[512,1152]{1,0:T(8,128)} %get-tuple-element.146.middle_back_ref, f32[8,2304]{1,0:T(8,128)} %fusion.30.mod_ref, bf16[4,1152,1152]{2,1,0:T(8,128)(2,1)} %get-tuple-element.99.weight), custom_call_target="tpu_custom_call" | custom-call | flops 12999999488 | bytes 1000 | tf_op jit(solution)/shard_map/pallas_call | solution.py:791
  372.9 10.3 %shard_map.199 = (bf16[2,4,80,1152]{3,2,1,0:T(8,128)(2,1)}, bf16[2,4,80,1152]{3,2,1,0:T(8,128)(2,1)}, bf16[2,4,64,1152]{3,2,1,0:T(8,128)(2,1)}, bf16[2,4,64,1152]{3,2,1,0:T(8,128)(2,1)}) custom-call(s32[7]{0:T(128)} %stack.123.where_ref.refs_0_, bf16[1152,512]{1,0:T(8,128)(2,1)} %get-tuple-element.139.first_ref, ...), custom_call_target="tpu_custom_call" | custom-call | flops 10000000000 | bytes 1000 | tf_op jit(solution)/shard_map/pallas_call | solution.py:695
  386.2 27.0 %collective-permute-done.55 = bf16[48,1152]{1,0:T(8,128)(2,1)S(1)} collective-permute-done((bf16[48,1152]{1,0:T(8,128)(2,1)S(1)}, bf16[48,1152]{1,0:T(8,128)(2,1)S(1)}, u32[]{:S(2)}, u32[]{:S(2)}) %collective-permute-start.55) | collective-permute-done | bytes 110624 | tf_op jit(solution)/shard_map/ppermute | solution.py:822
  413.2 10.0 %collective-permute-done.56 = bf16[48,1152]{1,0:T(8,128)(2,1)S(1)} collective-permute-done((bf16[48,1152]{1,0:T(8,128)(2,1)S(1)}, bf16[48,1152]{1,0:T(8,128)(2,1)S(1)}, u32[]{:S(2)}, u32[]{:S(2)}) %collective-permute-start.56) | collective-permute-done | bytes 110624 | tf_op jit(solution)/shard_map/ppermute | solution.py:822
  426.4 9.7 %collective-permute-done.51 = bf16[4,64,1152]{2,1,0:T(8,128)(2,1)S(1)} collective-permute-done((bf16[4,64,1152]{2,1,0:T(8,128)(2,1)S(1)}, bf16[4,64,1152]{2,1,0:T(8,128)(2,1)S(1)}, u32[]{:S(2)}, u32[]{:S(2)}) %collective-permute-start.51) | collective-permute-done | bytes 589856 | tf_op jit(solution)/shard_map/ppermute | solution.py:822
  436.3 8.2 %collective-permute-done.49 = bf16[4,80,1152]{2,1,0:T(8,128)(2,1)S(1)} collective-permute-done((bf16[4,80,1152]{2,1,0:T(8,128)(2,1)S(1)}, bf16[4,80,1152]{2,1,0:T(8,128)(2,1)S(1)}, u32[]{:S(2)}, u32[]{:S(2)}) %collective-permute-start.49) | collective-permute-done | bytes 737312 | tf_op jit(solution)/shard_map/ppermute | solution.py:822
  447.8 6.8 %collective-permute-start.52 = (bf16[144,1152]{1,0:T(8,128)(2,1)S(1)}, bf16[144,1152]{1,0:T(8,128)(2,1)S(1)}, u32[]{:S(2)}, u32[]{:S(2)}) collective-permute-start(bf16[144,1152]{1,0:T(8,128)(2,1)S(1)} %get-tuple-element.193), channel_id=1, source_target_pairs={{0,1},{1,2},{2,3},{3,0},{4,5},{5,6},{6,7},{7,4},{8,9},{9,10},{10,1... | collective-permute-start | bytes 995336 | tf_op jit(solution)/shard_map/ppermute | solution.py:1126
  468.2 13.8 %collective-permute-start.64 = (bf16[48,1152]{1,0:T(8,128)(2,1)S(1)}, bf16[48,1152]{1,0:T(8,128)(2,1)}, u32[]{:S(2)}, u32[]{:S(2)}) collective-permute-start(bf16[48,1152]{1,0:T(8,128)(2,1)S(1)} %slice.144), channel_id=1, source_target_pairs={{0,8},{4,12},{8,0},{12,4},{16,24},{20,28},{24,16},{28,20},{1,9},{5... | collective-permute-start | bytes 331784 | tf_op jit(solution)/shard_map/ppermute | solution.py:822
  510.3 6.7 %collective-permute-done.68.refs_1_ = bf16[144,1152]{1,0:T(8,128)(2,1)S(1)} collective-permute-done((bf16[144,1152]{1,0:T(8,128)(2,1)S(1)}, bf16[144,1152]{1,0:T(8,128)(2,1)S(1)}, u32[]{:S(2)}, u32[]{:S(2)}) %collective-permute-start.68) | collective-permute-done | bytes 331808 | tf_op jit(solution)/shard_map/ppermute | solution.py:822
  (399 shorter events, 210.3 us)
Async XLA Ops:
  7.2 41.3 %all-gather.8.cloned.1.call-start = ((), (), s32[]{:S(2)}) async-start(), calls=%async_computation.5 | async-start | bytes 1658880 | tf_op jit(solution)/shard_map/all_gather | solution.py:841
  9.2 123.1 %all-gather.10.cloned.1.call-start = ((), (), s32[]{:S(2)}) async-start(), calls=%async_computation.6 | async-start | bytes 2211840 | tf_op jit(solution)/shard_map/all_gather | solution.py:841
  50.0 23.3 %collective-permute-start.6 = (bf16[3,144,1152]{2,1,0:T(8,128)(2,1)S(1)}, bf16[3,144,1152]{2,1,0:T(8,128)(2,1)S(1)}, u32[]{:S(2)}, u32[]{:S(2)}) collective-permute-start(bf16[3,144,1152]{2,1,0:T(8,128)(2,1)S(1)} %pad_maximum_fusion.3.refs_0_), channel_id=1, source_target_pairs={{0,8},{4,12},{8,0},{12,4},{16,24},{20,28},{24,16},{28,20},{1,9},{5... | collective-permute-start | bytes 2985992 | tf_op jit(solution)/shard_map/ppermute | solution.py:822
  51.5 23.4 %collective-permute-start.7 = (bf16[3,144,1152]{2,1,0:T(8,128)(2,1)S(1)}, bf16[3,144,1152]{2,1,0:T(8,128)(2,1)}, u32[]{:S(2)}, u32[]{:S(2)}) collective-permute-start(bf16[3,144,1152]{2,1,0:T(8,128)(2,1)S(1)} %pad_maximum_fusion.3.refs_0_), channel_id=1, source_target_pairs={{0,16},{4,20},{8,24},{12,28},{16,0},{20,4},{24,8},{28,12},{1,17},{... | collective-permute-start | bytes 2985992 | tf_op jit(solution)/shard_map/ppermute | solution.py:822
  57.2 292.3 %reduce-scatter.3.cloned.1.call-start = ((), (), s32[]{:S(2)}) async-start(), calls=%async_computation.2 | async-start | bytes 4423680 | tf_op jit(solution)/shard_map/reduce_scatter | solution.py:1094
  58.7 30.0 %collective-permute-start.10 = (bf16[3,144,1152]{2,1,0:T(8,128)(2,1)S(1)}, bf16[3,144,1152]{2,1,0:T(8,128)(2,1)S(1)}, u32[]{:S(2)}, u32[]{:S(2)}) collective-permute-start(bf16[3,144,1152]{2,1,0:T(8,128)(2,1)S(1)} %pad_maximum_fusion.3.refs_0_), channel_id=1, source_target_pairs={{0,4},{4,0},{8,12},{12,8},{16,20},{20,16},{24,28},{28,24},{1,5},{5... | collective-permute-start | bytes 2985992 | tf_op jit(solution)/shard_map/ppermute | solution.py:822
  88.7 27.3 %collective-permute-start.18 = (bf16[96,1152]{1,0:T(8,128)(2,1)S(1)}, bf16[96,1152]{1,0:T(8,128)(2,1)S(1)}, u32[]{:S(2)}, u32[]{:S(2)}) collective-permute-start(bf16[96,1152]{1,0:T(8,128)(2,1)S(1)} %constant_dynamic-slice_fusion.9), channel_id=1, source_target_pairs={{0,1},{1,2},{2,3},{3,0},{4,5},{5,6},{6,7},{7,4},{8,9},{9,10},{10,1... | collective-permute-start | bytes 663560 | tf_op jit(solution)/shard_map/ppermute | solution.py:835
  90.5 26.1 %collective-permute-start.19 = (bf16[96,1152]{1,0:T(8,128)(2,1)S(1)}, bf16[96,1152]{1,0:T(8,128)(2,1)S(1)}, u32[]{:S(2)}, u32[]{:S(2)}) collective-permute-start(bf16[96,1152]{1,0:T(8,128)(2,1)S(1)} %constant_dynamic-slice_fusion.9), channel_id=1, source_target_pairs={{0,2},{1,3},{2,0},{3,1},{4,6},{5,7},{6,4},{7,5},{8,10},{9,11},{10,... | collective-permute-start | bytes 663560 | tf_op jit(solution)/shard_map/ppermute | solution.py:835
  90.6 26.0 %collective-permute-start.20 = (bf16[96,1152]{1,0:T(8,128)(2,1)S(1)}, bf16[96,1152]{1,0:T(8,128)(2,1)S(1)}, u32[]{:S(2)}, u32[]{:S(2)}) collective-permute-start(bf16[96,1152]{1,0:T(8,128)(2,1)S(1)} %constant_dynamic-slice_fusion.9), channel_id=1, source_target_pairs={{0,3},{1,0},{2,1},{3,2},{4,7},{5,4},{6,5},{7,6},{8,11},{9,8},{10,9... | collective-permute-start | bytes 663560 | tf_op jit(solution)/shard_map/ppermute | solution.py:835
  152.2 30.7 %collective-permute-start.31 = (bf16[3,288,768]{2,1,0:T(8,128)(2,1)S(1)}, bf16[3,288,768]{2,1,0:T(8,128)(2,1)S(1)}, u32[]{:S(2)}, u32[]{:S(2)}) collective-permute-start(bf16[3,288,768]{2,1,0:T(8,128)(2,1)S(1)} %pad_maximum_fusion.2.refs_8_), channel_id=1, source_target_pairs={{0,8},{4,12},{8,0},{12,4},{16,24},{20,28},{24,16},{28,20},{1,9},{5... | collective-permute-start | bytes 3981320 | tf_op jit(solution)/shard_map/ppermute | solution.py:822
  153.6 30.7 %collective-permute-start.32 = (bf16[3,288,768]{2,1,0:T(8,128)(2,1)S(1)}, bf16[3,288,768]{2,1,0:T(8,128)(2,1)}, u32[]{:S(2)}, u32[]{:S(2)}) collective-permute-start(bf16[3,288,768]{2,1,0:T(8,128)(2,1)S(1)} %pad_maximum_fusion.2.refs_8_), channel_id=1, source_target_pairs={{0,16},{4,20},{8,24},{12,28},{16,0},{20,4},{24,8},{28,12},{1,17},{... | collective-permute-start | bytes 3981320 | tf_op jit(solution)/shard_map/ppermute | solution.py:822
  186.5 28.6 %collective-permute-start.35 = (bf16[3,144,768]{2,1,0:T(8,128)(2,1)S(1)}, bf16[3,144,768]{2,1,0:T(8,128)(2,1)S(1)}, u32[]{:S(2)}, u32[]{:S(2)}) collective-permute-start(bf16[3,144,768]{2,1,0:T(8,128)(2,1)S(1)} %slice.121), channel_id=1, source_target_pairs={{0,16},{4,20},{8,24},{12,28},{16,0},{20,4},{24,8},{28,12},{1,17},{... | collective-permute-start | bytes 1990664 | tf_op jit(solution)/shard_map/ppermute | solution.py:822
  187.4 27.7 %collective-permute-start.36 = (bf16[3,144,768]{2,1,0:T(8,128)(2,1)S(1)}, bf16[3,144,768]{2,1,0:T(8,128)(2,1)S(1)}, u32[]{:S(2)}, u32[]{:S(2)}) collective-permute-start(bf16[3,144,768]{2,1,0:T(8,128)(2,1)S(1)} %slice.122), channel_id=1, source_target_pairs={{0,8},{4,12},{8,0},{12,4},{16,24},{20,28},{24,16},{28,20},{1,9},{5... | collective-permute-start | bytes 1990664 | tf_op jit(solution)/shard_map/ppermute | solution.py:822
  260.9 183.8 %reduce-scatter.5.cloned.1.call-start = ((), (), s32[]{:S(2)}) async-start(), calls=%async_computation.4 | async-start | bytes 2211840 | tf_op jit(solution)/shard_map/reduce_scatter | solution.py:1108
  274.4 40.4 %collective-permute-start.42 = (bf16[2,4,144,768]{3,2,1,0:T(8,128)(2,1)}, bf16[2,4,144,768]{3,2,1,0:T(8,128)(2,1)S(1)}, u32[]{:S(2)}, u32[]{:S(2)}) collective-permute-start(bf16[2,4,144,768]{3,2,1,0:T(8,128)(2,1)} %get-tuple-element.135), channel_id=1, source_target_pairs={{0,16},{4,20},{8,24},{12,28},{16,0},{20,4},{24,8},{28,12},{1,17},{... | collective-permute-start | bytes 5308424 | tf_op jit(solution)/shard_map/ppermute | solution.py:822
  275.1 41.3 %collective-permute-start.41 = (bf16[2,4,144,768]{3,2,1,0:T(8,128)(2,1)}, bf16[2,4,144,768]{3,2,1,0:T(8,128)(2,1)S(1)}, u32[]{:S(2)}, u32[]{:S(2)}) collective-permute-start(bf16[2,4,144,768]{3,2,1,0:T(8,128)(2,1)} %get-tuple-element.133), channel_id=1, source_target_pairs={{0,8},{4,12},{8,0},{12,4},{16,24},{20,28},{24,16},{28,20},{1,9},{5... | collective-permute-start | bytes 5308424 | tf_op jit(solution)/shard_map/ppermute | solution.py:822
  346.1 26.8 %collective-permute-start.45 = (bf16[4,4,144,1152]{3,2,1,0:T(8,128)(2,1)}, bf16[4,4,144,1152]{3,2,1,0:T(8,128)(2,1)}, u32[]{:S(2)}, u32[]{:S(2)}) collective-permute-start(bf16[4,4,144,1152]{3,2,1,0:T(8,128)(2,1)} %shard_map.197), channel_id=1, source_target_pairs={{0,4},{4,0},{8,12},{12,8},{16,20},{20,16},{24,28},{28,24},{1,5},{5... | collective-permute-start | bytes 15925256 | tf_op jit(solution)/shard_map/ppermute | solution.py:822
  349.5 142.6 %all-gather.6.cloned.1.call-start = ((), (), s32[]{:S(2)}) async-start(), calls=%async_computation.3 | async-start | bytes 4257792 | tf_op jit(solution)/shard_map/all_gather | solution.py:1166
  383.2 40.1 %collective-permute-start.50 = (bf16[2,4,64,1152]{3,2,1,0:T(8,128)(2,1)}, bf16[2,4,64,1152]{3,2,1,0:T(8,128)(2,1)S(1)}, u32[]{:S(2)}, u32[]{:S(2)}) collective-permute-start(bf16[2,4,64,1152]{3,2,1,0:T(8,128)(2,1)} %get-tuple-element.156), channel_id=1, source_target_pairs={{0,16},{4,20},{8,24},{12,28},{16,0},{20,4},{24,8},{28,12},{1,17},{... | collective-permute-start | bytes 3538952 | tf_op jit(solution)/shard_map/ppermute | solution.py:822
  384.2 29.0 %collective-permute-start.55 = (bf16[48,1152]{1,0:T(8,128)(2,1)S(1)}, bf16[48,1152]{1,0:T(8,128)(2,1)S(1)}, u32[]{:S(2)}, u32[]{:S(2)}) collective-permute-start(bf16[48,1152]{1,0:T(8,128)(2,1)S(1)} %get-tuple-element.159), channel_id=1, source_target_pairs={{0,16},{4,20},{8,24},{12,28},{16,0},{20,4},{24,8},{28,12},{1,17},{... | collective-permute-start | bytes 331784 | tf_op jit(solution)/shard_map/ppermute | solution.py:822
  384.8 41.3 %collective-permute-start.48 = (bf16[2,4,80,1152]{3,2,1,0:T(8,128)(2,1)}, bf16[2,4,80,1152]{3,2,1,0:T(8,128)(2,1)S(1)}, u32[]{:S(2)}, u32[]{:S(2)}) collective-permute-start(bf16[2,4,80,1152]{3,2,1,0:T(8,128)(2,1)} %get-tuple-element.154), channel_id=1, source_target_pairs={{0,8},{4,12},{8,0},{12,4},{16,24},{20,28},{24,16},{28,20},{1,9},{5... | collective-permute-start | bytes 4423688 | tf_op jit(solution)/shard_map/ppermute | solution.py:822
  385.5 37.7 %collective-permute-start.56 = (bf16[48,1152]{1,0:T(8,128)(2,1)S(1)}, bf16[48,1152]{1,0:T(8,128)(2,1)S(1)}, u32[]{:S(2)}, u32[]{:S(2)}) collective-permute-start(bf16[48,1152]{1,0:T(8,128)(2,1)S(1)} %get-tuple-element.161), channel_id=1, source_target_pairs={{0,8},{4,12},{8,0},{12,4},{16,24},{20,28},{24,16},{28,20},{1,9},{5... | collective-permute-start | bytes 331784 | tf_op jit(solution)/shard_map/ppermute | solution.py:822
  462.5 28.8 %collective-permute-start.61 = (bf16[144,768]{1,0:T(8,128)(2,1)S(1)}, bf16[144,768]{1,0:T(8,128)(2,1)}, u32[]{:S(2)}, u32[]{:S(2)}) collective-permute-start(bf16[144,768]{1,0:T(8,128)(2,1)S(1)} %slice.141), channel_id=1, source_target_pairs={{0,16},{4,20},{8,24},{12,28},{16,0},{20,4},{24,8},{28,12},{1,17},{... | collective-permute-start | bytes 663560 | tf_op jit(solution)/shard_map/ppermute | solution.py:822
  466.6 24.8 %collective-permute-start.62 = (bf16[144,768]{1,0:T(8,128)(2,1)S(1)}, bf16[144,768]{1,0:T(8,128)(2,1)}, u32[]{:S(2)}, u32[]{:S(2)}) collective-permute-start(bf16[144,768]{1,0:T(8,128)(2,1)S(1)} %slice.142), channel_id=1, source_target_pairs={{0,8},{4,12},{8,0},{12,4},{16,24},{20,28},{24,16},{28,20},{1,9},{5... | collective-permute-start | bytes 663560 | tf_op jit(solution)/shard_map/ppermute | solution.py:822
  (131 other events, 1314.6 us)
Sparse Core Ops, SparseCore 0:
  10.2 38.2 all-gather.7
  57.3 44.6 all-gather.9
  261.1 65.1 reduce-scatter.2
  349.6 36.4 reduce-scatter.4
  389.3 71.1 all-gather.5

commit v5 on v4

--- a/solution.py
+++ b/solution.py
@@ -86,7 +86,7 @@
 
 
 def rotate(values, cos, sin):
-    lane = lax.broadcasted_iota(jnp.int32, values.shape, 1)
+    lane = lax.broadcasted_iota(jnp.int32, (1, WIDTH), 1)
     leading = lane % (2 * QUARTER) < QUARTER
     partner = jnp.where(
         leading,
@@ -104,19 +104,28 @@
     return -(-rows // 32) * 16
 
 
+def placed(refs, rows):
+    first = first_part(rows)
+    each = len(refs) // HALVES
+    for other in range(HALVES):
+        here = refs[each * other : each * other + each]
+        for j in range(3):
+            yield j, other, 0, rows, here[j]
+        if each == COLUMNS:
+            yield 3, other, 0, rows, here[3]
+        else:
+            yield 3, other, 0, first, here[3]
+            yield 3, other, first, rows - first, here[4]
+
+
 def piece_copies(where, count, sources, target, rows, sem):
     place, column, side = where
-    first = first_part(rows)
     copies = []
-    for other in range(HALVES):
-        here = sources[5 * other : 5 * other + 5]
+    for j, other, start, size, ref in placed(sources, rows):
         for by in range(1, count):
             owner = (place + (count - by)) % count
-            for j in range(COLUMNS):
-                spans = [(here[j], 0, rows)] if j < 3 else [(here[3], 0, first), (here[4], first, rows - first)]
-                for ref, start, size in spans:
-                    to = target(column ^ j, side ^ other, owner, start, size)
-                    copies.append(pltpu.make_async_copy(ref.at[by - 1], to, sem(column ^ j, side ^ other, owner)))
+            to = target(column ^ j, side ^ other, owner, start, size)
+            copies.append(pltpu.make_async_copy(ref.at[by - 1], to, sem(column ^ j, side ^ other, owner)))
     return copies
 
 
@@ -127,8 +136,8 @@
 def first_kernel(
     count, where_ref, x_ref, mod_ref, cos_ref, sin_ref, joint_ref, project_ref, *refs
 ):
-    sources = refs[:10]
-    turned_ref, query_ref, keys_ref, values_ref, weight_ref, weight, first_ref, total, sems = refs[10:]
+    sources, refs = refs[:-9], refs[-9:]
+    turned_ref, query_ref, keys_ref, values_ref, weight_ref, weight, first_ref, total, sems = refs
     where = where_ref[0], where_ref[1], where_ref[2]
     rows_in = joint_ref.shape[0]
     half = rows_in // HALVES
@@ -150,8 +159,14 @@
             normed * (1.0 + mod_ref[i : i + 1, part(1)]) + mod_ref[i : i + 1, part(0)]
         ).astype(bf16)
     turned_ref[...] = first_ref[...].T
+    writes = [
+        pltpu.make_async_copy(weight.at[c], weight_ref.at[c], sems.at[c]) for c in range(COLUMNS)
+    ]
+    wait_for(weight.at[3], sems.at[3])
+    writes[3].start()
     for c, out in enumerate((query_ref, keys_ref, values_ref)):
         wait_for(weight.at[c], sems.at[c])
+        writes[c].start()
         if c == 2:
             out[...] = matmul(first_ref[...], weight[c]).astype(bf16)
         else:
@@ -162,10 +177,8 @@
                 rows = pl.ds(pl.multiple_of(i * CHUNK, CHUNK), CHUNK)
                 out[rows, :] = rotate(total[rows, :], cos_ref[rows, :], sin_ref[rows, :]).astype(bf16)
 
-    wait_for(weight.at[3], sems.at[3])
-    write = pltpu.make_async_copy(weight, weight_ref, sems.at[0])
-    write.start()
-    write.wait()
+    for write in writes:
+        write.wait()
 
 
 def window(head):
@@ -176,11 +189,11 @@
     return slice(start, stop), inside
 
 
-def soft_scores(query, keys, allowed):
-    scores = times_transposed(query, keys) * HEAD_DIM ** (-0.5)
+def soft_scores(left, right, allowed, axis):
+    scores = times_transposed(left, right) * HEAD_DIM ** (-0.5)
     scores = jnp.where(allowed, scores, masked_score)
-    exponent = jnp.exp(scores - jnp.max(scores, axis=-1, keepdims=True))
-    return exponent * (1.0 / jnp.sum(exponent, axis=-1, keepdims=True))
+    exponent = jnp.exp(scores - jnp.max(scores, axis=axis, keepdims=True))
+    return exponent * (1.0 / jnp.sum(exponent, axis=axis, keepdims=True))
 
 
 def attend_kernel(
@@ -191,7 +204,7 @@
     for head in range(HEADS):
         lanes, inside = window(head)
         query = jnp.where(inside, query_ref[:, lanes], jnp.zeros((), bf16))
-        probs = soft_scores(query, keys_ref[:, lanes], allowed).astype(bf16)
+        probs = soft_scores(query, keys_ref[:, lanes], allowed, 1).astype(bf16)
         mixed[:, lanes] = jnp.where(inside, matmul(probs, values_ref[:, lanes]), mixed[:, lanes])
     attended = mixed[...].astype(bf16)
     turned_ref[...] = attended.T
@@ -205,16 +218,6 @@
         second_ref[rows, :] = (
             normed * (1.0 + mod[i : i + 1, part(2)]) + mod[i : i + 1, part(1)]
         ).astype(bf16)
-
-
-def placed(refs, rows):
-    first = first_part(rows)
-    for other in range(HALVES):
-        here = refs[5 * other : 5 * other + 5]
-        for j in range(3):
-            yield j, other, 0, rows, here[j]
-        yield 3, other, 0, first, here[3]
-        yield 3, other, first, rows - first, here[4]
 
 
 def tile_copies(r, where, count, tile, pair, downs):
@@ -277,7 +280,7 @@
                 [r[f"pair{j}_{other}_{i}"] for i in range(1 if j < 3 else 2)]
                 for other in range(HALVES)
             ]
-            tile_copies(r, where, count, (t, j), pair, [r[f"down_{i}"] for i in range(10)])
+            tile_copies(r, where, count, (t, j), pair, [r[name] for name in names if name[:4] == "down" and name[5:].isdigit()])
         if first:
             r["turned"][...] = second[...].T
             for i in range(tokens // CHUNK):
@@ -433,7 +436,7 @@
 
 
 def place_pair_kernel(where_ref, *refs):
-    sources, outs = refs[:10], refs[10:]
+    sources, outs = refs[:-2], refs[-2:]
     rows, tile = sources[0].shape
     for way in range(HALVES):
 
@@ -444,17 +447,15 @@
                 outs[way ^ other][start : start + size, lanes] = ref[...].astype(f32)
 
 
-def place_down_kernel(where_ref, *refs):
-    sources, out = refs[:10], refs[10]
-    rows = sources[0].shape[0]
+def place_down_kernel(rows, offset, where_ref, *refs):
+    sources, out = refs[:-1], refs[-1]
     for j, other, start, size, ref in placed(sources, rows):
         piece = (where_ref[1] ^ j) * HALVES + (where_ref[2] ^ other)
-        out[take(piece * rows + start, size), :] = ref[...].astype(f32)
-
-
-def place_attn_kernel(where_ref, *refs):
-    sources, joint_ref, project_ref = refs[:10], refs[10], refs[11]
-    rows = sources[0].shape[0]
+        out[take(piece * rows + start, size), :] = ref[offset : offset + size, :].astype(f32)
+
+
+def place_attn_kernel(rows, where_ref, *refs):
+    sources, joint_ref, project_ref = refs[:-2], refs[-2], refs[-1]
     for column in range(COLUMNS):
 
         @pl.when(where_ref[1] == column)
@@ -462,9 +463,9 @@
             for j, other, start, size, ref in placed(sources, rows):
                 to = take((where_ref[2] ^ other) * rows + start, size)
                 if column ^ j == 3:
-                    project_ref[to, :] = ref[...].astype(f32)
+                    project_ref[to, :] = ref[:size, :].astype(f32)
                 else:
-                    joint_ref[to, part(column ^ j)] = ref[...].astype(f32)
+                    joint_ref[to, part(column ^ j)] = ref[:size, :].astype(f32)
 
 
 def attend_back_kernel(
@@ -479,19 +480,19 @@
         zero = jnp.zeros((), bf16)
         query = jnp.where(inside, query_ref[:, lanes], zero)
         back = jnp.where(inside, mixed_back[:, lanes], zero)
-        soft = soft_scores(query, keys_ref[:, lanes], allowed)
-        probs_back = times_transposed(back, values_ref[:, lanes])
+        soft = soft_scores(keys_ref[:, lanes], query, allowed, 0)
+        probs_back = times_transposed(values_ref[:, lanes], back)
         scores_back = (
-            soft * (probs_back - jnp.sum(soft * probs_back, axis=-1, keepdims=True))
+            soft * (probs_back - jnp.sum(soft * probs_back, axis=0, keepdims=True))
         ).astype(bf16)
         query_back[:, lanes] = jnp.where(
-            inside, matmul(scores_back, keys_ref[:, lanes]) * scaling, query_back[:, lanes]
+            inside, contract_rows(scores_back, keys_ref[:, lanes]) * scaling, query_back[:, lanes]
         )
         keys_back[:, lanes] = jnp.where(
-            inside, contract_rows(scores_back, query) * scaling, keys_back[:, lanes]
+            inside, matmul(scores_back, query) * scaling, keys_back[:, lanes]
         )
         values_back[:, lanes] = jnp.where(
-            inside, contract_rows(soft.astype(bf16), back), values_back[:, lanes]
+            inside, matmul(soft.astype(bf16), back), values_back[:, lanes]
         )
 
     @pl.loop(0, BLOCK // CHUNK)
@@ -598,7 +599,7 @@
         out_specs=(pl.BlockSpec((WIDTH, BLOCK), lambda b: (0, b)),) + (by_block(BLOCK, WIDTH),) * 3,
         scratch_shapes=[pltpu.VMEM((BLOCK, WIDTH), f32)],
         compiler_params=params(),
-        cost_estimate=cost(12),
+        cost_estimate=cost(2),
     )(
         query, keys, values, ids[:, None], ids[None, :], x,
         mod.reshape(tokens // BLOCK, BLOCK // CHUNK, 4 * WIDTH), weight,
@@ -680,7 +681,7 @@
         out_specs=tuple(spec for _, _, spec in outputs),
         scratch_shapes=[shape for _, shape in scratch],
         compiler_params=params(),
-        cost_estimate=cost(12 * len(js)),
+        cost_estimate=cost(2 if first else 12 * len(js)),
     )(*[array for _, array, _ in inputs])
     return {name: array for (name, _, _), array in zip(outputs, found, strict=True)}
 
@@ -699,7 +700,7 @@
             num_scalar_prefetch=1, grid=(COLUMNS,), in_specs=in_specs, out_specs=specs
         ),
         compiler_params=params(),
-        cost_estimate=cost(10),
+        cost_estimate=cost(3),
     )(where, *arrays)
     return found[0] if other is None else found
 
@@ -747,7 +748,7 @@
         in_specs=[SMEM] + [VMEM] * len(arrays),
         out_specs=VMEM,
         compiler_params=params(),
-        cost_estimate=cost(7),
+        cost_estimate=cost(3),
     )(where, *arrays)
 
 
@@ -780,7 +781,7 @@
             pltpu.VMEM((BLOCK, WIDTH), f32),
         ],
         compiler_params=params(),
-        cost_estimate=cost(29),
+        cost_estimate=cost(8),
     )(query, keys, values, branch_back, ids[:, None], ids[None, :], cos, sin, weight)
 
 
@@ -802,7 +803,7 @@
         out_specs=(full, whole(chunks, 2 * WIDTH)),
         scratch_shapes=[pltpu.VMEM((tokens, WIDTH), f32)],
         compiler_params=params(),
-        cost_estimate=cost(13),
+        cost_estimate=cost(2),
     )(joint_back, x, middle_back, mod, weight)
 
 
@@ -835,10 +836,10 @@
     return [lax.ppermute(piece, "fsdp", shifts(count, by)) for by in range(1, count)]
 
 
-def gather_z(piece):
+def gather_z(piece, *others):
     count = lax.axis_size("fsdp")
     place = lax.axis_index("fsdp")
-    full = lax.all_gather(piece, "fsdp", axis=0, tiled=False)
+    full = after(lax.all_gather(piece, "fsdp", axis=0, tiled=False), *others)
     return jnp.stack([pick(full, (place + count - by) % count) for by in range(1, count)])
 
 
@@ -852,9 +853,8 @@
     return here + tuple(None if array is None else swap(array, 1) for array in here)
 
 
-def spread(total):
-    by_x, by_y = swap(total, 2), swap(total, 4)
-    return both((total, by_x, by_y) + cross(by_x, by_y, first_part(total.shape[0])))
+def direct(piece):
+    return piece, swap(piece, 2), swap(piece, 4), swap(piece, 6)
 
 
 def spread_whole(pieces):
@@ -873,20 +873,31 @@
     return add(a0, from_x[0]), add(a2, from_x[1]), add(b0, from_y[1]), add(b1, from_y[0])
 
 
-def halve_twice(once):
+def halve_twice(once, *others):
     a0, a2, b0, b1 = once
+    if others:
+        a0, b0 = after((a0, b0), *others)
     return jnp.concatenate([add(a0, swap(a2, 4)), add(b0, swap(b1, 2))], axis=-2)
 
 
-def sum_z(parts):
+def send_z(parts):
     count = lax.axis_size("fsdp")
     place = lax.axis_index("fsdp")
-    total = pick(parts, place).astype(f32)
-    for by in range(1, count):
-        total = total + lax.ppermute(
-            pick(parts, (place + by) % count), "fsdp", shifts(count, by)
-        ).astype(f32)
+    return [
+        lax.ppermute(pick(parts, (place + by) % count), "fsdp", shifts(count, by))
+        for by in range(1, count)
+    ]
+
+
+def total_z(parts, others):
+    total = pick(parts, lax.axis_index("fsdp")).astype(f32)
+    for array in others:
+        total = total + array.astype(f32)
     return total.astype(bf16)
+
+
+def sum_z(parts):
+    return total_z(parts, send_z(parts))
 
 
 def cut_down(part, first):
@@ -964,6 +975,32 @@
     down_rows = down_weight.shape[0] // PIECES
     slots = condition.shape[0]
 
+    cond_float = condition.astype(f32)
+    lifted = jax.nn.silu(cond_float).astype(bf16)
+    lifted_rows = to_group(
+        lifted.reshape(slots, fsdp_count, height).transpose(1, 0, 2), fsdp_count, place
+    ).reshape(fsdp_count * slots, height)
+    one_hot = (
+        segment_ids[::CHUNK, None] == jnp.arange(slots, dtype=jnp.int32)[None, :]
+    ).astype(f32)
+
+    def modulation_parts(weight, rows):
+        parts = matmul(rows, weight).reshape(fsdp_count, slots, weight.shape[1])
+        return [pick(parts, place)] + [
+            lax.ppermute(pick(parts, (place + by) % fsdp_count), "fsdp", shifts(fsdp_count, by))
+            for by in range(1, fsdp_count)
+        ]
+
+    def modulation(parts):
+        return jnp.dot(
+            one_hot,
+            sum(parts[1:], parts[0]),
+            precision=lax.Precision.HIGHEST,
+            preferred_element_type=f32,
+        )
+
+    first_rows = modulation_parts(modulate_weight[:, : 2 * WIDTH], lifted_rows)
+    mod_one = modulation(first_rows)
     fast = lax.axis_size("bucket") == PIECES
     if fast:
         column, side = bucket // HALVES, bucket % HALVES
@@ -979,11 +1016,17 @@
             lax.dynamic_slice(up_weight, (0, column * tile), (height, tile)),
         )
         down_piece = lax.dynamic_slice_in_dim(down_weight, bucket * down_rows, down_rows, 0)
-        attn_z = gather_z(attn_piece)
-        pair_z = gather_z(after(ffn_piece, attn_z))
+        attn_z = gather_z(attn_piece, first_rows)
         down_k = over_z(after(down_piece, attn_z))
         attn_x, attn_y = swap(attn_z, 2), swap(attn_z, 4)
-        attn_arrived = both((attn_z, attn_x, attn_y) + cross(attn_x, attn_y, first_part(half)))
+        attn_x, attn_y, down_k = after((attn_x, attn_y, down_k))
+        attn_far = cross(attn_x, attn_y, first_part(half))
+        pair_z = gather_z(after(ffn_piece, down_k))
+        down_z = jnp.stack(down_k)
+        attn_arrived = both((attn_z, attn_x, attn_y) + attn_far)
+        inputs, down_z = after((inputs, down_z), attn_far)
+        down_x, down_y = swap(down_z, 2), swap(down_z, 4)
+        inputs = after(inputs, down_z)
     else:
         where = jnp.stack([place, 0 * place, 0 * place] + [jnp.int32(j) for j in ORDER])
         attn_arrived = arrived_whole(
@@ -1000,31 +1043,9 @@
         )
         downs = arrived_whole(down_weight.reshape(PIECES, down_rows, WIDTH))
 
-    cond_float = condition.astype(f32)
-    lifted = jax.nn.silu(cond_float).astype(bf16)
-    lifted_rows = to_group(
-        lifted.reshape(slots, fsdp_count, height).transpose(1, 0, 2), fsdp_count, place
-    ).reshape(fsdp_count * slots, height)
-    one_hot = (
-        segment_ids[::CHUNK, None] == jnp.arange(slots, dtype=jnp.int32)[None, :]
-    ).astype(f32)
-
-    def modulation_parts(weight, rows):
-        parts = matmul(rows, weight).reshape(fsdp_count, slots, weight.shape[1])
-        return to_group(parts, fsdp_count, place)
-
-    def modulation(parts):
-        return jnp.dot(
-            one_hot,
-            jnp.sum(parts, axis=0),
-            precision=lax.Precision.HIGHEST,
-            preferred_element_type=f32,
-        )
-
-    mod_one = modulation(modulation_parts(modulate_weight[:, : 2 * WIDTH], lifted_rows))
     if fast:
-        lifted_rows = after(lifted_rows, attn_z)
-    mod_parts = modulation_parts(modulate_weight[:, 2 * WIDTH :], lifted_rows)
+        lifted_rows = after(lifted_rows, down_k)
+    late_rows = modulation_parts(modulate_weight[:, 2 * WIDTH :], lifted_rows)
     counts = bucket_counts.astype(f32)
     mine = jnp.sum(jnp.where(jnp.arange(counts.shape[0], dtype=jnp.int32) == bucket, counts, 0.0))
     factor = (mine * counts.shape[0] / jnp.sum(counts)).reshape(1)
@@ -1034,10 +1055,13 @@
         where, inputs, mod_one, cos, sin, joint_weight, project_weight, attn_arrived
     )
     if fast:
-        mod_parts, down_k = after((mod_parts, down_k), query)
-        down_z = jnp.stack(down_k)
-        down_x, down_y = swap(down_z, 2), swap(down_z, 4)
-    mod = modulation(mod_parts)
+        late_rows = [late_rows[0], *after(late_rows[1:], query)]
+        down_x, down_y = after((down_x, down_y), query)
+        down_far = cross(down_x, down_y, first_part(down_rows))
+        downs = (down_z, down_x, down_y) + down_far
+        pair_z = after(pair_z, query)
+        pair_x, pair_y = swap(pair_z, 2), swap(pair_z, 4)
+    mod = modulation(late_rows)
     attended, branch, middle, second = attend_call(
         query, keys, values, segment_ids, inputs, mod, weight
     )
@@ -1046,11 +1070,7 @@
         second=second, factor=factor, cot=cotangent, mod=mod, middle=middle, branch=branch
     )
     if fast:
-        down_x, down_y, pair_z = after((down_x, down_y, pair_z), second)
-        down_far = cross(down_x, down_y, first_part(down_rows))
-        downs = both((down_z, down_x, down_y) + down_far)
-        pair_z = after(pair_z, down_far)
-        pair_x, pair_y = swap(pair_z, 2), swap(pair_z, 4)
+        downs = both(after(downs, second))
         pairs = (pair_z, pair_x, pair_y, None, None, swap(pair_z, 1), None, None, None, None)
     pairs = [
         [[group] for group in pairs[5 * k : 5 * k + 3]] + [list(pairs[5 * k + 3 : 5 * k + 5])]
@@ -1073,87 +1093,6 @@
     output, middle_back, branch_back = found["output"], found["middle_back"], found["branch_back"]
     late_sums = found["sums"]
 
-    count = fsdp_count
-    hiddens = [step["hidden_turned"] for step in steps]
-    backs = [step["pair_back"] for step in steps]
-    down_theirs = down_grad_call(count, where, hiddens, feed_back)
-    if fast:
-        turned = after(turned, down_theirs)
-    pair_theirs = pair_grad_call(count, where, turned, backs)
-    if fast:
-        down_other = swap(down_theirs, 1)
-        down_other, pair_theirs = after((down_other, pair_theirs))
-        pair_other = swap(pair_theirs, 1)
-    else:
-        down_other, pair_other = jnp.zeros_like(down_theirs), jnp.zeros_like(pair_theirs)
-    down_mine = down_grad_call(count, where, hiddens, feed_back, down_other)
-    if fast:
-        turned = after(turned, down_mine)
-    pair_cut = pair_grad_call(count, where, turned, backs, pair_other)
-    if fast:
-        down_part = lax.psum_scatter(down_mine, "fsdp", scatter_dimension=0, tiled=False)
-        branch_back = after(branch_back, pair_cut)
-    joint_back = attend_back_call(
-        query, keys, values, branch_back, segment_ids, cos, sin, weight
-    )
-    if fast:
-        send_x, keep_x, send_y, keep_y = pair_cut
-        keep_x, keep_y = after((keep_x, keep_y), joint_back)
-        pair_once = halve_once((send_x, keep_x, send_y, keep_y))
-        branch_back = after(branch_back, pair_once)
-        branch_back = after(branch_back, pair_once)
-    attn_theirs = attn_grad_call(count, where, first, attended, joint_back, branch_back)
-    if fast:
-        pair_parts, down_part = after((halve_twice(pair_once), down_part), attn_theirs)
-        pair_sum = lax.psum_scatter(pair_parts, "fsdp", scatter_dimension=0, tiled=False)
-        down_cut = cut_down(down_part, first_part(down_rows))
-        middle_back = after(middle_back, attn_theirs, down_cut)
-    grad_inputs, early_sums = first_back_call(joint_back, inputs, middle_back, mod_one, weight)
-    if fast:
-        down_cut = [down_cut[0], after(down_cut[1], grad_inputs), down_cut[2], after(down_cut[3], grad_inputs)]
-        down_once = halve_once(down_cut)
-        attn_other, down_once = after((swap(attn_theirs, 1), down_once), grad_inputs)
-        attn_cut = attn_grad_call(
-            count, where, first, attended, joint_back, branch_back, attn_other
-        )
-        down_total = after(halve_twice(down_once), attn_cut)
-        attn_once = halve_once(attn_cut)
-        pair_sum, down_total = after((pair_sum, down_total), attn_once)
-        attn_parts = halve_twice(attn_once)
-        pair_x, pair_y = swap(pair_sum, 2), swap(pair_sum, 4)
-        down_x, down_y = swap(down_total, 2), swap(down_total, 4)
-        attn_z = [
-            lax.ppermute(pick(attn_parts, (place + by) % count), "fsdp", shifts(count, by))
-            for by in range(1, count)
-        ]
-        pair_x, pair_y, down_x, down_y = after((pair_x, pair_y, down_x, down_y), attn_parts)
-        down_far = cross(down_x, down_y, first_part(down_rows))
-        pair_far = cross(pair_x, pair_y, first_part(height))
-        attn_sum = pick(attn_parts, place).astype(f32)
-        for array in after(attn_z, pair_far, down_far):
-            attn_sum = attn_sum + array.astype(f32)
-        attn_sum = attn_sum.astype(bf16)
-        down_sums = both((down_total, down_x, down_y) + down_far)
-        pair_sums = both((pair_sum, pair_x, pair_y) + pair_far)
-        attn_sums = spread(attn_sum)
-    else:
-        down_sums = sum_whole(down_mine.swapaxes(0, 1), down_theirs.swapaxes(0, 1))
-        pair_sums = sum_whole(uncut(pair_cut), pair_theirs)
-        attn_cut = attn_grad_call(
-            count, where, first, attended, joint_back, branch_back, jnp.zeros_like(attn_theirs)
-        )
-        attn_sums = sum_whole(uncut(attn_cut), attn_theirs)
-    down_grad = place_call(place_down_kernel, where, down_sums, struct(down_weight.shape, f32))
-    pair_grad = place_call(
-        place_pair_kernel, where, pair_sums, (struct(gate_weight.shape, f32),) * 2
-    )
-    attn_grad = place_call(
-        place_attn_kernel,
-        where,
-        attn_sums,
-        (struct(joint_weight.shape, f32), struct(project_weight.shape, f32)),
-    )
-
     def by_slot(chunk_sums):
         return lax.dot_general(
             one_hot,
@@ -1163,27 +1102,113 @@
             preferred_element_type=f32,
         ).astype(bf16)
 
-    everyone = lax.all_gather(
-        jnp.concatenate([by_slot(early_sums), by_slot(late_sums), lifted], axis=1),
-        ("bucket", "fsdp"),
-        axis=0,
-        tiled=True,
-    )
+    late = lax.all_gather(
+        jnp.concatenate([by_slot(late_sums), lifted], axis=1), ("bucket", "fsdp"), axis=0, tiled=True
+    )
+
+    count = fsdp_count
+    hiddens = [step["hidden_turned"] for step in steps]
+    backs = [step["pair_back"] for step in steps]
+    pair_theirs = pair_grad_call(count, where, turned, backs)
     if fast:
-        everyone = after(everyone, attn_sum)
-    all_back = everyone[:, : 6 * WIDTH]
-    all_lifted = lax.dynamic_slice_in_dim(everyone, 6 * WIDTH + place * height, height, 1)
+        pair_other = swap(pair_theirs, 1)
+        feed_back = after(feed_back, pair_theirs)
+    else:
+        pair_other = jnp.zeros_like(pair_theirs)
+    down_theirs = down_grad_call(count, where, hiddens, feed_back)
+    if fast:
+        pair_other, down_theirs = after((pair_other, down_theirs))
+        down_other = swap(down_theirs, 1)
+    else:
+        down_other = jnp.zeros_like(down_theirs)
+    pair_cut = pair_grad_call(count, where, turned, backs, pair_other)
+    if fast:
+        feed_back = after(feed_back, pair_cut)
+    down_mine = down_grad_call(count, where, hiddens, feed_back, down_other)
+    if fast:
+        down_mine, late = after((down_mine, late))
+        down_part = lax.psum_scatter(down_mine, "fsdp", scatter_dimension=0, tiled=False)
+        branch_back = after(branch_back, down_mine)
+    joint_back = attend_back_call(
+        query, keys, values, branch_back, segment_ids, cos, sin, weight
+    )
+    attn_theirs = attn_grad_call(count, where, first, attended, joint_back, branch_back)
+    if fast:
+        send_x, keep_x, send_y, keep_y = pair_cut
+        keep_x, keep_y, attn_theirs = after((keep_x, keep_y, attn_theirs))
+        pair_once = halve_once((send_x, keep_x, send_y, keep_y))
+        pair_once, attn_theirs, middle_back = after((pair_once, attn_theirs, middle_back))
+        attn_other = swap(attn_theirs, 1)
+    grad_inputs, early_sums = first_back_call(joint_back, inputs, middle_back, mod_one, weight)
+    if fast:
+        a0, a2, b0, b1 = pair_once
+        a0, b0, grad_inputs = after((a0, b0, grad_inputs))
+        pair_parts, branch_back = after((halve_twice((a0, a2, b0, b1)), branch_back))
+        pair_z = send_z(pair_parts)
+        attn_cut = attn_grad_call(
+            count, where, first, attended, joint_back, branch_back, attn_other
+        )
+        attn_cut, down_part = after((attn_cut, down_part))
+        down_cut = cut_down(down_part, first_part(down_rows))
+        cut = [
+            jnp.concatenate([attn.reshape(2, -1, WIDTH), down], axis=1)
+            for attn, down in zip(attn_cut, down_cut, strict=True)
+        ]
+        once, pair_z = after((halve_once(cut), pair_z))
+        pair_sum = total_z(pair_parts, pair_z)
+        pair_x, pair_y = swap(pair_sum, 2), swap(pair_sum, 4)
+        a0, a2, b0, b1 = once
+        ahead, behind = add(a0, swap(a2, 4)), add(b0, swap(b1, 2))
+        at, other_at = (part.shape[1] * part.shape[2] for part in (attn_cut[0], attn_cut[2]))
+        attn_parts = jnp.concatenate(
+            [half.reshape(count, -1, WIDTH) for half in (ahead[:at], behind[:other_at])], axis=1
+        )
+        down_total = jnp.concatenate([ahead[at:], behind[other_at:]], axis=0)
+        attn_parts, down_total, pair_x, pair_y = after((attn_parts, down_total, pair_x, pair_y))
+        attn_z = send_z(attn_parts)
+        pair_sums = (pair_sum, pair_x, pair_y) + cross(pair_x, pair_y, first_part(height))
+        attn_z, pair_sums = after((attn_z, both(pair_sums)))
+        attn_sum = total_z(attn_parts, attn_z)
+    else:
+        down_sums = sum_whole(down_mine.swapaxes(0, 1), down_theirs.swapaxes(0, 1))
+        pair_sums = sum_whole(uncut(pair_cut), pair_theirs)
+        attn_cut = attn_grad_call(
+            count, where, first, attended, joint_back, branch_back, jnp.zeros_like(attn_theirs)
+        )
+        attn_sums = sum_whole(uncut(attn_cut), attn_theirs)
+    early = lax.all_gather(by_slot(early_sums), ("bucket", "fsdp"), axis=0, tiled=True)
+    if fast:
+        early, attn_sum = after((early, attn_sum))
+        both_sums = direct(jnp.concatenate([attn_sum, down_total], axis=0))
+    all_back = jnp.concatenate([early, late[:, : 4 * WIDTH]], axis=1)
+    all_lifted = lax.dynamic_slice_in_dim(late, 4 * WIDTH + place * height, height, 1)
     modulate_gradient = contract_rows(all_lifted, all_back)
     group_back = lax.dynamic_slice_in_dim(
         all_back, bucket * fsdp_count * slots, fsdp_count * slots, 0
     )
     slope_rows = times_transposed(group_back, modulate_weight)
+    pair_grad = place_call(
+        place_pair_kernel, where, pair_sums, (struct(gate_weight.shape, f32),) * 2
+    )
+    if fast:
+        both_sums, pair_grad, modulate_gradient, slope_rows = after(
+            (both_sums, pair_grad, modulate_gradient, slope_rows)
+        )
+        attn_sums = down_sums = both(both_sums)
     condition_slope = (
         to_group(slope_rows.reshape(fsdp_count, slots, height), fsdp_count, place)
         .transpose(1, 0, 2)
         .reshape(slots, WIDTH)
     )
     grad_condition = condition_slope * silu_slope(cond_float)
+    down_grad = place_call(functools.partial(place_down_kernel, down_rows, half if fast else 0), where, down_sums, struct(down_weight.shape, f32))
+    attn_grad = place_call(
+        functools.partial(place_attn_kernel, half),
+        where,
+        attn_sums,
+        (struct(joint_weight.shape, f32), struct(project_weight.shape, f32)),
+    )
+
     return (
         output,
         grad_inputs,

time: 554 us -> 549 us (level)
  starting transfers between devices: 104 us -> 72.6 us
  waiting for transfers between devices: 175 us -> 193 us
  Pallas kernels: 196 us -> 189 us
    ppermute x69 -> x54, waiting for transfers between devices: 147 us -> 89.9 us  [swap(): return lax.ppermute(array, 'bucket', across(bit))]
    ppermute x3 -> x12, waiting for transfers between devices: 1.37 us -> 44.3 us  [the longest x6 25.3 us: send_z(): lax.ppermute(pick(parts, (place + by) % count), 'fsdp', shifts(count, by))]
    all_gather x3 -> x4, waiting for transfers between devices: 5.85 us -> 46.7 us  [the longest x1 33.1 us: on_device(): lax.all_gather(jnp.concatenate([by_slot(late_sums), lifted], axis=1), ('b...]
    ppermute x69 -> x54, starting transfers between devices: 77.7 us -> 49 us  [swap(): return lax.ppermute(array, 'bucket', across(bit))]
    ppermute x12 -> x6, waiting for transfers between devices: 20.5 us -> 1.69 us  [to_group(): lax.ppermute(pick(rows, (place + by) % count), 'fsdp', shifts(count, by))]
    ppermute x3, waiting for transfers between devices: 0.55 us -> 10.5 us  [over_z(): lax.ppermute(piece, 'fsdp', shifts(count, by))]
    unnamed x129 -> x112, local copies, waits for them, and re-layouts: 12.1 us -> 8.89 us
    ppermute x3 -> x12, starting transfers between devices: 13.9 us -> 13.1 us  [the longest x6 9.22 us: send_z(): lax.ppermute(pick(parts, (place + by) % count), 'fsdp', shifts(count, by))]
  transfers between devices with their start and end apart: 92 -> 80, of which waited for: 33 -> 28; matrix products, arithmetic and copies ran while one was open for 7% -> 10% of each run, Pallas kernels for 31% -> 28%
where the time goes in v5:
time: 549 us; the launch traced here: 539 us
  waiting for transfers between devices  193 us (35%)
  Pallas kernels  189 us (34%)
  starting transfers between devices  72.6 us (13%)
  local copies, waits for them, and re-layouts  32.5 us (6%)
  other arithmetic  19.8 us (4%)
  between operations  16.4 us (3%)
  matrix products  16.3 us (3%)
    ppermute x54, waiting for transfers between devices, swap(): return lax.ppermute(array, 'bucket', across(bit))  89.9 us
    pallas_call x3, Pallas kernels, ffn_call(): pl.pallas_call(functools.partial(ffn_kernel, count, js, names), grid=(len...  52.6 us
    ppermute x54, starting transfers between devices, swap(): return lax.ppermute(array, 'bucket', across(bit))  49 us
    pallas_call x4, Pallas kernels, by_column(): pl.pallas_call(call, out_shape=shapes, grid_spec=pltpu.PrefetchScalarGrid...  39.3 us
    all_gather x1, waiting for transfers between devices, on_device(): lax.all_gather(jnp.concatenate([by_slot(late_sums), lifted], axis=1), ('b...  33.1 us
    ppermute x6, waiting for transfers between devices, send_z(): lax.ppermute(pick(parts, (place + by) % count), 'fsdp', shifts(count, by))  25.3 us
    pallas_call x1, Pallas kernels, attend_back_call(): pl.pallas_call(attend_back_kernel, grid=(tokens // BLOCK,), out_shape=str...  24 us
    ppermute x6, waiting for transfers between devices, modulation_parts(): lax.ppermute(pick(parts, (place + by) % fsdp_count), 'fsdp', shifts(fsdp_...  18.9 us
  transfers between devices with their start and end apart: 80, of which 28 were waited for; matrix products, arithmetic and copies ran while one was open for 10% of the time, Pallas kernels for 28%

profile of v5, /device:TPU:25, one launch (start us, length us, event | category | flops | bytes accessed | tf_op | source)
XLA Modules:
  0.0 539.5 jit_solution(14544228574073427930)
XLA Ops:
  25.5 8.6 %collective-permute-done.4 = f32[8,2304]{1,0:T(8,128)S(1)} collective-permute-done((f32[8,2304]{1,0:T(8,128)S(1)}, f32[8,2304]{1,0:T(8,128)S(1)}, u32[]{:S(2)}, u32[]{:S(2)}) %collective-permute-start.4) | collective-permute-done | bytes 73760 | tf_op jit(solution)/shard_map/ppermute | solution.py:990
  34.8 13.6 %all-gather.11.cloned.1.call-done = bf16[576,1152]{1,0:T(8,128)(2,1)} async-done(((bf16[144,1152]{1,0:T(8,128)(2,1)}), bf16[576,1152]{1,0:T(8,128)(2,1)}) %all-gather.11.cloned.1.call-update) | async-done | bytes 1327120 | tf_op jit(solution)/shard_map/all_gather | solution.py:842
  66.2 10.5 %collective-permute-done.9 = bf16[96,1152]{1,0:T(8,128)(2,1)} collective-permute-done((bf16[96,1152]{1,0:T(8,128)(2,1)}, bf16[96,1152]{1,0:T(8,128)(2,1)}, u32[]{:S(2)}, u32[]{:S(2)}) %collective-permute-start.9) | collective-permute-done | bytes 221216 | tf_op jit(solution)/shard_map/ppermute | solution.py:836
  97.1 18.9 %shard_map.187 = (bf16[1152,512]{1,0:T(8,128)(2,1)}, bf16[512,1152]{1,0:T(8,128)(2,1)}, bf16[512,1152]{1,0:T(8,128)(2,1)}, bf16[512,1152]{1,0:T(8,128)(2,1)}, bf16[4,1152,1152]{2,1,0:T(8,128)(2,1)}) custom-call(s32[7]{0:T(128)} %stack.85.where_ref.refs_0_, bf16[512,1152]{1,0:T(8,128)(2,1)} %x_ref.2, f32[8,2304]{1,0:T(8,128)} %fusion.33.mod_ref, ...), custom_call_target="tpu_custom_call" | custom-call | flops 20000000000 | bytes 1000 | tf_op jit(solution)/shard_map/pallas_call | solution.py:567
  116.0 6.4 %collective-permute-done.19 = f32[8,4608]{1,0:T(8,128)S(1)} collective-permute-done((f32[8,4608]{1,0:T(8,128)S(1)}, f32[8,4608]{1,0:T(8,128)S(1)}, u32[]{:S(2)}, u32[]{:S(2)}) %collective-permute-start.19) | collective-permute-done | bytes 147488 | tf_op jit(solution)/shard_map/ppermute | solution.py:990
  124.3 12.6 %shard_map.188 = (bf16[1152,512]{1,0:T(8,128)(2,1)}, f32[512,1152]{1,0:T(8,128)}, f32[512,1152]{1,0:T(8,128)}, bf16[512,1152]{1,0:T(8,128)(2,1)}) custom-call(bf16[512,1152]{1,0:T(8,128)(2,1)} %get-tuple-element.145.query_ref, bf16[512,1152]{1,0:T(8,128)(2,1)} %get-tuple-element.146.keys_ref, bf16[512,1152]{1,0:T(8,128)(2,1)} %get-tuple-element.147.values_ref, ...), custom_call_target="tpu_custom_call" | custom-call | flops 2000000000 | bytes 1000 | tf_op jit(solution)/shard_map/pallas_call | solution.py:587
  148.1 12.4 %shard_map.189 = (bf16[1,768,512]{2,1,0:T(8,128)(2,1)}, bf16[1,2,512,768]{3,2,1,0:T(8,128)(2,1)}, bf16[1152,512]{1,0:T(8,128)(2,1)}, bf16[512,1152]{1,0:T(8,128)...) custom-call(s32[7]{0:T(128)} %stack.85.where_ref.refs_0_, bf16[512,1152]{1,0:T(8,128)(2,1)} %get-tuple-element.153.refs_1_, ...), custom_call_target="tpu_custom_call" | custom-call | flops 2000000000 | bytes 1000 | tf_op jit(solution)/shard_map/pallas_call | solution.py:676
  160.5 11.1 %collective-permute-done.31.refs_8_ = bf16[3,288,768]{2,1,0:T(8,128)(2,1)} collective-permute-done((bf16[3,288,768]{2,1,0:T(8,128)(2,1)S(1)}, bf16[3,288,768]{2,1,0:T(8,128)(2,1)}, u32[]{:S(2)}, u32[]{:S(2)}) %collective-permute-start.31) | collective-permute-done | bytes 1327136 | tf_op jit(solution)/shard_map/ppermute | solution.py:823
  179.6 23.3 %shard_map.190 = (bf16[2,768,512]{2,1,0:T(8,128)(2,1)}, bf16[2,2,512,768]{3,2,1,0:T(8,128)(2,1)}, f32[512,1152]{1,0:T(8,128)}, f32[512,1152]{1,0:T(8,128)}) custom-call(s32[7]{0:T(128)} %stack.85.where_ref.refs_0_, bf16[512,1152]{1,0:T(8,128)(2,1)} %get-tuple-element.153.refs_1_, bf16[512,1152]{1,0:T(8,128)(2,1)} %get-tuple-element.191.refs_2_.refs_5_.refs_3_, ...), custom_call_target="tpu_custom_call" | custom-call | flops 24000000000 | bytes 1000 | tf_op jit(solution)/shard_map/pallas_call | solution.py:676
  207.1 16.9 %shard_map.191 = (bf16[1,768,512]{2,1,0:T(8,128)(2,1)}, bf16[1,2,512,768]{3,2,1,0:T(8,128)(2,1)}, bf16[512,1152]{1,0:T(8,128)(2,1)}, f32[512,1152]{1,0:T(8,128)}...) custom-call(s32[7]{0:T(128)} %stack.85.where_ref.refs_0_, bf16[512,1152]{1,0:T(8,128)(2,1)} %get-tuple-element.153.refs_1_, ...), custom_call_target="tpu_custom_call" | custom-call | flops 12000000000 | bytes 1000 | tf_op jit(solution)/shard_map/pallas_call | solution.py:676
  224.0 9.1 %shard_map.192 = bf16[4,4,288,768]{3,2,1,0:T(8,128)(2,1)} custom-call(s32[7]{0:T(128)} %stack.85.where_ref.refs_0_, bf16[1152,512]{1,0:T(8,128)(2,1)} %get-tuple-element.175.turned_ref, bf16[1,2,512,768]{3,2,1,0:T(8,128)(2,1)} %get-tuple-element.176.own_ref, bf16[2,2,512,768]{3,2,1,0:T(8,128)(2,1)} %get-tuple-element.177.near_ref, ...), custom_call_target="tpu_custom_call" | custom-call | flops 3000000000 | bytes 1000 | tf_op jit(solution)/shard_map/pallas_call | solution.py:696
  234.7 6.3 %shard_map.193 = bf16[4,4,96,1152]{3,2,1,0:T(8,128)(2,1)} custom-call(s32[7]{0:T(128)} %stack.85.where_ref.refs_0_, bf16[1,768,512]{2,1,0:T(8,128)(2,1)} %get-tuple-element.179.refs_0_, bf16[2,768,512]{2,1,0:T(8,128)(2,1)} %get-tuple-element.180.refs_1_, bf16[1,768,512]{2,1,0:T(8,128)(2,1)} %get-tuple-element.181.refs_2_, ...), custom_call_target="tpu_custom_call" | custom-call | flops 3000000000 | bytes 1000 | tf_op jit(solution)/shard_map/pallas_call | solution.py:745
  245.1 11.0 %shard_map.194 = (bf16[2,4,144,768]{3,2,1,0:T(8,128)(2,1)}, bf16[2,4,144,768]{3,2,1,0:T(8,128)(2,1)}, bf16[2,4,144,768]{3,2,1,0:T(8,128)(2,1)}, bf16[2,4,144,768]{3,2,1,0:T(8,128)(2,1)}) custom-call(s32[7]{0:T(128)} %stack.85.where_ref.refs_0_, bf16[1152,512]{1,0:T(8,128)(2,1)} %get-tuple-element.175.turned_ref, ...), custom_call_target="tpu_custom_call" | custom-call | flops 3000000000 | bytes 1000 | tf_op jit(solution)/shard_map/pallas_call | solution.py:696
  259.3 7.4 %shard_map.195 = bf16[4,4,96,1152]{3,2,1,0:T(8,128)(2,1)} custom-call(s32[7]{0:T(128)} %stack.85.where_ref.refs_0_, bf16[1,768,512]{2,1,0:T(8,128)(2,1)} %get-tuple-element.179.refs_0_, bf16[2,768,512]{2,1,0:T(8,128)(2,1)} %get-tuple-element.180.refs_1_, bf16[1,768,512]{2,1,0:T(8,128)(2,1)} %get-tuple-element.181.refs_2_, ...), custom_call_target="tpu_custom_call" | custom-call | flops 3000000000 | bytes 1000 | tf_op jit(solution)/shard_map/pallas_call | solution.py:745
  266.7 33.1 %all-gather.7.cloned.1.call-done = bf16[256,5760]{1,0:T(8,128)(2,1)} async-done(((bf16[8,5760]{1,0:T(8,128)(2,1)}), bf16[256,5760]{1,0:T(8,128)(2,1)}) %all-gather.7.cloned.1.call-update) | async-done | bytes 2949136 | tf_op jit(solution)/shard_map/all_gather | solution.py:1105
  300.1 24.0 %shard_map.196.joint_back_ref = bf16[512,3456]{1,0:T(8,128)(2,1)} custom-call(bf16[512,1152]{1,0:T(8,128)(2,1)} %get-tuple-element.145.query_ref, bf16[512,1152]{1,0:T(8,128)(2,1)} %get-tuple-element.146.keys_ref, bf16[512,1152]{1,0:T(8,128)(2,1)} %get-tuple-element.147.values_ref, bf16[512,1152]{1,0:T(8,128)(2,1)} %get-tuple-element.210.branch_back_ref, ...), custom_call_target="tpu_custom_call" | custom-call | flops 8000000000 | bytes 1000 | tf_op jit(solution)/shard_map/pallas_call | solution.py:769
  324.1 8.9 %shard_map.197 = bf16[4,4,144,1152]{3,2,1,0:T(8,128)(2,1)} custom-call(s32[7]{0:T(128)} %stack.85.where_ref.refs_0_, bf16[1152,512]{1,0:T(8,128)(2,1)} %get-tuple-element.186.first_ref, bf16[1152,512]{1,0:T(8,128)(2,1)} %get-tuple-element.187.attended_ref, bf16[512,3456]{1,0:T(8,128)(2,1)} %shard_map.196.joint_back_ref, ...), custom_call_target="tpu_custom_call" | custom-call | flops 3000000000 | bytes 1000 | tf_op jit(solution)/shard_map/pallas_call | solution.py:696
  336.8 13.1 %shard_map.198 = (f32[512,1152]{1,0:T(8,128)}, f32[8,2304]{1,0:T(8,128)}) custom-call(bf16[512,3456]{1,0:T(8,128)(2,1)} %shard_map.196.joint_back_ref, bf16[512,1152]{1,0:T(8,128)(2,1)} %x_ref.2, f32[512,1152]{1,0:T(8,128)} %get-tuple-element.202.middle_back_ref, f32[8,2304]{1,0:T(8,128)} %fusion.33.mod_ref, bf16[4,1152,1152]{2,1,0:T(8,128)(2,1)} %get-tuple-element.152.weight), custom_call_target="tpu_custom_call" | custom-call | flops 2000000000 | bytes 1000 | tf_op jit(solution)/shard_map/pallas_call | solution.py:792
  349.9 6.5 %collective-permute-done.43 = bf16[4,144,768]{2,1,0:T(8,128)(2,1)S(1)} collective-permute-done((bf16[4,144,768]{2,1,0:T(8,128)(2,1)S(1)}, bf16[4,144,768]{2,1,0:T(8,128)(2,1)S(1)}, u32[]{:S(2)}, u32[]{:S(2)}) %collective-permute-start.43) | collective-permute-done | bytes 884768 | tf_op jit(solution)/shard_map/ppermute | solution.py:823
  357.7 10.3 %shard_map.199 = (bf16[2,4,80,1152]{3,2,1,0:T(8,128)(2,1)}, bf16[2,4,80,1152]{3,2,1,0:T(8,128)(2,1)}, bf16[2,4,64,1152]{3,2,1,0:T(8,128)(2,1)}, bf16[2,4,64,1152]{3,2,1,0:T(8,128)(2,1)}) custom-call(s32[7]{0:T(128)} %stack.85.where_ref.refs_0_, bf16[1152,512]{1,0:T(8,128)(2,1)} %get-tuple-element.186.first_ref, ...), custom_call_target="tpu_custom_call" | custom-call | flops 3000000000 | bytes 1000 | tf_op jit(solution)/shard_map/pallas_call | solution.py:696
  374.9 26.0 %collective-permute-done.47 = bf16[2,304,1152]{2,1,0:T(8,128)(2,1)S(1)} collective-permute-done((bf16[2,304,1152]{2,1,0:T(8,128)(2,1)S(1)}, bf16[2,304,1152]{2,1,0:T(8,128)(2,1)S(1)}, u32[]{:S(2)}, u32[]{:S(2)}) %collective-permute-start.47) | collective-permute-done | bytes 1400864 | tf_op jit(solution)/shard_map/ppermute | solution.py:823
  420.8 6.7 %collective-permute-done.52 = bf16[304,1152]{1,0:T(8,128)(2,1)} collective-permute-done((bf16[304,1152]{1,0:T(8,128)(2,1)}, bf16[304,1152]{1,0:T(8,128)(2,1)}, u32[]{:S(2)}, u32[]{:S(2)}) %collective-permute-start.52) | collective-permute-done | bytes 700448 | tf_op jit(solution)/shard_map/ppermute | solution.py:823
  456.4 22.9 %collective-permute-done.56 = bf16[144,1152]{1,0:T(8,128)(2,1)S(1)} collective-permute-done((bf16[144,1152]{1,0:T(8,128)(2,1)S(1)}, bf16[144,1152]{1,0:T(8,128)(2,1)S(1)}, u32[]{:S(2)}, u32[]{:S(2)}) %collective-permute-start.56) | collective-permute-done | bytes 331808 | tf_op jit(solution)/shard_map/ppermute | solution.py:887
  503.5 9.5 %collective-permute-done.67.refs_3_ = bf16[240,1152]{1,0:T(8,128)(2,1)} collective-permute-done((bf16[240,1152]{1,0:T(8,128)(2,1)S(1)}, bf16[240,1152]{1,0:T(8,128)(2,1)}, u32[]{:S(2)}, u32[]{:S(2)}) %collective-permute-start.67) | collective-permute-done | bytes 552992 | tf_op jit(solution)/shard_map/ppermute | solution.py:823
  (356 shorter events, 194.1 us)
Async XLA Ops:
  7.2 41.3 %all-gather.11.cloned.1.call-start = ((), (), s32[]{:S(2)}) async-start(), calls=%async_computation.4 | async-start | bytes 1658880 | tf_op jit(solution)/shard_map/all_gather | solution.py:842
  9.2 129.1 %all-gather.13.cloned.1.call-start = ((), (), s32[]{:S(2)}) async-start(), calls=%async_computation.5 | async-start | bytes 2211840 | tf_op jit(solution)/shard_map/all_gather | solution.py:842
  49.9 26.8 %collective-permute-start.6 = (bf16[3,144,1152]{2,1,0:T(8,128)(2,1)S(1)}, bf16[3,144,1152]{2,1,0:T(8,128)(2,1)}, u32[]{:S(2)}, u32[]{:S(2)}) collective-permute-start(bf16[3,144,1152]{2,1,0:T(8,128)(2,1)S(1)} %pad_maximum_fusion.7.refs_0_), channel_id=1, source_target_pairs={{0,8},{4,12},{8,0},{12,4},{16,24},{20,28},{24,16},{28,20},{1,9},{5... | collective-permute-start | bytes 2985992 | tf_op jit(solution)/shard_map/ppermute | solution.py:823
  83.8 216.0 %all-gather.7.cloned.1.call-start = ((), (), s32[]{:S(2)}) async-start(), calls=%async_computation.1 | async-start | bytes 3041280 | tf_op jit(solution)/shard_map/all_gather | solution.py:1105
  94.4 28.0 %collective-permute-start.19 = (f32[8,4608]{1,0:T(8,128)S(1)}, f32[8,4608]{1,0:T(8,128)S(1)}, u32[]{:S(2)}, u32[]{:S(2)}) collective-permute-start(f32[8,4608]{1,0:T(8,128)S(1)} %get-tuple-element.291), channel_id=1, source_target_pairs={{0,2},{1,3},{2,0},{3,1},{4,6},{5,7},{6,4},{7,5},{8,10},{9,11},{10,... | collective-permute-start | bytes 442376 | tf_op jit(solution)/shard_map/ppermute | solution.py:990
  94.5 27.9 %collective-permute-start.20 = (f32[8,4608]{1,0:T(8,128)S(1)}, f32[8,4608]{1,0:T(8,128)S(1)}, u32[]{:S(2)}, u32[]{:S(2)}) collective-permute-start(f32[8,4608]{1,0:T(8,128)S(1)} %get-tuple-element.290), channel_id=1, source_target_pairs={{0,3},{1,0},{2,1},{3,2},{4,7},{5,4},{6,5},{7,6},{8,11},{9,8},{10,9... | collective-permute-start | bytes 442376 | tf_op jit(solution)/shard_map/ppermute | solution.py:990
  140.3 31.2 %collective-permute-start.31 = (bf16[3,288,768]{2,1,0:T(8,128)(2,1)S(1)}, bf16[3,288,768]{2,1,0:T(8,128)(2,1)}, u32[]{:S(2)}, u32[]{:S(2)}) collective-permute-start(bf16[3,288,768]{2,1,0:T(8,128)(2,1)S(1)} %pad_maximum_fusion.5.refs_8_), channel_id=1, source_target_pairs={{0,8},{4,12},{8,0},{12,4},{16,24},{20,28},{24,16},{28,20},{1,9},{5... | collective-permute-start | bytes 3981320 | tf_op jit(solution)/shard_map/ppermute | solution.py:823
  142.1 30.5 %collective-permute-start.32 = (bf16[3,288,768]{2,1,0:T(8,128)(2,1)S(1)}, bf16[3,288,768]{2,1,0:T(8,128)(2,1)}, u32[]{:S(2)}, u32[]{:S(2)}) collective-permute-start(bf16[3,288,768]{2,1,0:T(8,128)(2,1)S(1)} %pad_maximum_fusion.5.refs_8_), channel_id=1, source_target_pairs={{0,16},{4,20},{8,24},{12,28},{16,0},{20,4},{24,8},{28,12},{1,17},{... | collective-permute-start | bytes 3981320 | tf_op jit(solution)/shard_map/ppermute | solution.py:823
  176.0 26.9 %collective-permute-start.35 = (bf16[3,144,768]{2,1,0:T(8,128)(2,1)S(1)}, bf16[3,144,768]{2,1,0:T(8,128)(2,1)S(1)}, u32[]{:S(2)}, u32[]{:S(2)}) collective-permute-start(bf16[3,144,768]{2,1,0:T(8,128)(2,1)S(1)} %slice.109), channel_id=1, source_target_pairs={{0,16},{4,20},{8,24},{12,28},{16,0},{20,4},{24,8},{28,12},{1,17},{... | collective-permute-start | bytes 1990664 | tf_op jit(solution)/shard_map/ppermute | solution.py:823
  234.5 133.6 %reduce-scatter.2.cloned.1.call-start = ((), (), s32[]{:S(2)}) async-start(), calls=%async_computation.3 | async-start | bytes 4423680 | tf_op jit(solution)/shard_map/reduce_scatter | solution.py:1130
  256.1 76.9 %collective-permute-start.42 = (bf16[2,4,144,768]{3,2,1,0:T(8,128)(2,1)}, bf16[2,4,144,768]{3,2,1,0:T(8,128)(2,1)S(1)}, u32[]{:S(2)}, u32[]{:S(2)}) collective-permute-start(bf16[2,4,144,768]{3,2,1,0:T(8,128)(2,1)} %get-tuple-element.190), channel_id=1, source_target_pairs={{0,16},{4,20},{8,24},{12,28},{16,0},{20,4},{24,8},{28,12},{1,17},{... | collective-permute-start | bytes 5308424 | tf_op jit(solution)/shard_map/ppermute | solution.py:823
  256.1 77.3 %collective-permute-start.41 = (bf16[2,4,144,768]{3,2,1,0:T(8,128)(2,1)}, bf16[2,4,144,768]{3,2,1,0:T(8,128)(2,1)S(1)}, u32[]{:S(2)}, u32[]{:S(2)}) collective-permute-start(bf16[2,4,144,768]{3,2,1,0:T(8,128)(2,1)} %get-tuple-element.189), channel_id=1, source_target_pairs={{0,8},{4,12},{8,0},{12,4},{16,24},{20,28},{24,16},{28,20},{1,9},{5... | collective-permute-start | bytes 5308424 | tf_op jit(solution)/shard_map/ppermute | solution.py:823
  299.8 186.4 %all-gather.9.cloned.1.call-start = ((), (), s32[]{:S(2)}) async-start(), calls=%async_computation.2 | async-start | bytes 1216512 | tf_op jit(solution)/shard_map/all_gather | solution.py:1179
  369.7 31.2 %collective-permute-start.47 = (bf16[2,304,1152]{2,1,0:T(8,128)(2,1)S(1)}, bf16[2,304,1152]{2,1,0:T(8,128)(2,1)S(1)}, u32[]{:S(2)}, u32[]{:S(2)}) collective-permute-start(bf16[2,304,1152]{2,1,0:T(8,128)(2,1)S(1)} %pad_maximum_fusion.4), channel_id=1, source_target_pairs={{0,16},{4,20},{8,24},{12,28},{16,0},{20,4},{24,8},{28,12},{1,17},{... | collective-permute-start | bytes 4202504 | tf_op jit(solution)/shard_map/ppermute | solution.py:823
  370.7 37.6 %collective-permute-start.46 = (bf16[2,368,1152]{2,1,0:T(8,128)(2,1)S(1)}, bf16[2,368,1152]{2,1,0:T(8,128)(2,1)S(1)}, u32[]{:S(2)}, u32[]{:S(2)}) collective-permute-start(bf16[2,368,1152]{2,1,0:T(8,128)(2,1)S(1)} %pad_maximum_fusion.3), channel_id=1, source_target_pairs={{0,8},{4,12},{8,0},{12,4},{16,24},{20,28},{24,16},{28,20},{1,9},{5... | collective-permute-start | bytes 5087240 | tf_op jit(solution)/shard_map/ppermute | solution.py:823
  372.1 37.6 %collective-permute-start.48 = (bf16[288,768]{1,0:T(8,128)(2,1)S(1)}, bf16[288,768]{1,0:T(8,128)(2,1)}, u32[]{:S(2)}, u32[]{:S(2)}) collective-permute-start(bf16[288,768]{1,0:T(8,128)(2,1)S(1)} %get-tuple-element.275), channel_id=1, source_target_pairs={{0,1},{1,2},{2,3},{3,0},{4,5},{5,6},{6,7},{7,4},{8,9},{9,10},{10,1... | collective-permute-start | bytes 1327112 | tf_op jit(solution)/shard_map/ppermute | solution.py:887
  373.0 39.2 %collective-permute-start.49 = (bf16[288,768]{1,0:T(8,128)(2,1)S(1)}, bf16[288,768]{1,0:T(8,128)(2,1)}, u32[]{:S(2)}, u32[]{:S(2)}) collective-permute-start(bf16[288,768]{1,0:T(8,128)(2,1)S(1)} %get-tuple-element.274), channel_id=1, source_target_pairs={{0,2},{1,3},{2,0},{3,1},{4,6},{5,7},{6,4},{7,5},{8,10},{9,11},{10,... | collective-permute-start | bytes 1327112 | tf_op jit(solution)/shard_map/ppermute | solution.py:887
  374.6 37.5 %collective-permute-start.50 = (bf16[288,768]{1,0:T(8,128)(2,1)S(1)}, bf16[288,768]{1,0:T(8,128)(2,1)}, u32[]{:S(2)}, u32[]{:S(2)}) collective-permute-start(bf16[288,768]{1,0:T(8,128)(2,1)S(1)} %get-tuple-element.273), channel_id=1, source_target_pairs={{0,3},{1,0},{2,1},{3,2},{4,7},{5,4},{6,5},{7,6},{8,11},{9,8},{10,9... | collective-permute-start | bytes 1327112 | tf_op jit(solution)/shard_map/ppermute | solution.py:887
  417.6 31.2 %collective-permute-start.60 = (bf16[288,768]{1,0:T(8,128)(2,1)S(1)}, bf16[288,768]{1,0:T(8,128)(2,1)S(1)}, u32[]{:S(2)}, u32[]{:S(2)}) collective-permute-start(bf16[288,768]{1,0:T(8,128)(2,1)S(1)} %fusion.15.refs_0_), channel_id=1, source_target_pairs={{0,4},{4,0},{8,12},{12,8},{16,20},{20,16},{24,28},{28,24},{1,5},{5... | collective-permute-start | bytes 1327112 | tf_op jit(solution)/shard_map/ppermute | solution.py:823
  444.1 35.2 %collective-permute-start.56 = (bf16[144,1152]{1,0:T(8,128)(2,1)S(1)}, bf16[144,1152]{1,0:T(8,128)(2,1)S(1)}, u32[]{:S(2)}, u32[]{:S(2)}) collective-permute-start(bf16[144,1152]{1,0:T(8,128)(2,1)S(1)} %get-tuple-element.280), channel_id=1, source_target_pairs={{0,2},{1,3},{2,0},{3,1},{4,6},{5,7},{6,4},{7,5},{8,10},{9,11},{10,... | collective-permute-start | bytes 995336 | tf_op jit(solution)/shard_map/ppermute | solution.py:887
  448.8 36.1 %collective-permute-start.61 = (bf16[288,768]{1,0:T(8,128)(2,1)}, bf16[288,768]{1,0:T(8,128)(2,1)}, u32[]{:S(2)}, u32[]{:S(2)}) collective-permute-start(bf16[288,768]{1,0:T(8,128)(2,1)} %collective-permute-done.53.refs_1_), channel_id=1, source_target_pairs={{0,4},{4,0},{8,12},{12,8},{16,20},{20,16},{24,28},{28,24},{1,5},{5... | collective-permute-start | bytes 1327112 | tf_op jit(solution)/shard_map/ppermute | solution.py:823
  451.5 33.4 %collective-permute-start.62 = (bf16[288,768]{1,0:T(8,128)(2,1)}, bf16[288,768]{1,0:T(8,128)(2,1)}, u32[]{:S(2)}, u32[]{:S(2)}) collective-permute-start(bf16[288,768]{1,0:T(8,128)(2,1)} %collective-permute-done.54.refs_2_), channel_id=1, source_target_pairs={{0,4},{4,0},{8,12},{12,8},{16,20},{20,16},{24,28},{28,24},{1,5},{5... | collective-permute-start | bytes 1327112 | tf_op jit(solution)/shard_map/ppermute | solution.py:823
  451.6 33.3 %collective-permute-start.57 = (bf16[144,1152]{1,0:T(8,128)(2,1)S(1)}, bf16[144,1152]{1,0:T(8,128)(2,1)}, u32[]{:S(2)}, u32[]{:S(2)}) collective-permute-start(bf16[144,1152]{1,0:T(8,128)(2,1)S(1)} %get-tuple-element.279), channel_id=1, source_target_pairs={{0,3},{1,0},{2,1},{3,2},{4,7},{5,4},{6,5},{7,6},{8,11},{9,8},{10,9... | collective-permute-start | bytes 995336 | tf_op jit(solution)/shard_map/ppermute | solution.py:887
  453.4 31.5 %collective-permute-start.63 = (bf16[144,768]{1,0:T(8,128)(2,1)S(1)}, bf16[144,768]{1,0:T(8,128)(2,1)}, u32[]{:S(2)}, u32[]{:S(2)}) collective-permute-start(bf16[144,768]{1,0:T(8,128)(2,1)S(1)} %collective-permute-done.58.refs_3_), channel_id=1, source_target_pairs={{0,4},{4,0},{8,12},{12,8},{16,20},{20,16},{24,28},{28,24},{1,5},{5... | collective-permute-start | bytes 663560 | tf_op jit(solution)/shard_map/ppermute | solution.py:823
  (111 other events, 1156.9 us)
Sparse Core Ops, SparseCore 0:
  10.2 38.2 all-gather.10
  83.9 51.2 all-gather.12
  234.6 65.1 all-gather.6
  302.6 65.1 reduce-scatter.1
  413.5 70.7 all-gather.8

commit v6 on v5

--- a/solution.py
+++ b/solution.py
@@ -578,7 +578,7 @@
             pltpu.SemaphoreType.DMA((COLUMNS,)),
         ],
         compiler_params=params(),
-        cost_estimate=cost(20),
+        cost_estimate=cost(5),
     )(where, x, mod, cos, sin, joint, project, *arrived)
 
 
@@ -1102,14 +1102,19 @@
             preferred_element_type=f32,
         ).astype(bf16)
 
-    late = lax.all_gather(
-        jnp.concatenate([by_slot(late_sums), lifted], axis=1), ("bucket", "fsdp"), axis=0, tiled=True
-    )
+    def near_rows(rows):
+        return jnp.concatenate([rows] + over_z(rows), axis=0)
+
+    late_rows = jnp.concatenate([by_slot(late_sums), lifted], axis=1)
+    late_k = over_z(late_rows)
 
     count = fsdp_count
     hiddens = [step["hidden_turned"] for step in steps]
     backs = [step["pair_back"] for step in steps]
     pair_theirs = pair_grad_call(count, where, turned, backs)
+    late_k, pair_theirs = after((late_k, pair_theirs))
+    near_late = jnp.concatenate([late_rows] + late_k, axis=0)
+    late = lax.all_gather(near_late, "bucket", axis=0, tiled=True)
     if fast:
         pair_other = swap(pair_theirs, 1)
         feed_back = after(feed_back, pair_theirs)
@@ -1140,15 +1145,26 @@
         pair_once, attn_theirs, middle_back = after((pair_once, attn_theirs, middle_back))
         attn_other = swap(attn_theirs, 1)
     grad_inputs, early_sums = first_back_call(joint_back, inputs, middle_back, mod_one, weight)
+    near_early = near_rows(by_slot(early_sums))
     if fast:
         a0, a2, b0, b1 = pair_once
         a0, b0, grad_inputs = after((a0, b0, grad_inputs))
-        pair_parts, branch_back = after((halve_twice((a0, a2, b0, b1)), branch_back))
+        pair_parts, branch_back, near_early = after(
+            (halve_twice((a0, a2, b0, b1)), branch_back, near_early)
+        )
         pair_z = send_z(pair_parts)
+    early = lax.all_gather(near_early, "bucket", axis=0, tiled=True)
+    slope_rows = times_transposed(
+        jnp.concatenate([near_early, near_late[:, : 4 * WIDTH]], axis=1), modulate_weight
+    ).reshape(fsdp_count, slots, height)
+    slopes = [slope_rows[0]] + [
+        lax.ppermute(slope_rows[count - by], "fsdp", shifts(count, by)) for by in range(1, count)
+    ]
+    if fast:
         attn_cut = attn_grad_call(
             count, where, first, attended, joint_back, branch_back, attn_other
         )
-        attn_cut, down_part = after((attn_cut, down_part))
+        attn_cut, down_part, slopes = after((attn_cut, down_part, slopes))
         down_cut = cut_down(down_part, first_part(down_rows))
         cut = [
             jnp.concatenate([attn.reshape(2, -1, WIDTH), down], axis=1)
@@ -1176,27 +1192,21 @@
             count, where, first, attended, joint_back, branch_back, jnp.zeros_like(attn_theirs)
         )
         attn_sums = sum_whole(uncut(attn_cut), attn_theirs)
-    early = lax.all_gather(by_slot(early_sums), ("bucket", "fsdp"), axis=0, tiled=True)
     if fast:
         early, attn_sum = after((early, attn_sum))
         both_sums = direct(jnp.concatenate([attn_sum, down_total], axis=0))
     all_back = jnp.concatenate([early, late[:, : 4 * WIDTH]], axis=1)
     all_lifted = lax.dynamic_slice_in_dim(late, 4 * WIDTH + place * height, height, 1)
     modulate_gradient = contract_rows(all_lifted, all_back)
-    group_back = lax.dynamic_slice_in_dim(
-        all_back, bucket * fsdp_count * slots, fsdp_count * slots, 0
-    )
-    slope_rows = times_transposed(group_back, modulate_weight)
     pair_grad = place_call(
         place_pair_kernel, where, pair_sums, (struct(gate_weight.shape, f32),) * 2
     )
     if fast:
-        both_sums, pair_grad, modulate_gradient, slope_rows = after(
-            (both_sums, pair_grad, modulate_gradient, slope_rows)
-        )
+        both_sums, pair_grad, modulate_gradient = after((both_sums, pair_grad, modulate_gradient))
         attn_sums = down_sums = both(both_sums)
+    slopes = jnp.stack(slopes)
     condition_slope = (
-        to_group(slope_rows.reshape(fsdp_count, slots, height), fsdp_count, place)
+        jnp.stack([pick(slopes, (place + count - j) % count) for j in range(count)])
         .transpose(1, 0, 2)
         .reshape(slots, WIDTH)
     )

time: 549 us -> 538 us (0.980)
  waiting for transfers between devices: 193 us -> 163 us
  starting transfers between devices: 72.6 us -> 92.9 us
    all_gather x2, waiting for transfers between devices: 33.1 us -> 4.79 us  [the longest x1 4.77 us: on_device(): late = lax.all_gather(near_late, 'bucket', axis=0, tiled=True)]
    ppermute x3 -> x9, waiting for transfers between devices: 10.5 us -> 25.1 us  [over_z(): lax.ppermute(piece, 'fsdp', shifts(count, by))]
    ppermute x6, waiting for transfers between devices: 25.3 us -> 15.3 us  [send_z(): lax.ppermute(pick(parts, (place + by) % count), 'fsdp', shifts(count, by))]
    ppermute x6, starting transfers between devices: 9.22 us -> 17 us  [send_z(): lax.ppermute(pick(parts, (place + by) % count), 'fsdp', shifts(count, by))]
    ppermute x54, starting transfers between devices: 49 us -> 56.7 us  [swap(): return lax.ppermute(array, 'bucket', across(bit))]
    unnamed x112 -> x131, local copies, waits for them, and re-layouts: 8.89 us -> 11.1 us
  transfers between devices with their start and end apart: 80 -> 86, of which waited for: 28 -> 34; matrix products, arithmetic and copies ran while one was open for 10% -> 10% of each run, Pallas kernels for 28% -> 31%
where the time goes in v6:
time: 538 us; the launch traced here: 532 us
  Pallas kernels  188 us (35%)
  waiting for transfers between devices  163 us (30%)
  starting transfers between devices  92.9 us (17%)
  local copies, waits for them, and re-layouts  31.4 us (6%)
  other arithmetic  23.8 us (4%)
  between operations  16.4 us (3%)
  matrix products  15.7 us (3%)
    ppermute x54, waiting for transfers between devices, swap(): return lax.ppermute(array, 'bucket', across(bit))  87.2 us
    ppermute x54, starting transfers between devices, swap(): return lax.ppermute(array, 'bucket', across(bit))  56.7 us
    pallas_call x3, Pallas kernels, ffn_call(): pl.pallas_call(functools.partial(ffn_kernel, count, js, names), grid=(len...  52.6 us
    pallas_call x4, Pallas kernels, by_column(): pl.pallas_call(call, out_shape=shapes, grid_spec=pltpu.PrefetchScalarGrid...  39.1 us
    ppermute x9, waiting for transfers between devices, over_z(): lax.ppermute(piece, 'fsdp', shifts(count, by))  25.1 us
    pallas_call x1, Pallas kernels, attend_back_call(): pl.pallas_call(attend_back_kernel, grid=(tokens // BLOCK,), out_shape=str...  24 us
    pallas_call x1, Pallas kernels, first_call(): pl.pallas_call(functools.partial(first_kernel, count), out_shape=(struct(...  18.8 us
    ppermute x6, starting transfers between devices, send_z(): lax.ppermute(pick(parts, (place + by) % count), 'fsdp', shifts(count, by))  17 us
  transfers between devices with their start and end apart: 86, of which 34 were waited for; matrix products, arithmetic and copies ran while one was open for 10% of the time, Pallas kernels for 31%

profile of v6, /device:TPU:25, one launch (start us, length us, event | category | flops | bytes accessed | tf_op | source)
XLA Modules:
  0.0 531.6 jit_solution(11854119359881985111)
XLA Ops:
  22.4 11.5 %collective-permute-done.4 = f32[8,2304]{1,0:T(8,128)S(1)} collective-permute-done((f32[8,2304]{1,0:T(8,128)S(1)}, f32[8,2304]{1,0:T(8,128)S(1)}, u32[]{:S(2)}, u32[]{:S(2)}) %collective-permute-start.4) | collective-permute-done | bytes 73760 | tf_op jit(solution)/shard_map/ppermute | solution.py:990
  33.8 14.6 %all-gather.11.cloned.1.call-done = bf16[576,1152]{1,0:T(8,128)(2,1)} async-done(((bf16[144,1152]{1,0:T(8,128)(2,1)}), bf16[576,1152]{1,0:T(8,128)(2,1)}) %all-gather.11.cloned.1.call-update) | async-done | bytes 1327120 | tf_op jit(solution)/shard_map/all_gather | solution.py:842
  66.2 10.4 %collective-permute-done.9 = bf16[96,1152]{1,0:T(8,128)(2,1)S(1)} collective-permute-done((bf16[96,1152]{1,0:T(8,128)(2,1)S(1)}, bf16[96,1152]{1,0:T(8,128)(2,1)S(1)}, u32[]{:S(2)}, u32[]{:S(2)}) %collective-permute-start.9) | collective-permute-done | bytes 221216 | tf_op jit(solution)/shard_map/ppermute | solution.py:836
  108.5 18.8 %shard_map.187 = (bf16[1152,512]{1,0:T(8,128)(2,1)}, bf16[512,1152]{1,0:T(8,128)(2,1)}, bf16[512,1152]{1,0:T(8,128)(2,1)}, bf16[512,1152]{1,0:T(8,128)(2,1)}, bf16[4,1152,1152]{2,1,0:T(8,128)(2,1)}) custom-call(s32[7]{0:T(128)} %stack.87.where_ref.refs_0_, bf16[512,1152]{1,0:T(8,128)(2,1)} %x_ref.2, f32[8,2304]{1,0:T(8,128)} %fusion.37.mod_ref, ...), custom_call_target="tpu_custom_call" | custom-call | flops 5000000000 | bytes 1000 | tf_op jit(solution)/shard_map/pallas_call | solution.py:567
  131.8 12.6 %shard_map.188 = (bf16[1152,512]{1,0:T(8,128)(2,1)}, f32[512,1152]{1,0:T(8,128)}, f32[512,1152]{1,0:T(8,128)}, bf16[512,1152]{1,0:T(8,128)(2,1)}) custom-call(bf16[512,1152]{1,0:T(8,128)(2,1)} %get-tuple-element.153.query_ref, bf16[512,1152]{1,0:T(8,128)(2,1)} %get-tuple-element.154.keys_ref, bf16[512,1152]{1,0:T(8,128)(2,1)} %get-tuple-element.155.values_ref, ...), custom_call_target="tpu_custom_call" | custom-call | flops 2000000000 | bytes 1000 | tf_op jit(solution)/shard_map/pallas_call | solution.py:587
  154.7 12.4 %shard_map.189 = (bf16[1,768,512]{2,1,0:T(8,128)(2,1)}, bf16[1,2,512,768]{3,2,1,0:T(8,128)(2,1)}, bf16[1152,512]{1,0:T(8,128)(2,1)}, bf16[512,1152]{1,0:T(8,128)...) custom-call(s32[7]{0:T(128)} %stack.87.where_ref.refs_0_, bf16[512,1152]{1,0:T(8,128)(2,1)} %get-tuple-element.161.refs_1_, ...), custom_call_target="tpu_custom_call" | custom-call | flops 2000000000 | bytes 1000 | tf_op jit(solution)/shard_map/pallas_call | solution.py:676
  167.1 11.3 %collective-permute-done.31.refs_8_ = bf16[3,288,768]{2,1,0:T(8,128)(2,1)} collective-permute-done((bf16[3,288,768]{2,1,0:T(8,128)(2,1)S(1)}, bf16[3,288,768]{2,1,0:T(8,128)(2,1)}, u32[]{:S(2)}, u32[]{:S(2)}) %collective-permute-start.31) | collective-permute-done | bytes 1327136 | tf_op jit(solution)/shard_map/ppermute | solution.py:823
  185.4 23.3 %shard_map.190 = (bf16[2,768,512]{2,1,0:T(8,128)(2,1)}, bf16[2,2,512,768]{3,2,1,0:T(8,128)(2,1)}, f32[512,1152]{1,0:T(8,128)}, f32[512,1152]{1,0:T(8,128)}) custom-call(s32[7]{0:T(128)} %stack.87.where_ref.refs_0_, bf16[512,1152]{1,0:T(8,128)(2,1)} %get-tuple-element.161.refs_1_, bf16[512,1152]{1,0:T(8,128)(2,1)} %get-tuple-element.201.refs_2_.refs_5_.refs_3_, ...), custom_call_target="tpu_custom_call" | custom-call | flops 24000000000 | bytes 1000 | tf_op jit(solution)/shard_map/pallas_call | solution.py:676
  212.9 16.9 %shard_map.191 = (bf16[1,768,512]{2,1,0:T(8,128)(2,1)}, bf16[1,2,512,768]{3,2,1,0:T(8,128)(2,1)}, bf16[512,1152]{1,0:T(8,128)(2,1)}, f32[512,1152]{1,0:T(8,128)}...) custom-call(s32[7]{0:T(128)} %stack.87.where_ref.refs_0_, bf16[512,1152]{1,0:T(8,128)(2,1)} %get-tuple-element.161.refs_1_, ...), custom_call_target="tpu_custom_call" | custom-call | flops 12000000000 | bytes 1000 | tf_op jit(solution)/shard_map/pallas_call | solution.py:676
  233.8 9.0 %shard_map.192 = bf16[4,4,288,768]{3,2,1,0:T(8,128)(2,1)} custom-call(s32[7]{0:T(128)} %stack.87.where_ref.refs_0_, bf16[1152,512]{1,0:T(8,128)(2,1)} %get-tuple-element.183.turned_ref, bf16[1,2,512,768]{3,2,1,0:T(8,128)(2,1)} %get-tuple-element.184.own_ref, bf16[2,2,512,768]{3,2,1,0:T(8,128)(2,1)} %get-tuple-element.185.near_ref, ...), custom_call_target="tpu_custom_call" | custom-call | flops 3000000000 | bytes 1000 | tf_op jit(solution)/shard_map/pallas_call | solution.py:696
  245.1 6.3 %shard_map.193 = bf16[4,4,96,1152]{3,2,1,0:T(8,128)(2,1)} custom-call(s32[7]{0:T(128)} %stack.87.where_ref.refs_0_, bf16[1,768,512]{2,1,0:T(8,128)(2,1)} %get-tuple-element.189.refs_0_, bf16[2,768,512]{2,1,0:T(8,128)(2,1)} %get-tuple-element.190.refs_1_, bf16[1,768,512]{2,1,0:T(8,128)(2,1)} %get-tuple-element.191.refs_2_, ...), custom_call_target="tpu_custom_call" | custom-call | flops 3000000000 | bytes 1000 | tf_op jit(solution)/shard_map/pallas_call | solution.py:745
  255.7 11.0 %shard_map.194 = (bf16[2,4,144,768]{3,2,1,0:T(8,128)(2,1)}, bf16[2,4,144,768]{3,2,1,0:T(8,128)(2,1)}, bf16[2,4,144,768]{3,2,1,0:T(8,128)(2,1)}, bf16[2,4,144,768]{3,2,1,0:T(8,128)(2,1)}) custom-call(s32[7]{0:T(128)} %stack.87.where_ref.refs_0_, bf16[1152,512]{1,0:T(8,128)(2,1)} %get-tuple-element.183.turned_ref, ...), custom_call_target="tpu_custom_call" | custom-call | flops 3000000000 | bytes 1000 | tf_op jit(solution)/shard_map/pallas_call | solution.py:696
  270.6 7.4 %shard_map.195 = bf16[4,4,96,1152]{3,2,1,0:T(8,128)(2,1)} custom-call(s32[7]{0:T(128)} %stack.87.where_ref.refs_0_, bf16[1,768,512]{2,1,0:T(8,128)(2,1)} %get-tuple-element.189.refs_0_, bf16[2,768,512]{2,1,0:T(8,128)(2,1)} %get-tuple-element.190.refs_1_, bf16[1,768,512]{2,1,0:T(8,128)(2,1)} %get-tuple-element.191.refs_2_, ...), custom_call_target="tpu_custom_call" | custom-call | flops 3000000000 | bytes 1000 | tf_op jit(solution)/shard_map/pallas_call | solution.py:745
  283.1 24.0 %shard_map.196.joint_back_ref = bf16[512,3456]{1,0:T(8,128)(2,1)} custom-call(bf16[512,1152]{1,0:T(8,128)(2,1)} %get-tuple-element.153.query_ref, bf16[512,1152]{1,0:T(8,128)(2,1)} %get-tuple-element.154.keys_ref, bf16[512,1152]{1,0:T(8,128)(2,1)} %get-tuple-element.155.values_ref, bf16[512,1152]{1,0:T(8,128)(2,1)} %get-tuple-element.222.branch_back_ref, ...), custom_call_target="tpu_custom_call" | custom-call | flops 8000000000 | bytes 1000 | tf_op jit(solution)/shard_map/pallas_call | solution.py:769
  307.0 8.9 %shard_map.197 = bf16[4,4,144,1152]{3,2,1,0:T(8,128)(2,1)} custom-call(s32[7]{0:T(128)} %stack.87.where_ref.refs_0_, bf16[1152,512]{1,0:T(8,128)(2,1)} %get-tuple-element.196.first_ref, bf16[1152,512]{1,0:T(8,128)(2,1)} %get-tuple-element.197.attended_ref, bf16[512,3456]{1,0:T(8,128)(2,1)} %shard_map.196.joint_back_ref, ...), custom_call_target="tpu_custom_call" | custom-call | flops 3000000000 | bytes 1000 | tf_op jit(solution)/shard_map/pallas_call | solution.py:696
  321.6 13.1 %shard_map.198 = (f32[512,1152]{1,0:T(8,128)}, f32[8,2304]{1,0:T(8,128)}) custom-call(bf16[512,3456]{1,0:T(8,128)(2,1)} %shard_map.196.joint_back_ref, bf16[512,1152]{1,0:T(8,128)(2,1)} %x_ref.2, f32[512,1152]{1,0:T(8,128)} %get-tuple-element.214.middle_back_ref, f32[8,2304]{1,0:T(8,128)} %fusion.37.mod_ref, bf16[4,1152,1152]{2,1,0:T(8,128)(2,1)} %get-tuple-element.160.weight), custom_call_target="tpu_custom_call" | custom-call | flops 2000000000 | bytes 1000 | tf_op jit(solution)/shard_map/pallas_call | solution.py:792
  354.4 10.3 %shard_map.199 = (bf16[2,4,80,1152]{3,2,1,0:T(8,128)(2,1)}, bf16[2,4,80,1152]{3,2,1,0:T(8,128)(2,1)}, bf16[2,4,64,1152]{3,2,1,0:T(8,128)(2,1)}, bf16[2,4,64,1152]{3,2,1,0:T(8,128)(2,1)}) custom-call(s32[7]{0:T(128)} %stack.87.where_ref.refs_0_, bf16[1152,512]{1,0:T(8,128)(2,1)} %get-tuple-element.196.first_ref, ...), custom_call_target="tpu_custom_call" | custom-call | flops 3000000000 | bytes 1000 | tf_op jit(solution)/shard_map/pallas_call | solution.py:696
  373.3 24.1 %collective-permute-done.56 = bf16[2,304,1152]{2,1,0:T(8,128)(2,1)S(1)} collective-permute-done((bf16[2,304,1152]{2,1,0:T(8,128)(2,1)S(1)}, bf16[2,304,1152]{2,1,0:T(8,128)(2,1)S(1)}, u32[]{:S(2)}, u32[]{:S(2)}) %collective-permute-start.56) | collective-permute-done | bytes 1400864 | tf_op jit(solution)/shard_map/ppermute | solution.py:823
  398.6 6.4 %collective-permute-done.55 = bf16[2,368,1152]{2,1,0:T(8,128)(2,1)S(1)} collective-permute-done((bf16[2,368,1152]{2,1,0:T(8,128)(2,1)S(1)}, bf16[2,368,1152]{2,1,0:T(8,128)(2,1)S(1)}, u32[]{:S(2)}, u32[]{:S(2)}) %collective-permute-start.55) | collective-permute-done | bytes 1695776 | tf_op jit(solution)/shard_map/ppermute | solution.py:823
  426.2 6.3 %collective-permute-done.62.refs_1_ = bf16[288,768]{1,0:T(8,128)(2,1)} collective-permute-done((bf16[288,768]{1,0:T(8,128)(2,1)S(1)}, bf16[288,768]{1,0:T(8,128)(2,1)}, u32[]{:S(2)}, u32[]{:S(2)}) %collective-permute-start.62) | collective-permute-done | bytes 442400 | tf_op jit(solution)/shard_map/ppermute | solution.py:823
  438.0 6.3 %collective-permute-start.64 = (bf16[144,1152]{1,0:T(8,128)(2,1)}, bf16[144,1152]{1,0:T(8,128)(2,1)}, u32[]{:S(2)}, u32[]{:S(2)}) collective-permute-start(bf16[144,1152]{1,0:T(8,128)(2,1)} %get-tuple-element.297), channel_id=1, source_target_pairs={{0,1},{1,2},{2,3},{3,0},{4,5},{5,6},{6,7},{7,4},{8,9},{9,10},{10,1... | collective-permute-start | bytes 995336 | tf_op jit(solution)/shard_map/ppermute | solution.py:887
  462.8 14.0 %collective-permute-done.65 = bf16[144,1152]{1,0:T(8,128)(2,1)} collective-permute-done((bf16[144,1152]{1,0:T(8,128)(2,1)S(1)}, bf16[144,1152]{1,0:T(8,128)(2,1)}, u32[]{:S(2)}, u32[]{:S(2)}) %collective-permute-start.65) | collective-permute-done | bytes 331808 | tf_op jit(solution)/shard_map/ppermute | solution.py:887
  485.3 6.0 %fusion = f32[288,6912]{1,0:T(8,128)} fusion(bf16[256,4608]{1,0:T(8,128)(2,1)S(1)} %slice-done, bf16[256,2304]{1,0:T(8,128)(2,1)} %all-gather.9.cloned.1.call-done, bf16[256,5760]{1,0:T(8,128)(2,1)} %all-gather.7.cloned.1.call-done, s32[]{:T(128)S(6)} %select_n.236), kind=kOutput, calls=%fused_computation.2 | convolution fusion | flops 1026293760 | bytes 11698180 | tf_op jit(solution)/shard_map/dot_general | solution.py:48
  497.3 12.0 %collective-permute-done.76.refs_3_ = bf16[240,1152]{1,0:T(8,128)(2,1)} collective-permute-done((bf16[240,1152]{1,0:T(8,128)(2,1)S(1)}, bf16[240,1152]{1,0:T(8,128)(2,1)}, u32[]{:S(2)}, u32[]{:S(2)}) %collective-permute-start.76) | collective-permute-done | bytes 552992 | tf_op jit(solution)/shard_map/ppermute | solution.py:823
  (388 shorter events, 218.5 us)
Async XLA Ops:
  7.2 41.3 %all-gather.11.cloned.1.call-start = ((), (), s32[]{:S(2)}) async-start(), calls=%async_computation.4 | async-start | bytes 1658880 | tf_op jit(solution)/shard_map/all_gather | solution.py:842
  9.2 136.4 %all-gather.13.cloned.1.call-start = ((), (), s32[]{:S(2)}) async-start(), calls=%async_computation.5 | async-start | bytes 2211840 | tf_op jit(solution)/shard_map/all_gather | solution.py:842
  62.5 38.1 %collective-permute-start.13 = (bf16[3,144,1152]{2,1,0:T(8,128)(2,1)}, bf16[3,144,1152]{2,1,0:T(8,128)(2,1)}, u32[]{:S(2)}, u32[]{:S(2)}) collective-permute-start(bf16[3,144,1152]{2,1,0:T(8,128)(2,1)} %pad_maximum_fusion.5.refs_0_), channel_id=1, source_target_pairs={{0,4},{4,0},{8,12},{12,8},{16,20},{20,16},{24,28},{28,24},{1,5},{5... | collective-permute-start | bytes 2985992 | tf_op jit(solution)/shard_map/ppermute | solution.py:823
  76.7 206.1 %all-gather.7.cloned.1.call-start = ((), (), s32[]{:S(2)}) async-start(), calls=%async_computation.1 | async-start | bytes 3317760 | tf_op jit(solution)/shard_map/all_gather | solution.py:1117
  99.4 28.9 %collective-permute-start.22 = (bf16[3,96,1152]{2,1,0:T(8,128)(2,1)S(1)}, bf16[3,96,1152]{2,1,0:T(8,128)(2,1)S(1)}, u32[]{:S(2)}, u32[]{:S(2)}) collective-permute-start(bf16[3,96,1152]{2,1,0:T(8,128)(2,1)S(1)} %pad_maximum_fusion.7.refs_10_.refs_12_.refs_17_), channel_id=1, source_target_pairs={{0,8},{4,12},{8,0},{12,4},{16,24},{20,28},{24,16},{28,20},{1,9},{5... | collective-permute-start | bytes 1990664 | tf_op jit(solution)/shard_map/ppermute | solution.py:823
  100.6 27.7 %collective-permute-start.23 = (bf16[3,96,1152]{2,1,0:T(8,128)(2,1)S(1)}, bf16[3,96,1152]{2,1,0:T(8,128)(2,1)S(1)}, u32[]{:S(2)}, u32[]{:S(2)}) collective-permute-start(bf16[3,96,1152]{2,1,0:T(8,128)(2,1)S(1)} %pad_maximum_fusion.7.refs_10_.refs_12_.refs_17_), channel_id=1, source_target_pairs={{0,16},{4,20},{8,24},{12,28},{16,0},{20,4},{24,8},{28,12},{1,17},{... | collective-permute-start | bytes 1990664 | tf_op jit(solution)/shard_map/ppermute | solution.py:823
  147.6 30.8 %collective-permute-start.31 = (bf16[3,288,768]{2,1,0:T(8,128)(2,1)S(1)}, bf16[3,288,768]{2,1,0:T(8,128)(2,1)}, u32[]{:S(2)}, u32[]{:S(2)}) collective-permute-start(bf16[3,288,768]{2,1,0:T(8,128)(2,1)S(1)} %pad_maximum_fusion.3.refs_8_), channel_id=1, source_target_pairs={{0,8},{4,12},{8,0},{12,4},{16,24},{20,28},{24,16},{28,20},{1,9},{5... | collective-permute-start | bytes 3981320 | tf_op jit(solution)/shard_map/ppermute | solution.py:823
  147.9 30.5 %collective-permute-start.32 = (bf16[3,288,768]{2,1,0:T(8,128)(2,1)S(1)}, bf16[3,288,768]{2,1,0:T(8,128)(2,1)}, u32[]{:S(2)}, u32[]{:S(2)}) collective-permute-start(bf16[3,288,768]{2,1,0:T(8,128)(2,1)S(1)} %pad_maximum_fusion.3.refs_8_), channel_id=1, source_target_pairs={{0,16},{4,20},{8,24},{12,28},{16,0},{20,4},{24,8},{28,12},{1,17},{... | collective-permute-start | bytes 3981320 | tf_op jit(solution)/shard_map/ppermute | solution.py:823
  181.8 26.9 %collective-permute-start.35 = (bf16[3,144,768]{2,1,0:T(8,128)(2,1)S(1)}, bf16[3,144,768]{2,1,0:T(8,128)(2,1)S(1)}, u32[]{:S(2)}, u32[]{:S(2)}) collective-permute-start(bf16[3,144,768]{2,1,0:T(8,128)(2,1)S(1)} %slice.128), channel_id=1, source_target_pairs={{0,16},{4,20},{8,24},{12,28},{16,0},{20,4},{24,8},{28,12},{1,17},{... | collective-permute-start | bytes 1990664 | tf_op jit(solution)/shard_map/ppermute | solution.py:823
  244.9 119.8 %reduce-scatter.2.cloned.1.call-start = ((), (), s32[]{:S(2)}) async-start(), calls=%async_computation.2 | async-start | bytes 4423680 | tf_op jit(solution)/shard_map/reduce_scatter | solution.py:1135
  266.7 49.2 %collective-permute-start.44 = (bf16[2,4,144,768]{3,2,1,0:T(8,128)(2,1)}, bf16[2,4,144,768]{3,2,1,0:T(8,128)(2,1)}, u32[]{:S(2)}, u32[]{:S(2)}) collective-permute-start(bf16[2,4,144,768]{3,2,1,0:T(8,128)(2,1)} %get-tuple-element.199), channel_id=1, source_target_pairs={{0,8},{4,12},{8,0},{12,4},{16,24},{20,28},{24,16},{28,20},{1,9},{5... | collective-permute-start | bytes 5308424 | tf_op jit(solution)/shard_map/ppermute | solution.py:823
  267.9 50.9 %collective-permute-start.45 = (bf16[2,4,144,768]{3,2,1,0:T(8,128)(2,1)}, bf16[2,4,144,768]{3,2,1,0:T(8,128)(2,1)S(1)}, u32[]{:S(2)}, u32[]{:S(2)}) collective-permute-start(bf16[2,4,144,768]{3,2,1,0:T(8,128)(2,1)} %get-tuple-element.200), channel_id=1, source_target_pairs={{0,16},{4,20},{8,24},{12,28},{16,0},{20,4},{24,8},{28,12},{1,17},{... | collective-permute-start | bytes 5308424 | tf_op jit(solution)/shard_map/ppermute | solution.py:823
  282.8 199.7 %all-gather.9.cloned.1.call-start = ((), (), s32[]{:S(2)}) async-start(), calls=%async_computation.3 | async-start | bytes 1327104 | tf_op jit(solution)/shard_map/all_gather | solution.py:1156
  320.1 34.2 %collective-permute-start.51 = (bf16[4,4,144,1152]{3,2,1,0:T(8,128)(2,1)}, bf16[4,4,144,1152]{3,2,1,0:T(8,128)(2,1)}, u32[]{:S(2)}, u32[]{:S(2)}) collective-permute-start(bf16[4,4,144,1152]{3,2,1,0:T(8,128)(2,1)} %shard_map.197), channel_id=1, source_target_pairs={{0,4},{4,0},{8,12},{12,8},{16,20},{20,16},{24,28},{28,24},{1,5},{5... | collective-permute-start | bytes 15925256 | tf_op jit(solution)/shard_map/ppermute | solution.py:823
  320.5 27.5 %collective-permute-start.47 = (bf16[4,144,768]{2,1,0:T(8,128)(2,1)}, bf16[4,144,768]{2,1,0:T(8,128)(2,1)}, u32[]{:S(2)}, u32[]{:S(2)}) collective-permute-start(bf16[4,144,768]{2,1,0:T(8,128)(2,1)} %get-tuple-element.220), channel_id=1, source_target_pairs={{0,8},{4,12},{8,0},{12,4},{16,24},{20,28},{24,16},{28,20},{1,9},{5... | collective-permute-start | bytes 2654216 | tf_op jit(solution)/shard_map/ppermute | solution.py:823
  321.4 28.0 %collective-permute-start.46 = (bf16[4,144,768]{2,1,0:T(8,128)(2,1)}, bf16[4,144,768]{2,1,0:T(8,128)(2,1)S(1)}, u32[]{:S(2)}, u32[]{:S(2)}) collective-permute-start(bf16[4,144,768]{2,1,0:T(8,128)(2,1)} %get-tuple-element.218), channel_id=1, source_target_pairs={{0,16},{4,20},{8,24},{12,28},{16,0},{20,4},{24,8},{28,12},{1,17},{... | collective-permute-start | bytes 2654216 | tf_op jit(solution)/shard_map/ppermute | solution.py:823
  366.4 31.0 %collective-permute-start.56 = (bf16[2,304,1152]{2,1,0:T(8,128)(2,1)S(1)}, bf16[2,304,1152]{2,1,0:T(8,128)(2,1)S(1)}, u32[]{:S(2)}, u32[]{:S(2)}) collective-permute-start(bf16[2,304,1152]{2,1,0:T(8,128)(2,1)S(1)} %pad_maximum_fusion.2), channel_id=1, source_target_pairs={{0,16},{4,20},{8,24},{12,28},{16,0},{20,4},{24,8},{28,12},{1,17},{... | collective-permute-start | bytes 4202504 | tf_op jit(solution)/shard_map/ppermute | solution.py:823
  368.0 37.0 %collective-permute-start.55 = (bf16[2,368,1152]{2,1,0:T(8,128)(2,1)S(1)}, bf16[2,368,1152]{2,1,0:T(8,128)(2,1)S(1)}, u32[]{:S(2)}, u32[]{:S(2)}) collective-permute-start(bf16[2,368,1152]{2,1,0:T(8,128)(2,1)S(1)} %pad_maximum_fusion.1), channel_id=1, source_target_pairs={{0,8},{4,12},{8,0},{12,4},{16,24},{20,28},{24,16},{28,20},{1,9},{5... | collective-permute-start | bytes 5087240 | tf_op jit(solution)/shard_map/ppermute | solution.py:823
  369.2 37.2 %collective-permute-start.57 = (bf16[288,768]{1,0:T(8,128)(2,1)S(1)}, bf16[288,768]{1,0:T(8,128)(2,1)}, u32[]{:S(2)}, u32[]{:S(2)}) collective-permute-start(bf16[288,768]{1,0:T(8,128)(2,1)S(1)} %get-tuple-element.291), channel_id=1, source_target_pairs={{0,1},{1,2},{2,3},{3,0},{4,5},{5,6},{6,7},{7,4},{8,9},{9,10},{10,1... | collective-permute-start | bytes 1327112 | tf_op jit(solution)/shard_map/ppermute | solution.py:887
  372.2 35.4 %collective-permute-start.58 = (bf16[288,768]{1,0:T(8,128)(2,1)S(1)}, bf16[288,768]{1,0:T(8,128)(2,1)}, u32[]{:S(2)}, u32[]{:S(2)}) collective-permute-start(bf16[288,768]{1,0:T(8,128)(2,1)S(1)} %get-tuple-element.290), channel_id=1, source_target_pairs={{0,2},{1,3},{2,0},{3,1},{4,6},{5,7},{6,4},{7,5},{8,10},{9,11},{10,... | collective-permute-start | bytes 1327112 | tf_op jit(solution)/shard_map/ppermute | solution.py:887
  372.2 35.4 %collective-permute-start.59 = (bf16[288,768]{1,0:T(8,128)(2,1)S(1)}, bf16[288,768]{1,0:T(8,128)(2,1)}, u32[]{:S(2)}, u32[]{:S(2)}) collective-permute-start(bf16[288,768]{1,0:T(8,128)(2,1)S(1)} %get-tuple-element.289), channel_id=1, source_target_pairs={{0,3},{1,0},{2,1},{3,2},{4,7},{5,4},{6,5},{7,6},{8,11},{9,8},{10,9... | collective-permute-start | bytes 1327112 | tf_op jit(solution)/shard_map/ppermute | solution.py:887
  412.2 39.4 %collective-permute-start.69 = (bf16[288,768]{1,0:T(8,128)(2,1)S(1)}, bf16[288,768]{1,0:T(8,128)(2,1)S(1)}, u32[]{:S(2)}, u32[]{:S(2)}) collective-permute-start(bf16[288,768]{1,0:T(8,128)(2,1)S(1)} %fusion.18.refs_0_), channel_id=1, source_target_pairs={{0,4},{4,0},{8,12},{12,8},{16,20},{20,16},{24,28},{28,24},{1,5},{5... | collective-permute-start | bytes 1327112 | tf_op jit(solution)/shard_map/ppermute | solution.py:823
  444.3 32.5 %collective-permute-start.65 = (bf16[144,1152]{1,0:T(8,128)(2,1)S(1)}, bf16[144,1152]{1,0:T(8,128)(2,1)}, u32[]{:S(2)}, u32[]{:S(2)}) collective-permute-start(bf16[144,1152]{1,0:T(8,128)(2,1)S(1)} %get-tuple-element.296), channel_id=1, source_target_pairs={{0,2},{1,3},{2,0},{3,1},{4,6},{5,7},{6,4},{7,5},{8,10},{9,11},{10,... | collective-permute-start | bytes 995336 | tf_op jit(solution)/shard_map/ppermute | solution.py:887
  451.6 28.3 %collective-permute-start.70 = (bf16[288,768]{1,0:T(8,128)(2,1)}, bf16[288,768]{1,0:T(8,128)(2,1)}, u32[]{:S(2)}, u32[]{:S(2)}) collective-permute-start(bf16[288,768]{1,0:T(8,128)(2,1)} %collective-permute-done.62.refs_1_), channel_id=1, source_target_pairs={{0,4},{4,0},{8,12},{12,8},{16,20},{20,16},{24,28},{28,24},{1,5},{5... | collective-permute-start | bytes 1327112 | tf_op jit(solution)/shard_map/ppermute | solution.py:823
  (127 other events, 1266.0 us)
Sparse Core Ops, SparseCore 0:
  10.2 38.2 all-gather.10
  76.8 49.5 all-gather.12
  245.0 37.7 all-gather.6
  285.5 67.4 reduce-scatter.1
  408.3 33.2 all-gather.8

commit v7 on v6

--- a/solution.py
+++ b/solution.py
@@ -578,7 +578,7 @@
             pltpu.SemaphoreType.DMA((COLUMNS,)),
         ],
         compiler_params=params(),
-        cost_estimate=cost(5),
+        cost_estimate=cost(20),
     )(where, x, mod, cos, sin, joint, project, *arrived)
 
 
@@ -1145,14 +1145,18 @@
         pair_once, attn_theirs, middle_back = after((pair_once, attn_theirs, middle_back))
         attn_other = swap(attn_theirs, 1)
     grad_inputs, early_sums = first_back_call(joint_back, inputs, middle_back, mod_one, weight)
-    near_early = near_rows(by_slot(early_sums))
     if fast:
         a0, a2, b0, b1 = pair_once
         a0, b0, grad_inputs = after((a0, b0, grad_inputs))
-        pair_parts, branch_back, near_early = after(
-            (halve_twice((a0, a2, b0, b1)), branch_back, near_early)
-        )
-        pair_z = send_z(pair_parts)
+        pair_parts, branch_back = after((halve_twice((a0, a2, b0, b1)), branch_back))
+        attn_cut = attn_grad_call(
+            count, where, first, attended, joint_back, branch_back, attn_other
+        )
+        attn_cut, down_part, pair_parts, early_sums = after(
+            (attn_cut, down_part, pair_parts, early_sums)
+        )
+        pair_sum = lax.psum_scatter(pair_parts, "fsdp", scatter_dimension=0, tiled=False)
+    near_early = near_rows(by_slot(early_sums))
     early = lax.all_gather(near_early, "bucket", axis=0, tiled=True)
     slope_rows = times_transposed(
         jnp.concatenate([near_early, near_late[:, : 4 * WIDTH]], axis=1), modulate_weight
@@ -1161,19 +1165,14 @@
         lax.ppermute(slope_rows[count - by], "fsdp", shifts(count, by)) for by in range(1, count)
     ]
     if fast:
-        attn_cut = attn_grad_call(
-            count, where, first, attended, joint_back, branch_back, attn_other
-        )
-        attn_cut, down_part, slopes = after((attn_cut, down_part, slopes))
         down_cut = cut_down(down_part, first_part(down_rows))
-        cut = [
+        send_x, keep_x, send_y, keep_y = (
             jnp.concatenate([attn.reshape(2, -1, WIDTH), down], axis=1)
             for attn, down in zip(attn_cut, down_cut, strict=True)
-        ]
-        once, pair_z = after((halve_once(cut), pair_z))
-        pair_sum = total_z(pair_parts, pair_z)
+        )
+        keep_x, keep_y, slopes = after((keep_x, keep_y, slopes))
+        (a0, a2, b0, b1), pair_sum = after((halve_once((send_x, keep_x, send_y, keep_y)), pair_sum))
         pair_x, pair_y = swap(pair_sum, 2), swap(pair_sum, 4)
-        a0, a2, b0, b1 = once
         ahead, behind = add(a0, swap(a2, 4)), add(b0, swap(b1, 2))
         at, other_at = (part.shape[1] * part.shape[2] for part in (attn_cut[0], attn_cut[2]))
         attn_parts = jnp.concatenate(

time: 538 us -> 519 us (0.965)
  starting transfers between devices: 92.9 us -> 80 us
    ppermute x9, waiting for transfers between devices: 25.1 us -> 9.83 us  [over_z(): lax.ppermute(piece, 'fsdp', shifts(count, by))]
    ppermute x6 -> x3, starting transfers between devices: 17 us -> 4.37 us  [send_z(): lax.ppermute(pick(parts, (place + by) % count), 'fsdp', shifts(count, by))]
    ppermute x54, waiting for transfers between devices: 87.2 us -> 94.4 us  [swap(): return lax.ppermute(array, 'bucket', across(bit))]
    convert_element_type x8, other arithmetic: 11.1 us -> 4.4 us  [add(): return (left.astype(f32) + right.astype(f32)).astype(bf16)]
    ppermute x6, waiting for transfers between devices: 14.5 us -> 20.3 us  [modulation_parts(): lax.ppermute(pick(parts, (place + by) % fsdp_count), 'fsdp', shifts(fsdp_...]
    unnamed x131 -> x117, local copies, waits for them, and re-layouts: 11.1 us -> 11.5 us
    ppermute x6 -> x3, waiting for transfers between devices: 15.3 us -> 15.2 us  [send_z(): lax.ppermute(pick(parts, (place + by) % count), 'fsdp', shifts(count, by))]
  transfers between devices with their start and end apart: 86 -> 84, of which waited for: 34 -> 33; matrix products, arithmetic and copies ran while one was open for 10% -> 9% of each run, Pallas kernels for 31% -> 32%
where the time goes in v7:
time: 519 us; the launch traced here: 513 us
  Pallas kernels  189 us (36%)
  waiting for transfers between devices  162 us (31%)
  starting transfers between devices  80 us (15%)
  local copies, waits for them, and re-layouts  32.4 us (6%)
  other arithmetic  18.5 us (4%)
  between operations  16.8 us (3%)
  matrix products  14.7 us (3%)
    ppermute x54, waiting for transfers between devices, swap(): return lax.ppermute(array, 'bucket', across(bit))  94.4 us
    pallas_call x3, Pallas kernels, ffn_call(): pl.pallas_call(functools.partial(ffn_kernel, count, js, names), grid=(len...  52.6 us
    ppermute x54, starting transfers between devices, swap(): return lax.ppermute(array, 'bucket', across(bit))  52.4 us
    pallas_call x4, Pallas kernels, by_column(): pl.pallas_call(call, out_shape=shapes, grid_spec=pltpu.PrefetchScalarGrid...  39.3 us
    pallas_call x1, Pallas kernels, attend_back_call(): pl.pallas_call(attend_back_kernel, grid=(tokens // BLOCK,), out_shape=str...  24 us
    ppermute x6, waiting for transfers between devices, modulation_parts(): lax.ppermute(pick(parts, (place + by) % fsdp_count), 'fsdp', shifts(fsdp_...  20.3 us
    pallas_call x1, Pallas kernels, first_call(): pl.pallas_call(functools.partial(first_kernel, count), out_shape=(struct(...  18.9 us
    ppermute x3, waiting for transfers between devices, send_z(): lax.ppermute(pick(parts, (place + by) % count), 'fsdp', shifts(count, by))  15.2 us
  transfers between devices with their start and end apart: 84, of which 33 were waited for; matrix products, arithmetic and copies ran while one was open for 9% of the time, Pallas kernels for 32%

profile of v7, /device:TPU:25, one launch (start us, length us, event | category | flops | bytes accessed | tf_op | source)
XLA Modules:
  0.0 513.3 jit_solution(16586143268207143039)
XLA Ops:
  23.4 10.6 %collective-permute-done.4 = f32[8,2304]{1,0:T(8,128)S(1)} collective-permute-done((f32[8,2304]{1,0:T(8,128)S(1)}, f32[8,2304]{1,0:T(8,128)S(1)}, u32[]{:S(2)}, u32[]{:S(2)}) %collective-permute-start.4) | collective-permute-done | bytes 73760 | tf_op jit(solution)/shard_map/ppermute | solution.py:990
  34.6 13.9 %all-gather.11.cloned.1.call-done = bf16[576,1152]{1,0:T(8,128)(2,1)} async-done(((bf16[144,1152]{1,0:T(8,128)(2,1)}), bf16[576,1152]{1,0:T(8,128)(2,1)}) %all-gather.11.cloned.1.call-update) | async-done | bytes 1327120 | tf_op jit(solution)/shard_map/all_gather | solution.py:842
  65.3 9.8 %collective-permute-done.9 = bf16[96,1152]{1,0:T(8,128)(2,1)} collective-permute-done((bf16[96,1152]{1,0:T(8,128)(2,1)}, bf16[96,1152]{1,0:T(8,128)(2,1)}, u32[]{:S(2)}, u32[]{:S(2)}) %collective-permute-start.9) | collective-permute-done | bytes 221216 | tf_op jit(solution)/shard_map/ppermute | solution.py:836
  98.1 18.9 %shard_map.187 = (bf16[1152,512]{1,0:T(8,128)(2,1)}, bf16[512,1152]{1,0:T(8,128)(2,1)}, bf16[512,1152]{1,0:T(8,128)(2,1)}, bf16[512,1152]{1,0:T(8,128)(2,1)}, bf16[4,1152,1152]{2,1,0:T(8,128)(2,1)}) custom-call(s32[7]{0:T(128)} %stack.87.where_ref.refs_0_, bf16[512,1152]{1,0:T(8,128)(2,1)} %x_ref.2, f32[8,2304]{1,0:T(8,128)} %fusion.39.mod_ref, ...), custom_call_target="tpu_custom_call" | custom-call | flops 20000000000 | bytes 1000 | tf_op jit(solution)/shard_map/pallas_call | solution.py:567
  117.0 7.0 %collective-permute-done.19 = f32[8,4608]{1,0:T(8,128)S(1)} collective-permute-done((f32[8,4608]{1,0:T(8,128)S(1)}, f32[8,4608]{1,0:T(8,128)S(1)}, u32[]{:S(2)}, u32[]{:S(2)}) %collective-permute-start.19) | collective-permute-done | bytes 147488 | tf_op jit(solution)/shard_map/ppermute | solution.py:990
  126.7 12.5 %shard_map.188 = (bf16[1152,512]{1,0:T(8,128)(2,1)}, f32[512,1152]{1,0:T(8,128)}, f32[512,1152]{1,0:T(8,128)}, bf16[512,1152]{1,0:T(8,128)(2,1)}) custom-call(bf16[512,1152]{1,0:T(8,128)(2,1)} %get-tuple-element.154.query_ref, bf16[512,1152]{1,0:T(8,128)(2,1)} %get-tuple-element.155.keys_ref, bf16[512,1152]{1,0:T(8,128)(2,1)} %get-tuple-element.156.values_ref, ...), custom_call_target="tpu_custom_call" | custom-call | flops 2000000000 | bytes 1000 | tf_op jit(solution)/shard_map/pallas_call | solution.py:587
  150.9 12.4 %shard_map.189 = (bf16[1,768,512]{2,1,0:T(8,128)(2,1)}, bf16[1,2,512,768]{3,2,1,0:T(8,128)(2,1)}, bf16[1152,512]{1,0:T(8,128)(2,1)}, bf16[512,1152]{1,0:T(8,128)...) custom-call(s32[7]{0:T(128)} %stack.87.where_ref.refs_0_, bf16[512,1152]{1,0:T(8,128)(2,1)} %get-tuple-element.162.refs_1_, ...), custom_call_target="tpu_custom_call" | custom-call | flops 2000000000 | bytes 1000 | tf_op jit(solution)/shard_map/pallas_call | solution.py:676
  163.4 10.5 %collective-permute-done.31.refs_8_ = bf16[3,288,768]{2,1,0:T(8,128)(2,1)} collective-permute-done((bf16[3,288,768]{2,1,0:T(8,128)(2,1)S(1)}, bf16[3,288,768]{2,1,0:T(8,128)(2,1)}, u32[]{:S(2)}, u32[]{:S(2)}) %collective-permute-start.31) | collective-permute-done | bytes 1327136 | tf_op jit(solution)/shard_map/ppermute | solution.py:823
  181.4 23.3 %shard_map.190 = (bf16[2,768,512]{2,1,0:T(8,128)(2,1)}, bf16[2,2,512,768]{3,2,1,0:T(8,128)(2,1)}, f32[512,1152]{1,0:T(8,128)}, f32[512,1152]{1,0:T(8,128)}) custom-call(s32[7]{0:T(128)} %stack.87.where_ref.refs_0_, bf16[512,1152]{1,0:T(8,128)(2,1)} %get-tuple-element.162.refs_1_, bf16[512,1152]{1,0:T(8,128)(2,1)} %get-tuple-element.202.refs_2_.refs_5_.refs_3_, ...), custom_call_target="tpu_custom_call" | custom-call | flops 24000000000 | bytes 1000 | tf_op jit(solution)/shard_map/pallas_call | solution.py:676
  208.9 16.9 %shard_map.191 = (bf16[1,768,512]{2,1,0:T(8,128)(2,1)}, bf16[1,2,512,768]{3,2,1,0:T(8,128)(2,1)}, bf16[512,1152]{1,0:T(8,128)(2,1)}, f32[512,1152]{1,0:T(8,128)}...) custom-call(s32[7]{0:T(128)} %stack.87.where_ref.refs_0_, bf16[512,1152]{1,0:T(8,128)(2,1)} %get-tuple-element.162.refs_1_, ...), custom_call_target="tpu_custom_call" | custom-call | flops 12000000000 | bytes 1000 | tf_op jit(solution)/shard_map/pallas_call | solution.py:676
  230.2 9.0 %shard_map.192 = bf16[4,4,288,768]{3,2,1,0:T(8,128)(2,1)} custom-call(s32[7]{0:T(128)} %stack.87.where_ref.refs_0_, bf16[1152,512]{1,0:T(8,128)(2,1)} %get-tuple-element.184.turned_ref, bf16[1,2,512,768]{3,2,1,0:T(8,128)(2,1)} %get-tuple-element.185.own_ref, bf16[2,2,512,768]{3,2,1,0:T(8,128)(2,1)} %get-tuple-element.186.near_ref, ...), custom_call_target="tpu_custom_call" | custom-call | flops 3000000000 | bytes 1000 | tf_op jit(solution)/shard_map/pallas_call | solution.py:696
  252.1 11.0 %shard_map.194 = (bf16[2,4,144,768]{3,2,1,0:T(8,128)(2,1)}, bf16[2,4,144,768]{3,2,1,0:T(8,128)(2,1)}, bf16[2,4,144,768]{3,2,1,0:T(8,128)(2,1)}, bf16[2,4,144,768]{3,2,1,0:T(8,128)(2,1)}) custom-call(s32[7]{0:T(128)} %stack.87.where_ref.refs_0_, bf16[1152,512]{1,0:T(8,128)(2,1)} %get-tuple-element.184.turned_ref, ...), custom_call_target="tpu_custom_call" | custom-call | flops 3000000000 | bytes 1000 | tf_op jit(solution)/shard_map/pallas_call | solution.py:696
  267.2 7.4 %shard_map.195 = bf16[4,4,96,1152]{3,2,1,0:T(8,128)(2,1)} custom-call(s32[7]{0:T(128)} %stack.87.where_ref.refs_0_, bf16[1,768,512]{2,1,0:T(8,128)(2,1)} %get-tuple-element.190.refs_0_, bf16[2,768,512]{2,1,0:T(8,128)(2,1)} %get-tuple-element.191.refs_1_, bf16[1,768,512]{2,1,0:T(8,128)(2,1)} %get-tuple-element.192.refs_2_, ...), custom_call_target="tpu_custom_call" | custom-call | flops 3000000000 | bytes 1000 | tf_op jit(solution)/shard_map/pallas_call | solution.py:745
  279.7 24.0 %shard_map.196.joint_back_ref = bf16[512,3456]{1,0:T(8,128)(2,1)} custom-call(bf16[512,1152]{1,0:T(8,128)(2,1)} %get-tuple-element.154.query_ref, bf16[512,1152]{1,0:T(8,128)(2,1)} %get-tuple-element.155.keys_ref, bf16[512,1152]{1,0:T(8,128)(2,1)} %get-tuple-element.156.values_ref, bf16[512,1152]{1,0:T(8,128)(2,1)} %get-tuple-element.222.branch_back_ref, ...), custom_call_target="tpu_custom_call" | custom-call | flops 8000000000 | bytes 1000 | tf_op jit(solution)/shard_map/pallas_call | solution.py:769
  303.7 8.9 %shard_map.197 = bf16[4,4,144,1152]{3,2,1,0:T(8,128)(2,1)} custom-call(s32[7]{0:T(128)} %stack.87.where_ref.refs_0_, bf16[1152,512]{1,0:T(8,128)(2,1)} %get-tuple-element.197.first_ref, bf16[1152,512]{1,0:T(8,128)(2,1)} %get-tuple-element.198.attended_ref, bf16[512,3456]{1,0:T(8,128)(2,1)} %shard_map.196.joint_back_ref, ...), custom_call_target="tpu_custom_call" | custom-call | flops 3000000000 | bytes 1000 | tf_op jit(solution)/shard_map/pallas_call | solution.py:696
  316.4 13.2 %shard_map.198 = (f32[512,1152]{1,0:T(8,128)}, f32[8,2304]{1,0:T(8,128)}) custom-call(bf16[512,3456]{1,0:T(8,128)(2,1)} %shard_map.196.joint_back_ref, bf16[512,1152]{1,0:T(8,128)(2,1)} %x_ref.2, f32[512,1152]{1,0:T(8,128)} %get-tuple-element.215.middle_back_ref, f32[8,2304]{1,0:T(8,128)} %fusion.39.mod_ref, bf16[4,1152,1152]{2,1,0:T(8,128)(2,1)} %get-tuple-element.161.weight), custom_call_target="tpu_custom_call" | custom-call | flops 2000000000 | bytes 1000 | tf_op jit(solution)/shard_map/pallas_call | solution.py:792
  329.6 6.5 %collective-permute-done.47 = bf16[4,144,768]{2,1,0:T(8,128)(2,1)S(1)} collective-permute-done((bf16[4,144,768]{2,1,0:T(8,128)(2,1)S(1)}, bf16[4,144,768]{2,1,0:T(8,128)(2,1)S(1)}, u32[]{:S(2)}, u32[]{:S(2)}) %collective-permute-start.47) | collective-permute-done | bytes 884768 | tf_op jit(solution)/shard_map/ppermute | solution.py:823
  338.2 10.4 %shard_map.199 = (bf16[2,4,80,1152]{3,2,1,0:T(8,128)(2,1)}, bf16[2,4,80,1152]{3,2,1,0:T(8,128)(2,1)}, bf16[2,4,64,1152]{3,2,1,0:T(8,128)(2,1)}, bf16[2,4,64,1152]{3,2,1,0:T(8,128)(2,1)}) custom-call(s32[7]{0:T(128)} %stack.87.where_ref.refs_0_, bf16[1152,512]{1,0:T(8,128)(2,1)} %get-tuple-element.197.first_ref, ...), custom_call_target="tpu_custom_call" | custom-call | flops 3000000000 | bytes 1000 | tf_op jit(solution)/shard_map/pallas_call | solution.py:696
  364.3 18.8 %collective-permute-done.56 = bf16[2,304,1152]{2,1,0:T(8,128)(2,1)S(1)} collective-permute-done((bf16[2,304,1152]{2,1,0:T(8,128)(2,1)S(1)}, bf16[2,304,1152]{2,1,0:T(8,128)(2,1)S(1)}, u32[]{:S(2)}, u32[]{:S(2)}) %collective-permute-start.56) | collective-permute-done | bytes 1400864 | tf_op jit(solution)/shard_map/ppermute | solution.py:823
  384.3 6.8 %collective-permute-done.55 = bf16[2,368,1152]{2,1,0:T(8,128)(2,1)S(1)} collective-permute-done((bf16[2,368,1152]{2,1,0:T(8,128)(2,1)S(1)}, bf16[2,368,1152]{2,1,0:T(8,128)(2,1)S(1)}, u32[]{:S(2)}, u32[]{:S(2)}) %collective-permute-start.55) | collective-permute-done | bytes 1695776 | tf_op jit(solution)/shard_map/ppermute | solution.py:823
  399.0 8.3 %collective-permute-done.58 = bf16[304,1152]{1,0:T(8,128)(2,1)} collective-permute-done((bf16[304,1152]{1,0:T(8,128)(2,1)}, bf16[304,1152]{1,0:T(8,128)(2,1)}, u32[]{:S(2)}, u32[]{:S(2)}) %collective-permute-start.58) | collective-permute-done | bytes 700448 | tf_op jit(solution)/shard_map/ppermute | solution.py:823
  418.4 6.3 %collective-permute-done.60.refs_2_ = bf16[288,768]{1,0:T(8,128)(2,1)} collective-permute-done((bf16[288,768]{1,0:T(8,128)(2,1)}, bf16[288,768]{1,0:T(8,128)(2,1)}, u32[]{:S(2)}, u32[]{:S(2)}) %collective-permute-start.60) | collective-permute-done | bytes 442400 | tf_op jit(solution)/shard_map/ppermute | solution.py:823
  443.7 15.2 %collective-permute-done.62 = bf16[144,1152]{1,0:T(8,128)(2,1)} collective-permute-done((bf16[144,1152]{1,0:T(8,128)(2,1)S(1)}, bf16[144,1152]{1,0:T(8,128)(2,1)}, u32[]{:S(2)}, u32[]{:S(2)}) %collective-permute-start.62) | collective-permute-done | bytes 331808 | tf_op jit(solution)/shard_map/ppermute | solution.py:887
  479.3 11.2 %collective-permute-done.73.refs_3_ = bf16[240,1152]{1,0:T(8,128)(2,1)} collective-permute-done((bf16[240,1152]{1,0:T(8,128)(2,1)S(1)}, bf16[240,1152]{1,0:T(8,128)(2,1)}, u32[]{:S(2)}, u32[]{:S(2)}) %collective-permute-start.73) | collective-permute-done | bytes 552992 | tf_op jit(solution)/shard_map/ppermute | solution.py:823
  (370 shorter events, 204.0 us)
Async XLA Ops:
  7.2 41.3 %all-gather.11.cloned.1.call-start = ((), (), s32[]{:S(2)}) async-start(), calls=%async_computation.6 | async-start | bytes 1658880 | tf_op jit(solution)/shard_map/all_gather | solution.py:842
  9.2 131.8 %all-gather.13.cloned.1.call-start = ((), (), s32[]{:S(2)}) async-start(), calls=%async_computation.7 | async-start | bytes 2211840 | tf_op jit(solution)/shard_map/all_gather | solution.py:842
  82.5 197.0 %all-gather.7.cloned.1.call-start = ((), (), s32[]{:S(2)}) async-start(), calls=%async_computation.2 | async-start | bytes 3317760 | tf_op jit(solution)/shard_map/all_gather | solution.py:1117
  93.7 30.3 %collective-permute-start.19 = (f32[8,4608]{1,0:T(8,128)S(1)}, f32[8,4608]{1,0:T(8,128)S(1)}, u32[]{:S(2)}, u32[]{:S(2)}) collective-permute-start(f32[8,4608]{1,0:T(8,128)S(1)} %get-tuple-element.306), channel_id=1, source_target_pairs={{0,2},{1,3},{2,0},{3,1},{4,6},{5,7},{6,4},{7,5},{8,10},{9,11},{10,... | collective-permute-start | bytes 442376 | tf_op jit(solution)/shard_map/ppermute | solution.py:990
  95.5 28.5 %collective-permute-start.20 = (f32[8,4608]{1,0:T(8,128)S(1)}, f32[8,4608]{1,0:T(8,128)S(1)}, u32[]{:S(2)}, u32[]{:S(2)}) collective-permute-start(f32[8,4608]{1,0:T(8,128)S(1)} %get-tuple-element.305), channel_id=1, source_target_pairs={{0,3},{1,0},{2,1},{3,2},{4,7},{5,4},{6,5},{7,6},{8,11},{9,8},{10,9... | collective-permute-start | bytes 442376 | tf_op jit(solution)/shard_map/ppermute | solution.py:990
  97.0 27.0 %collective-permute-start.22 = (bf16[3,96,1152]{2,1,0:T(8,128)(2,1)S(1)}, bf16[3,96,1152]{2,1,0:T(8,128)(2,1)S(1)}, u32[]{:S(2)}, u32[]{:S(2)}) collective-permute-start(bf16[3,96,1152]{2,1,0:T(8,128)(2,1)S(1)} %pad_maximum_fusion.7.refs_10_.refs_12_.refs_17_), channel_id=1, source_target_pairs={{0,8},{4,12},{8,0},{12,4},{16,24},{20,28},{24,16},{28,20},{1,9},{5... | collective-permute-start | bytes 1990664 | tf_op jit(solution)/shard_map/ppermute | solution.py:823
  97.3 26.7 %collective-permute-start.23 = (bf16[3,96,1152]{2,1,0:T(8,128)(2,1)S(1)}, bf16[3,96,1152]{2,1,0:T(8,128)(2,1)S(1)}, u32[]{:S(2)}, u32[]{:S(2)}) collective-permute-start(bf16[3,96,1152]{2,1,0:T(8,128)(2,1)S(1)} %pad_maximum_fusion.7.refs_10_.refs_12_.refs_17_), channel_id=1, source_target_pairs={{0,16},{4,20},{8,24},{12,28},{16,0},{20,4},{24,8},{28,12},{1,17},{... | collective-permute-start | bytes 1990664 | tf_op jit(solution)/shard_map/ppermute | solution.py:823
  143.0 30.8 %collective-permute-start.31 = (bf16[3,288,768]{2,1,0:T(8,128)(2,1)S(1)}, bf16[3,288,768]{2,1,0:T(8,128)(2,1)}, u32[]{:S(2)}, u32[]{:S(2)}) collective-permute-start(bf16[3,288,768]{2,1,0:T(8,128)(2,1)S(1)} %pad_maximum_fusion.4.refs_8_), channel_id=1, source_target_pairs={{0,8},{4,12},{8,0},{12,4},{16,24},{20,28},{24,16},{28,20},{1,9},{5... | collective-permute-start | bytes 3981320 | tf_op jit(solution)/shard_map/ppermute | solution.py:823
  143.8 30.5 %collective-permute-start.32 = (bf16[3,288,768]{2,1,0:T(8,128)(2,1)S(1)}, bf16[3,288,768]{2,1,0:T(8,128)(2,1)}, u32[]{:S(2)}, u32[]{:S(2)}) collective-permute-start(bf16[3,288,768]{2,1,0:T(8,128)(2,1)S(1)} %pad_maximum_fusion.4.refs_8_), channel_id=1, source_target_pairs={{0,16},{4,20},{8,24},{12,28},{16,0},{20,4},{24,8},{28,12},{1,17},{... | collective-permute-start | bytes 3981320 | tf_op jit(solution)/shard_map/ppermute | solution.py:823
  177.8 26.9 %collective-permute-start.35 = (bf16[3,144,768]{2,1,0:T(8,128)(2,1)S(1)}, bf16[3,144,768]{2,1,0:T(8,128)(2,1)S(1)}, u32[]{:S(2)}, u32[]{:S(2)}) collective-permute-start(bf16[3,144,768]{2,1,0:T(8,128)(2,1)S(1)} %slice.128), channel_id=1, source_target_pairs={{0,16},{4,20},{8,24},{12,28},{16,0},{20,4},{24,8},{28,12},{1,17},{... | collective-permute-start | bytes 1990664 | tf_op jit(solution)/shard_map/ppermute | solution.py:823
  179.1 25.6 %collective-permute-start.36 = (bf16[3,144,768]{2,1,0:T(8,128)(2,1)S(1)}, bf16[3,144,768]{2,1,0:T(8,128)(2,1)S(1)}, u32[]{:S(2)}, u32[]{:S(2)}) collective-permute-start(bf16[3,144,768]{2,1,0:T(8,128)(2,1)S(1)} %slice.129), channel_id=1, source_target_pairs={{0,8},{4,12},{8,0},{12,4},{16,24},{20,28},{24,16},{28,20},{1,9},{5... | collective-permute-start | bytes 1990664 | tf_op jit(solution)/shard_map/ppermute | solution.py:823
  241.3 107.3 %reduce-scatter.3.cloned.1.call-start = ((), (), s32[]{:S(2)}) async-start(), calls=%async_computation.3 | async-start | bytes 4423680 | tf_op jit(solution)/shard_map/reduce_scatter | solution.py:1135
  263.1 49.5 %collective-permute-start.44 = (bf16[2,4,144,768]{3,2,1,0:T(8,128)(2,1)}, bf16[2,4,144,768]{3,2,1,0:T(8,128)(2,1)S(1)}, u32[]{:S(2)}, u32[]{:S(2)}) collective-permute-start(bf16[2,4,144,768]{3,2,1,0:T(8,128)(2,1)} %get-tuple-element.200), channel_id=1, source_target_pairs={{0,8},{4,12},{8,0},{12,4},{16,24},{20,28},{24,16},{28,20},{1,9},{5... | collective-permute-start | bytes 5308424 | tf_op jit(solution)/shard_map/ppermute | solution.py:823
  263.9 49.1 %collective-permute-start.45 = (bf16[2,4,144,768]{3,2,1,0:T(8,128)(2,1)}, bf16[2,4,144,768]{3,2,1,0:T(8,128)(2,1)S(1)}, u32[]{:S(2)}, u32[]{:S(2)}) collective-permute-start(bf16[2,4,144,768]{3,2,1,0:T(8,128)(2,1)} %get-tuple-element.201), channel_id=1, source_target_pairs={{0,16},{4,20},{8,24},{12,28},{16,0},{20,4},{24,8},{28,12},{1,17},{... | collective-permute-start | bytes 5308424 | tf_op jit(solution)/shard_map/ppermute | solution.py:823
  279.5 112.4 %reduce-scatter.5.cloned.1.call-start = ((), (), s32[]{:S(2)}) async-start(), calls=%async_computation.5 | async-start | bytes 2211840 | tf_op jit(solution)/shard_map/reduce_scatter | solution.py:1158
  352.3 112.7 %all-gather.9.cloned.1.call-start = ((), (), s32[]{:S(2)}) async-start(), calls=%async_computation.4 | async-start | bytes 1327104 | tf_op jit(solution)/shard_map/all_gather | solution.py:1160
  352.5 30.5 %collective-permute-start.56 = (bf16[2,304,1152]{2,1,0:T(8,128)(2,1)S(1)}, bf16[2,304,1152]{2,1,0:T(8,128)(2,1)S(1)}, u32[]{:S(2)}, u32[]{:S(2)}) collective-permute-start(bf16[2,304,1152]{2,1,0:T(8,128)(2,1)S(1)} %pad_maximum_fusion.3), channel_id=1, source_target_pairs={{0,16},{4,20},{8,24},{12,28},{16,0},{20,4},{24,8},{28,12},{1,17},{... | collective-permute-start | bytes 4202504 | tf_op jit(solution)/shard_map/ppermute | solution.py:823
  354.1 36.9 %collective-permute-start.55 = (bf16[2,368,1152]{2,1,0:T(8,128)(2,1)S(1)}, bf16[2,368,1152]{2,1,0:T(8,128)(2,1)S(1)}, u32[]{:S(2)}, u32[]{:S(2)}) collective-permute-start(bf16[2,368,1152]{2,1,0:T(8,128)(2,1)S(1)} %pad_maximum_fusion.2), channel_id=1, source_target_pairs={{0,8},{4,12},{8,0},{12,4},{16,24},{20,28},{24,16},{28,20},{1,9},{5... | collective-permute-start | bytes 5087240 | tf_op jit(solution)/shard_map/ppermute | solution.py:823
  395.2 29.5 %collective-permute-start.60 = (bf16[288,768]{1,0:T(8,128)(2,1)}, bf16[288,768]{1,0:T(8,128)(2,1)}, u32[]{:S(2)}, u32[]{:S(2)}) collective-permute-start(bf16[288,768]{1,0:T(8,128)(2,1)} %bitcast.130), channel_id=1, source_target_pairs={{0,16},{4,20},{8,24},{12,28},{16,0},{20,4},{24,8},{28,12},{1,17},{... | collective-permute-start | bytes 1327112 | tf_op jit(solution)/shard_map/ppermute | solution.py:823
  395.6 37.3 %collective-permute-start.66 = (bf16[288,768]{1,0:T(8,128)(2,1)}, bf16[288,768]{1,0:T(8,128)(2,1)S(1)}, u32[]{:S(2)}, u32[]{:S(2)}) collective-permute-start(bf16[288,768]{1,0:T(8,128)(2,1)} %bitcast.131), channel_id=1, source_target_pairs={{0,4},{4,0},{8,12},{12,8},{16,20},{20,16},{24,28},{28,24},{1,5},{5... | collective-permute-start | bytes 1327112 | tf_op jit(solution)/shard_map/ppermute | solution.py:823
  431.0 27.8 %collective-permute-start.62 = (bf16[144,1152]{1,0:T(8,128)(2,1)S(1)}, bf16[144,1152]{1,0:T(8,128)(2,1)}, u32[]{:S(2)}, u32[]{:S(2)}) collective-permute-start(bf16[144,1152]{1,0:T(8,128)(2,1)S(1)} %get-tuple-element.295), channel_id=1, source_target_pairs={{0,2},{1,3},{2,0},{3,1},{4,6},{5,7},{6,4},{7,5},{8,10},{9,11},{10,... | collective-permute-start | bytes 995336 | tf_op jit(solution)/shard_map/ppermute | solution.py:887
  432.9 29.4 %collective-permute-start.67 = (bf16[288,768]{1,0:T(8,128)(2,1)}, bf16[288,768]{1,0:T(8,128)(2,1)}, u32[]{:S(2)}, u32[]{:S(2)}) collective-permute-start(bf16[288,768]{1,0:T(8,128)(2,1)} %collective-permute-done.59.refs_1_), channel_id=1, source_target_pairs={{0,4},{4,0},{8,12},{12,8},{16,20},{20,16},{24,28},{28,24},{1,5},{5... | collective-permute-start | bytes 1327112 | tf_op jit(solution)/shard_map/ppermute | solution.py:823
  436.2 26.1 %collective-permute-start.68 = (bf16[288,768]{1,0:T(8,128)(2,1)}, bf16[288,768]{1,0:T(8,128)(2,1)}, u32[]{:S(2)}, u32[]{:S(2)}) collective-permute-start(bf16[288,768]{1,0:T(8,128)(2,1)} %collective-permute-done.60.refs_2_), channel_id=1, source_target_pairs={{0,4},{4,0},{8,12},{12,8},{16,20},{20,16},{24,28},{28,24},{1,5},{5... | collective-permute-start | bytes 1327112 | tf_op jit(solution)/shard_map/ppermute | solution.py:823
  465.2 25.4 %collective-permute-start.73 = (bf16[240,1152]{1,0:T(8,128)(2,1)S(1)}, bf16[240,1152]{1,0:T(8,128)(2,1)}, u32[]{:S(2)}, u32[]{:S(2)}) collective-permute-start(bf16[240,1152]{1,0:T(8,128)(2,1)S(1)} %constant_dynamic-update-slice_fusion.refs_0_), channel_id=1, source_target_pairs={{0,24},{4,28},{8,16},{12,20},{16,8},{20,12},{24,0},{28,4},{1,25},{... | collective-permute-start | bytes 1658888 | tf_op jit(solution)/shard_map/ppermute | solution.py:823
  (118 other events, 1129.2 us)
Sparse Core Ops, SparseCore 0:
  10.2 38.2 all-gather.10
  82.6 51.6 all-gather.12
  241.4 37.9 all-gather.6
  282.2 65.4 reduce-scatter.2
  352.4 39.4 reduce-scatter.4
  394.6 31.1 all-gather.8

commit v8 on v7

--- a/solution.py
+++ b/solution.py
@@ -1147,11 +1147,12 @@
     grad_inputs, early_sums = first_back_call(joint_back, inputs, middle_back, mod_one, weight)
     if fast:
         a0, a2, b0, b1 = pair_once
-        a0, b0, grad_inputs = after((a0, b0, grad_inputs))
-        pair_parts, branch_back = after((halve_twice((a0, a2, b0, b1)), branch_back))
+        branch_back, grad_inputs = after((branch_back, grad_inputs))
         attn_cut = attn_grad_call(
             count, where, first, attended, joint_back, branch_back, attn_other
         )
+        a0, b0, attn_cut = after((a0, b0, attn_cut))
+        pair_parts = halve_twice((a0, a2, b0, b1))
         attn_cut, down_part, pair_parts, early_sums = after(
             (attn_cut, down_part, pair_parts, early_sums)
         )
@@ -1179,8 +1180,9 @@
             [half.reshape(count, -1, WIDTH) for half in (ahead[:at], behind[:other_at])], axis=1
         )
         down_total = jnp.concatenate([ahead[at:], behind[other_at:]], axis=0)
-        attn_parts, down_total, pair_x, pair_y = after((attn_parts, down_total, pair_x, pair_y))
+        attn_parts, down_total = after((attn_parts, down_total))
         attn_z = send_z(attn_parts)
+        pair_x, pair_y, attn_z[1] = after((pair_x, pair_y, attn_z[1]))
         pair_sums = (pair_sum, pair_x, pair_y) + cross(pair_x, pair_y, first_part(height))
         attn_z, pair_sums = after((attn_z, both(pair_sums)))
         attn_sum = total_z(attn_parts, attn_z)

time: 519 us -> 513 us (0.988)
  waiting for transfers between devices: 162 us -> 144 us
  starting transfers between devices: 80 us -> 86.9 us
    ppermute x54, waiting for transfers between devices: 94.4 us -> 82.2 us  [swap(): return lax.ppermute(array, 'bucket', across(bit))]
    ppermute x3, waiting for transfers between devices: 15.2 us -> 7.81 us  [send_z(): lax.ppermute(pick(parts, (place + by) % count), 'fsdp', shifts(count, by))]
    ppermute x54, starting transfers between devices: 52.4 us -> 58.9 us  [swap(): return lax.ppermute(array, 'bucket', across(bit))]
    unnamed x117 -> x125, local copies, waits for them, and re-layouts: 11.5 us -> 10.9 us
  transfers between devices with their start and end apart: 84 -> 84, of which waited for: 33 -> 29; matrix products, arithmetic and copies ran while one was open for 9% -> 10% of each run, Pallas kernels for 32% -> 32%
where the time goes in v8:
time: 513 us; the launch traced here: 505 us
  Pallas kernels  188 us (37%)
  waiting for transfers between devices  144 us (28%)
  starting transfers between devices  86.9 us (17%)
  local copies, waits for them, and re-layouts  30.9 us (6%)
  other arithmetic  23 us (4%)
  between operations  16.7 us (3%)
  matrix products  14.8 us (3%)
    ppermute x54, waiting for transfers between devices, swap(): return lax.ppermute(array, 'bucket', across(bit))  82.2 us
    ppermute x54, starting transfers between devices, swap(): return lax.ppermute(array, 'bucket', across(bit))  58.9 us
    pallas_call x3, Pallas kernels, ffn_call(): pl.pallas_call(functools.partial(ffn_kernel, count, js, names), grid=(len...  52.6 us
    pallas_call x4, Pallas kernels, by_column(): pl.pallas_call(call, out_shape=shapes, grid_spec=pltpu.PrefetchScalarGrid...  39.1 us
    pallas_call x1, Pallas kernels, attend_back_call(): pl.pallas_call(attend_back_kernel, grid=(tokens // BLOCK,), out_shape=str...  24 us
    ppermute x6, waiting for transfers between devices, modulation_parts(): lax.ppermute(pick(parts, (place + by) % fsdp_count), 'fsdp', shifts(fsdp_...  20.3 us
    pallas_call x1, Pallas kernels, first_call(): pl.pallas_call(functools.partial(first_kernel, count), out_shape=(struct(...  18.9 us
    pallas_call x3, Pallas kernels, place_call(): pl.pallas_call(kernel, out_shape=outs, in_specs=[SMEM] + [VMEM] * len(arr...  14.7 us
  transfers between devices with their start and end apart: 84, of which 29 were waited for; matrix products, arithmetic and copies ran while one was open for 10% of the time, Pallas kernels for 32%

profile of v8, /device:TPU:25, one launch (start us, length us, event | category | flops | bytes accessed | tf_op | source)
XLA Modules:
  0.0 505.2 jit_solution(5939474536299925032)
XLA Ops:
  23.4 10.6 %collective-permute-done.4 = f32[8,2304]{1,0:T(8,128)S(1)} collective-permute-done((f32[8,2304]{1,0:T(8,128)S(1)}, f32[8,2304]{1,0:T(8,128)S(1)}, u32[]{:S(2)}, u32[]{:S(2)}) %collective-permute-start.4) | collective-permute-done | bytes 73760 | tf_op jit(solution)/shard_map/ppermute | solution.py:990
  34.6 13.9 %all-gather.11.cloned.1.call-done = bf16[576,1152]{1,0:T(8,128)(2,1)} async-done(((bf16[144,1152]{1,0:T(8,128)(2,1)}), bf16[576,1152]{1,0:T(8,128)(2,1)}) %all-gather.11.cloned.1.call-update) | async-done | bytes 1327120 | tf_op jit(solution)/shard_map/all_gather | solution.py:842
  65.3 9.8 %collective-permute-done.9 = bf16[96,1152]{1,0:T(8,128)(2,1)} collective-permute-done((bf16[96,1152]{1,0:T(8,128)(2,1)}, bf16[96,1152]{1,0:T(8,128)(2,1)}, u32[]{:S(2)}, u32[]{:S(2)}) %collective-permute-start.9) | collective-permute-done | bytes 221216 | tf_op jit(solution)/shard_map/ppermute | solution.py:836
  98.1 18.9 %shard_map.187 = (bf16[1152,512]{1,0:T(8,128)(2,1)}, bf16[512,1152]{1,0:T(8,128)(2,1)}, bf16[512,1152]{1,0:T(8,128)(2,1)}, bf16[512,1152]{1,0:T(8,128)(2,1)}, bf16[4,1152,1152]{2,1,0:T(8,128)(2,1)}) custom-call(s32[7]{0:T(128)} %stack.87.where_ref.refs_0_, bf16[512,1152]{1,0:T(8,128)(2,1)} %x_ref.2, f32[8,2304]{1,0:T(8,128)} %fusion.39.mod_ref, ...), custom_call_target="tpu_custom_call" | custom-call | flops 20000000000 | bytes 1000 | tf_op jit(solution)/shard_map/pallas_call | solution.py:567
  117.0 7.0 %collective-permute-done.19 = f32[8,4608]{1,0:T(8,128)S(1)} collective-permute-done((f32[8,4608]{1,0:T(8,128)S(1)}, f32[8,4608]{1,0:T(8,128)S(1)}, u32[]{:S(2)}, u32[]{:S(2)}) %collective-permute-start.19) | collective-permute-done | bytes 147488 | tf_op jit(solution)/shard_map/ppermute | solution.py:990
  126.7 12.6 %shard_map.188 = (bf16[1152,512]{1,0:T(8,128)(2,1)}, f32[512,1152]{1,0:T(8,128)}, f32[512,1152]{1,0:T(8,128)}, bf16[512,1152]{1,0:T(8,128)(2,1)}) custom-call(bf16[512,1152]{1,0:T(8,128)(2,1)} %get-tuple-element.158.query_ref, bf16[512,1152]{1,0:T(8,128)(2,1)} %get-tuple-element.159.keys_ref, bf16[512,1152]{1,0:T(8,128)(2,1)} %get-tuple-element.160.values_ref, ...), custom_call_target="tpu_custom_call" | custom-call | flops 2000000000 | bytes 1000 | tf_op jit(solution)/shard_map/pallas_call | solution.py:587
  150.9 12.4 %shard_map.189 = (bf16[1,768,512]{2,1,0:T(8,128)(2,1)}, bf16[1,2,512,768]{3,2,1,0:T(8,128)(2,1)}, bf16[1152,512]{1,0:T(8,128)(2,1)}, bf16[512,1152]{1,0:T(8,128)...) custom-call(s32[7]{0:T(128)} %stack.87.where_ref.refs_0_, bf16[512,1152]{1,0:T(8,128)(2,1)} %get-tuple-element.166.refs_1_, ...), custom_call_target="tpu_custom_call" | custom-call | flops 2000000000 | bytes 1000 | tf_op jit(solution)/shard_map/pallas_call | solution.py:676
  163.4 10.5 %collective-permute-done.31.refs_8_ = bf16[3,288,768]{2,1,0:T(8,128)(2,1)} collective-permute-done((bf16[3,288,768]{2,1,0:T(8,128)(2,1)S(1)}, bf16[3,288,768]{2,1,0:T(8,128)(2,1)}, u32[]{:S(2)}, u32[]{:S(2)}) %collective-permute-start.31) | collective-permute-done | bytes 1327136 | tf_op jit(solution)/shard_map/ppermute | solution.py:823
  181.4 23.3 %shard_map.190 = (bf16[2,768,512]{2,1,0:T(8,128)(2,1)}, bf16[2,2,512,768]{3,2,1,0:T(8,128)(2,1)}, f32[512,1152]{1,0:T(8,128)}, f32[512,1152]{1,0:T(8,128)}) custom-call(s32[7]{0:T(128)} %stack.87.where_ref.refs_0_, bf16[512,1152]{1,0:T(8,128)(2,1)} %get-tuple-element.166.refs_1_, bf16[512,1152]{1,0:T(8,128)(2,1)} %get-tuple-element.204.refs_2_.refs_5_.refs_3_, ...), custom_call_target="tpu_custom_call" | custom-call | flops 24000000000 | bytes 1000 | tf_op jit(solution)/shard_map/pallas_call | solution.py:676
  208.9 16.9 %shard_map.191 = (bf16[1,768,512]{2,1,0:T(8,128)(2,1)}, bf16[1,2,512,768]{3,2,1,0:T(8,128)(2,1)}, bf16[512,1152]{1,0:T(8,128)(2,1)}, f32[512,1152]{1,0:T(8,128)}...) custom-call(s32[7]{0:T(128)} %stack.87.where_ref.refs_0_, bf16[512,1152]{1,0:T(8,128)(2,1)} %get-tuple-element.166.refs_1_, ...), custom_call_target="tpu_custom_call" | custom-call | flops 12000000000 | bytes 1000 | tf_op jit(solution)/shard_map/pallas_call | solution.py:676
  230.2 9.0 %shard_map.192 = bf16[4,4,288,768]{3,2,1,0:T(8,128)(2,1)} custom-call(s32[7]{0:T(128)} %stack.87.where_ref.refs_0_, bf16[1152,512]{1,0:T(8,128)(2,1)} %get-tuple-element.193.turned_ref, bf16[1,2,512,768]{3,2,1,0:T(8,128)(2,1)} %get-tuple-element.194.own_ref, bf16[2,2,512,768]{3,2,1,0:T(8,128)(2,1)} %get-tuple-element.195.near_ref, ...), custom_call_target="tpu_custom_call" | custom-call | flops 3000000000 | bytes 1000 | tf_op jit(solution)/shard_map/pallas_call | solution.py:696
  241.6 6.3 %shard_map.193 = bf16[4,4,96,1152]{3,2,1,0:T(8,128)(2,1)} custom-call(s32[7]{0:T(128)} %stack.87.where_ref.refs_0_, bf16[1,768,512]{2,1,0:T(8,128)(2,1)} %get-tuple-element.189.refs_0_, bf16[2,768,512]{2,1,0:T(8,128)(2,1)} %get-tuple-element.190.refs_1_, bf16[1,768,512]{2,1,0:T(8,128)(2,1)} %get-tuple-element.191.refs_2_, ...), custom_call_target="tpu_custom_call" | custom-call | flops 3000000000 | bytes 1000 | tf_op jit(solution)/shard_map/pallas_call | solution.py:745
  252.1 11.0 %shard_map.194 = (bf16[2,4,144,768]{3,2,1,0:T(8,128)(2,1)}, bf16[2,4,144,768]{3,2,1,0:T(8,128)(2,1)}, bf16[2,4,144,768]{3,2,1,0:T(8,128)(2,1)}, bf16[2,4,144,768]{3,2,1,0:T(8,128)(2,1)}) custom-call(s32[7]{0:T(128)} %stack.87.where_ref.refs_0_, bf16[1152,512]{1,0:T(8,128)(2,1)} %get-tuple-element.193.turned_ref, ...), custom_call_target="tpu_custom_call" | custom-call | flops 3000000000 | bytes 1000 | tf_op jit(solution)/shard_map/pallas_call | solution.py:696
  267.2 7.4 %shard_map.195 = bf16[4,4,96,1152]{3,2,1,0:T(8,128)(2,1)} custom-call(s32[7]{0:T(128)} %stack.87.where_ref.refs_0_, bf16[1,768,512]{2,1,0:T(8,128)(2,1)} %get-tuple-element.189.refs_0_, bf16[2,768,512]{2,1,0:T(8,128)(2,1)} %get-tuple-element.190.refs_1_, bf16[1,768,512]{2,1,0:T(8,128)(2,1)} %get-tuple-element.191.refs_2_, ...), custom_call_target="tpu_custom_call" | custom-call | flops 3000000000 | bytes 1000 | tf_op jit(solution)/shard_map/pallas_call | solution.py:745
  279.7 24.0 %shard_map.196.joint_back_ref = bf16[512,3456]{1,0:T(8,128)(2,1)} custom-call(bf16[512,1152]{1,0:T(8,128)(2,1)} %get-tuple-element.158.query_ref, bf16[512,1152]{1,0:T(8,128)(2,1)} %get-tuple-element.159.keys_ref, bf16[512,1152]{1,0:T(8,128)(2,1)} %get-tuple-element.160.values_ref, bf16[512,1152]{1,0:T(8,128)(2,1)} %get-tuple-element.222.branch_back_ref, ...), custom_call_target="tpu_custom_call" | custom-call | flops 8000000000 | bytes 1000 | tf_op jit(solution)/shard_map/pallas_call | solution.py:769
  303.7 8.9 %shard_map.197 = bf16[4,4,144,1152]{3,2,1,0:T(8,128)(2,1)} custom-call(s32[7]{0:T(128)} %stack.87.where_ref.refs_0_, bf16[1152,512]{1,0:T(8,128)(2,1)} %get-tuple-element.211.first_ref, bf16[1152,512]{1,0:T(8,128)(2,1)} %get-tuple-element.212.attended_ref, bf16[512,3456]{1,0:T(8,128)(2,1)} %shard_map.196.joint_back_ref, ...), custom_call_target="tpu_custom_call" | custom-call | flops 3000000000 | bytes 1000 | tf_op jit(solution)/shard_map/pallas_call | solution.py:696
  319.2 13.1 %shard_map.198 = (f32[512,1152]{1,0:T(8,128)}, f32[8,2304]{1,0:T(8,128)}) custom-call(bf16[512,3456]{1,0:T(8,128)(2,1)} %shard_map.196.joint_back_ref, bf16[512,1152]{1,0:T(8,128)(2,1)} %x_ref.2, f32[512,1152]{1,0:T(8,128)} %get-tuple-element.217.middle_back_ref, f32[8,2304]{1,0:T(8,128)} %fusion.39.mod_ref, bf16[4,1152,1152]{2,1,0:T(8,128)(2,1)} %get-tuple-element.165.weight), custom_call_target="tpu_custom_call" | custom-call | flops 2000000000 | bytes 1000 | tf_op jit(solution)/shard_map/pallas_call | solution.py:792
  332.4 10.3 %shard_map.199 = (bf16[2,4,80,1152]{3,2,1,0:T(8,128)(2,1)}, bf16[2,4,80,1152]{3,2,1,0:T(8,128)(2,1)}, bf16[2,4,64,1152]{3,2,1,0:T(8,128)(2,1)}, bf16[2,4,64,1152]{3,2,1,0:T(8,128)(2,1)}) custom-call(s32[7]{0:T(128)} %stack.87.where_ref.refs_0_, bf16[1152,512]{1,0:T(8,128)(2,1)} %get-tuple-element.211.first_ref, ...), custom_call_target="tpu_custom_call" | custom-call | flops 3000000000 | bytes 1000 | tf_op jit(solution)/shard_map/pallas_call | solution.py:696
  363.2 19.9 %collective-permute-done.56 = bf16[2,304,1152]{2,1,0:T(8,128)(2,1)S(1)} collective-permute-done((bf16[2,304,1152]{2,1,0:T(8,128)(2,1)S(1)}, bf16[2,304,1152]{2,1,0:T(8,128)(2,1)S(1)}, u32[]{:S(2)}, u32[]{:S(2)}) %collective-permute-start.56) | collective-permute-done | bytes 1400864 | tf_op jit(solution)/shard_map/ppermute | solution.py:823
  398.2 7.9 %collective-permute-done.58 = bf16[304,1152]{1,0:T(8,128)(2,1)} collective-permute-done((bf16[304,1152]{1,0:T(8,128)(2,1)}, bf16[304,1152]{1,0:T(8,128)(2,1)}, u32[]{:S(2)}, u32[]{:S(2)}) %collective-permute-start.58) | collective-permute-done | bytes 700448 | tf_op jit(solution)/shard_map/ppermute | solution.py:823
  417.1 7.1 %collective-permute-done.61.refs_2_ = bf16[288,768]{1,0:T(8,128)(2,1)} collective-permute-done((bf16[288,768]{1,0:T(8,128)(2,1)}, bf16[288,768]{1,0:T(8,128)(2,1)}, u32[]{:S(2)}, u32[]{:S(2)}) %collective-permute-start.61) | collective-permute-done | bytes 442400 | tf_op jit(solution)/shard_map/ppermute | solution.py:823
  428.7 11.4 %collective-permute-start.67 = (bf16[288,768]{1,0:T(8,128)(2,1)}, bf16[288,768]{1,0:T(8,128)(2,1)}, u32[]{:S(2)}, u32[]{:S(2)}) collective-permute-start(bf16[288,768]{1,0:T(8,128)(2,1)} %collective-permute-done.60.refs_1_), channel_id=1, source_target_pairs={{0,4},{4,0},{8,12},{12,8},{16,20},{20,16},{24,28},{28,24},{1,5},{5... | collective-permute-start | bytes 1327112 | tf_op jit(solution)/shard_map/ppermute | solution.py:823
  445.7 7.8 %collective-permute-done.63 = bf16[144,1152]{1,0:T(8,128)(2,1)} collective-permute-done((bf16[144,1152]{1,0:T(8,128)(2,1)S(1)}, bf16[144,1152]{1,0:T(8,128)(2,1)}, u32[]{:S(2)}, u32[]{:S(2)}) %collective-permute-start.63) | collective-permute-done | bytes 331808 | tf_op jit(solution)/shard_map/ppermute | solution.py:887
  471.3 9.2 %collective-permute-done.73.refs_3_ = bf16[240,1152]{1,0:T(8,128)(2,1)} collective-permute-done((bf16[240,1152]{1,0:T(8,128)(2,1)S(1)}, bf16[240,1152]{1,0:T(8,128)(2,1)}, u32[]{:S(2)}, u32[]{:S(2)}) %collective-permute-start.73) | collective-permute-done | bytes 552992 | tf_op jit(solution)/shard_map/ppermute | solution.py:823
  (377 shorter events, 199.7 us)
Async XLA Ops:
  7.2 41.3 %all-gather.11.cloned.1.call-start = ((), (), s32[]{:S(2)}) async-start(), calls=%async_computation.6 | async-start | bytes 1658880 | tf_op jit(solution)/shard_map/all_gather | solution.py:842
  9.2 131.8 %all-gather.13.cloned.1.call-start = ((), (), s32[]{:S(2)}) async-start(), calls=%async_computation.7 | async-start | bytes 2211840 | tf_op jit(solution)/shard_map/all_gather | solution.py:842
  49.9 25.2 %collective-permute-start.6 = (bf16[3,144,1152]{2,1,0:T(8,128)(2,1)S(1)}, bf16[3,144,1152]{2,1,0:T(8,128)(2,1)}, u32[]{:S(2)}, u32[]{:S(2)}) collective-permute-start(bf16[3,144,1152]{2,1,0:T(8,128)(2,1)S(1)} %pad_maximum_fusion.6.refs_0_), channel_id=1, source_target_pairs={{0,8},{4,12},{8,0},{12,4},{16,24},{20,28},{24,16},{28,20},{1,9},{5... | collective-permute-start | bytes 2985992 | tf_op jit(solution)/shard_map/ppermute | solution.py:823
  82.5 196.9 %all-gather.7.cloned.1.call-start = ((), (), s32[]{:S(2)}) async-start(), calls=%async_computation.2 | async-start | bytes 3317760 | tf_op jit(solution)/shard_map/all_gather | solution.py:1117
  93.7 30.3 %collective-permute-start.19 = (f32[8,4608]{1,0:T(8,128)S(1)}, f32[8,4608]{1,0:T(8,128)S(1)}, u32[]{:S(2)}, u32[]{:S(2)}) collective-permute-start(f32[8,4608]{1,0:T(8,128)S(1)} %get-tuple-element.314), channel_id=1, source_target_pairs={{0,2},{1,3},{2,0},{3,1},{4,6},{5,7},{6,4},{7,5},{8,10},{9,11},{10,... | collective-permute-start | bytes 442376 | tf_op jit(solution)/shard_map/ppermute | solution.py:990
  95.5 28.5 %collective-permute-start.20 = (f32[8,4608]{1,0:T(8,128)S(1)}, f32[8,4608]{1,0:T(8,128)S(1)}, u32[]{:S(2)}, u32[]{:S(2)}) collective-permute-start(f32[8,4608]{1,0:T(8,128)S(1)} %get-tuple-element.313), channel_id=1, source_target_pairs={{0,3},{1,0},{2,1},{3,2},{4,7},{5,4},{6,5},{7,6},{8,11},{9,8},{10,9... | collective-permute-start | bytes 442376 | tf_op jit(solution)/shard_map/ppermute | solution.py:990
  97.0 27.0 %collective-permute-start.22 = (bf16[3,96,1152]{2,1,0:T(8,128)(2,1)S(1)}, bf16[3,96,1152]{2,1,0:T(8,128)(2,1)S(1)}, u32[]{:S(2)}, u32[]{:S(2)}) collective-permute-start(bf16[3,96,1152]{2,1,0:T(8,128)(2,1)S(1)} %pad_maximum_fusion.7.refs_10_.refs_12_.refs_17_), channel_id=1, source_target_pairs={{0,8},{4,12},{8,0},{12,4},{16,24},{20,28},{24,16},{28,20},{1,9},{5... | collective-permute-start | bytes 1990664 | tf_op jit(solution)/shard_map/ppermute | solution.py:823
  97.3 26.7 %collective-permute-start.23 = (bf16[3,96,1152]{2,1,0:T(8,128)(2,1)S(1)}, bf16[3,96,1152]{2,1,0:T(8,128)(2,1)S(1)}, u32[]{:S(2)}, u32[]{:S(2)}) collective-permute-start(bf16[3,96,1152]{2,1,0:T(8,128)(2,1)S(1)} %pad_maximum_fusion.7.refs_10_.refs_12_.refs_17_), channel_id=1, source_target_pairs={{0,16},{4,20},{8,24},{12,28},{16,0},{20,4},{24,8},{28,12},{1,17},{... | collective-permute-start | bytes 1990664 | tf_op jit(solution)/shard_map/ppermute | solution.py:823
  143.0 30.8 %collective-permute-start.31 = (bf16[3,288,768]{2,1,0:T(8,128)(2,1)S(1)}, bf16[3,288,768]{2,1,0:T(8,128)(2,1)}, u32[]{:S(2)}, u32[]{:S(2)}) collective-permute-start(bf16[3,288,768]{2,1,0:T(8,128)(2,1)S(1)} %pad_maximum_fusion.4.refs_8_), channel_id=1, source_target_pairs={{0,8},{4,12},{8,0},{12,4},{16,24},{20,28},{24,16},{28,20},{1,9},{5... | collective-permute-start | bytes 3981320 | tf_op jit(solution)/shard_map/ppermute | solution.py:823
  143.9 30.5 %collective-permute-start.32 = (bf16[3,288,768]{2,1,0:T(8,128)(2,1)S(1)}, bf16[3,288,768]{2,1,0:T(8,128)(2,1)}, u32[]{:S(2)}, u32[]{:S(2)}) collective-permute-start(bf16[3,288,768]{2,1,0:T(8,128)(2,1)S(1)} %pad_maximum_fusion.4.refs_8_), channel_id=1, source_target_pairs={{0,16},{4,20},{8,24},{12,28},{16,0},{20,4},{24,8},{28,12},{1,17},{... | collective-permute-start | bytes 3981320 | tf_op jit(solution)/shard_map/ppermute | solution.py:823
  177.8 26.9 %collective-permute-start.35 = (bf16[3,144,768]{2,1,0:T(8,128)(2,1)S(1)}, bf16[3,144,768]{2,1,0:T(8,128)(2,1)S(1)}, u32[]{:S(2)}, u32[]{:S(2)}) collective-permute-start(bf16[3,144,768]{2,1,0:T(8,128)(2,1)S(1)} %slice.128), channel_id=1, source_target_pairs={{0,16},{4,20},{8,24},{12,28},{16,0},{20,4},{24,8},{28,12},{1,17},{... | collective-permute-start | bytes 1990664 | tf_op jit(solution)/shard_map/ppermute | solution.py:823
  179.1 25.6 %collective-permute-start.36 = (bf16[3,144,768]{2,1,0:T(8,128)(2,1)S(1)}, bf16[3,144,768]{2,1,0:T(8,128)(2,1)S(1)}, u32[]{:S(2)}, u32[]{:S(2)}) collective-permute-start(bf16[3,144,768]{2,1,0:T(8,128)(2,1)S(1)} %slice.129), channel_id=1, source_target_pairs={{0,8},{4,12},{8,0},{12,4},{16,24},{20,28},{24,16},{28,20},{1,9},{5... | collective-permute-start | bytes 1990664 | tf_op jit(solution)/shard_map/ppermute | solution.py:823
  241.3 106.3 %reduce-scatter.3.cloned.1.call-start = ((), (), s32[]{:S(2)}) async-start(), calls=%async_computation.3 | async-start | bytes 4423680 | tf_op jit(solution)/shard_map/reduce_scatter | solution.py:1135
  263.1 49.5 %collective-permute-start.44 = (bf16[2,4,144,768]{3,2,1,0:T(8,128)(2,1)}, bf16[2,4,144,768]{3,2,1,0:T(8,128)(2,1)S(1)}, u32[]{:S(2)}, u32[]{:S(2)}) collective-permute-start(bf16[2,4,144,768]{3,2,1,0:T(8,128)(2,1)} %get-tuple-element.200), channel_id=1, source_target_pairs={{0,8},{4,12},{8,0},{12,4},{16,24},{20,28},{24,16},{28,20},{1,9},{5... | collective-permute-start | bytes 5308424 | tf_op jit(solution)/shard_map/ppermute | solution.py:823
  263.9 50.0 %collective-permute-start.45 = (bf16[2,4,144,768]{3,2,1,0:T(8,128)(2,1)}, bf16[2,4,144,768]{3,2,1,0:T(8,128)(2,1)}, u32[]{:S(2)}, u32[]{:S(2)}) collective-permute-start(bf16[2,4,144,768]{3,2,1,0:T(8,128)(2,1)} %get-tuple-element.202), channel_id=1, source_target_pairs={{0,16},{4,20},{8,24},{12,28},{16,0},{20,4},{24,8},{28,12},{1,17},{... | collective-permute-start | bytes 5308424 | tf_op jit(solution)/shard_map/ppermute | solution.py:823
  279.5 111.4 %reduce-scatter.5.cloned.1.call-start = ((), (), s32[]{:S(2)}) async-start(), calls=%async_computation.5 | async-start | bytes 2211840 | tf_op jit(solution)/shard_map/reduce_scatter | solution.py:1159
  317.7 25.0 %collective-permute-start.48 = (bf16[4,144,768]{2,1,0:T(8,128)(2,1)}, bf16[4,144,768]{2,1,0:T(8,128)(2,1)}, u32[]{:S(2)}, u32[]{:S(2)}) collective-permute-start(bf16[4,144,768]{2,1,0:T(8,128)(2,1)} %get-tuple-element.235), channel_id=1, source_target_pairs={{0,8},{4,12},{8,0},{12,4},{16,24},{20,28},{24,16},{28,20},{1,9},{5... | collective-permute-start | bytes 2654216 | tf_op jit(solution)/shard_map/ppermute | solution.py:823
  318.5 25.5 %collective-permute-start.47 = (bf16[4,144,768]{2,1,0:T(8,128)(2,1)}, bf16[4,144,768]{2,1,0:T(8,128)(2,1)S(1)}, u32[]{:S(2)}, u32[]{:S(2)}) collective-permute-start(bf16[4,144,768]{2,1,0:T(8,128)(2,1)} %get-tuple-element.233), channel_id=1, source_target_pairs={{0,16},{4,20},{8,24},{12,28},{16,0},{20,4},{24,8},{28,12},{1,17},{... | collective-permute-start | bytes 2654216 | tf_op jit(solution)/shard_map/ppermute | solution.py:823
  351.6 104.0 %all-gather.9.cloned.1.call-start = ((), (), s32[]{:S(2)}) async-start(), calls=%async_computation.4 | async-start | bytes 1327104 | tf_op jit(solution)/shard_map/all_gather | solution.py:1161
  351.9 31.2 %collective-permute-start.56 = (bf16[2,304,1152]{2,1,0:T(8,128)(2,1)S(1)}, bf16[2,304,1152]{2,1,0:T(8,128)(2,1)S(1)}, u32[]{:S(2)}, u32[]{:S(2)}) collective-permute-start(bf16[2,304,1152]{2,1,0:T(8,128)(2,1)S(1)} %pad_maximum_fusion.3), channel_id=1, source_target_pairs={{0,16},{4,20},{8,24},{12,28},{16,0},{20,4},{24,8},{28,12},{1,17},{... | collective-permute-start | bytes 4202504 | tf_op jit(solution)/shard_map/ppermute | solution.py:823
  353.3 37.1 %collective-permute-start.55 = (bf16[2,368,1152]{2,1,0:T(8,128)(2,1)S(1)}, bf16[2,368,1152]{2,1,0:T(8,128)(2,1)S(1)}, u32[]{:S(2)}, u32[]{:S(2)}) collective-permute-start(bf16[2,368,1152]{2,1,0:T(8,128)(2,1)S(1)} %pad_maximum_fusion.2), channel_id=1, source_target_pairs={{0,8},{4,12},{8,0},{12,4},{16,24},{20,28},{24,16},{28,20},{1,9},{5... | collective-permute-start | bytes 5087240 | tf_op jit(solution)/shard_map/ppermute | solution.py:823
  394.6 29.6 %collective-permute-start.61 = (bf16[288,768]{1,0:T(8,128)(2,1)}, bf16[288,768]{1,0:T(8,128)(2,1)}, u32[]{:S(2)}, u32[]{:S(2)}) collective-permute-start(bf16[288,768]{1,0:T(8,128)(2,1)} %bitcast.130), channel_id=1, source_target_pairs={{0,16},{4,20},{8,24},{12,28},{16,0},{20,4},{24,8},{28,12},{1,17},{... | collective-permute-start | bytes 1327112 | tf_op jit(solution)/shard_map/ppermute | solution.py:823
  394.6 45.4 %collective-permute-start.66 = (bf16[288,768]{1,0:T(8,128)(2,1)}, bf16[288,768]{1,0:T(8,128)(2,1)S(1)}, u32[]{:S(2)}, u32[]{:S(2)}) collective-permute-start(bf16[288,768]{1,0:T(8,128)(2,1)} %bitcast.131), channel_id=1, source_target_pairs={{0,4},{4,0},{8,12},{12,8},{16,20},{20,16},{24,28},{28,24},{1,5},{5... | collective-permute-start | bytes 1327112 | tf_op jit(solution)/shard_map/ppermute | solution.py:823
  414.0 26.2 %collective-permute-start.59 = (bf16[144,1152]{1,0:T(8,128)(2,1)S(1)}, bf16[144,1152]{1,0:T(8,128)(2,1)S(1)}, u32[]{:S(2)}, u32[]{:S(2)}) collective-permute-start(bf16[144,1152]{1,0:T(8,128)(2,1)S(1)} %get-tuple-element.304), channel_id=1, source_target_pairs={{0,1},{1,2},{2,3},{3,0},{4,5},{5,6},{6,7},{7,4},{8,9},{9,10},{10,1... | collective-permute-start | bytes 995336 | tf_op jit(solution)/shard_map/ppermute | solution.py:887
  (121 other events, 1107.1 us)
Sparse Core Ops, SparseCore 0:
  10.2 38.2 all-gather.10
  82.6 51.6 all-gather.12
  241.5 37.9 all-gather.6
  282.2 65.4 reduce-scatter.2
  351.7 39.0 reduce-scatter.4
  394.4 30.6 all-gather.8

commit v9 on v8

--- a/solution.py
+++ b/solution.py
@@ -451,7 +451,8 @@
     sources, out = refs[:-1], refs[-1]
     for j, other, start, size, ref in placed(sources, rows):
         piece = (where_ref[1] ^ j) * HALVES + (where_ref[2] ^ other)
-        out[take(piece * rows + start, size), :] = ref[offset : offset + size, :].astype(f32)
+        at = offset if ref.shape[0] > rows else 0
+        out[take(piece * rows + start, size), :] = ref[at : at + size, :].astype(f32)
 
 
 def place_attn_kernel(rows, where_ref, *refs):
@@ -466,6 +467,17 @@
                     project_ref[to, :] = ref[:size, :].astype(f32)
                 else:
                     joint_ref[to, part(column ^ j)] = ref[:size, :].astype(f32)
+
+
+def place_both_kernel(attn_rows, down_rows, where_ref, *refs):
+    sources, outs = refs[:-3], refs[-3:]
+    each = len(sources) // HALVES
+    sides = [sources[each * k : each * k + each] for k in range(HALVES)]
+    place_attn_kernel(
+        attn_rows, where_ref, *[ref for side in sides for ref in side[:4]], outs[0], outs[1]
+    )
+    downs = [ref for side in sides for ref in side[:3] + side[4:]]
+    place_down_kernel(down_rows, attn_rows, where_ref, *downs, outs[2])
 
 
 def attend_back_kernel(
@@ -1195,7 +1207,8 @@
         attn_sums = sum_whole(uncut(attn_cut), attn_theirs)
     if fast:
         early, attn_sum = after((early, attn_sum))
-        both_sums = direct(jnp.concatenate([attn_sum, down_total], axis=0))
+        both_sum = jnp.concatenate([attn_sum, down_total], axis=0)
+        both_x, both_y = swap(both_sum, 2), swap(both_sum, 4)
     all_back = jnp.concatenate([early, late[:, : 4 * WIDTH]], axis=1)
     all_lifted = lax.dynamic_slice_in_dim(late, 4 * WIDTH + place * height, height, 1)
     modulate_gradient = contract_rows(all_lifted, all_back)
@@ -1203,8 +1216,10 @@
         place_pair_kernel, where, pair_sums, (struct(gate_weight.shape, f32),) * 2
     )
     if fast:
-        both_sums, pair_grad, modulate_gradient = after((both_sums, pair_grad, modulate_gradient))
-        attn_sums = down_sums = both(both_sums)
+        both_x, both_y, pair_grad, modulate_gradient = after(
+            (both_x, both_y, pair_grad, modulate_gradient)
+        )
+        both_sums = both((both_sum, both_x, both_y) + cross(both_x, both_y, half))
     slopes = jnp.stack(slopes)
     condition_slope = (
         jnp.stack([pick(slopes, (place + count - j) % count) for j in range(count)])
@@ -1212,14 +1227,22 @@
         .reshape(slots, WIDTH)
     )
     grad_condition = condition_slope * silu_slope(cond_float)
-    down_grad = place_call(functools.partial(place_down_kernel, down_rows, half if fast else 0), where, down_sums, struct(down_weight.shape, f32))
-    attn_grad = place_call(
-        functools.partial(place_attn_kernel, half),
-        where,
-        attn_sums,
-        (struct(joint_weight.shape, f32), struct(project_weight.shape, f32)),
-    )
-
+    attn_shapes = (struct(joint_weight.shape, f32), struct(project_weight.shape, f32))
+    down_shape = struct(down_weight.shape, f32)
+    if fast:
+        *attn_grad, down_grad = place_call(
+            functools.partial(place_both_kernel, half, down_rows),
+            where,
+            both_sums,
+            attn_shapes + (down_shape,),
+        )
+    else:
+        down_grad = place_call(
+            functools.partial(place_down_kernel, down_rows, 0), where, down_sums, down_shape
+        )
+        attn_grad = place_call(
+            functools.partial(place_attn_kernel, half), where, attn_sums, attn_shapes
+        )
     return (
         output,
         grad_inputs,

time: 513 us -> 501 us (0.977)
  waiting for transfers between devices: 144 us -> 133 us
    ppermute x54 -> x56, waiting for transfers between devices: 82.2 us -> 74.7 us  [swap(): return lax.ppermute(array, 'bucket', across(bit))]
    pallas_call x3 -> x2, Pallas kernels: 14.7 us -> 11.6 us  [place_call(): pl.pallas_call(kernel, out_shape=outs, in_specs=[SMEM] + [VMEM] * len(arr...]
    ppermute x54 -> x56, starting transfers between devices: 58.9 us -> 61.4 us  [swap(): return lax.ppermute(array, 'bucket', across(bit))]
  transfers between devices with their start and end apart: 84 -> 86, of which waited for: 29 -> 28; matrix products, arithmetic and copies ran while one was open for 10% -> 11% of each run, Pallas kernels for 32% -> 33%
where the time goes in v9:
time: 501 us; the launch traced here: 493 us
  Pallas kernels  185 us (37%)
  waiting for transfers between devices  133 us (27%)
  starting transfers between devices  89.5 us (18%)
  local copies, waits for them, and re-layouts  30.1 us (6%)
  other arithmetic  22.9 us (5%)
  between operations  16.7 us (3%)
  matrix products  14.7 us (3%)
    ppermute x56, waiting for transfers between devices, swap(): return lax.ppermute(array, 'bucket', across(bit))  74.7 us
    ppermute x56, starting transfers between devices, swap(): return lax.ppermute(array, 'bucket', across(bit))  61.4 us
    pallas_call x3, Pallas kernels, ffn_call(): pl.pallas_call(functools.partial(ffn_kernel, count, js, names), grid=(len...  52.6 us
    pallas_call x4, Pallas kernels, by_column(): pl.pallas_call(call, out_shape=shapes, grid_spec=pltpu.PrefetchScalarGrid...  39.1 us
    pallas_call x1, Pallas kernels, attend_back_call(): pl.pallas_call(attend_back_kernel, grid=(tokens // BLOCK,), out_shape=str...  24 us
    ppermute x6, waiting for transfers between devices, modulation_parts(): lax.ppermute(pick(parts, (place + by) % fsdp_count), 'fsdp', shifts(fsdp_...  20.2 us
    pallas_call x1, Pallas kernels, first_call(): pl.pallas_call(functools.partial(first_kernel, count), out_shape=(struct(...  18.9 us
    all_gather x2, waiting for transfers between devices, gather_z(): full = after(lax.all_gather(piece, 'fsdp', axis=0, tiled=False), *others)  13.9 us
  transfers between devices with their start and end apart: 86, of which 28 were waited for; matrix products, arithmetic and copies ran while one was open for 11% of the time, Pallas kernels for 33%

profile of v9, /device:TPU:25, one launch (start us, length us, event | category | flops | bytes accessed | tf_op | source)
XLA Modules:
  0.0 492.7 jit_solution(3517323167171995246)
XLA Ops:
  23.2 10.8 %collective-permute-done.4 = f32[8,2304]{1,0:T(8,128)S(1)} collective-permute-done((f32[8,2304]{1,0:T(8,128)S(1)}, f32[8,2304]{1,0:T(8,128)S(1)}, u32[]{:S(2)}, u32[]{:S(2)}) %collective-permute-start.4) | collective-permute-done | bytes 73760 | tf_op jit(solution)/shard_map/ppermute | solution.py:1002
  34.6 13.9 %all-gather.11.cloned.1.call-done = bf16[576,1152]{1,0:T(8,128)(2,1)} async-done(((bf16[144,1152]{1,0:T(8,128)(2,1)}), bf16[576,1152]{1,0:T(8,128)(2,1)}) %all-gather.11.cloned.1.call-update) | async-done | bytes 1327120 | tf_op jit(solution)/shard_map/all_gather | solution.py:854
  65.2 9.9 %collective-permute-done.9 = bf16[96,1152]{1,0:T(8,128)(2,1)} collective-permute-done((bf16[96,1152]{1,0:T(8,128)(2,1)}, bf16[96,1152]{1,0:T(8,128)(2,1)}, u32[]{:S(2)}, u32[]{:S(2)}) %collective-permute-start.9) | collective-permute-done | bytes 221216 | tf_op jit(solution)/shard_map/ppermute | solution.py:848
  98.1 18.9 %shard_map.187 = (bf16[1152,512]{1,0:T(8,128)(2,1)}, bf16[512,1152]{1,0:T(8,128)(2,1)}, bf16[512,1152]{1,0:T(8,128)(2,1)}, bf16[512,1152]{1,0:T(8,128)(2,1)}, bf16[4,1152,1152]{2,1,0:T(8,128)(2,1)}) custom-call(s32[7]{0:T(128)} %stack.87.where_ref.refs_0_, bf16[512,1152]{1,0:T(8,128)(2,1)} %x_ref.2, f32[8,2304]{1,0:T(8,128)} %fusion.39.mod_ref, ...), custom_call_target="tpu_custom_call" | custom-call | flops 20000000000 | bytes 1000 | tf_op jit(solution)/shard_map/pallas_call | solution.py:579
  117.0 7.0 %collective-permute-done.19 = f32[8,4608]{1,0:T(8,128)S(1)} collective-permute-done((f32[8,4608]{1,0:T(8,128)S(1)}, f32[8,4608]{1,0:T(8,128)S(1)}, u32[]{:S(2)}, u32[]{:S(2)}) %collective-permute-start.19) | collective-permute-done | bytes 147488 | tf_op jit(solution)/shard_map/ppermute | solution.py:1002
  126.7 12.6 %shard_map.188 = (bf16[1152,512]{1,0:T(8,128)(2,1)}, f32[512,1152]{1,0:T(8,128)}, f32[512,1152]{1,0:T(8,128)}, bf16[512,1152]{1,0:T(8,128)(2,1)}) custom-call(bf16[512,1152]{1,0:T(8,128)(2,1)} %get-tuple-element.157.query_ref, bf16[512,1152]{1,0:T(8,128)(2,1)} %get-tuple-element.158.keys_ref, bf16[512,1152]{1,0:T(8,128)(2,1)} %get-tuple-element.159.values_ref, ...), custom_call_target="tpu_custom_call" | custom-call | flops 2000000000 | bytes 1000 | tf_op jit(solution)/shard_map/pallas_call | solution.py:599
  150.9 12.4 %shard_map.189 = (bf16[1,768,512]{2,1,0:T(8,128)(2,1)}, bf16[1,2,512,768]{3,2,1,0:T(8,128)(2,1)}, bf16[1152,512]{1,0:T(8,128)(2,1)}, bf16[512,1152]{1,0:T(8,128)...) custom-call(s32[7]{0:T(128)} %stack.87.where_ref.refs_0_, bf16[512,1152]{1,0:T(8,128)(2,1)} %get-tuple-element.165.refs_1_, ...), custom_call_target="tpu_custom_call" | custom-call | flops 2000000000 | bytes 1000 | tf_op jit(solution)/shard_map/pallas_call | solution.py:688
  163.3 10.5 %collective-permute-done.31.refs_8_ = bf16[3,288,768]{2,1,0:T(8,128)(2,1)} collective-permute-done((bf16[3,288,768]{2,1,0:T(8,128)(2,1)S(1)}, bf16[3,288,768]{2,1,0:T(8,128)(2,1)}, u32[]{:S(2)}, u32[]{:S(2)}) %collective-permute-start.31) | collective-permute-done | bytes 1327136 | tf_op jit(solution)/shard_map/ppermute | solution.py:835
  181.4 23.3 %shard_map.190 = (bf16[2,768,512]{2,1,0:T(8,128)(2,1)}, bf16[2,2,512,768]{3,2,1,0:T(8,128)(2,1)}, f32[512,1152]{1,0:T(8,128)}, f32[512,1152]{1,0:T(8,128)}) custom-call(s32[7]{0:T(128)} %stack.87.where_ref.refs_0_, bf16[512,1152]{1,0:T(8,128)(2,1)} %get-tuple-element.165.refs_1_, bf16[512,1152]{1,0:T(8,128)(2,1)} %get-tuple-element.203.refs_2_.refs_5_.refs_3_, ...), custom_call_target="tpu_custom_call" | custom-call | flops 24000000000 | bytes 1000 | tf_op jit(solution)/shard_map/pallas_call | solution.py:688
  208.9 16.9 %shard_map.191 = (bf16[1,768,512]{2,1,0:T(8,128)(2,1)}, bf16[1,2,512,768]{3,2,1,0:T(8,128)(2,1)}, bf16[512,1152]{1,0:T(8,128)(2,1)}, f32[512,1152]{1,0:T(8,128)}...) custom-call(s32[7]{0:T(128)} %stack.87.where_ref.refs_0_, bf16[512,1152]{1,0:T(8,128)(2,1)} %get-tuple-element.165.refs_1_, ...), custom_call_target="tpu_custom_call" | custom-call | flops 12000000000 | bytes 1000 | tf_op jit(solution)/shard_map/pallas_call | solution.py:688
  230.3 9.0 %shard_map.192 = bf16[4,4,288,768]{3,2,1,0:T(8,128)(2,1)} custom-call(s32[7]{0:T(128)} %stack.87.where_ref.refs_0_, bf16[1152,512]{1,0:T(8,128)(2,1)} %get-tuple-element.192.turned_ref, bf16[1,2,512,768]{3,2,1,0:T(8,128)(2,1)} %get-tuple-element.193.own_ref, bf16[2,2,512,768]{3,2,1,0:T(8,128)(2,1)} %get-tuple-element.194.near_ref, ...), custom_call_target="tpu_custom_call" | custom-call | flops 3000000000 | bytes 1000 | tf_op jit(solution)/shard_map/pallas_call | solution.py:708
  241.6 6.3 %shard_map.193 = bf16[4,4,96,1152]{3,2,1,0:T(8,128)(2,1)} custom-call(s32[7]{0:T(128)} %stack.87.where_ref.refs_0_, bf16[1,768,512]{2,1,0:T(8,128)(2,1)} %get-tuple-element.188.refs_0_, bf16[2,768,512]{2,1,0:T(8,128)(2,1)} %get-tuple-element.189.refs_1_, bf16[1,768,512]{2,1,0:T(8,128)(2,1)} %get-tuple-element.190.refs_2_, ...), custom_call_target="tpu_custom_call" | custom-call | flops 3000000000 | bytes 1000 | tf_op jit(solution)/shard_map/pallas_call | solution.py:757
  252.2 11.0 %shard_map.194 = (bf16[2,4,144,768]{3,2,1,0:T(8,128)(2,1)}, bf16[2,4,144,768]{3,2,1,0:T(8,128)(2,1)}, bf16[2,4,144,768]{3,2,1,0:T(8,128)(2,1)}, bf16[2,4,144,768]{3,2,1,0:T(8,128)(2,1)}) custom-call(s32[7]{0:T(128)} %stack.87.where_ref.refs_0_, bf16[1152,512]{1,0:T(8,128)(2,1)} %get-tuple-element.192.turned_ref, ...), custom_call_target="tpu_custom_call" | custom-call | flops 3000000000 | bytes 1000 | tf_op jit(solution)/shard_map/pallas_call | solution.py:708
  267.2 7.4 %shard_map.195 = bf16[4,4,96,1152]{3,2,1,0:T(8,128)(2,1)} custom-call(s32[7]{0:T(128)} %stack.87.where_ref.refs_0_, bf16[1,768,512]{2,1,0:T(8,128)(2,1)} %get-tuple-element.188.refs_0_, bf16[2,768,512]{2,1,0:T(8,128)(2,1)} %get-tuple-element.189.refs_1_, bf16[1,768,512]{2,1,0:T(8,128)(2,1)} %get-tuple-element.190.refs_2_, ...), custom_call_target="tpu_custom_call" | custom-call | flops 3000000000 | bytes 1000 | tf_op jit(solution)/shard_map/pallas_call | solution.py:757
  279.7 24.0 %shard_map.196.joint_back_ref = bf16[512,3456]{1,0:T(8,128)(2,1)} custom-call(bf16[512,1152]{1,0:T(8,128)(2,1)} %get-tuple-element.157.query_ref, bf16[512,1152]{1,0:T(8,128)(2,1)} %get-tuple-element.158.keys_ref, bf16[512,1152]{1,0:T(8,128)(2,1)} %get-tuple-element.159.values_ref, bf16[512,1152]{1,0:T(8,128)(2,1)} %get-tuple-element.221.branch_back_ref, ...), custom_call_target="tpu_custom_call" | custom-call | flops 8000000000 | bytes 1000 | tf_op jit(solution)/shard_map/pallas_call | solution.py:781
  303.7 8.9 %shard_map.197 = bf16[4,4,144,1152]{3,2,1,0:T(8,128)(2,1)} custom-call(s32[7]{0:T(128)} %stack.87.where_ref.refs_0_, bf16[1152,512]{1,0:T(8,128)(2,1)} %get-tuple-element.210.first_ref, bf16[1152,512]{1,0:T(8,128)(2,1)} %get-tuple-element.211.attended_ref, bf16[512,3456]{1,0:T(8,128)(2,1)} %shard_map.196.joint_back_ref, ...), custom_call_target="tpu_custom_call" | custom-call | flops 3000000000 | bytes 1000 | tf_op jit(solution)/shard_map/pallas_call | solution.py:708
  319.2 13.1 %shard_map.198 = (f32[512,1152]{1,0:T(8,128)}, f32[8,2304]{1,0:T(8,128)}) custom-call(bf16[512,3456]{1,0:T(8,128)(2,1)} %shard_map.196.joint_back_ref, bf16[512,1152]{1,0:T(8,128)(2,1)} %x_ref.2, f32[512,1152]{1,0:T(8,128)} %get-tuple-element.216.middle_back_ref, f32[8,2304]{1,0:T(8,128)} %fusion.39.mod_ref, bf16[4,1152,1152]{2,1,0:T(8,128)(2,1)} %get-tuple-element.164.weight), custom_call_target="tpu_custom_call" | custom-call | flops 2000000000 | bytes 1000 | tf_op jit(solution)/shard_map/pallas_call | solution.py:804
  332.3 10.3 %shard_map.199 = (bf16[2,4,80,1152]{3,2,1,0:T(8,128)(2,1)}, bf16[2,4,80,1152]{3,2,1,0:T(8,128)(2,1)}, bf16[2,4,64,1152]{3,2,1,0:T(8,128)(2,1)}, bf16[2,4,64,1152]{3,2,1,0:T(8,128)(2,1)}) custom-call(s32[7]{0:T(128)} %stack.87.where_ref.refs_0_, bf16[1152,512]{1,0:T(8,128)(2,1)} %get-tuple-element.210.first_ref, ...), custom_call_target="tpu_custom_call" | custom-call | flops 3000000000 | bytes 1000 | tf_op jit(solution)/shard_map/pallas_call | solution.py:708
  363.2 19.8 %collective-permute-done.56 = bf16[2,304,1152]{2,1,0:T(8,128)(2,1)S(1)} collective-permute-done((bf16[2,304,1152]{2,1,0:T(8,128)(2,1)S(1)}, bf16[2,304,1152]{2,1,0:T(8,128)(2,1)S(1)}, u32[]{:S(2)}, u32[]{:S(2)}) %collective-permute-start.56) | collective-permute-done | bytes 1400864 | tf_op jit(solution)/shard_map/ppermute | solution.py:835
  384.2 6.3 %collective-permute-done.55 = bf16[2,368,1152]{2,1,0:T(8,128)(2,1)S(1)} collective-permute-done((bf16[2,368,1152]{2,1,0:T(8,128)(2,1)S(1)}, bf16[2,368,1152]{2,1,0:T(8,128)(2,1)S(1)}, u32[]{:S(2)}, u32[]{:S(2)}) %collective-permute-start.55) | collective-permute-done | bytes 1695776 | tf_op jit(solution)/shard_map/ppermute | solution.py:835
  398.2 7.9 %collective-permute-done.58 = bf16[304,1152]{1,0:T(8,128)(2,1)} collective-permute-done((bf16[304,1152]{1,0:T(8,128)(2,1)}, bf16[304,1152]{1,0:T(8,128)(2,1)}, u32[]{:S(2)}, u32[]{:S(2)}) %collective-permute-start.58) | collective-permute-done | bytes 700448 | tf_op jit(solution)/shard_map/ppermute | solution.py:835
  417.2 6.9 %collective-permute-done.61.refs_2_ = bf16[288,768]{1,0:T(8,128)(2,1)} collective-permute-done((bf16[288,768]{1,0:T(8,128)(2,1)}, bf16[288,768]{1,0:T(8,128)(2,1)}, u32[]{:S(2)}, u32[]{:S(2)}) %collective-permute-start.61) | collective-permute-done | bytes 442400 | tf_op jit(solution)/shard_map/ppermute | solution.py:835
  425.1 10.9 %collective-permute-start.67 = (bf16[288,768]{1,0:T(8,128)(2,1)}, bf16[288,768]{1,0:T(8,128)(2,1)}, u32[]{:S(2)}, u32[]{:S(2)}) collective-permute-start(bf16[288,768]{1,0:T(8,128)(2,1)} %collective-permute-done.60.refs_1_), channel_id=1, source_target_pairs={{0,4},{4,0},{8,12},{12,8},{16,20},{20,16},{24,28},{28,24},{1,5},{5... | collective-permute-start | bytes 1327112 | tf_op jit(solution)/shard_map/ppermute | solution.py:835
  479.5 6.2 %shard_map.201 = (f32[288,3456]{1,0:T(8,128)}, f32[288,1152]{1,0:T(8,128)}, f32[768,1152]{1,0:T(8,128)}) custom-call(s32[7]{0:T(128)} %stack.87.where_ref.refs_0_, bf16[240,1152]{1,0:T(8,128)(2,1)} %copy-done.26, bf16[240,1152]{1,0:T(8,128)(2,1)} %copy-done.25, bf16[240,1152]{1,0:T(8,128)(2,1)} %collective-permute-done.72.refs_2_, ...), custom_call_target="tpu_custom_call" | custom-call | flops 4000000000 | bytes 1000 | tf_op jit(solution)/shard_map/pallas_call | solution.py:768
  (382 shorter events, 192.2 us)
Async XLA Ops:
  7.2 41.3 %all-gather.11.cloned.1.call-start = ((), (), s32[]{:S(2)}) async-start(), calls=%async_computation.6 | async-start | bytes 1658880 | tf_op jit(solution)/shard_map/all_gather | solution.py:854
  9.2 131.8 %all-gather.13.cloned.1.call-start = ((), (), s32[]{:S(2)}) async-start(), calls=%async_computation.7 | async-start | bytes 2211840 | tf_op jit(solution)/shard_map/all_gather | solution.py:854
  49.9 25.2 %collective-permute-start.6 = (bf16[3,144,1152]{2,1,0:T(8,128)(2,1)S(1)}, bf16[3,144,1152]{2,1,0:T(8,128)(2,1)}, u32[]{:S(2)}, u32[]{:S(2)}) collective-permute-start(bf16[3,144,1152]{2,1,0:T(8,128)(2,1)S(1)} %pad_maximum_fusion.6.refs_0_), channel_id=1, source_target_pairs={{0,8},{4,12},{8,0},{12,4},{16,24},{20,28},{24,16},{28,20},{1,9},{5... | collective-permute-start | bytes 2985992 | tf_op jit(solution)/shard_map/ppermute | solution.py:835
  82.5 196.9 %all-gather.7.cloned.1.call-start = ((), (), s32[]{:S(2)}) async-start(), calls=%async_computation.2 | async-start | bytes 3317760 | tf_op jit(solution)/shard_map/all_gather | solution.py:1129
  93.7 30.2 %collective-permute-start.19 = (f32[8,4608]{1,0:T(8,128)S(1)}, f32[8,4608]{1,0:T(8,128)S(1)}, u32[]{:S(2)}, u32[]{:S(2)}) collective-permute-start(f32[8,4608]{1,0:T(8,128)S(1)} %get-tuple-element.312), channel_id=1, source_target_pairs={{0,2},{1,3},{2,0},{3,1},{4,6},{5,7},{6,4},{7,5},{8,10},{9,11},{10,... | collective-permute-start | bytes 442376 | tf_op jit(solution)/shard_map/ppermute | solution.py:1002
  95.5 28.5 %collective-permute-start.20 = (f32[8,4608]{1,0:T(8,128)S(1)}, f32[8,4608]{1,0:T(8,128)S(1)}, u32[]{:S(2)}, u32[]{:S(2)}) collective-permute-start(f32[8,4608]{1,0:T(8,128)S(1)} %get-tuple-element.311), channel_id=1, source_target_pairs={{0,3},{1,0},{2,1},{3,2},{4,7},{5,4},{6,5},{7,6},{8,11},{9,8},{10,9... | collective-permute-start | bytes 442376 | tf_op jit(solution)/shard_map/ppermute | solution.py:1002
  97.0 26.9 %collective-permute-start.22 = (bf16[3,96,1152]{2,1,0:T(8,128)(2,1)S(1)}, bf16[3,96,1152]{2,1,0:T(8,128)(2,1)S(1)}, u32[]{:S(2)}, u32[]{:S(2)}) collective-permute-start(bf16[3,96,1152]{2,1,0:T(8,128)(2,1)S(1)} %pad_maximum_fusion.7.refs_10_.refs_12_.refs_17_), channel_id=1, source_target_pairs={{0,8},{4,12},{8,0},{12,4},{16,24},{20,28},{24,16},{28,20},{1,9},{5... | collective-permute-start | bytes 1990664 | tf_op jit(solution)/shard_map/ppermute | solution.py:835
  97.3 26.7 %collective-permute-start.23 = (bf16[3,96,1152]{2,1,0:T(8,128)(2,1)S(1)}, bf16[3,96,1152]{2,1,0:T(8,128)(2,1)S(1)}, u32[]{:S(2)}, u32[]{:S(2)}) collective-permute-start(bf16[3,96,1152]{2,1,0:T(8,128)(2,1)S(1)} %pad_maximum_fusion.7.refs_10_.refs_12_.refs_17_), channel_id=1, source_target_pairs={{0,16},{4,20},{8,24},{12,28},{16,0},{20,4},{24,8},{28,12},{1,17},{... | collective-permute-start | bytes 1990664 | tf_op jit(solution)/shard_map/ppermute | solution.py:835
  143.0 30.8 %collective-permute-start.31 = (bf16[3,288,768]{2,1,0:T(8,128)(2,1)S(1)}, bf16[3,288,768]{2,1,0:T(8,128)(2,1)}, u32[]{:S(2)}, u32[]{:S(2)}) collective-permute-start(bf16[3,288,768]{2,1,0:T(8,128)(2,1)S(1)} %pad_maximum_fusion.4.refs_8_), channel_id=1, source_target_pairs={{0,8},{4,12},{8,0},{12,4},{16,24},{20,28},{24,16},{28,20},{1,9},{5... | collective-permute-start | bytes 3981320 | tf_op jit(solution)/shard_map/ppermute | solution.py:835
  143.9 30.5 %collective-permute-start.32 = (bf16[3,288,768]{2,1,0:T(8,128)(2,1)S(1)}, bf16[3,288,768]{2,1,0:T(8,128)(2,1)}, u32[]{:S(2)}, u32[]{:S(2)}) collective-permute-start(bf16[3,288,768]{2,1,0:T(8,128)(2,1)S(1)} %pad_maximum_fusion.4.refs_8_), channel_id=1, source_target_pairs={{0,16},{4,20},{8,24},{12,28},{16,0},{20,4},{24,8},{28,12},{1,17},{... | collective-permute-start | bytes 3981320 | tf_op jit(solution)/shard_map/ppermute | solution.py:835
  177.8 26.9 %collective-permute-start.35 = (bf16[3,144,768]{2,1,0:T(8,128)(2,1)S(1)}, bf16[3,144,768]{2,1,0:T(8,128)(2,1)S(1)}, u32[]{:S(2)}, u32[]{:S(2)}) collective-permute-start(bf16[3,144,768]{2,1,0:T(8,128)(2,1)S(1)} %slice.134), channel_id=1, source_target_pairs={{0,16},{4,20},{8,24},{12,28},{16,0},{20,4},{24,8},{28,12},{1,17},{... | collective-permute-start | bytes 1990664 | tf_op jit(solution)/shard_map/ppermute | solution.py:835
  179.1 25.6 %collective-permute-start.36 = (bf16[3,144,768]{2,1,0:T(8,128)(2,1)S(1)}, bf16[3,144,768]{2,1,0:T(8,128)(2,1)S(1)}, u32[]{:S(2)}, u32[]{:S(2)}) collective-permute-start(bf16[3,144,768]{2,1,0:T(8,128)(2,1)S(1)} %slice.135), channel_id=1, source_target_pairs={{0,8},{4,12},{8,0},{12,4},{16,24},{20,28},{24,16},{28,20},{1,9},{5... | collective-permute-start | bytes 1990664 | tf_op jit(solution)/shard_map/ppermute | solution.py:835
  241.3 106.4 %reduce-scatter.3.cloned.1.call-start = ((), (), s32[]{:S(2)}) async-start(), calls=%async_computation.3 | async-start | bytes 4423680 | tf_op jit(solution)/shard_map/reduce_scatter | solution.py:1147
  263.1 49.5 %collective-permute-start.44 = (bf16[2,4,144,768]{3,2,1,0:T(8,128)(2,1)}, bf16[2,4,144,768]{3,2,1,0:T(8,128)(2,1)S(1)}, u32[]{:S(2)}, u32[]{:S(2)}) collective-permute-start(bf16[2,4,144,768]{3,2,1,0:T(8,128)(2,1)} %get-tuple-element.199), channel_id=1, source_target_pairs={{0,8},{4,12},{8,0},{12,4},{16,24},{20,28},{24,16},{28,20},{1,9},{5... | collective-permute-start | bytes 5308424 | tf_op jit(solution)/shard_map/ppermute | solution.py:835
  263.9 50.1 %collective-permute-start.45 = (bf16[2,4,144,768]{3,2,1,0:T(8,128)(2,1)}, bf16[2,4,144,768]{3,2,1,0:T(8,128)(2,1)}, u32[]{:S(2)}, u32[]{:S(2)}) collective-permute-start(bf16[2,4,144,768]{3,2,1,0:T(8,128)(2,1)} %get-tuple-element.201), channel_id=1, source_target_pairs={{0,16},{4,20},{8,24},{12,28},{16,0},{20,4},{24,8},{28,12},{1,17},{... | collective-permute-start | bytes 5308424 | tf_op jit(solution)/shard_map/ppermute | solution.py:835
  279.5 111.4 %reduce-scatter.5.cloned.1.call-start = ((), (), s32[]{:S(2)}) async-start(), calls=%async_computation.5 | async-start | bytes 2211840 | tf_op jit(solution)/shard_map/reduce_scatter | solution.py:1171
  318.5 25.5 %collective-permute-start.47 = (bf16[4,144,768]{2,1,0:T(8,128)(2,1)}, bf16[4,144,768]{2,1,0:T(8,128)(2,1)S(1)}, u32[]{:S(2)}, u32[]{:S(2)}) collective-permute-start(bf16[4,144,768]{2,1,0:T(8,128)(2,1)} %get-tuple-element.232), channel_id=1, source_target_pairs={{0,16},{4,20},{8,24},{12,28},{16,0},{20,4},{24,8},{28,12},{1,17},{... | collective-permute-start | bytes 2654216 | tf_op jit(solution)/shard_map/ppermute | solution.py:835
  351.6 100.6 %all-gather.9.cloned.1.call-start = ((), (), s32[]{:S(2)}) async-start(), calls=%async_computation.4 | async-start | bytes 1327104 | tf_op jit(solution)/shard_map/all_gather | solution.py:1173
  351.9 31.2 %collective-permute-start.56 = (bf16[2,304,1152]{2,1,0:T(8,128)(2,1)S(1)}, bf16[2,304,1152]{2,1,0:T(8,128)(2,1)S(1)}, u32[]{:S(2)}, u32[]{:S(2)}) collective-permute-start(bf16[2,304,1152]{2,1,0:T(8,128)(2,1)S(1)} %pad_maximum_fusion.3), channel_id=1, source_target_pairs={{0,16},{4,20},{8,24},{12,28},{16,0},{20,4},{24,8},{28,12},{1,17},{... | collective-permute-start | bytes 4202504 | tf_op jit(solution)/shard_map/ppermute | solution.py:835
  353.3 37.1 %collective-permute-start.55 = (bf16[2,368,1152]{2,1,0:T(8,128)(2,1)S(1)}, bf16[2,368,1152]{2,1,0:T(8,128)(2,1)S(1)}, u32[]{:S(2)}, u32[]{:S(2)}) collective-permute-start(bf16[2,368,1152]{2,1,0:T(8,128)(2,1)S(1)} %pad_maximum_fusion.2), channel_id=1, source_target_pairs={{0,8},{4,12},{8,0},{12,4},{16,24},{20,28},{24,16},{28,20},{1,9},{5... | collective-permute-start | bytes 5087240 | tf_op jit(solution)/shard_map/ppermute | solution.py:835
  394.6 29.5 %collective-permute-start.61 = (bf16[288,768]{1,0:T(8,128)(2,1)}, bf16[288,768]{1,0:T(8,128)(2,1)}, u32[]{:S(2)}, u32[]{:S(2)}) collective-permute-start(bf16[288,768]{1,0:T(8,128)(2,1)} %bitcast.130), channel_id=1, source_target_pairs={{0,16},{4,20},{8,24},{12,28},{16,0},{20,4},{24,8},{28,12},{1,17},{... | collective-permute-start | bytes 1327112 | tf_op jit(solution)/shard_map/ppermute | solution.py:835
  394.7 44.0 %collective-permute-start.66 = (bf16[288,768]{1,0:T(8,128)(2,1)}, bf16[288,768]{1,0:T(8,128)(2,1)S(1)}, u32[]{:S(2)}, u32[]{:S(2)}) collective-permute-start(bf16[288,768]{1,0:T(8,128)(2,1)} %bitcast.131), channel_id=1, source_target_pairs={{0,4},{4,0},{8,12},{12,8},{16,20},{20,16},{24,28},{28,24},{1,5},{5... | collective-permute-start | bytes 1327112 | tf_op jit(solution)/shard_map/ppermute | solution.py:835
  414.0 25.1 %collective-permute-start.59 = (bf16[144,1152]{1,0:T(8,128)(2,1)S(1)}, bf16[144,1152]{1,0:T(8,128)(2,1)S(1)}, u32[]{:S(2)}, u32[]{:S(2)}) collective-permute-start(bf16[144,1152]{1,0:T(8,128)(2,1)S(1)} %get-tuple-element.302), channel_id=1, source_target_pairs={{0,1},{1,2},{2,3},{3,0},{4,5},{5,6},{6,7},{7,4},{8,9},{9,10},{10,1... | collective-permute-start | bytes 995336 | tf_op jit(solution)/shard_map/ppermute | solution.py:899
  425.1 25.8 %collective-permute-start.67 = (bf16[288,768]{1,0:T(8,128)(2,1)}, bf16[288,768]{1,0:T(8,128)(2,1)}, u32[]{:S(2)}, u32[]{:S(2)}) collective-permute-start(bf16[288,768]{1,0:T(8,128)(2,1)} %collective-permute-done.60.refs_1_), channel_id=1, source_target_pairs={{0,4},{4,0},{8,12},{12,8},{16,20},{20,16},{24,28},{28,24},{1,5},{5... | collective-permute-start | bytes 1327112 | tf_op jit(solution)/shard_map/ppermute | solution.py:835
  (123 other events, 1054.9 us)
Sparse Core Ops, SparseCore 0:
  10.2 38.2 all-gather.10
  82.6 51.6 all-gather.12
  241.4 37.9 all-gather.6
  282.2 65.4 reduce-scatter.2
  351.7 39.1 reduce-scatter.4
  394.4 30.6 all-gather.8

commit v10 on v9

--- a/solution.py
+++ b/solution.py
@@ -291,7 +291,7 @@
     pair_w, down_w = r["pair_w"].at[step], r["down_w"].at[step]
     wait_for(pair_w, r["pair_sems"].at[step])
     wait_for(down_w, r["down_sems"].at[step])
-    sub = 256
+    sub = tile
     for n in range(tile // sub):
         lanes = slice(n * sub, (n + 1) * sub)
         gate = matmul(second[...], pair_w[0, :, lanes])

time: 501 us -> 501 us (level)
  no operation moved by 1% of the time
where the time goes in v10:
time: 501 us; the launch traced here: 493 us
  Pallas kernels  185 us (37%)
  waiting for transfers between devices  134 us (27%)
  starting transfers between devices  89.4 us (18%)
  local copies, waits for them, and re-layouts  30 us (6%)
  other arithmetic  22.9 us (5%)
  between operations  16.7 us (3%)
  matrix products  14.7 us (3%)
    ppermute x56, waiting for transfers between devices, swap(): return lax.ppermute(array, 'bucket', across(bit))  75.6 us
    ppermute x56, starting transfers between devices, swap(): return lax.ppermute(array, 'bucket', across(bit))  61.3 us
    pallas_call x3, Pallas kernels, ffn_call(): pl.pallas_call(functools.partial(ffn_kernel, count, js, names), grid=(len...  51.8 us
    pallas_call x4, Pallas kernels, by_column(): pl.pallas_call(call, out_shape=shapes, grid_spec=pltpu.PrefetchScalarGrid...  39.1 us
    pallas_call x1, Pallas kernels, attend_back_call(): pl.pallas_call(attend_back_kernel, grid=(tokens // BLOCK,), out_shape=str...  24 us
    ppermute x6, waiting for transfers between devices, modulation_parts(): lax.ppermute(pick(parts, (place + by) % fsdp_count), 'fsdp', shifts(fsdp_...  20.2 us
    pallas_call x1, Pallas kernels, first_call(): pl.pallas_call(functools.partial(first_kernel, count), out_shape=(struct(...  18.9 us
    all_gather x2, waiting for transfers between devices, gather_z(): full = after(lax.all_gather(piece, 'fsdp', axis=0, tiled=False), *others)  13.9 us
  transfers between devices with their start and end apart: 86, of which 28 were waited for; matrix products, arithmetic and copies ran while one was open for 11% of the time, Pallas kernels for 33%

profile of v10, /device:TPU:25, one launch (start us, length us, event | category | flops | bytes accessed | tf_op | source)
XLA Modules:
  0.0 492.5 jit_solution(5525606711968203029)
XLA Ops:
  23.2 10.8 %collective-permute-done.4 = f32[8,2304]{1,0:T(8,128)S(1)} collective-permute-done((f32[8,2304]{1,0:T(8,128)S(1)}, f32[8,2304]{1,0:T(8,128)S(1)}, u32[]{:S(2)}, u32[]{:S(2)}) %collective-permute-start.4) | collective-permute-done | bytes 73760 | tf_op jit(solution)/shard_map/ppermute | solution.py:1002
  34.6 13.9 %all-gather.11.cloned.1.call-done = bf16[576,1152]{1,0:T(8,128)(2,1)} async-done(((bf16[144,1152]{1,0:T(8,128)(2,1)}), bf16[576,1152]{1,0:T(8,128)(2,1)}) %all-gather.11.cloned.1.call-update) | async-done | bytes 1327120 | tf_op jit(solution)/shard_map/all_gather | solution.py:854
  65.2 9.9 %collective-permute-done.9 = bf16[96,1152]{1,0:T(8,128)(2,1)} collective-permute-done((bf16[96,1152]{1,0:T(8,128)(2,1)}, bf16[96,1152]{1,0:T(8,128)(2,1)}, u32[]{:S(2)}, u32[]{:S(2)}) %collective-permute-start.9) | collective-permute-done | bytes 221216 | tf_op jit(solution)/shard_map/ppermute | solution.py:848
  98.1 18.9 %shard_map.187 = (bf16[1152,512]{1,0:T(8,128)(2,1)}, bf16[512,1152]{1,0:T(8,128)(2,1)}, bf16[512,1152]{1,0:T(8,128)(2,1)}, bf16[512,1152]{1,0:T(8,128)(2,1)}, bf16[4,1152,1152]{2,1,0:T(8,128)(2,1)}) custom-call(s32[7]{0:T(128)} %stack.87.where_ref.refs_0_, bf16[512,1152]{1,0:T(8,128)(2,1)} %x_ref.2, f32[8,2304]{1,0:T(8,128)} %fusion.39.mod_ref, ...), custom_call_target="tpu_custom_call" | custom-call | flops 20000000000 | bytes 1000 | tf_op jit(solution)/shard_map/pallas_call | solution.py:579
  117.0 7.0 %collective-permute-done.19 = f32[8,4608]{1,0:T(8,128)S(1)} collective-permute-done((f32[8,4608]{1,0:T(8,128)S(1)}, f32[8,4608]{1,0:T(8,128)S(1)}, u32[]{:S(2)}, u32[]{:S(2)}) %collective-permute-start.19) | collective-permute-done | bytes 147488 | tf_op jit(solution)/shard_map/ppermute | solution.py:1002
  126.7 12.6 %shard_map.188 = (bf16[1152,512]{1,0:T(8,128)(2,1)}, f32[512,1152]{1,0:T(8,128)}, f32[512,1152]{1,0:T(8,128)}, bf16[512,1152]{1,0:T(8,128)(2,1)}) custom-call(bf16[512,1152]{1,0:T(8,128)(2,1)} %get-tuple-element.157.query_ref, bf16[512,1152]{1,0:T(8,128)(2,1)} %get-tuple-element.158.keys_ref, bf16[512,1152]{1,0:T(8,128)(2,1)} %get-tuple-element.159.values_ref, ...), custom_call_target="tpu_custom_call" | custom-call | flops 2000000000 | bytes 1000 | tf_op jit(solution)/shard_map/pallas_call | solution.py:599
  150.9 12.0 %shard_map.189 = (bf16[1,768,512]{2,1,0:T(8,128)(2,1)}, bf16[1,2,512,768]{3,2,1,0:T(8,128)(2,1)}, bf16[1152,512]{1,0:T(8,128)(2,1)}, bf16[512,1152]{1,0:T(8,128)...) custom-call(s32[7]{0:T(128)} %stack.87.where_ref.refs_0_, bf16[512,1152]{1,0:T(8,128)(2,1)} %get-tuple-element.165.refs_1_, ...), custom_call_target="tpu_custom_call" | custom-call | flops 2000000000 | bytes 1000 | tf_op jit(solution)/shard_map/pallas_call | solution.py:688
  162.9 10.9 %collective-permute-done.31.refs_8_ = bf16[3,288,768]{2,1,0:T(8,128)(2,1)} collective-permute-done((bf16[3,288,768]{2,1,0:T(8,128)(2,1)S(1)}, bf16[3,288,768]{2,1,0:T(8,128)(2,1)}, u32[]{:S(2)}, u32[]{:S(2)}) %collective-permute-start.31) | collective-permute-done | bytes 1327136 | tf_op jit(solution)/shard_map/ppermute | solution.py:835
  181.4 22.7 %shard_map.190 = (bf16[2,768,512]{2,1,0:T(8,128)(2,1)}, bf16[2,2,512,768]{3,2,1,0:T(8,128)(2,1)}, f32[512,1152]{1,0:T(8,128)}, f32[512,1152]{1,0:T(8,128)}) custom-call(s32[7]{0:T(128)} %stack.87.where_ref.refs_0_, bf16[512,1152]{1,0:T(8,128)(2,1)} %get-tuple-element.165.refs_1_, bf16[512,1152]{1,0:T(8,128)(2,1)} %get-tuple-element.203.refs_2_.refs_5_.refs_3_, ...), custom_call_target="tpu_custom_call" | custom-call | flops 24000000000 | bytes 1000 | tf_op jit(solution)/shard_map/pallas_call | solution.py:688
  208.3 17.0 %shard_map.191 = (bf16[1,768,512]{2,1,0:T(8,128)(2,1)}, bf16[1,2,512,768]{3,2,1,0:T(8,128)(2,1)}, bf16[512,1152]{1,0:T(8,128)(2,1)}, f32[512,1152]{1,0:T(8,128)}...) custom-call(s32[7]{0:T(128)} %stack.87.where_ref.refs_0_, bf16[512,1152]{1,0:T(8,128)(2,1)} %get-tuple-element.165.refs_1_, ...), custom_call_target="tpu_custom_call" | custom-call | flops 12000000000 | bytes 1000 | tf_op jit(solution)/shard_map/pallas_call | solution.py:688
  229.9 9.0 %shard_map.192 = bf16[4,4,288,768]{3,2,1,0:T(8,128)(2,1)} custom-call(s32[7]{0:T(128)} %stack.87.where_ref.refs_0_, bf16[1152,512]{1,0:T(8,128)(2,1)} %get-tuple-element.192.turned_ref, bf16[1,2,512,768]{3,2,1,0:T(8,128)(2,1)} %get-tuple-element.193.own_ref, bf16[2,2,512,768]{3,2,1,0:T(8,128)(2,1)} %get-tuple-element.194.near_ref, ...), custom_call_target="tpu_custom_call" | custom-call | flops 3000000000 | bytes 1000 | tf_op jit(solution)/shard_map/pallas_call | solution.py:708
  241.2 6.3 %shard_map.193 = bf16[4,4,96,1152]{3,2,1,0:T(8,128)(2,1)} custom-call(s32[7]{0:T(128)} %stack.87.where_ref.refs_0_, bf16[1,768,512]{2,1,0:T(8,128)(2,1)} %get-tuple-element.188.refs_0_, bf16[2,768,512]{2,1,0:T(8,128)(2,1)} %get-tuple-element.189.refs_1_, bf16[1,768,512]{2,1,0:T(8,128)(2,1)} %get-tuple-element.190.refs_2_, ...), custom_call_target="tpu_custom_call" | custom-call | flops 3000000000 | bytes 1000 | tf_op jit(solution)/shard_map/pallas_call | solution.py:757
  251.8 11.0 %shard_map.194 = (bf16[2,4,144,768]{3,2,1,0:T(8,128)(2,1)}, bf16[2,4,144,768]{3,2,1,0:T(8,128)(2,1)}, bf16[2,4,144,768]{3,2,1,0:T(8,128)(2,1)}, bf16[2,4,144,768]{3,2,1,0:T(8,128)(2,1)}) custom-call(s32[7]{0:T(128)} %stack.87.where_ref.refs_0_, bf16[1152,512]{1,0:T(8,128)(2,1)} %get-tuple-element.192.turned_ref, ...), custom_call_target="tpu_custom_call" | custom-call | flops 3000000000 | bytes 1000 | tf_op jit(solution)/shard_map/pallas_call | solution.py:708
  266.8 7.4 %shard_map.195 = bf16[4,4,96,1152]{3,2,1,0:T(8,128)(2,1)} custom-call(s32[7]{0:T(128)} %stack.87.where_ref.refs_0_, bf16[1,768,512]{2,1,0:T(8,128)(2,1)} %get-tuple-element.188.refs_0_, bf16[2,768,512]{2,1,0:T(8,128)(2,1)} %get-tuple-element.189.refs_1_, bf16[1,768,512]{2,1,0:T(8,128)(2,1)} %get-tuple-element.190.refs_2_, ...), custom_call_target="tpu_custom_call" | custom-call | flops 3000000000 | bytes 1000 | tf_op jit(solution)/shard_map/pallas_call | solution.py:757
  279.4 24.0 %shard_map.196.joint_back_ref = bf16[512,3456]{1,0:T(8,128)(2,1)} custom-call(bf16[512,1152]{1,0:T(8,128)(2,1)} %get-tuple-element.157.query_ref, bf16[512,1152]{1,0:T(8,128)(2,1)} %get-tuple-element.158.keys_ref, bf16[512,1152]{1,0:T(8,128)(2,1)} %get-tuple-element.159.values_ref, bf16[512,1152]{1,0:T(8,128)(2,1)} %get-tuple-element.221.branch_back_ref, ...), custom_call_target="tpu_custom_call" | custom-call | flops 8000000000 | bytes 1000 | tf_op jit(solution)/shard_map/pallas_call | solution.py:781
  303.3 8.9 %shard_map.197 = bf16[4,4,144,1152]{3,2,1,0:T(8,128)(2,1)} custom-call(s32[7]{0:T(128)} %stack.87.where_ref.refs_0_, bf16[1152,512]{1,0:T(8,128)(2,1)} %get-tuple-element.210.first_ref, bf16[1152,512]{1,0:T(8,128)(2,1)} %get-tuple-element.211.attended_ref, bf16[512,3456]{1,0:T(8,128)(2,1)} %shard_map.196.joint_back_ref, ...), custom_call_target="tpu_custom_call" | custom-call | flops 3000000000 | bytes 1000 | tf_op jit(solution)/shard_map/pallas_call | solution.py:708
  318.9 13.1 %shard_map.198 = (f32[512,1152]{1,0:T(8,128)}, f32[8,2304]{1,0:T(8,128)}) custom-call(bf16[512,3456]{1,0:T(8,128)(2,1)} %shard_map.196.joint_back_ref, bf16[512,1152]{1,0:T(8,128)(2,1)} %x_ref.2, f32[512,1152]{1,0:T(8,128)} %get-tuple-element.216.middle_back_ref, f32[8,2304]{1,0:T(8,128)} %fusion.39.mod_ref, bf16[4,1152,1152]{2,1,0:T(8,128)(2,1)} %get-tuple-element.164.weight), custom_call_target="tpu_custom_call" | custom-call | flops 2000000000 | bytes 1000 | tf_op jit(solution)/shard_map/pallas_call | solution.py:804
  332.0 10.3 %shard_map.199 = (bf16[2,4,80,1152]{3,2,1,0:T(8,128)(2,1)}, bf16[2,4,80,1152]{3,2,1,0:T(8,128)(2,1)}, bf16[2,4,64,1152]{3,2,1,0:T(8,128)(2,1)}, bf16[2,4,64,1152]{3,2,1,0:T(8,128)(2,1)}) custom-call(s32[7]{0:T(128)} %stack.87.where_ref.refs_0_, bf16[1152,512]{1,0:T(8,128)(2,1)} %get-tuple-element.210.first_ref, ...), custom_call_target="tpu_custom_call" | custom-call | flops 3000000000 | bytes 1000 | tf_op jit(solution)/shard_map/pallas_call | solution.py:708
  362.9 19.8 %collective-permute-done.56 = bf16[2,304,1152]{2,1,0:T(8,128)(2,1)S(1)} collective-permute-done((bf16[2,304,1152]{2,1,0:T(8,128)(2,1)S(1)}, bf16[2,304,1152]{2,1,0:T(8,128)(2,1)S(1)}, u32[]{:S(2)}, u32[]{:S(2)}) %collective-permute-start.56) | collective-permute-done | bytes 1400864 | tf_op jit(solution)/shard_map/ppermute | solution.py:835
  383.8 6.2 %collective-permute-done.55 = bf16[2,368,1152]{2,1,0:T(8,128)(2,1)S(1)} collective-permute-done((bf16[2,368,1152]{2,1,0:T(8,128)(2,1)S(1)}, bf16[2,368,1152]{2,1,0:T(8,128)(2,1)S(1)}, u32[]{:S(2)}, u32[]{:S(2)}) %collective-permute-start.55) | collective-permute-done | bytes 1695776 | tf_op jit(solution)/shard_map/ppermute | solution.py:835
  397.8 7.9 %collective-permute-done.58 = bf16[304,1152]{1,0:T(8,128)(2,1)} collective-permute-done((bf16[304,1152]{1,0:T(8,128)(2,1)}, bf16[304,1152]{1,0:T(8,128)(2,1)}, u32[]{:S(2)}, u32[]{:S(2)}) %collective-permute-start.58) | collective-permute-done | bytes 700448 | tf_op jit(solution)/shard_map/ppermute | solution.py:835
  416.8 7.1 %collective-permute-done.61.refs_2_ = bf16[288,768]{1,0:T(8,128)(2,1)} collective-permute-done((bf16[288,768]{1,0:T(8,128)(2,1)}, bf16[288,768]{1,0:T(8,128)(2,1)}, u32[]{:S(2)}, u32[]{:S(2)}) %collective-permute-start.61) | collective-permute-done | bytes 442400 | tf_op jit(solution)/shard_map/ppermute | solution.py:835
  424.8 10.9 %collective-permute-start.67 = (bf16[288,768]{1,0:T(8,128)(2,1)}, bf16[288,768]{1,0:T(8,128)(2,1)}, u32[]{:S(2)}, u32[]{:S(2)}) collective-permute-start(bf16[288,768]{1,0:T(8,128)(2,1)} %collective-permute-done.60.refs_1_), channel_id=1, source_target_pairs={{0,4},{4,0},{8,12},{12,8},{16,20},{20,16},{24,28},{28,24},{1,5},{5... | collective-permute-start | bytes 1327112 | tf_op jit(solution)/shard_map/ppermute | solution.py:835
  479.3 6.2 %shard_map.201 = (f32[288,3456]{1,0:T(8,128)}, f32[288,1152]{1,0:T(8,128)}, f32[768,1152]{1,0:T(8,128)}) custom-call(s32[7]{0:T(128)} %stack.87.where_ref.refs_0_, bf16[240,1152]{1,0:T(8,128)(2,1)} %copy-done.26, bf16[240,1152]{1,0:T(8,128)(2,1)} %copy-done.25, bf16[240,1152]{1,0:T(8,128)(2,1)} %collective-permute-done.72.refs_2_, ...), custom_call_target="tpu_custom_call" | custom-call | flops 4000000000 | bytes 1000 | tf_op jit(solution)/shard_map/pallas_call | solution.py:768
  (382 shorter events, 192.3 us)
Async XLA Ops:
  7.2 41.3 %all-gather.11.cloned.1.call-start = ((), (), s32[]{:S(2)}) async-start(), calls=%async_computation.6 | async-start | bytes 1658880 | tf_op jit(solution)/shard_map/all_gather | solution.py:854
  9.2 131.8 %all-gather.13.cloned.1.call-start = ((), (), s32[]{:S(2)}) async-start(), calls=%async_computation.7 | async-start | bytes 2211840 | tf_op jit(solution)/shard_map/all_gather | solution.py:854
  49.9 25.2 %collective-permute-start.6 = (bf16[3,144,1152]{2,1,0:T(8,128)(2,1)S(1)}, bf16[3,144,1152]{2,1,0:T(8,128)(2,1)}, u32[]{:S(2)}, u32[]{:S(2)}) collective-permute-start(bf16[3,144,1152]{2,1,0:T(8,128)(2,1)S(1)} %pad_maximum_fusion.6.refs_0_), channel_id=1, source_target_pairs={{0,8},{4,12},{8,0},{12,4},{16,24},{20,28},{24,16},{28,20},{1,9},{5... | collective-permute-start | bytes 2985992 | tf_op jit(solution)/shard_map/ppermute | solution.py:835
  82.5 196.6 %all-gather.7.cloned.1.call-start = ((), (), s32[]{:S(2)}) async-start(), calls=%async_computation.2 | async-start | bytes 3317760 | tf_op jit(solution)/shard_map/all_gather | solution.py:1129
  93.7 30.2 %collective-permute-start.19 = (f32[8,4608]{1,0:T(8,128)S(1)}, f32[8,4608]{1,0:T(8,128)S(1)}, u32[]{:S(2)}, u32[]{:S(2)}) collective-permute-start(f32[8,4608]{1,0:T(8,128)S(1)} %get-tuple-element.312), channel_id=1, source_target_pairs={{0,2},{1,3},{2,0},{3,1},{4,6},{5,7},{6,4},{7,5},{8,10},{9,11},{10,... | collective-permute-start | bytes 442376 | tf_op jit(solution)/shard_map/ppermute | solution.py:1002
  95.5 28.5 %collective-permute-start.20 = (f32[8,4608]{1,0:T(8,128)S(1)}, f32[8,4608]{1,0:T(8,128)S(1)}, u32[]{:S(2)}, u32[]{:S(2)}) collective-permute-start(f32[8,4608]{1,0:T(8,128)S(1)} %get-tuple-element.311), channel_id=1, source_target_pairs={{0,3},{1,0},{2,1},{3,2},{4,7},{5,4},{6,5},{7,6},{8,11},{9,8},{10,9... | collective-permute-start | bytes 442376 | tf_op jit(solution)/shard_map/ppermute | solution.py:1002
  97.0 26.9 %collective-permute-start.22 = (bf16[3,96,1152]{2,1,0:T(8,128)(2,1)S(1)}, bf16[3,96,1152]{2,1,0:T(8,128)(2,1)S(1)}, u32[]{:S(2)}, u32[]{:S(2)}) collective-permute-start(bf16[3,96,1152]{2,1,0:T(8,128)(2,1)S(1)} %pad_maximum_fusion.7.refs_10_.refs_12_.refs_17_), channel_id=1, source_target_pairs={{0,8},{4,12},{8,0},{12,4},{16,24},{20,28},{24,16},{28,20},{1,9},{5... | collective-permute-start | bytes 1990664 | tf_op jit(solution)/shard_map/ppermute | solution.py:835
  97.3 26.7 %collective-permute-start.23 = (bf16[3,96,1152]{2,1,0:T(8,128)(2,1)S(1)}, bf16[3,96,1152]{2,1,0:T(8,128)(2,1)S(1)}, u32[]{:S(2)}, u32[]{:S(2)}) collective-permute-start(bf16[3,96,1152]{2,1,0:T(8,128)(2,1)S(1)} %pad_maximum_fusion.7.refs_10_.refs_12_.refs_17_), channel_id=1, source_target_pairs={{0,16},{4,20},{8,24},{12,28},{16,0},{20,4},{24,8},{28,12},{1,17},{... | collective-permute-start | bytes 1990664 | tf_op jit(solution)/shard_map/ppermute | solution.py:835
  143.0 30.8 %collective-permute-start.31 = (bf16[3,288,768]{2,1,0:T(8,128)(2,1)S(1)}, bf16[3,288,768]{2,1,0:T(8,128)(2,1)}, u32[]{:S(2)}, u32[]{:S(2)}) collective-permute-start(bf16[3,288,768]{2,1,0:T(8,128)(2,1)S(1)} %pad_maximum_fusion.4.refs_8_), channel_id=1, source_target_pairs={{0,8},{4,12},{8,0},{12,4},{16,24},{20,28},{24,16},{28,20},{1,9},{5... | collective-permute-start | bytes 3981320 | tf_op jit(solution)/shard_map/ppermute | solution.py:835
  143.9 30.5 %collective-permute-start.32 = (bf16[3,288,768]{2,1,0:T(8,128)(2,1)S(1)}, bf16[3,288,768]{2,1,0:T(8,128)(2,1)}, u32[]{:S(2)}, u32[]{:S(2)}) collective-permute-start(bf16[3,288,768]{2,1,0:T(8,128)(2,1)S(1)} %pad_maximum_fusion.4.refs_8_), channel_id=1, source_target_pairs={{0,16},{4,20},{8,24},{12,28},{16,0},{20,4},{24,8},{28,12},{1,17},{... | collective-permute-start | bytes 3981320 | tf_op jit(solution)/shard_map/ppermute | solution.py:835
  177.8 26.3 %collective-permute-start.35 = (bf16[3,144,768]{2,1,0:T(8,128)(2,1)S(1)}, bf16[3,144,768]{2,1,0:T(8,128)(2,1)S(1)}, u32[]{:S(2)}, u32[]{:S(2)}) collective-permute-start(bf16[3,144,768]{2,1,0:T(8,128)(2,1)S(1)} %slice.134), channel_id=1, source_target_pairs={{0,16},{4,20},{8,24},{12,28},{16,0},{20,4},{24,8},{28,12},{1,17},{... | collective-permute-start | bytes 1990664 | tf_op jit(solution)/shard_map/ppermute | solution.py:835
  179.1 25.0 %collective-permute-start.36 = (bf16[3,144,768]{2,1,0:T(8,128)(2,1)S(1)}, bf16[3,144,768]{2,1,0:T(8,128)(2,1)S(1)}, u32[]{:S(2)}, u32[]{:S(2)}) collective-permute-start(bf16[3,144,768]{2,1,0:T(8,128)(2,1)S(1)} %slice.135), channel_id=1, source_target_pairs={{0,8},{4,12},{8,0},{12,4},{16,24},{20,28},{24,16},{28,20},{1,9},{5... | collective-permute-start | bytes 1990664 | tf_op jit(solution)/shard_map/ppermute | solution.py:835
  240.9 106.4 %reduce-scatter.3.cloned.1.call-start = ((), (), s32[]{:S(2)}) async-start(), calls=%async_computation.3 | async-start | bytes 4423680 | tf_op jit(solution)/shard_map/reduce_scatter | solution.py:1147
  262.7 49.5 %collective-permute-start.44 = (bf16[2,4,144,768]{3,2,1,0:T(8,128)(2,1)}, bf16[2,4,144,768]{3,2,1,0:T(8,128)(2,1)S(1)}, u32[]{:S(2)}, u32[]{:S(2)}) collective-permute-start(bf16[2,4,144,768]{3,2,1,0:T(8,128)(2,1)} %get-tuple-element.199), channel_id=1, source_target_pairs={{0,8},{4,12},{8,0},{12,4},{16,24},{20,28},{24,16},{28,20},{1,9},{5... | collective-permute-start | bytes 5308424 | tf_op jit(solution)/shard_map/ppermute | solution.py:835
  263.5 50.1 %collective-permute-start.45 = (bf16[2,4,144,768]{3,2,1,0:T(8,128)(2,1)}, bf16[2,4,144,768]{3,2,1,0:T(8,128)(2,1)}, u32[]{:S(2)}, u32[]{:S(2)}) collective-permute-start(bf16[2,4,144,768]{3,2,1,0:T(8,128)(2,1)} %get-tuple-element.201), channel_id=1, source_target_pairs={{0,16},{4,20},{8,24},{12,28},{16,0},{20,4},{24,8},{28,12},{1,17},{... | collective-permute-start | bytes 5308424 | tf_op jit(solution)/shard_map/ppermute | solution.py:835
  279.1 111.4 %reduce-scatter.5.cloned.1.call-start = ((), (), s32[]{:S(2)}) async-start(), calls=%async_computation.5 | async-start | bytes 2211840 | tf_op jit(solution)/shard_map/reduce_scatter | solution.py:1171
  318.1 25.5 %collective-permute-start.47 = (bf16[4,144,768]{2,1,0:T(8,128)(2,1)}, bf16[4,144,768]{2,1,0:T(8,128)(2,1)S(1)}, u32[]{:S(2)}, u32[]{:S(2)}) collective-permute-start(bf16[4,144,768]{2,1,0:T(8,128)(2,1)} %get-tuple-element.232), channel_id=1, source_target_pairs={{0,16},{4,20},{8,24},{12,28},{16,0},{20,4},{24,8},{28,12},{1,17},{... | collective-permute-start | bytes 2654216 | tf_op jit(solution)/shard_map/ppermute | solution.py:835
  351.2 100.6 %all-gather.9.cloned.1.call-start = ((), (), s32[]{:S(2)}) async-start(), calls=%async_computation.4 | async-start | bytes 1327104 | tf_op jit(solution)/shard_map/all_gather | solution.py:1173
  351.5 31.2 %collective-permute-start.56 = (bf16[2,304,1152]{2,1,0:T(8,128)(2,1)S(1)}, bf16[2,304,1152]{2,1,0:T(8,128)(2,1)S(1)}, u32[]{:S(2)}, u32[]{:S(2)}) collective-permute-start(bf16[2,304,1152]{2,1,0:T(8,128)(2,1)S(1)} %pad_maximum_fusion.3), channel_id=1, source_target_pairs={{0,16},{4,20},{8,24},{12,28},{16,0},{20,4},{24,8},{28,12},{1,17},{... | collective-permute-start | bytes 4202504 | tf_op jit(solution)/shard_map/ppermute | solution.py:835
  352.9 37.1 %collective-permute-start.55 = (bf16[2,368,1152]{2,1,0:T(8,128)(2,1)S(1)}, bf16[2,368,1152]{2,1,0:T(8,128)(2,1)S(1)}, u32[]{:S(2)}, u32[]{:S(2)}) collective-permute-start(bf16[2,368,1152]{2,1,0:T(8,128)(2,1)S(1)} %pad_maximum_fusion.2), channel_id=1, source_target_pairs={{0,8},{4,12},{8,0},{12,4},{16,24},{20,28},{24,16},{28,20},{1,9},{5... | collective-permute-start | bytes 5087240 | tf_op jit(solution)/shard_map/ppermute | solution.py:835
  394.2 29.7 %collective-permute-start.61 = (bf16[288,768]{1,0:T(8,128)(2,1)}, bf16[288,768]{1,0:T(8,128)(2,1)}, u32[]{:S(2)}, u32[]{:S(2)}) collective-permute-start(bf16[288,768]{1,0:T(8,128)(2,1)} %bitcast.130), channel_id=1, source_target_pairs={{0,16},{4,20},{8,24},{12,28},{16,0},{20,4},{24,8},{28,12},{1,17},{... | collective-permute-start | bytes 1327112 | tf_op jit(solution)/shard_map/ppermute | solution.py:835
  394.3 44.2 %collective-permute-start.66 = (bf16[288,768]{1,0:T(8,128)(2,1)}, bf16[288,768]{1,0:T(8,128)(2,1)S(1)}, u32[]{:S(2)}, u32[]{:S(2)}) collective-permute-start(bf16[288,768]{1,0:T(8,128)(2,1)} %bitcast.131), channel_id=1, source_target_pairs={{0,4},{4,0},{8,12},{12,8},{16,20},{20,16},{24,28},{28,24},{1,5},{5... | collective-permute-start | bytes 1327112 | tf_op jit(solution)/shard_map/ppermute | solution.py:835
  413.6 25.1 %collective-permute-start.59 = (bf16[144,1152]{1,0:T(8,128)(2,1)S(1)}, bf16[144,1152]{1,0:T(8,128)(2,1)S(1)}, u32[]{:S(2)}, u32[]{:S(2)}) collective-permute-start(bf16[144,1152]{1,0:T(8,128)(2,1)S(1)} %get-tuple-element.302), channel_id=1, source_target_pairs={{0,1},{1,2},{2,3},{3,0},{4,5},{5,6},{6,7},{7,4},{8,9},{9,10},{10,1... | collective-permute-start | bytes 995336 | tf_op jit(solution)/shard_map/ppermute | solution.py:899
  424.8 25.6 %collective-permute-start.67 = (bf16[288,768]{1,0:T(8,128)(2,1)}, bf16[288,768]{1,0:T(8,128)(2,1)}, u32[]{:S(2)}, u32[]{:S(2)}) collective-permute-start(bf16[288,768]{1,0:T(8,128)(2,1)} %collective-permute-done.60.refs_1_), channel_id=1, source_target_pairs={{0,4},{4,0},{8,12},{12,8},{16,20},{20,16},{24,28},{28,24},{1,5},{5... | collective-permute-start | bytes 1327112 | tf_op jit(solution)/shard_map/ppermute | solution.py:835
  (123 other events, 1055.9 us)
Sparse Core Ops, SparseCore 0:
  10.2 38.2 all-gather.10
  82.6 51.6 all-gather.12
  241.1 37.9 all-gather.6
  281.8 65.4 reduce-scatter.2
  351.3 39.0 reduce-scatter.4
  394.0 30.6 all-gather.8
